TPU v7x, 128 devices: a whole 4x4x4 slice. The times are simulated.
128 devices in a mesh: tok: 8 (over y_lo, x), chan: 16 (over z, y_hi, core).
Axes of the slice: x: 4, y: 4 (y_hi: 2, y_lo: 2; y = y_hi * 2 + y_lo), z: 4, core: 2. Of those that a mesh axis runs over, the one named last changes fastest.
Arguments:
- acts: bfloat16 [4096, 28672], P('tok', 'chan'), may hold values from -6 to 6
- target: bfloat16 [4096, 8192], P('tok', 'chan'), may hold values from -6 to 6
- proj_b: bfloat16 [2048, 28672], P(None, 'chan'), may hold values from -0.03125 to 0.03125
- proj_a: bfloat16 [8192, 2048], P('chan'), may hold values from -0.125 to 0.125
Outputs:
- grad_a: float32 [8192, 2048], P('chan', 'tok')
- grad_b: float32 [2048, 28672], P('tok', 'chan')
All inputs are finite; a program needn't handle non-finite values.
Results may differ from a plain program's by a relative error of at most 0.004.
Values may be sent and summed in bfloat16 or wider, within the bound.
No kernel may reach another device: no remote copies, remote signals or barrier semaphores. Data moves between devices by JAX's collectives and lax.ppermute only.
A program may use at most 192 MiB of HBM per device.

v0:
```python
import jax
import jax.numpy as jnp
from jax import lax
from jax.sharding import PartitionSpec as P


def contract_rows(left, right):
    return lax.dot_general(
        left, right, (((0,), (0,)), ((), ())), preferred_element_type=jnp.float32
    )


def local(acts, target, proj_b, proj_a):
    partial_value = lax.dot_general(
        acts, proj_b, (((1,), (1,)), ((), ())), preferred_element_type=jnp.float32
    )
    codes = lax.psum(partial_value, "chan").astype(jnp.bfloat16)
    predicted = lax.dot_general(
        codes, proj_a, (((1,), (1,)), ((), ())), preferred_element_type=jnp.float32
    )
    residual = (target.astype(jnp.float32) - predicted).astype(jnp.bfloat16)
    grad_partial = jnp.dot(residual, proj_a, preferred_element_type=jnp.float32)
    grad_codes = lax.psum(grad_partial, "chan").astype(jnp.bfloat16)
    factor_scale = -2.0 / (acts.shape[0] * lax.axis_size("tok"))
    term_a = contract_rows(residual, codes)
    grad_a = lax.psum_scatter(term_a, "tok", scatter_dimension=1, tiled=True) * factor_scale
    grad_b = (
        lax.psum_scatter(contract_rows(grad_codes, acts), "tok", scatter_dimension=0, tiled=True)
        * factor_scale
    )
    return (grad_a, grad_b)


def solution(mesh):
    return jax.shard_map(
        local,
        mesh=mesh,
        in_specs=(P("tok", "chan"), P("tok", "chan"), P(None, "chan"), P("chan", None)),
        out_specs=(P("chan", "tok"), P("tok", "chan")),
        check_vma=False,
    )
```

profile of v0, /device:TPU:1, one launch (start us, length us, event | category | flops | bytes accessed | tf_op | source)
XLA Modules:
  0.0 443.0 jit_solution(3188283281578601597)
XLA Ops:
  7.2 0.0 copy-start
  7.2 0.0 reduce-scatter.3.cloned.1.call-start
  7.2 9.7 %fusion.6 = f32[512,2048]{1,0:T(8,128)} fusion(bf16[512,1792]{1,0:T(8,128)(2,1)} %param.4, bf16[2048,1792]{1,0:T(8,128)(2,1)} %param.6), kind=kOutput, calls=%fused_computation.9 | convolution fusion | flops 3758096384 | bytes 13369344 | tf_op jit(solution)/shard_map/dot_general | solution.py:14
  16.9 0.0 copy-start.2
  16.9 102.1 %all-reduce.2 = bf16[512,2048]{1,0:T(8,128)(2,1)} all-reduce(f32[512,2048]{1,0:T(8,128)} %fusion.6), channel_id=1, replica_groups=mesh['tok'=8,'chan'=16] {'chan'}, use_global_device_ids=true, to_apply=%region_0.0 | all-reduce | flops 1048576 | bytes 6291456 | tf_op jit(solution)/shard_map/psum | solution.py:17
  119.1 0.0 copy-done
  119.1 0.0 copy-done.2
  119.1 0.0 copy-start.1
  119.1 3.0 fusion.2
  122.1 0.0 copy-done.1
  122.1 3.3 fusion.9
  125.4 0.0 reduce-scatter.3.cloned.1.call-update
  125.4 0.0 reduce-scatter.5.cloned.1.call-start
  125.4 3.2 fusion.7
  128.6 140.3 %all-reduce.3 = bf16[512,2048]{1,0:T(8,128)(2,1)} all-reduce(f32[512,2048]{1,0:T(8,128)} %fusion.7), channel_id=1, replica_groups=mesh['tok'=8,'chan'=16] {'chan'}, use_global_device_ids=true, to_apply=%region_2.0 | all-reduce | flops 1048576 | bytes 6291456 | tf_op jit(solution)/shard_map/psum | solution.py:23
  268.9 11.4 %fusion.8 = f32[2048,1792]{1,0:T(8,128)} fusion(bf16[512,2048]{1,0:T(8,128)(2,1)} %all-reduce.3, bf16[512,1792]{1,0:T(8,128)(2,1)} %param.4), kind=kOutput, calls=%fused_computation.11 | convolution fusion | flops 3758096384 | bytes 18612224 | tf_op jit(solution)/shard_map/dot_general | solution.py:8
  280.2 0.0 reduce-scatter.5.cloned.1.call-update
  280.3 0.0 reduce-scatter.3.cloned.1.call-done
  280.3 1.9 broadcast_multiply_fusion.1
  282.2 151.2 %reduce-scatter.5.cloned.1.call-done = f32[256,1792]{1,0:T(8,128)} async-done(((f32[2048,1792]{1,0:T(8,128)}), f32[256,1792]{1,0:T(8,128)}) %reduce-scatter.5.cloned.1.call-update) | async-done | bytes 1835024 | tf_op jit(solution)/shard_map/reduce_scatter | solution.py:28
  433.4 2.8 broadcast_multiply_fusion
Async XLA Ops:
  7.2 111.9 %copy-start = (bf16[512,2048]{1,0:T(8,128)(2,1)S(1)}, bf16[512,2048]{1,0:T(8,128)(2,1)}, u32[]{:S(2)}) copy-start(bf16[512,2048]{1,0:T(8,128)(2,1)} %param.7) | copy-start | bytes 6291460
  7.2 273.1 %reduce-scatter.3.cloned.1.call-start = ((), (), s32[]{:S(2)}) async-start(), calls=%async_computation.2 | async-start | bytes 4718592 | tf_op jit(solution)/shard_map/reduce_scatter | solution.py:26
  16.9 102.2 %copy-start.2 = (bf16[512,512]{1,0:T(8,128)(2,1)S(1)}, bf16[512,512]{1,0:T(8,128)(2,1)}, u32[]{:S(2)}) copy-start(bf16[512,512]{1,0:T(8,128)(2,1)} %param.5) | copy-start | bytes 1572868
  119.1 3.0 copy-start.1
  125.4 308.0 %reduce-scatter.5.cloned.1.call-start = ((), (), s32[]{:S(2)}) async-start(), calls=%async_computation.3 | async-start | bytes 16515072 | tf_op jit(solution)/shard_map/reduce_scatter | solution.py:28
Sparse Core Ops, SparseCore 0:
  125.5 54.4 reduce-scatter.2
  280.4 152.9 reduce-scatter.4
where the time goes:
time: 443 us
  blocking collectives  242 us (55%)
  waiting for transfers between devices  151 us (34%)
  matrix products  30.5 us (7%)
  between operations  14.1 us (3%)
  other arithmetic  4.72 us (1%)
    reduce_scatter x1, waiting for transfers between devices, local(): lax.psum_scatter(contract_rows(grad_codes, acts), 'tok', scatter_dimensio...  151 us
    psum x1, blocking collectives, local(): grad_codes = lax.psum(grad_partial, 'chan').astype(jnp.bfloat16)  140 us
    psum x1, blocking collectives, local(): codes = lax.psum(partial_value, 'chan').astype(jnp.bfloat16)  102 us
    dot_general x2, matrix products, contract_rows(): lax.dot_general(left, right, (((0,), (0,)), ((), ())), preferred_element_...  14.6 us
    dot_general x1, matrix products, local(): lax.dot_general(acts, proj_b, (((1,), (1,)), ((), ())), preferred_element...  9.68 us
  transfers between devices with their start and end apart: 2, of which 1 were waited for; matrix products, arithmetic and copies ran while one was open for 4% of the time, Pallas kernels for 0%

commit v1 on v0

v1 whole, which is shorter than its diff:
```python
import jax
import jax.numpy as jnp
import numpy as np
from jax import lax
from jax.sharding import Mesh, PartitionSpec as P

BF, F32 = jnp.bfloat16, jnp.float32
TOK, CHAN, ZY = ("y_lo", "x"), ("z", "y_hi", "core"), ("z", "y_hi")


def shift(array, axis, size, step):
    return lax.ppermute(array, axis, [(i, (i + step) % size) for i in range(size)])


def swap(array, axis):
    return shift(array, axis, 2, 1)


def rows_dot(left, right):
    return lax.dot_general(left, right, (((1,), (1,)), ((), ())), preferred_element_type=F32)


def cols_dot(left, right):
    return lax.dot_general(left, right, (((0,), (0,)), ((), ())), preferred_element_type=F32)


def scatter_sum(partial, axes, parts):
    blocks = partial.astype(BF).reshape(parts, partial.shape[0] // parts, partial.shape[1])
    blocks = lax.all_to_all(blocks, axes, 0, 0)
    total = blocks[0].astype(F32)
    for i in range(1, parts):
        total = total + blocks[i].astype(F32)
    return total


def local(acts, target, proj_b, proj_a):
    core, y_lo, x = lax.axis_index("core"), lax.axis_index("y_lo"), lax.axis_index("x")
    tokens, rank = acts.shape[0], proj_b.shape[0]
    half = tokens // 2
    sub = half // 8
    width = rank // 8
    scale = -2.0 / (tokens * 8)

    def half_of(array, which):
        return lax.dynamic_slice_in_dim(array, which * half, half, 0)

    far = [shift(acts, "x", 4, k) for k in (1, 2, 3)]

    both_a = jnp.concatenate([proj_a, swap(proj_a, "core")], 0)
    both_t = jnp.concatenate([half_of(target, core), swap(half_of(target, 1 - core), "core")], 1)

    theirs = rows_dot(half_of(acts, 1 - core), proj_b)
    arrived = swap(theirs, "core")
    mine = rows_dot(half_of(acts, core), proj_b)
    mine = lax.optimization_barrier(mine) + arrived
    codes_sub = scatter_sum(mine, ZY, 8).astype(BF)
    codes = lax.all_to_all(jnp.broadcast_to(codes_sub[None], (8, sub, rank)), ZY, 0, 0).reshape(half, rank)

    residual = (both_t.astype(F32) - rows_dot(codes, both_a)).astype(BF)
    partial = jnp.dot(residual, both_a, preferred_element_type=F32)
    grad_sub = scatter_sum(partial, ZY, 8).astype(BF)

    split = grad_sub.reshape(sub, 2, 4, width)
    own = lax.dynamic_index_in_dim(split, y_lo, 1, False)
    other = lax.dynamic_index_in_dim(split, 1 - y_lo, 1, False)
    split = jnp.concatenate([own, other], 2).transpose(1, 0, 2)
    split = jnp.broadcast_to(split[:, None], (4, 8, sub, 2 * width)).reshape(32, sub, 2 * width)
    gathered = lax.all_to_all(split, ("x", "z", "y_hi"), 0, 0).reshape(4, half, 2 * width)
    gathered_o = swap(gathered, "core")
    first = core == 0
    grad_codes = jnp.stack(
        [jnp.where(first, gathered, gathered_o), jnp.where(first, gathered_o, gathered)], 1
    ).reshape(4, tokens, 2 * width)
    acts_all = jnp.concatenate([acts] + far, 0)
    grad_codes = jnp.concatenate(
        [lax.dynamic_index_in_dim(grad_codes, (x + 4 - k) % 4, 0, False) for k in range(4)], 0
    )
    away = cols_dot(grad_codes[:, width:], acts_all).astype(BF)
    away = swap(away, "y_lo")
    here = lax.optimization_barrier(cols_dot(grad_codes[:, :width], acts_all))
    grad_b = (here + away.astype(F32)) * scale

    outs = target.shape[1]
    codes_all = jnp.concatenate([codes, swap(codes, "core")], 0)
    residual_all = jnp.concatenate([residual[:, :outs], swap(residual[:, outs:], "core")], 0)
    term = cols_dot(codes_all, residual_all)
    grad_a = (scatter_sum(term, TOK, 8) * scale).T
    return (grad_a, grad_b)


def solution(mesh):
    fine = Mesh(np.reshape(mesh.devices, (2, 4, 4, 2, 2)), ("y_lo", "x", "z", "y_hi", "core"))
    return jax.shard_map(
        local,
        mesh=fine,
        in_specs=(P(TOK, CHAN), P(TOK, CHAN), P(None, CHAN), P(CHAN, None)),
        out_specs=(P(CHAN, TOK), P(TOK, CHAN)),
        check_vma=False,
    )
```

time: 443 us -> 235 us (0.53)
  blocking collectives: 242 us -> 23.9 us
  waiting for transfers between devices: 151 us -> 110 us
  starting transfers between devices: 0.08 us -> 37.3 us
  local copies, waits for them, and re-layouts: 0.02 us -> 22.4 us
  between operations: 14.1 us -> 0.82 us
    psum x2 -> x0, blocking collectives: 242 us -> none  [the longest x1 140 us: local(): grad_codes = lax.psum(grad_partial, 'chan').astype(jnp.bfloat16)]
    reduce_scatter x2 -> x0, waiting for transfers between devices: 151 us -> none  [the longest x1 151 us: local(): lax.psum_scatter(contract_rows(grad_codes, acts), 'tok', scatter_dimensio...]
    all_to_all x0 -> x4, waiting for transfers between devices: none -> 97.3 us  [the longest x1 62.6 us: local(): lax.all_to_all(split, ('x', 'z', 'y_hi'), 0, 0).reshape(4, half, 2 * width)]
    all_to_all x0 -> x1, blocking collectives: none -> 23.9 us  [scatter_sum(): blocks = lax.all_to_all(blocks, axes, 0, 0)]
    ppermute x0 -> x10, starting transfers between devices: none -> 19 us  [shift(): lax.ppermute(array, axis, [(i, (i + step) % size) for i in range(size)])]
    all_to_all x0 -> x4, starting transfers between devices: none -> 18.4 us  [the longest x2 8.47 us: scatter_sum(): blocks = lax.all_to_all(blocks, axes, 0, 0)]
    ppermute x0 -> x10, waiting for transfers between devices: none -> 12.6 us  [shift(): lax.ppermute(array, axis, [(i, (i + step) % size) for i in range(size)])]
    unnamed x6 -> x16, local copies, waits for them, and re-layouts: 0.02 us -> 10.3 us
  transfers between devices with their start and end apart: 2 -> 14, of which waited for: 1 -> 7; matrix products, arithmetic and copies ran while one was open for 4% -> 18% of each run, Pallas kernels for 0% -> 0%
where the time goes in v1:
time: 235 us
  waiting for transfers between devices  110 us (47%)
  starting transfers between devices  37.3 us (16%)
  matrix products  32.4 us (14%)
  blocking collectives  23.9 us (10%)
  local copies, waits for them, and re-layouts  22.4 us (10%)
  other arithmetic  8.02 us (3%)
    all_to_all x1, waiting for transfers between devices, local(): lax.all_to_all(split, ('x', 'z', 'y_hi'), 0, 0).reshape(4, half, 2 * width)  62.6 us
    all_to_all x2, waiting for transfers between devices, scatter_sum(): blocks = lax.all_to_all(blocks, axes, 0, 0)  27.3 us
    all_to_all x1, blocking collectives, scatter_sum(): blocks = lax.all_to_all(blocks, axes, 0, 0)  23.9 us
    ppermute x10, starting transfers between devices, shift(): lax.ppermute(array, axis, [(i, (i + step) % size) for i in range(size)])  19 us
    dot_general x3, matrix products, rows_dot(): lax.dot_general(left, right, (((1,), (1,)), ((), ())), preferred_element_...  17.1 us
    ppermute x10, waiting for transfers between devices, shift(): lax.ppermute(array, axis, [(i, (i + step) % size) for i in range(size)])  12.6 us
    dot_general x3, matrix products, cols_dot(): lax.dot_general(left, right, (((0,), (0,)), ((), ())), preferred_element_...  10.7 us
    unnamed x16, local copies, waits for them, and re-layouts  10.3 us
  transfers between devices with their start and end apart: 14, of which 7 were waited for; matrix products, arithmetic and copies ran while one was open for 18% of the time, Pallas kernels for 0%

profile of v1, /device:TPU:1, one launch (start us, length us, event | category | flops | bytes accessed | tf_op | source)
XLA Modules:
  0.0 234.7 jit_solution(16176948888211043924)
XLA Ops:
  0.6 7.0 %fusion.6 = f32[256,2048]{1,0:T(8,128)} fusion(bf16[2048,1792]{1,0:T(8,128)(2,1)} %param.6, bf16[512,1792]{1,0:T(8,128)(2,1)} %param.4, s32[]{:T(128)S(6)} %select_n.60), kind=kOutput, calls=%fused_computation.16 | convolution fusion | flops 1879048192 | bytes 10354692 | tf_op jit(solution)/shard_map/dot_general | solution.py:20
  9.0 5.5 %fusion.8 = f32[256,2048]{1,0:T(8,128)S(1)} fusion(bf16[2048,1792]{1,0:T(8,128)(2,1)} %param.6, bf16[512,1792]{1,0:T(8,128)(2,1)} %param.4, s32[]{:T(128)S(6)} %select_n.59), kind=kOutput, calls=%fused_computation.18 | convolution fusion | flops 1879048192 | bytes 10354692 | tf_op jit(solution)/shard_map/dot_general | solution.py:20
  18.0 23.9 %all_to_all.25 = bf16[8,32,2048]{2,1,0:T(8,128)(2,1)S(1)} all-to-all(bf16[8,32,2048]{2,1,0:T(8,128)(2,1)S(1)} %bitcast.48), channel_id=1, replica_groups=mesh['y_lo'=2,'x'=4,'z'=4,'y_hi'=2,'core'=2] {'z','y_hi'}, dimensions={0} | all-to-all | bytes 2097152 | tf_op jit(solution)/shard_map/all_to_all | solution.py:29
  43.1 3.6 %all-to-all-start.1 = ((bf16[8,32,2048]{2,1,0:T(8,128)(2,1)}), bf16[8,32,2048]{2,1,0:T(8,128)(2,1)S(1)}, u32[]{:S(2)}, u32[]{:S(2)}) async-start(bf16[8,32,2048]{2,1,0:T(8,128)(2,1)} %broadcast_in_dim.7), calls=%async_computation.1 | async-start | bytes 2097152 | tf_op jit(solution)/shard_map/all_to_all | solution.py:57
  51.1 3.2 %constant_dynamic-update-slice_fusion = bf16[1024,2048]{1,0:T(8,128)(2,1)} fusion(bf16[1024,2048]{1,0:T(8,128)(2,1)} %constant_dynamic-update-slice_fusion.1, bf16[512,2048]{1,0:T(8,128)(2,1)} %collective-permute-done.3), kind=kLoop, calls=%fused_computation.35 | loop fusion | bytes 4194304 | tf_op jit(solution)/shard_map/concatenate | solution.py:49
  54.3 7.4 %all-to-all-done.1 = bf16[8,32,2048]{2,1,0:T(8,128)(2,1)S(1)} async-done(((bf16[8,32,2048]{2,1,0:T(8,128)(2,1)}), bf16[8,32,2048]{2,1,0:T(8,128)(2,1)S(1)}, u32[]{:S(2)}, u32[]{:S(2)}) %all-to-all-start.1) | async-done | bytes 1048608 | tf_op jit(solution)/shard_map/all_to_all | solution.py:57
  61.7 4.7 %subtract_convert_fusion = (bf16[256,1024]{1,0:T(8,128)(2,1)}, f32[256,1024]{1,0:T(8,128)S(1)}) fusion(bf16[256,512]{1,0:T(8,128)(2,1)} %collective-permute-done.2, bf16[256,512]{1,0:T(8,128)(2,1)S(1)} %get-tuple-element.10, bf16[256,2048]{1,0:T(8,128)(2,1)S(1)} %bitcast.50, bf16[1024,2048]{1,0:T(8,128)(2,1)} %constant_dynamic-update-slice_fusion), kind=kOutput, calls=%fused_computation.15 | convolution fusion | flops 1075314688 | bytes 7340032 | tf_op jit(solution)/shard_map/dot_general | solution.py:20
  66.4 4.5 %convolution_convert_fusion.2 = bf16[256,2048]{1,0:T(8,128)(2,1)} fusion(bf16[1024,2048]{1,0:T(8,128)(2,1)} %constant_dynamic-update-slice_fusion, f32[256,1024]{1,0:T(8,128)S(1)} %get-tuple-element.15, bf16[256,512]{1,0:T(8,128)(2,1)} %collective-permute-done.2, bf16[256,512]{1,0:T(8,128)(2,1)S(1)} %get-tuple-element.10), kind=kOutput, calls=%fused_computation.2 | convolution fusion | flops 1075838976 | bytes 6815744 | tf_op jit(solution)/shard_map/dot_general | solution.py:60
  70.9 4.1 %all-to-all-start.3 = ((bf16[8,32,2048]{2,1,0:T(8,128)(2,1)}), bf16[8,32,2048]{2,1,0:T(8,128)(2,1)S(1)}, u32[]{:S(2)}, u32[]{:S(2)}) async-start(bf16[8,32,2048]{2,1,0:T(8,128)(2,1)} %bitcast.6), calls=%async_computation.3 | async-start | bytes 2097152 | tf_op jit(solution)/shard_map/all_to_all | solution.py:29
  78.7 11.2 %all-to-all-done.3 = bf16[8,32,2048]{2,1,0:T(8,128)(2,1)S(1)} async-done(((bf16[8,32,2048]{2,1,0:T(8,128)(2,1)}), bf16[8,32,2048]{2,1,0:T(8,128)(2,1)S(1)}, u32[]{:S(2)}, u32[]{:S(2)}) %all-to-all-start.3) | async-done | bytes 1048608 | tf_op jit(solution)/shard_map/all_to_all | solution.py:29
  91.3 6.3 %all-to-all-start.4 = ((bf16[32,32,512]{2,1,0:T(8,128)(2,1)}), bf16[32,32,512]{2,1,0:T(8,128)(2,1)S(1)}, u32[]{:S(2)}, u32[]{:S(2)}) async-start(bf16[32,32,512]{2,1,0:T(8,128)(2,1)} %bitcast.10), calls=%async_computation.4 | async-start | bytes 2097152 | tf_op jit(solution)/shard_map/all_to_all | solution.py:68
  97.7 2.6 %collective-permute-start.8 = (bf16[512,1792]{1,0:T(8,128)(2,1)}, bf16[512,1792]{1,0:T(8,128)(2,1)}, u32[]{:S(2)}, u32[]{:S(2)}) collective-permute-start(bf16[512,1792]{1,0:T(8,128)(2,1)} %param.4), channel_id=1, source_target_pairs={{0,48},{16,0},{32,16},{48,32},{1,49},{17,1},{33,17},{49,33},{2,50}... | collective-permute-start | bytes 5505032 | tf_op jit(solution)/shard_map/ppermute | solution.py:12
  100.2 3.1 %collective-permute-start.1 = (bf16[256,2048]{1,0:T(8,128)(2,1)}, bf16[256,2048]{1,0:T(8,128)(2,1)}, u32[]{:S(2)}, u32[]{:S(2)}) collective-permute-start(bf16[256,2048]{1,0:T(8,128)(2,1)} %bitcast.51), channel_id=1, source_target_pairs={{0,1},{1,0},{2,3},{3,2},{4,5},{5,4},{6,7},{7,6},{8,9},{9,8},{10,11... | collective-permute-start | bytes 3145736 | tf_op jit(solution)/shard_map/ppermute | solution.py:12
  103.4 2.9 %constant_dynamic-update-slice_fusion.5 = bf16[2048,1792]{1,0:T(8,128)(2,1)} fusion(bf16[512,1792]{1,0:T(8,128)(2,1)} %param.4), kind=kLoop, calls=%fused_computation.40 | loop fusion | bytes 3670016
  106.2 62.6 %all-to-all-done.4 = bf16[32,32,512]{2,1,0:T(8,128)(2,1)S(1)} async-done(((bf16[32,32,512]{2,1,0:T(8,128)(2,1)}), bf16[32,32,512]{2,1,0:T(8,128)(2,1)S(1)}, u32[]{:S(2)}, u32[]{:S(2)}) %all-to-all-start.4) | async-done | bytes 1048608 | tf_op jit(solution)/shard_map/all_to_all | solution.py:68
  168.8 4.7 %collective-permute-start.5 = (bf16[4,256,512]{2,1,0:T(8,128)(2,1)S(1)}, bf16[4,256,512]{2,1,0:T(8,128)(2,1)}, u32[]{:S(2)}, u32[]{:S(2)}) collective-permute-start(bf16[4,256,512]{2,1,0:T(8,128)(2,1)S(1)} %bitcast.46), channel_id=1, source_target_pairs={{0,1},{1,0},{2,3},{3,2},{4,5},{5,4},{6,7},{7,6},{8,9},{9,8},{10,11... | collective-permute-start | bytes 3145736 | tf_op jit(solution)/shard_map/ppermute | solution.py:12
  173.5 2.8 %constant_dynamic-update-slice_fusion.4 = bf16[2048,1792]{1,0:T(8,128)(2,1)} fusion(bf16[2048,1792]{1,0:T(8,128)(2,1)} %constant_dynamic-update-slice_fusion.5, bf16[512,1792]{1,0:T(8,128)(2,1)} %collective-permute-done.6), kind=kLoop, calls=%fused_computation.39 | loop fusion | bytes 3670016
  183.1 4.4 %all-to-all-start.2 = ((bf16[8,256,512]{1,2,0:T(8,128)(2,1)}), bf16[8,256,512]{1,2,0:T(8,128)(2,1)}, u32[]{:S(2)}, u32[]{:S(2)}) async-start(bf16[8,256,512]{1,2,0:T(8,128)(2,1)} %copy.9), calls=%async_computation.2 | async-start | bytes 4194304 | tf_op jit(solution)/shard_map/all_to_all | solution.py:29
  187.5 2.9 %constant_dynamic-update-slice_fusion.2 = bf16[2048,1792]{1,0:T(8,128)(2,1)} fusion(bf16[2048,1792]{1,0:T(8,128)(2,1)} %constant_dynamic-update-slice_fusion.3, bf16[512,1792]{1,0:T(8,128)(2,1)} %collective-permute-done.8), kind=kLoop, calls=%fused_computation.37 | loop fusion | bytes 3670016 | tf_op jit(solution)/shard_map/concatenate | solution.py:74
  194.2 3.0 %convolution_convert_fusion.1 = bf16[256,1792]{1,0:T(8,128)(2,1)} fusion(bf16[2048,1792]{1,0:T(8,128)(2,1)S(1)} %bitcast.44, bf16[2048,512]{1,0:T(8,128)(2,1)S(1)} %pad_maximum_fusion.1), kind=kOutput, calls=%fused_computation.1 | convolution fusion | flops 1879506944 | bytes 9306112 | tf_op jit(solution)/shard_map/dot_general | solution.py:24
  198.5 16.1 %all-to-all-done.2 = bf16[8,256,512]{1,2,0:T(8,128)(2,1)} async-done(((bf16[8,256,512]{1,2,0:T(8,128)(2,1)}), bf16[8,256,512]{1,2,0:T(8,128)(2,1)}, u32[]{:S(2)}, u32[]{:S(2)}) %all-to-all-start.2) | async-done | bytes 2097184 | tf_op jit(solution)/shard_map/all_to_all | solution.py:29
  214.7 2.6 %multiply_bitcast_fusion = f32[512,256]{1,0:T(8,128)} fusion(bf16[8,256,512]{1,2,0:T(8,128)(2,1)} %all-to-all-done.2), kind=kLoop, calls=%fused_computation.24 | loop fusion | flops 2097152 | bytes 2621440 | tf_op jit(solution)/shard_map/transpose | solution.py:87
  217.2 5.2 %fusion.4 = f32[256,1792]{1,0:T(8,128)S(1)} fusion(bf16[2048,1792]{1,0:T(8,128)(2,1)} %constant_dynamic-update-slice_fusion.2, bf16[2048,512]{1,0:T(8,128)(2,1)S(1)} %pad_maximum_fusion.1), kind=kOutput, calls=%fused_computation.11 | convolution fusion | flops 1879048192 | bytes 10223616 | tf_op jit(solution)/shard_map/dot_general | solution.py:24
  222.4 10.8 %collective-permute-done.9 = bf16[256,1792]{1,0:T(8,128)(2,1)S(1)} collective-permute-done((bf16[256,1792]{1,0:T(8,128)(2,1)}, bf16[256,1792]{1,0:T(8,128)(2,1)S(1)}, u32[]{:S(2)}, u32[]{:S(2)}) %collective-permute-start.9) | collective-permute-done | bytes 917536 | tf_op jit(solution)/shard_map/ppermute | solution.py:12
  (49 shorter events, 29.0 us)
Async XLA Ops:
  0.6 8.4 %copy-start = (bf16[512,2048]{1,0:T(8,128)(2,1)S(1)}, bf16[512,2048]{1,0:T(8,128)(2,1)}, u32[]{:S(2)}) copy-start(bf16[512,2048]{1,0:T(8,128)(2,1)} %param.7) | copy-start | bytes 6291460
  7.6 8.5 %collective-permute-start = (f32[256,2048]{1,0:T(8,128)}, f32[256,2048]{1,0:T(8,128)}, u32[]{:S(2)}, u32[]{:S(2)}) collective-permute-start(f32[256,2048]{1,0:T(8,128)} %fusion.6), channel_id=1, source_target_pairs={{0,1},{1,0},{2,3},{3,2},{4,5},{5,4},{6,7},{7,6},{8,9},{9,8},{10,11... | collective-permute-start | bytes 6291464 | tf_op jit(solution)/shard_map/ppermute | solution.py:12
  9.0 42.1 %collective-permute-start.3 = (bf16[512,2048]{1,0:T(8,128)(2,1)S(1)}, bf16[512,2048]{1,0:T(8,128)(2,1)}, u32[]{:S(2)}, u32[]{:S(2)}) collective-permute-start(bf16[512,2048]{1,0:T(8,128)(2,1)S(1)} %copy-done), channel_id=1, source_target_pairs={{0,1},{1,0},{2,3},{3,2},{4,5},{5,4},{6,7},{7,6},{8,9},{9,8},{10,11... | collective-permute-start | bytes 6291464 | tf_op jit(solution)/shard_map/ppermute | solution.py:12
  43.1 18.6 %all-to-all-start.1 = ((bf16[8,32,2048]{2,1,0:T(8,128)(2,1)}), bf16[8,32,2048]{2,1,0:T(8,128)(2,1)S(1)}, u32[]{:S(2)}, u32[]{:S(2)}) async-start(bf16[8,32,2048]{2,1,0:T(8,128)(2,1)} %broadcast_in_dim.7), calls=%async_computation.1 | async-start | bytes 2097152 | tf_op jit(solution)/shard_map/all_to_all | solution.py:57
  47.7 6.6 %collective-permute-start.2 = (bf16[256,512]{1,0:T(8,128)(2,1)S(1)}, bf16[256,512]{1,0:T(8,128)(2,1)}, u32[]{:S(2)}, u32[]{:S(2)}) collective-permute-start(bf16[256,512]{1,0:T(8,128)(2,1)S(1)} %get-tuple-element.11), channel_id=1, source_target_pairs={{0,1},{1,0},{2,3},{3,2},{4,5},{5,4},{6,7},{7,6},{8,9},{9,8},{10,11... | collective-permute-start | bytes 786440 | tf_op jit(solution)/shard_map/ppermute | solution.py:12
  61.7 9.2 %copy-start.1 = (bf16[8,32,2048]{2,1,0:T(8,128)(2,1)}, bf16[8,32,2048]{2,1,0:T(8,128)(2,1)S(1)}, u32[]{:S(2)}) copy-start(bf16[8,32,2048]{2,1,0:T(8,128)(2,1)S(1)} %all-to-all-done.1) | copy-start | bytes 3145732
  70.9 18.9 %all-to-all-start.3 = ((bf16[8,32,2048]{2,1,0:T(8,128)(2,1)}), bf16[8,32,2048]{2,1,0:T(8,128)(2,1)S(1)}, u32[]{:S(2)}, u32[]{:S(2)}) async-start(bf16[8,32,2048]{2,1,0:T(8,128)(2,1)} %bitcast.6), calls=%async_computation.3 | async-start | bytes 2097152 | tf_op jit(solution)/shard_map/all_to_all | solution.py:29
  75.1 98.4 %collective-permute-start.6 = (bf16[512,1792]{1,0:T(8,128)(2,1)}, bf16[512,1792]{1,0:T(8,128)(2,1)}, u32[]{:S(2)}, u32[]{:S(2)}) collective-permute-start(bf16[512,1792]{1,0:T(8,128)(2,1)} %param.4), channel_id=1, source_target_pairs={{0,16},{16,32},{32,48},{48,0},{1,17},{17,33},{33,49},{49,1},{2,18}... | collective-permute-start | bytes 5505032 | tf_op jit(solution)/shard_map/ppermute | solution.py:12
  76.3 100.4 %collective-permute-start.7 = (bf16[512,1792]{1,0:T(8,128)(2,1)}, bf16[512,1792]{1,0:T(8,128)(2,1)S(1)}, u32[]{:S(2)}, u32[]{:S(2)}) collective-permute-start(bf16[512,1792]{1,0:T(8,128)(2,1)} %param.4), channel_id=1, source_target_pairs={{0,32},{16,48},{32,0},{48,16},{1,33},{17,49},{33,1},{49,17},{2,34}... | collective-permute-start | bytes 5505032 | tf_op jit(solution)/shard_map/ppermute | solution.py:12
  91.3 77.5 %all-to-all-start.4 = ((bf16[32,32,512]{2,1,0:T(8,128)(2,1)}), bf16[32,32,512]{2,1,0:T(8,128)(2,1)S(1)}, u32[]{:S(2)}, u32[]{:S(2)}) async-start(bf16[32,32,512]{2,1,0:T(8,128)(2,1)} %bitcast.10), calls=%async_computation.4 | async-start | bytes 2097152 | tf_op jit(solution)/shard_map/all_to_all | solution.py:68
  97.7 89.8 %collective-permute-start.8 = (bf16[512,1792]{1,0:T(8,128)(2,1)}, bf16[512,1792]{1,0:T(8,128)(2,1)}, u32[]{:S(2)}, u32[]{:S(2)}) collective-permute-start(bf16[512,1792]{1,0:T(8,128)(2,1)} %param.4), channel_id=1, source_target_pairs={{0,48},{16,0},{32,16},{48,32},{1,49},{17,1},{33,17},{49,33},{2,50}... | collective-permute-start | bytes 5505032 | tf_op jit(solution)/shard_map/ppermute | solution.py:12
  100.2 78.0 %collective-permute-start.1 = (bf16[256,2048]{1,0:T(8,128)(2,1)}, bf16[256,2048]{1,0:T(8,128)(2,1)}, u32[]{:S(2)}, u32[]{:S(2)}) collective-permute-start(bf16[256,2048]{1,0:T(8,128)(2,1)} %bitcast.51), channel_id=1, source_target_pairs={{0,1},{1,0},{2,3},{3,2},{4,5},{5,4},{6,7},{7,6},{8,9},{9,8},{10,11... | collective-permute-start | bytes 3145736 | tf_op jit(solution)/shard_map/ppermute | solution.py:12
  106.2 70.1 %copy-start.3 = (bf16[256,1024]{1,0:T(8,128)(2,1)S(1)}, bf16[256,1024]{1,0:T(8,128)(2,1)}, u32[]{:S(2)}) copy-start(bf16[256,1024]{1,0:T(8,128)(2,1)} %get-tuple-element.14) | copy-start | bytes 1572868
  168.8 21.5 %collective-permute-start.5 = (bf16[4,256,512]{2,1,0:T(8,128)(2,1)S(1)}, bf16[4,256,512]{2,1,0:T(8,128)(2,1)}, u32[]{:S(2)}, u32[]{:S(2)}) collective-permute-start(bf16[4,256,512]{2,1,0:T(8,128)(2,1)S(1)} %bitcast.46), channel_id=1, source_target_pairs={{0,1},{1,0},{2,3},{3,2},{4,5},{5,4},{6,7},{7,6},{8,9},{9,8},{10,11... | collective-permute-start | bytes 3145736 | tf_op jit(solution)/shard_map/ppermute | solution.py:12
  176.4 1.8 copy-start.2
  176.4 1.8 collective-permute-start.4
  183.1 31.6 %all-to-all-start.2 = ((bf16[8,256,512]{1,2,0:T(8,128)(2,1)}), bf16[8,256,512]{1,2,0:T(8,128)(2,1)}, u32[]{:S(2)}, u32[]{:S(2)}) async-start(bf16[8,256,512]{1,2,0:T(8,128)(2,1)} %copy.9), calls=%async_computation.2 | async-start | bytes 4194304 | tf_op jit(solution)/shard_map/all_to_all | solution.py:29
  190.4 2.5 %slice-start = ((s8[7340032]{0:T(1024)(128)(4,1)}), s8[4194304]{0:T(1024)(128)(4,1)S(1)}, s32[]{:S(2)}) async-start(s8[7340032]{0:T(1024)(128)(4,1)} %bitcast.43), calls=%async_computation.5 | async-start | bytes 8388608
  192.1 2.1 slice-start.1
  197.2 36.1 %collective-permute-start.9 = (bf16[256,1792]{1,0:T(8,128)(2,1)}, bf16[256,1792]{1,0:T(8,128)(2,1)S(1)}, u32[]{:S(2)}, u32[]{:S(2)}) collective-permute-start(bf16[256,1792]{1,0:T(8,128)(2,1)} %convolution_convert_fusion.1), channel_id=1, source_target_pairs={{0,64},{64,0},{1,65},{65,1},{2,66},{66,2},{3,67},{67,3},{4,68},{68... | collective-permute-start | bytes 2752520 | tf_op jit(solution)/shard_map/ppermute | solution.py:12

commit v2 on v1

v2 whole, which is shorter than its diff:
```python
import jax
import jax.numpy as jnp
import numpy as np
from jax import lax
from jax.sharding import Mesh, PartitionSpec as P

BF, F32 = jnp.bfloat16, jnp.float32
TOK, CHAN, ZY = ("y_lo", "x"), ("z", "y_hi", "core"), ("z", "y_hi")


def shift(array, axis, size, step):
    return lax.ppermute(array, axis, [(i, (i + step) % size) for i in range(size)])


def swap(array, axis):
    return shift(array, axis, 2, 1)


def rows_dot(left, right):
    return lax.dot_general(left, right, (((1,), (1,)), ((), ())), preferred_element_type=F32)


def cols_dot(left, right):
    return lax.dot_general(left, right, (((0,), (0,)), ((), ())), preferred_element_type=F32)


def pick(array, index, axis=0):
    return lax.dynamic_index_in_dim(array, index, axis, False)


def total(blocks):
    out = blocks[0].astype(F32)
    for i in range(1, blocks.shape[0]):
        out = out + blocks[i].astype(F32)
    return out


def local(acts, target, proj_b, proj_a):
    core, y_lo, x = lax.axis_index("core"), lax.axis_index("y_lo"), lax.axis_index("x")
    y_hi = lax.axis_index("y_hi")
    tokens, rank = acts.shape[0], proj_b.shape[0]
    outs = target.shape[1]
    half, sub, width = tokens // 2, tokens // 16, rank // 8
    scale = -2.0 / (tokens * 8)

    def half_of(array, which):
        return lax.dynamic_slice_in_dim(array, which * half, half, 0)

    cut = 1280
    mid = cut // 2
    near_a, near_b = acts[:, :cut], acts[:, cut:]
    plus_a, minus_a = shift(near_a, "x", 4, 1), shift(near_a, "x", 4, 3)

    def across(array):
        return lax.ppermute(array, ("y_lo", "y_hi"), [(0, 3), (3, 0), (1, 2), (2, 1)])

    across_a = across(proj_a)
    both_a = [proj_a, swap(proj_a, "core"), across_a, swap(across_a, "core")]
    both_a = jnp.concatenate(both_a, 0)
    wide_t = jnp.concatenate([half_of(target, core), swap(half_of(target, 1 - core), "core")], 1)
    wide_t = wide_t.reshape(4, 2, sub, 2 * outs)
    quarter_t = jnp.concatenate([pick(wide_t, y_hi, 1), swap(pick(wide_t, 1 - y_hi, 1), "y_hi")], 2)
    quarter_t = quarter_t.reshape(4 * sub, 4 * outs)

    theirs = rows_dot(half_of(acts, 1 - core), proj_b)
    arrived = swap(theirs, "core")
    mine = rows_dot(half_of(acts, core), proj_b)
    mine = lax.optimization_barrier(mine) + arrived
    blocks = lax.all_to_all(mine.astype(BF).reshape(8, sub, rank), ZY, 0, 0)
    blocks, plus_a, minus_a = lax.optimization_barrier((blocks, plus_a, minus_a))
    plus_b, minus_b = shift(near_b, "x", 4, 1), shift(near_b, "x", 4, 3)
    far_a = shift(plus_a[:, :mid], "x", 4, 1), shift(minus_a[:, mid:], "x", 4, 3)
    codes_sub = total(blocks).astype(BF)
    codes = lax.all_to_all(jnp.broadcast_to(codes_sub[None], (4, sub, rank)), "z", 0, 0)
    codes = codes.reshape(4 * sub, rank)

    residual = (quarter_t.astype(F32) - rows_dot(codes, both_a)).astype(BF)
    partial = jnp.dot(residual, both_a, preferred_element_type=F32)
    blocks = lax.all_to_all(partial.astype(BF).reshape(4, sub, rank), "z", 0, 0)
    blocks, plus_b, minus_b, far_a = lax.optimization_barrier((blocks, plus_b, minus_b, far_a))
    far_b = shift(plus_b[:, : plus_b.shape[1] // 2], "x", 4, 1), shift(minus_b[:, plus_b.shape[1] // 2 :], "x", 4, 3)
    grad_sub = total(blocks).astype(BF)

    far = jnp.concatenate(list(far_a) + list(far_b), 1)
    row = [acts, jnp.concatenate([plus_a, plus_b], 1), far, jnp.concatenate([minus_a, minus_b], 1)]
    acts_m = jnp.zeros((4, half, acts.shape[1]), BF)
    acts_o = acts_m
    for k in range(4):
        at = ((x + 4 - k) % 4, 0, 0)
        acts_m = lax.dynamic_update_slice(acts_m, half_of(row[k], core)[None], at)
        acts_o = lax.dynamic_update_slice(acts_o, half_of(row[k], 1 - core)[None], at)
    acts_m = acts_m.reshape(4 * half, -1)
    acts_o = acts_o.reshape(4 * half, -1)

    split = grad_sub.reshape(sub, 2, 4, width)
    split = jnp.stack([pick(split, y_lo, 1), pick(split, 1 - y_lo, 1)], 2).reshape(sub, 4, 2 * width)
    split = split.transpose(1, 0, 2)
    split = jnp.broadcast_to(split[:, None], (4, 8, sub, 2 * width)).reshape(32, sub, 2 * width)
    grad_m = lax.all_to_all(split, ("x", "z", "y_hi"), 0, 0).reshape(4 * half, 2 * width)
    grad_o = swap(grad_m, "core")
    away = lax.optimization_barrier(cols_dot(grad_m[:, width:], acts_m))
    away = (away + cols_dot(grad_o[:, width:], acts_o)).astype(BF)
    away = swap(away, "y_lo")
    here = lax.optimization_barrier(cols_dot(grad_m[:, :width], acts_m))
    here = lax.optimization_barrier(here + cols_dot(grad_o[:, :width], acts_o))
    grad_b = (here + away.astype(F32)) * scale

    codes_all = jnp.concatenate([codes, swap(codes, "y_hi")], 0)
    codes_all = jnp.concatenate([codes_all, swap(codes_all, "core")], 0)
    resid = jnp.concatenate([residual[:, : 2 * outs], swap(residual[:, 2 * outs :], "y_hi")], 0)
    resid = jnp.concatenate([resid[:, :outs], swap(resid[:, outs:], "core")], 0)
    term = cols_dot(codes_all, resid).reshape(2, 4 * width, outs)
    term_o = swap(pick(term, 1 - y_lo).astype(BF), "y_lo")
    term = (pick(term, y_lo) + term_o.astype(F32)).astype(BF).reshape(4, width, outs)
    grad_a = (total(lax.all_to_all(term, "x", 0, 0)) * scale).T
    return (grad_a, grad_b)


def solution(mesh):
    fine = Mesh(np.reshape(mesh.devices, (2, 4, 4, 2, 2)), ("y_lo", "x", "z", "y_hi", "core"))
    return jax.shard_map(
        local,
        mesh=fine,
        in_specs=(P(TOK, CHAN), P(TOK, CHAN), P(None, CHAN), P(CHAN, None)),
        out_specs=(P(CHAN, TOK), P(TOK, CHAN)),
        check_vma=False,
    )
```

time: 235 us -> 216 us (0.919); the launches traced: 235 us -> 212 us
  waiting for transfers between devices: 110 us -> 52.7 us
  local copies, waits for them, and re-layouts: 22.4 us -> 52.7 us
  blocking collectives: 23.9 us -> 0 us
  starting transfers between devices: 37.3 us -> 56.7 us
  matrix products: 32.4 us -> 38 us
  other arithmetic: 8.02 us -> 11.1 us
    all_to_all x4 -> x5, waiting for transfers between devices: 97.3 us -> 0.99 us  [the longest x1 0.98 us: local(): grad_a = (total(lax.all_to_all(term, 'x', 0, 0)) * scale).T]
    ppermute x0 -> x1, waiting for transfers between devices: none -> 30 us  [across(): lax.ppermute(array, ('y_lo', 'y_hi'), [(0, 3), (3, 0), (1, 2), (2, 1)])]
    all_to_all x1 -> x0, blocking collectives: 23.9 us -> none  [scatter_sum(): blocks = lax.all_to_all(blocks, axes, 0, 0)]
    unnamed x16 -> x33, local copies, waits for them, and re-layouts: 10.3 us -> 23.5 us
    ppermute x10 -> x20, starting transfers between devices: 19 us -> 28.3 us  [shift(): lax.ppermute(array, axis, [(i, (i + step) % size) for i in range(size)])]
    slice x1 -> x7, local copies, waits for them, and re-layouts: 0.03 us -> 9.24 us  [the longest x1 2.02 us: local(): minus_a[:, mid:]]
    ppermute x10 -> x20, waiting for transfers between devices: 12.6 us -> 21.7 us  [shift(): lax.ppermute(array, axis, [(i, (i + step) % size) for i in range(size)])]
    all_to_all x4 -> x5, starting transfers between devices: 18.4 us -> 25.6 us  [the longest x1 7.37 us: local(): lax.all_to_all(split, ('x', 'z', 'y_hi'), 0, 0).reshape(4 * half, 2 * width)]
  transfers between devices with their start and end apart: 14 -> 26, of which waited for: 7 -> 4; matrix products, arithmetic and copies ran while one was open for 18% -> 43% of each run, Pallas kernels for 0% -> 0%
where the time goes in v2:
time: 216 us; the launch traced here: 212 us
  starting transfers between devices  56.7 us (26%)
  local copies, waits for them, and re-layouts  52.7 us (24%)
  waiting for transfers between devices  52.7 us (24%)
  matrix products  38 us (18%)
  other arithmetic  11.1 us (5%)
    ppermute x1, waiting for transfers between devices, across(): lax.ppermute(array, ('y_lo', 'y_hi'), [(0, 3), (3, 0), (1, 2), (2, 1)])  30 us
    ppermute x20, starting transfers between devices, shift(): lax.ppermute(array, axis, [(i, (i + step) % size) for i in range(size)])  28.3 us
    unnamed x33, local copies, waits for them, and re-layouts  23.5 us
    ppermute x20, waiting for transfers between devices, shift(): lax.ppermute(array, axis, [(i, (i + step) % size) for i in range(size)])  21.7 us
    dot_general x3, matrix products, rows_dot(): lax.dot_general(left, right, (((1,), (1,)), ((), ())), preferred_element_...  19.8 us
    dot_general x5, matrix products, cols_dot(): lax.dot_general(left, right, (((0,), (0,)), ((), ())), preferred_element_...  16 us
    all_to_all x1, starting transfers between devices, local(): lax.all_to_all(split, ('x', 'z', 'y_hi'), 0, 0).reshape(4 * half, 2 * width)  7.37 us
    all_to_all x1, starting transfers between devices, local(): blocks = lax.all_to_all(mine.astype(BF).reshape(8, sub, rank), ZY, 0, 0)  6.39 us
  transfers between devices with their start and end apart: 26, of which 4 were waited for; matrix products, arithmetic and copies ran while one was open for 43% of the time, Pallas kernels for 0%

profile of v2, /device:TPU:1, one launch (start us, length us, event | category | flops | bytes accessed | tf_op | source)
XLA Modules:
  0.0 212.0 jit_solution(12705051328279441525)
XLA Ops:
  0.6 6.9 %fusion.10 = f32[256,2048]{1,0:T(8,128)} fusion(bf16[2048,1792]{1,0:T(8,128)(2,1)} %param.6, bf16[512,1792]{1,0:T(8,128)(2,1)} %param.4, s32[]{:T(128)S(6)} %select_n.69), kind=kOutput, calls=%fused_computation.27 | convolution fusion | flops 1879048192 | bytes 10354692 | tf_op jit(solution)/shard_map/dot_general | solution.py:20
  9.0 2.8 %collective-permute-start.8 = (bf16[512,2048]{1,0:T(8,128)(2,1)}, bf16[512,2048]{1,0:T(8,128)(2,1)}, u32[]{:S(2)}, u32[]{:S(2)}) collective-permute-start(bf16[512,2048]{1,0:T(8,128)(2,1)} %param.7), channel_id=1, source_target_pairs={{0,66},{66,0},{2,64},{64,2},{1,67},{67,1},{3,65},{65,3},{4,70},{70... | collective-permute-start | bytes 6291464 | tf_op jit(solution)/shard_map/ppermute | solution.py:55
  16.4 6.5 %fusion.12 = f32[256,2048]{1,0:T(8,128)} fusion(bf16[2048,1792]{1,0:T(8,128)(2,1)} %param.6, bf16[512,1792]{1,0:T(8,128)(2,1)S(1)} %copy-done.3, s32[]{:T(128)S(6)} %select_n.68), kind=kOutput, calls=%fused_computation.29 | convolution fusion | flops 1879048192 | bytes 10354692 | tf_op jit(solution)/shard_map/dot_general | solution.py:20
  23.4 4.5 %constant_dynamic-update-slice_fusion.3 = bf16[2048,2048]{1,0:T(8,128)(2,1)} fusion(bf16[512,2048]{1,0:T(8,128)(2,1)} %param.7), kind=kLoop, calls=%fused_computation.56 | loop fusion | bytes 4194304
  27.9 30.0 %collective-permute-done.8 = bf16[512,2048]{1,0:T(8,128)(2,1)} collective-permute-done((bf16[512,2048]{1,0:T(8,128)(2,1)}, bf16[512,2048]{1,0:T(8,128)(2,1)}, u32[]{:S(2)}, u32[]{:S(2)}) %collective-permute-start.8) | collective-permute-done | bytes 2097184 | tf_op jit(solution)/shard_map/ppermute | solution.py:55
  58.7 2.9 %add_convert_fusion = bf16[256,2048]{1,0:T(8,128)(2,1)} fusion(f32[256,2048]{1,0:T(8,128)S(1)} %copy-done.7, f32[256,2048]{1,0:T(8,128)} %collective-permute-done), kind=kLoop, calls=%fused_computation.15 | loop fusion | flops 1048576 | bytes 5242880 | tf_op jit(solution)/shard_map/convert_element_type | solution.py:69
  61.5 6.4 %all-to-all-start = ((bf16[8,32,2048]{2,1,0:T(8,128)(2,1)}), bf16[8,32,2048]{2,1,0:T(8,128)(2,1)S(1)}, u32[]{:S(2)}, u32[]{:S(2)}) async-start(bf16[8,32,2048]{2,1,0:T(8,128)(2,1)} %bitcast), calls=%async_computation | async-start | bytes 2097152 | tf_op jit(solution)/shard_map/all_to_all | solution.py:69
  76.4 3.2 %constant_dynamic-update-slice_fusion.2 = bf16[2048,2048]{1,0:T(8,128)(2,1)} fusion(bf16[2048,2048]{1,0:T(8,128)(2,1)} %constant_dynamic-update-slice_fusion.3, bf16[512,2048]{1,0:T(8,128)(2,1)} %collective-permute-done.7), kind=kLoop, calls=%fused_computation.55 | loop fusion | bytes 4194304
  79.6 3.2 %constant_dynamic-update-slice_fusion.1 = bf16[2048,2048]{1,0:T(8,128)(2,1)} fusion(bf16[2048,2048]{1,0:T(8,128)(2,1)} %constant_dynamic-update-slice_fusion.2, bf16[512,2048]{1,0:T(8,128)(2,1)} %collective-permute-done.8), kind=kLoop, calls=%fused_computation.54 | loop fusion | bytes 4194304
  82.8 3.0 %collective-permute-start.6 = (bf16[4,32,1024]{2,1,0:T(8,128)(2,1)}, bf16[4,32,1024]{2,1,0:T(8,128)(2,1)}, u32[]{:S(2)}, u32[]{:S(2)}) collective-permute-start(bf16[4,32,1024]{2,1,0:T(8,128)(2,1)} %get-tuple-element.35), channel_id=1, source_target_pairs={{0,2},{2,0},{1,3},{3,1},{4,6},{6,4},{5,7},{7,5},{8,10},{10,8},{9,1... | collective-permute-start | bytes 786440 | tf_op jit(solution)/shard_map/ppermute | solution.py:12
  86.7 4.0 %all-to-all-start.1 = ((bf16[4,32,2048]{2,1,0:T(8,128)(2,1)}), bf16[4,32,2048]{2,1,0:T(8,128)(2,1)S(1)}, u32[]{:S(2)}, u32[]{:S(2)}) async-start(bf16[4,32,2048]{2,1,0:T(8,128)(2,1)} %broadcast_in_dim.42), calls=%async_computation.1 | async-start | bytes 1048576 | tf_op jit(solution)/shard_map/all_to_all | solution.py:74
  98.8 3.2 %constant_dynamic-update-slice_fusion = bf16[2048,2048]{1,0:T(8,128)(2,1)} fusion(bf16[2048,2048]{1,0:T(8,128)(2,1)} %constant_dynamic-update-slice_fusion.1, bf16[512,2048]{1,0:T(8,128)(2,1)} %collective-permute-done.9), kind=kLoop, calls=%fused_computation.53 | loop fusion | bytes 4194304 | tf_op jit(solution)/shard_map/concatenate | solution.py:59
  102.3 6.4 %fusion.1 = bf16[128,2048]{1,0:T(8,128)(2,1)S(1)} fusion(bf16[128,2048]{1,0:T(8,128)(2,1)S(1)} %bitcast.66, bf16[2048,2048]{1,0:T(8,128)(2,1)} %constant_dynamic-update-slice_fusion, bf16[128,1024]{1,0:T(8,128)(2,1)} %bitcast.6, bf16[128,1024]{1,0:T(8,128)(2,1)S(1)} %bitcast.72), kind=kOutput, calls=%fused_computation.5 | convolution fusion | flops 1075314688 | bytes 9961472 | tf_op jit(solution)/shard_map/dot_general | solution.py:20
  111.7 4.2 %all-to-all-start.3 = ((bf16[4,32,2048]{2,1,0:T(8,128)(2,1)}), bf16[4,32,2048]{2,1,0:T(8,128)(2,1)S(1)}, u32[]{:S(2)}, u32[]{:S(2)}) async-start(bf16[4,32,2048]{2,1,0:T(8,128)(2,1)} %bitcast.13), calls=%async_computation.3 | async-start | bytes 1048576 | tf_op jit(solution)/shard_map/all_to_all | solution.py:79
  116.0 2.8 %collective-permute-start.10 = (bf16[128,1024]{1,0:T(8,128)(2,1)}, bf16[128,1024]{1,0:T(8,128)(2,1)S(1)}, u32[]{:S(2)}, u32[]{:S(2)}) collective-permute-start(bf16[128,1024]{1,0:T(8,128)(2,1)} %get-tuple-element.33), channel_id=1, source_target_pairs={{0,2},{2,0},{1,3},{3,1},{4,6},{6,4},{5,7},{7,5},{8,10},{10,8},{9,1... | collective-permute-start | bytes 786440 | tf_op jit(solution)/shard_map/ppermute | solution.py:12
  123.3 3.9 %collective-permute-start.4 = (bf16[256,2048]{1,0:T(8,128)(2,1)}, bf16[256,2048]{1,0:T(8,128)(2,1)}, u32[]{:S(2)}, u32[]{:S(2)}) collective-permute-start(bf16[256,2048]{1,0:T(8,128)(2,1)} %pad_maximum_fusion), channel_id=1, source_target_pairs={{0,1},{1,0},{2,3},{3,2},{4,5},{5,4},{6,7},{7,6},{8,9},{9,8},{10,11... | collective-permute-start | bytes 3145736 | tf_op jit(solution)/shard_map/ppermute | solution.py:12
  134.6 7.4 %all-to-all-start.4 = ((bf16[32,32,512]{2,1,0:T(8,128)(2,1)}), bf16[32,32,512]{2,1,0:T(8,128)(2,1)}, u32[]{:S(2)}, u32[]{:S(2)}) async-start(bf16[32,32,512]{2,1,0:T(8,128)(2,1)} %bitcast.17), calls=%async_computation.4 | async-start | bytes 2097152 | tf_op jit(solution)/shard_map/all_to_all | solution.py:99
  161.9 2.8 %bitcast_dynamic-update-slice_fusion.1 = (bf16[4,256,1792]{2,1,0:T(8,128)(2,1)}, bf16[4,256,1792]{2,1,0:T(8,128)(2,1)}) fusion(bf16[4,256,1792]{2,1,0:T(8,128)(2,1)} %get-tuple-element.28, s32[]{:T(128)S(6)} %select_n.79, bf16[512,1792]{1,0:T(8,128)(2,1)} %constant_dynamic-update-slice_fusion.6, s32[]{:T(128)S(6)} %select_n.69, ...), kind=kLoop, calls=%fused_computation.20 | loop fusion | bytes 3670028 | tf_op jit(solution)/shard_map/dynamic_update_slice | solution.py:91
  166.0 3.5 %fusion.15 = f32[256,1792]{1,0:T(8,128)S(1)} fusion(bf16[1024,1792]{1,0:T(8,128)(2,1)} %bitcast.23, bf16[1024,512]{1,0:T(8,128)(2,1)} %bitcast.18), kind=kOutput, calls=%fused_computation.32 | convolution fusion | flops 939524096 | bytes 6029312 | tf_op jit(solution)/shard_map/dot_general | solution.py:24
  169.5 11.1 %collective-permute-done.12 = bf16[1024,512]{1,0:T(8,128)(2,1)S(1)} collective-permute-done((bf16[1024,512]{1,0:T(8,128)(2,1)}, bf16[1024,512]{1,0:T(8,128)(2,1)S(1)}, u32[]{:S(2)}, u32[]{:S(2)}) %collective-permute-start.12) | collective-permute-done | bytes 1048608 | tf_op jit(solution)/shard_map/ppermute | solution.py:12
  182.0 3.7 %all-to-all-start.2 = ((bf16[4,256,512]{2,1,0:T(8,128)(2,1)}), bf16[4,256,512]{2,1,0:T(8,128)(2,1)S(1)}, u32[]{:S(2)}, u32[]{:S(2)}) async-start(bf16[4,256,512]{2,1,0:T(8,128)(2,1)} %bitcast.10), calls=%async_computation.2 | async-start | bytes 2097152 | tf_op jit(solution)/shard_map/all_to_all | solution.py:115
  185.6 4.3 %fusion = bf16[256,1792]{1,0:T(8,128)(2,1)} fusion(f32[256,1792]{1,0:T(8,128)S(1)} %fusion.15, bf16[1024,1792]{1,0:T(8,128)(2,1)} %bitcast.63, bf16[1024,512]{1,0:T(8,128)(2,1)} %collective-permute-done.19), kind=kOutput, calls=%fused_computation.2 | convolution fusion | flops 940441600 | bytes 6946816 | tf_op jit(solution)/shard_map/dot_general | solution.py:24
  191.3 3.3 %fusion.18 = f32[256,1792]{1,0:T(8,128)S(1)} fusion(bf16[1024,1792]{1,0:T(8,128)(2,1)} %bitcast.23, bf16[1024,512]{1,0:T(8,128)(2,1)} %bitcast.18), kind=kOutput, calls=%fused_computation.35 | convolution fusion | flops 939524096 | bytes 6029312 | tf_op jit(solution)/shard_map/dot_general | solution.py:24
  198.9 10.5 %collective-permute-done.20 = bf16[256,1792]{1,0:T(8,128)(2,1)} collective-permute-done((bf16[256,1792]{1,0:T(8,128)(2,1)}, bf16[256,1792]{1,0:T(8,128)(2,1)}, u32[]{:S(2)}, u32[]{:S(2)}) %collective-permute-start.20) | collective-permute-done | bytes 917536 | tf_op jit(solution)/shard_map/ppermute | solution.py:12
  (106 shorter events, 70.7 us)
Async XLA Ops:
  7.5 20.4 %collective-permute-start = (f32[256,2048]{1,0:T(8,128)}, f32[256,2048]{1,0:T(8,128)}, u32[]{:S(2)}, u32[]{:S(2)}) collective-permute-start(f32[256,2048]{1,0:T(8,128)} %fusion.10), channel_id=1, source_target_pairs={{0,1},{1,0},{2,3},{3,2},{4,5},{5,4},{6,7},{7,6},{8,9},{9,8},{10,11... | collective-permute-start | bytes 6291464 | tf_op jit(solution)/shard_map/ppermute | solution.py:12
  9.0 49.0 %collective-permute-start.8 = (bf16[512,2048]{1,0:T(8,128)(2,1)}, bf16[512,2048]{1,0:T(8,128)(2,1)}, u32[]{:S(2)}, u32[]{:S(2)}) collective-permute-start(bf16[512,2048]{1,0:T(8,128)(2,1)} %param.7), channel_id=1, source_target_pairs={{0,66},{66,0},{2,64},{64,2},{1,67},{67,1},{3,65},{65,3},{4,70},{70... | collective-permute-start | bytes 6291464 | tf_op jit(solution)/shard_map/ppermute | solution.py:55
  12.9 69.9 %collective-permute-start.1 = (bf16[512,1280]{1,0:T(8,128)(2,1)}, bf16[512,1280]{1,0:T(8,128)(2,1)}, u32[]{:S(2)}, u32[]{:S(2)}) collective-permute-start(bf16[512,1280]{1,0:T(8,128)(2,1)} %slice.90), channel_id=1, source_target_pairs={{0,16},{16,32},{32,48},{48,0},{1,17},{17,33},{33,49},{49,1},{2,18}... | collective-permute-start | bytes 3932168 | tf_op jit(solution)/shard_map/ppermute | solution.py:12
  14.1 71.6 %collective-permute-start.2 = (bf16[512,1280]{1,0:T(8,128)(2,1)}, bf16[512,1280]{1,0:T(8,128)(2,1)}, u32[]{:S(2)}, u32[]{:S(2)}) collective-permute-start(bf16[512,1280]{1,0:T(8,128)(2,1)} %slice.90), channel_id=1, source_target_pairs={{0,48},{16,0},{32,16},{48,32},{1,49},{17,1},{33,17},{49,33},{2,50}... | collective-permute-start | bytes 3932168 | tf_op jit(solution)/shard_map/ppermute | solution.py:12
  15.6 59.2 %collective-permute-start.7 = (bf16[512,2048]{1,0:T(8,128)(2,1)}, bf16[512,2048]{1,0:T(8,128)(2,1)}, u32[]{:S(2)}, u32[]{:S(2)}) collective-permute-start(bf16[512,2048]{1,0:T(8,128)(2,1)} %param.7), channel_id=1, source_target_pairs={{0,1},{1,0},{2,3},{3,2},{4,5},{5,4},{6,7},{7,6},{8,9},{9,8},{10,11... | collective-permute-start | bytes 6291464 | tf_op jit(solution)/shard_map/ppermute | solution.py:12
  27.9 43.9 %collective-permute-start.5 = (bf16[256,512]{1,0:T(8,128)(2,1)S(1)}, bf16[256,512]{1,0:T(8,128)(2,1)}, u32[]{:S(2)}, u32[]{:S(2)}) collective-permute-start(bf16[256,512]{1,0:T(8,128)(2,1)S(1)} %get-tuple-element.37), channel_id=1, source_target_pairs={{0,1},{1,0},{2,3},{3,2},{4,5},{5,4},{6,7},{7,6},{8,9},{9,8},{10,11... | collective-permute-start | bytes 786440 | tf_op jit(solution)/shard_map/ppermute | solution.py:12
  58.0 38.2 %collective-permute-start.9 = (bf16[512,2048]{1,0:T(8,128)(2,1)}, bf16[512,2048]{1,0:T(8,128)(2,1)}, u32[]{:S(2)}, u32[]{:S(2)}) collective-permute-start(bf16[512,2048]{1,0:T(8,128)(2,1)} %collective-permute-done.8), channel_id=1, source_target_pairs={{0,1},{1,0},{2,3},{3,2},{4,5},{5,4},{6,7},{7,6},{8,9},{9,8},{10,11... | collective-permute-start | bytes 6291464 | tf_op jit(solution)/shard_map/ppermute | solution.py:12
  61.5 24.2 %all-to-all-start = ((bf16[8,32,2048]{2,1,0:T(8,128)(2,1)}), bf16[8,32,2048]{2,1,0:T(8,128)(2,1)S(1)}, u32[]{:S(2)}, u32[]{:S(2)}) async-start(bf16[8,32,2048]{2,1,0:T(8,128)(2,1)} %bitcast), calls=%async_computation | async-start | bytes 2097152 | tf_op jit(solution)/shard_map/all_to_all | solution.py:69
  71.9 56.2 %collective-permute-start.13 = (bf16[512,512]{1,0:T(8,128)(2,1)}, bf16[512,512]{1,0:T(8,128)(2,1)S(1)}, u32[]{:S(2)}, u32[]{:S(2)}) collective-permute-start(bf16[512,512]{1,0:T(8,128)(2,1)} %slice.107), channel_id=1, source_target_pairs={{0,16},{16,32},{32,48},{48,0},{1,17},{17,33},{33,49},{49,1},{2,18}... | collective-permute-start | bytes 1572872 | tf_op jit(solution)/shard_map/ppermute | solution.py:12
  74.8 53.2 %collective-permute-start.14 = (bf16[512,512]{1,0:T(8,128)(2,1)}, bf16[512,512]{1,0:T(8,128)(2,1)}, u32[]{:S(2)}, u32[]{:S(2)}) collective-permute-start(bf16[512,512]{1,0:T(8,128)(2,1)} %slice.107), channel_id=1, source_target_pairs={{0,48},{16,0},{32,16},{48,32},{1,49},{17,1},{33,17},{49,33},{2,50}... | collective-permute-start | bytes 1572872 | tf_op jit(solution)/shard_map/ppermute | solution.py:12
  82.8 19.3 %collective-permute-start.6 = (bf16[4,32,1024]{2,1,0:T(8,128)(2,1)}, bf16[4,32,1024]{2,1,0:T(8,128)(2,1)}, u32[]{:S(2)}, u32[]{:S(2)}) collective-permute-start(bf16[4,32,1024]{2,1,0:T(8,128)(2,1)} %get-tuple-element.35), channel_id=1, source_target_pairs={{0,2},{2,0},{1,3},{3,1},{4,6},{6,4},{5,7},{7,5},{8,10},{10,8},{9,1... | collective-permute-start | bytes 786440 | tf_op jit(solution)/shard_map/ppermute | solution.py:12
  86.7 15.3 %all-to-all-start.1 = ((bf16[4,32,2048]{2,1,0:T(8,128)(2,1)}), bf16[4,32,2048]{2,1,0:T(8,128)(2,1)S(1)}, u32[]{:S(2)}, u32[]{:S(2)}) async-start(bf16[4,32,2048]{2,1,0:T(8,128)(2,1)} %broadcast_in_dim.42), calls=%async_computation.1 | async-start | bytes 1048576 | tf_op jit(solution)/shard_map/all_to_all | solution.py:74
  94.1 34.0 %collective-permute-start.15 = (bf16[512,640]{1,0:T(8,128)(2,1)}, bf16[512,640]{1,0:T(8,128)(2,1)}, u32[]{:S(2)}, u32[]{:S(2)}) collective-permute-start(bf16[512,640]{1,0:T(8,128)(2,1)} %slice.108), channel_id=1, source_target_pairs={{0,16},{16,32},{32,48},{48,0},{1,17},{17,33},{33,49},{49,1},{2,18}... | collective-permute-start | bytes 1966088 | tf_op jit(solution)/shard_map/ppermute | solution.py:12
  96.1 31.9 %collective-permute-start.16 = (bf16[512,640]{1,0:T(8,128)(2,1)}, bf16[512,640]{1,0:T(8,128)(2,1)}, u32[]{:S(2)}, u32[]{:S(2)}) collective-permute-start(bf16[512,640]{1,0:T(8,128)(2,1)} %slice.109), channel_id=1, source_target_pairs={{0,48},{16,0},{32,16},{48,32},{1,49},{17,1},{33,17},{49,33},{2,50}... | collective-permute-start | bytes 1966088 | tf_op jit(solution)/shard_map/ppermute | solution.py:12
  111.7 16.3 %all-to-all-start.3 = ((bf16[4,32,2048]{2,1,0:T(8,128)(2,1)}), bf16[4,32,2048]{2,1,0:T(8,128)(2,1)S(1)}, u32[]{:S(2)}, u32[]{:S(2)}) async-start(bf16[4,32,2048]{2,1,0:T(8,128)(2,1)} %bitcast.13), calls=%async_computation.3 | async-start | bytes 1048576 | tf_op jit(solution)/shard_map/all_to_all | solution.py:79
  123.3 27.6 %collective-permute-start.4 = (bf16[256,2048]{1,0:T(8,128)(2,1)}, bf16[256,2048]{1,0:T(8,128)(2,1)}, u32[]{:S(2)}, u32[]{:S(2)}) collective-permute-start(bf16[256,2048]{1,0:T(8,128)(2,1)} %pad_maximum_fusion), channel_id=1, source_target_pairs={{0,1},{1,0},{2,3},{3,2},{4,5},{5,4},{6,7},{7,6},{8,9},{9,8},{10,11... | collective-permute-start | bytes 3145736 | tf_op jit(solution)/shard_map/ppermute | solution.py:12
  128.1 22.9 %collective-permute-start.11 = (bf16[256,512]{1,0:T(8,128)(2,1)}, bf16[256,512]{1,0:T(8,128)(2,1)}, u32[]{:S(2)}, u32[]{:S(2)}) collective-permute-start(bf16[256,512]{1,0:T(8,128)(2,1)} %get-tuple-element.31), channel_id=1, source_target_pairs={{0,1},{1,0},{2,3},{3,2},{4,5},{5,4},{6,7},{7,6},{8,9},{9,8},{10,11... | collective-permute-start | bytes 786440 | tf_op jit(solution)/shard_map/ppermute | solution.py:12
  128.8 20.5 %collective-permute-start.17 = (bf16[512,256]{1,0:T(8,128)(2,1)}, bf16[512,256]{1,0:T(8,128)(2,1)}, u32[]{:S(2)}, u32[]{:S(2)}) collective-permute-start(bf16[512,256]{1,0:T(8,128)(2,1)} %slice.115), channel_id=1, source_target_pairs={{0,16},{16,32},{32,48},{48,0},{1,17},{17,33},{33,49},{49,1},{2,18}... | collective-permute-start | bytes 786440 | tf_op jit(solution)/shard_map/ppermute | solution.py:12
  130.5 27.9 %collective-permute-start.18 = (bf16[512,256]{1,0:T(8,128)(2,1)}, bf16[512,256]{1,0:T(8,128)(2,1)}, u32[]{:S(2)}, u32[]{:S(2)}) collective-permute-start(bf16[512,256]{1,0:T(8,128)(2,1)} %slice.116), channel_id=1, source_target_pairs={{0,48},{16,0},{32,16},{48,32},{1,49},{17,1},{33,17},{49,33},{2,50}... | collective-permute-start | bytes 786440 | tf_op jit(solution)/shard_map/ppermute | solution.py:12
  134.6 25.5 %all-to-all-start.4 = ((bf16[32,32,512]{2,1,0:T(8,128)(2,1)}), bf16[32,32,512]{2,1,0:T(8,128)(2,1)}, u32[]{:S(2)}, u32[]{:S(2)}) async-start(bf16[32,32,512]{2,1,0:T(8,128)(2,1)} %bitcast.17), calls=%async_computation.4 | async-start | bytes 2097152 | tf_op jit(solution)/shard_map/all_to_all | solution.py:99
  156.8 23.8 %collective-permute-start.12 = (bf16[1024,512]{1,0:T(8,128)(2,1)}, bf16[1024,512]{1,0:T(8,128)(2,1)S(1)}, u32[]{:S(2)}, u32[]{:S(2)}) collective-permute-start(bf16[1024,512]{1,0:T(8,128)(2,1)} %fusion.9), channel_id=1, source_target_pairs={{0,64},{64,0},{1,65},{65,1},{2,66},{66,2},{3,67},{67,3},{4,68},{68... | collective-permute-start | bytes 3145736 | tf_op jit(solution)/shard_map/ppermute | solution.py:12
  160.1 25.5 %collective-permute-start.19 = (bf16[1024,512]{1,0:T(8,128)(2,1)}, bf16[1024,512]{1,0:T(8,128)(2,1)}, u32[]{:S(2)}, u32[]{:S(2)}) collective-permute-start(bf16[1024,512]{1,0:T(8,128)(2,1)} %bitcast.18), channel_id=1, source_target_pairs={{0,1},{1,0},{2,3},{3,2},{4,5},{5,4},{6,7},{7,6},{8,9},{9,8},{10,11... | collective-permute-start | bytes 3145736 | tf_op jit(solution)/shard_map/ppermute | solution.py:12
  182.0 15.8 %all-to-all-start.2 = ((bf16[4,256,512]{2,1,0:T(8,128)(2,1)}), bf16[4,256,512]{2,1,0:T(8,128)(2,1)S(1)}, u32[]{:S(2)}, u32[]{:S(2)}) async-start(bf16[4,256,512]{2,1,0:T(8,128)(2,1)} %bitcast.10), calls=%async_computation.2 | async-start | bytes 2097152 | tf_op jit(solution)/shard_map/all_to_all | solution.py:115
  189.9 19.5 %collective-permute-start.20 = (bf16[256,1792]{1,0:T(8,128)(2,1)}, bf16[256,1792]{1,0:T(8,128)(2,1)}, u32[]{:S(2)}, u32[]{:S(2)}) collective-permute-start(bf16[256,1792]{1,0:T(8,128)(2,1)} %fusion), channel_id=1, source_target_pairs={{0,64},{64,0},{1,65},{65,1},{2,66},{66,2},{3,67},{67,3},{4,68},{68... | collective-permute-start | bytes 2752520 | tf_op jit(solution)/shard_map/ppermute | solution.py:12
  (14 other events, 137.6 us)

commit v3 on v0

v3 whole, which is shorter than its diff:
```python
import functools

import jax
import jax.numpy as jnp
import numpy as np
from jax import lax
from jax.experimental import pallas as pl
from jax.experimental.pallas import tpu as pltpu
from jax.sharding import Mesh, PartitionSpec as P

BF, F32 = jnp.bfloat16, jnp.float32
TOK, CHAN, YZ, QUAD = ("y_lo", "x"), ("z", "y_hi", "core"), ("y_hi", "z"), ("y_hi", "core")
VMEM = pl.BlockSpec(memory_space=pltpu.VMEM)


def dot(left, right, left_dim=1, right_dim=0):
    return lax.dot_general(
        left, right, (((left_dim,), (right_dim,)), ((), ())), preferred_element_type=F32
    )


def shift(array, axis, size, step):
    return lax.ppermute(array, axis, [(i, (i + step) % size) for i in range(size)])


def swap(array, axis):
    return shift(array, axis, 2, 1)


def call(body, outs, *args, scratch=(), flops=0):
    moved = sum(a.size * a.dtype.itemsize for a in list(args) + list(outs))
    return pl.pallas_call(
        body,
        out_shape=outs if len(outs) > 1 else outs[0],
        in_specs=[VMEM] * len(args),
        out_specs=[VMEM] * len(outs) if len(outs) > 1 else VMEM,
        scratch_shapes=scratch,
        compiler_params=pltpu.CompilerParams(vmem_limit_bytes=48 * 1024 * 1024),
        cost_estimate=pl.CostEstimate(flops=flops, bytes_accessed=moved, transcendentals=0),
    )(*args)


def like(shape, dtype=BF):
    return jax.ShapeDtypeStruct(shape, dtype)


def total(ref, at=slice(None)):
    out = ref[0, at].astype(F32)
    for i in range(1, ref.shape[0]):
        out = out + ref[i, at].astype(F32)
    return out


def sum_and_copy(blocks, out):
    value = total(blocks).astype(BF)
    for i in range(out.shape[0]):
        out[i] = value


def residual_kernel(codes, near, far, a0, a1, a2, a3, message, partial, acc):
    y_hi, core = lax.axis_index("y_hi"), lax.axis_index("core")
    rank, outs = codes.shape[0], a0.shape[0]
    step = 256
    owners = (
        2 * y_hi + core,
        2 * y_hi + 1 - core,
        2 * (1 - y_hi) + core,
        2 * (1 - y_hi) + 1 - core,
    )
    for j, a in enumerate((a0, a1, a2, a3)):
        owner = owners[j]
        message[owner, :rank] = codes[...]
        for at in range(0, outs, step):
            rows = slice(at, at + step)
            target = (near if j < 2 else far)[j % 2, rows].astype(F32)
            left = target - dot(a[rows], codes[...])
            left = left.astype(BF)
            message[owner, rank + at : rank + at + step] = left
            term = dot(left, a[rows], 0, 0)
            if j == 0 and at == 0:
                acc[...] = term
            else:
                acc[...] += term
    sub = partial.shape[1]
    for z in range(partial.shape[0]):
        partial[z] = acc[z * sub : (z + 1) * sub].astype(BF)


def spread_kernel(blocks, out, held):
    y_lo = lax.axis_index("y_lo")
    held[...] = total(blocks).astype(BF)
    rank = held.shape[1]
    width = rank // 8
    for x in range(4):
        for side in range(2):
            start = (y_lo if side == 0 else 1 - y_lo) * (rank // 2) + x * width
            piece = held[:, pl.ds(pl.multiple_of(start, width), width)]
            for i in range(out.shape[1]):
                out[x, i, :, side * width : (side + 1) * width] = piece


def last_kernel(side, grad_m, grad_o, r0, r1, r2, r3, out, turned):
    core, x = lax.axis_index("core"), lax.axis_index("x")
    half, width = grad_m.shape[1], out.shape[0]
    at = slice(side * width, (side + 1) * width)
    tokens = 2 * half
    for k in range(4):
        row = lax.rem(x + 4 - k, 4)
        first = pl.multiple_of(core * half, half)
        other = pl.multiple_of((1 - core) * half, half)
        turned[k, :, pl.ds(first, half)] = grad_m[row, :, at].T
        turned[k, :, pl.ds(other, half)] = grad_o[row, :, at].T
    step = 256
    for c in range(0, out.shape[1], step):
        cols = slice(c, c + step)
        acc = dot(turned[0], r0[:, cols])
        for k, r in ((1, r1), (2, r2), (3, r3)):
            acc = acc + dot(turned[k], r[:, cols])
        out[:, cols] = acc.astype(out.dtype)


def term_kernel(message, out):
    rank = out.shape[0]
    outs = out.shape[1]
    step = 512
    for at in range(0, rank, step):
        acc = dot(message[0, at : at + step], message[0, rank:], 1, 1)
        for q in range(1, 4):
            acc = acc + dot(message[q, at : at + step], message[q, rank:], 1, 1)
        out[at : at + step] = acc.astype(BF)


def local(acts, target, proj_b, proj_a):
    core, y_hi = lax.axis_index("core"), lax.axis_index("y_hi")
    tokens, rank = acts.shape[0], proj_b.shape[0]
    outs, wide = target.shape[1], acts.shape[1]
    half, quarter, sub, width = tokens // 2, tokens // 4, tokens // 16, rank // 8
    scale = -2.0 / (tokens * 8)
    barrier = lax.optimization_barrier

    def part_of(array, which, size, axis):
        return lax.dynamic_slice_in_dim(array, which * size, size, axis)

    plus, minus = shift(acts, "x", 4, 1), shift(acts, "x", 4, 3)
    across_a = lax.ppermute(proj_a, ("y_lo", "y_hi"), [(0, 3), (3, 0), (1, 2), (2, 1)])
    pair_a = swap(proj_a, "core")
    target_t = target.T
    pair_t = swap(part_of(target_t, 1 - core, half, 1), "core")
    both_t = jnp.stack([part_of(target_t, core, half, 1), pair_t])
    near_t = part_of(both_t, y_hi, quarter, 2)
    far_t = swap(part_of(both_t, 1 - y_hi, quarter, 2), "y_hi")

    theirs = dot(proj_b, part_of(acts, 1 - core, half, 0), 1, 1)
    arrived = swap(theirs, "core")
    mine = barrier(dot(proj_b, part_of(acts, core, half, 0), 1, 1))
    mine = (mine + arrived).astype(BF).reshape(rank, 2, quarter).transpose(1, 0, 2).reshape(8, rank // 4, quarter)
    blocks = lax.all_to_all(mine, YZ, 0, 0)
    blocks, plus, minus, across_a, acts_2, far_t = barrier((blocks, plus, minus, across_a, acts, far_t))
    far = shift(acts_2, "x", 4, 2)
    pair_across = swap(across_a, "core")
    codes = call(sum_and_copy, [like((4, rank // 4, quarter))], blocks)
    codes = lax.all_to_all(codes, "z", 0, 0).reshape(rank, quarter)

    message, partial = call(
        residual_kernel,
        [like((4, rank + outs, quarter)), like((4, sub, rank))],
        codes, near_t, far_t, proj_a, pair_a, across_a, pair_across,
        scratch=[pltpu.VMEM((quarter, rank), F32)],
        flops=16 * quarter * rank * outs,
    )
    blocks = lax.all_to_all(partial, "z", 0, 0)
    blocks, far = barrier((blocks, far))
    message = lax.all_to_all(message, QUAD, 0, 0)

    split = call(spread_kernel, [like((4, 8, sub, 2 * width))], blocks, scratch=[pltpu.VMEM((sub, rank), BF)])
    split = split.reshape(32, sub, 2 * width)
    grad_m = lax.all_to_all(split, ("x", "y_hi", "z"), 0, 0).reshape(4, half, 2 * width)
    grad_o = swap(grad_m, "core")

    def last(side, dtype):
        return call(
            functools.partial(last_kernel, side),
            [like((width, wide), dtype)],
            grad_m, grad_o, acts, plus, far, minus,
            scratch=[pltpu.VMEM((4, width, tokens), BF)],
            flops=8 * tokens * width * wide,
        )

    away = swap(last(1, BF), "y_lo")
    grad_b = (last(0, F32) + away.astype(F32)) * scale

    term = call(term_kernel, [like((rank, outs))], message, flops=2 * tokens * rank * outs)
    term = lax.all_to_all(term.reshape(8, width, outs), TOK, 0, 0)
    sums = term[0].astype(F32)
    for i in range(1, 8):
        sums = sums + term[i].astype(F32)
    grad_a = (sums * scale).T
    return (grad_a, grad_b)


def solution(mesh):
    fine = Mesh(np.reshape(mesh.devices, (2, 4, 4, 2, 2)), ("y_lo", "x", "z", "y_hi", "core"))
    return jax.shard_map(
        local,
        mesh=fine,
        in_specs=(P(TOK, CHAN), P(TOK, CHAN), P(None, CHAN), P(CHAN, None)),
        out_specs=(P(CHAN, TOK), P(TOK, CHAN)),
        check_vma=False,
    )
```

time: 443 us -> 246 us (0.56)
  blocking collectives: 242 us -> 24 us
  starting transfers between devices: 0.08 us -> 41.4 us
  Pallas kernels: 0 us -> 24.3 us
  waiting for transfers between devices: 151 us -> 127 us
  matrix products: 30.5 us -> 12.1 us
  between operations: 14.1 us -> 0.76 us
  local copies, waits for them, and re-layouts: 0.02 us -> 8.55 us
    psum x2 -> x0, blocking collectives: 242 us -> none  [the longest x1 140 us: local(): grad_codes = lax.psum(grad_partial, 'chan').astype(jnp.bfloat16)]
    reduce_scatter x2 -> x0, waiting for transfers between devices: 151 us -> none  [the longest x1 151 us: local(): lax.psum_scatter(contract_rows(grad_codes, acts), 'tok', scatter_dimensio...]
    ppermute x0 -> x11, waiting for transfers between devices: none -> 86.1 us  [the longest x10 61 us: shift(): lax.ppermute(array, axis, [(i, (i + step) % size) for i in range(size)])]
    all_to_all x0 -> x5, waiting for transfers between devices: none -> 40.8 us  [the longest x1 31.7 us: local(): message = lax.all_to_all(message, QUAD, 0, 0)]
    all_to_all x0 -> x5, starting transfers between devices: none -> 24.7 us  [the longest x1 6.46 us: local(): message = lax.all_to_all(message, QUAD, 0, 0)]
    pallas_call x0 -> x6, Pallas kernels: none -> 24.3 us  [call(): pl.pallas_call(body, out_shape=outs if len(outs) > 1 else outs[0], in_spe...]
    all_to_all x0 -> x1, blocking collectives: none -> 24 us  [local(): lax.all_to_all(split, ('x', 'y_hi', 'z'), 0, 0).reshape(4, half, 2 * width)]
    dot_general x5 -> x2, matrix products: 30.5 us -> 12.1 us  [dot(): lax.dot_general(left, right, (((left_dim,), (right_dim,)), ((), ())), pre...]
  transfers between devices with their start and end apart: 2 -> 16, of which waited for: 1 -> 8; matrix products, arithmetic and copies ran while one was open for 4% -> 7% of each run, Pallas kernels for 0% -> 10%
where the time goes in v3:
time: 246 us; the launch traced here: 245 us
  waiting for transfers between devices  127 us (52%)
  starting transfers between devices  41.4 us (17%)
  Pallas kernels  24.3 us (10%)
  blocking collectives  24 us (10%)
  matrix products  12.1 us (5%)
  local copies, waits for them, and re-layouts  8.55 us (3%)
  other arithmetic  6.89 us (3%)
    ppermute x10, waiting for transfers between devices, shift(): lax.ppermute(array, axis, [(i, (i + step) % size) for i in range(size)])  61 us
    all_to_all x1, waiting for transfers between devices, local(): message = lax.all_to_all(message, QUAD, 0, 0)  31.7 us
    ppermute x1, waiting for transfers between devices, local(): lax.ppermute(proj_a, ('y_lo', 'y_hi'), [(0, 3), (3, 0), (1, 2), (2, 1)])  25 us
    pallas_call x6, Pallas kernels, call(): pl.pallas_call(body, out_shape=outs if len(outs) > 1 else outs[0], in_spe...  24.3 us
    all_to_all x1, blocking collectives, local(): lax.all_to_all(split, ('x', 'y_hi', 'z'), 0, 0).reshape(4, half, 2 * width)  24 us
    ppermute x10, starting transfers between devices, shift(): lax.ppermute(array, axis, [(i, (i + step) % size) for i in range(size)])  13.9 us
    dot_general x2, matrix products, dot(): lax.dot_general(left, right, (((left_dim,), (right_dim,)), ((), ())), pre...  12.1 us
    all_to_all x1, waiting for transfers between devices, local(): codes = lax.all_to_all(codes, 'z', 0, 0).reshape(rank, quarter)  9.11 us
  transfers between devices with their start and end apart: 16, of which 8 were waited for; matrix products, arithmetic and copies ran while one was open for 7% of the time, Pallas kernels for 10%

profile of v3, /device:TPU:1, one launch (start us, length us, event | category | flops | bytes accessed | tf_op | source)
XLA Modules:
  0.0 244.9 jit_solution(14195772004668241419)
XLA Ops:
  0.6 6.9 %convolution_bitcast_fusion = f32[2048,256]{0,1:T(8,128)} fusion(bf16[2048,1792]{1,0:T(8,128)(2,1)} %param.6, bf16[512,1792]{1,0:T(8,128)(2,1)} %r0.3, s32[]{:T(128)S(6)} %select_n.15), kind=kOutput, calls=%fused_computation | convolution fusion | flops 1879048192 | bytes 10354692 | tf_op jit(solution)/shard_map/dot_general | solution.py:17
  11.7 2.8 %collective-permute-start.3 = (bf16[512,2048]{1,0:T(8,128)(2,1)}, bf16[512,2048]{1,0:T(8,128)(2,1)}, u32[]{:S(2)}, u32[]{:S(2)}) collective-permute-start(bf16[512,2048]{1,0:T(8,128)(2,1)} %a0.1), channel_id=1, source_target_pairs={{0,66},{66,0},{2,64},{64,2},{1,67},{67,1},{3,65},{65,3},{4,70},{70... | collective-permute-start | bytes 6291464 | tf_op jit(solution)/shard_map/ppermute | solution.py:145
  14.5 5.2 %convolution_bitcast_fusion.1 = f32[2048,256]{0,1:T(8,128)S(1)} fusion(bf16[2048,1792]{1,0:T(8,128)(2,1)} %param.6, bf16[512,1792]{1,0:T(8,128)(2,1)S(1)} %copy-done.2, s32[]{:T(128)S(6)} %select_n.14), kind=kOutput, calls=%fused_computation.1 | convolution fusion | flops 1879048192 | bytes 10354692 | tf_op jit(solution)/shard_map/dot_general | solution.py:17
  19.7 1.9 add_convert_fusion
  22.9 5.1 %all-to-all-start = ((bf16[8,512,128]{2,1,0:T(8,128)(2,1)}), bf16[8,512,128]{2,1,0:T(8,128)(2,1)S(1)}, u32[]{:S(2)}, u32[]{:S(2)}) async-start(bf16[8,512,128]{2,1,0:T(8,128)(2,1)} %bitcast.30), calls=%async_computation | async-start | bytes 2097152 | tf_op jit(solution)/shard_map/all_to_all | solution.py:157
  33.5 3.3 %collective-permute-start.5 = (bf16[2,512,128]{2,1,0:T(8,128)(2,1)S(1)}, bf16[2,512,128]{2,1,0:T(8,128)(2,1)S(1)}, u32[]{:S(2)}, u32[]{:S(2)}) collective-permute-start(bf16[2,512,128]{2,1,0:T(8,128)(2,1)S(1)} %get-tuple-element.23), channel_id=1, source_target_pairs={{0,2},{2,0},{1,3},{3,1},{4,6},{6,4},{5,7},{7,5},{8,10},{10,8},{9,1... | collective-permute-start | bytes 786440 | tf_op jit(solution)/shard_map/ppermute | solution.py:23
  37.5 10.2 %collective-permute-done.5.far = bf16[2,512,128]{2,1,0:T(8,128)(2,1)S(1)} collective-permute-done((bf16[2,512,128]{2,1,0:T(8,128)(2,1)S(1)}, bf16[2,512,128]{2,1,0:T(8,128)(2,1)S(1)}, u32[]{:S(2)}, u32[]{:S(2)}) %collective-permute-start.5) | collective-permute-done | bytes 262176 | tf_op jit(solution)/shard_map/ppermute | solution.py:23
  47.7 4.3 %collective-permute-done.1.r1 = bf16[512,1792]{1,0:T(8,128)(2,1)} collective-permute-done((bf16[512,1792]{1,0:T(8,128)(2,1)S(1)}, bf16[512,1792]{1,0:T(8,128)(2,1)}, u32[]{:S(2)}, u32[]{:S(2)}) %collective-permute-start.1) | collective-permute-done | bytes 1835040 | tf_op jit(solution)/shard_map/ppermute | solution.py:23
  52.0 25.0 %collective-permute-done.3.a2 = bf16[512,2048]{1,0:T(8,128)(2,1)} collective-permute-done((bf16[512,2048]{1,0:T(8,128)(2,1)}, bf16[512,2048]{1,0:T(8,128)(2,1)}, u32[]{:S(2)}, u32[]{:S(2)}) %collective-permute-start.3) | collective-permute-done | bytes 2097184 | tf_op jit(solution)/shard_map/ppermute | solution.py:145
  80.7 5.0 %all-to-all-start.1 = ((bf16[4,512,128]{2,1,0:T(8,128)(2,1)}), bf16[4,512,128]{2,1,0:T(8,128)(2,1)S(1)}, u32[]{:S(2)}, u32[]{:S(2)}) async-start(bf16[4,512,128]{2,1,0:T(8,128)(2,1)} %shard_map.59), calls=%async_computation.1 | async-start | bytes 1048576 | tf_op jit(solution)/shard_map/all_to_all | solution.py:162
  85.7 9.1 %all-to-all-done.1 = bf16[4,512,128]{2,1,0:T(8,128)(2,1)S(1)} async-done(((bf16[4,512,128]{2,1,0:T(8,128)(2,1)}), bf16[4,512,128]{2,1,0:T(8,128)(2,1)S(1)}, u32[]{:S(2)}, u32[]{:S(2)}) %all-to-all-start.1) | async-done | bytes 524320 | tf_op jit(solution)/shard_map/all_to_all | solution.py:162
  94.8 10.3 %shard_map.60 = (bf16[4,2560,128]{2,1,0:T(8,128)(2,1)}, bf16[4,32,2048]{2,1,0:T(8,128)(2,1)}) custom-call(bf16[2048,128]{1,0:T(8,128)(2,1)S(1)} %bitcast.28, bf16[2,512,128]{2,1,0:T(8,128)(2,1)S(1)} %get-tuple-element.22.near, bf16[2,512,128]{2,1,0:T(8,128)(2,1)S(1)} %collective-permute-done.5.far, bf16[512,2048]{1,0:T(8,128)(2,1)} %a0.1, ...), custom_call_target="tpu_custom_call" | custom-call | flops 2147483648 | bytes 12582912 | tf_op jit(solution)/shard_map/pallas_call | solution.py:32
  105.2 3.5 %all-to-all-start.4 = ((bf16[4,32,2048]{2,1,0:T(8,128)(2,1)}), bf16[4,32,2048]{2,1,0:T(8,128)(2,1)S(1)}, u32[]{:S(2)}, u32[]{:S(2)}) async-start(bf16[4,32,2048]{2,1,0:T(8,128)(2,1)} %get-tuple-element.16), calls=%async_computation.4 | async-start | bytes 1048576 | tf_op jit(solution)/shard_map/all_to_all | solution.py:171
  108.6 12.9 %collective-permute-done.8.r2 = bf16[512,1792]{1,0:T(8,128)(2,1)} collective-permute-done((bf16[512,1792]{1,0:T(8,128)(2,1)S(1)}, bf16[512,1792]{1,0:T(8,128)(2,1)}, u32[]{:S(2)}, u32[]{:S(2)}) %collective-permute-start.8) | collective-permute-done | bytes 1835040 | tf_op jit(solution)/shard_map/ppermute | solution.py:23
  121.7 24.0 %all_to_all.30 = bf16[32,32,512]{2,1,0:T(8,128)(2,1)} all-to-all(bf16[32,32,512]{2,1,0:T(8,128)(2,1)S(1)} %bitcast.27), channel_id=1, replica_groups=mesh['y_lo'=2,'x'=4,'z'=4,'y_hi'=2,'core'=2] {'x','y_hi','z'}, dimensions={0} | all-to-all | bytes 2097152 | tf_op jit(solution)/shard_map/all_to_all | solution.py:177
  145.7 6.5 %all-to-all-start.2 = ((bf16[4,2560,128]{2,1,0:T(8,128)(2,1)}), bf16[4,2560,128]{2,1,0:T(8,128)(2,1)S(1)}, u32[]{:S(2)}, u32[]{:S(2)}) async-start(bf16[4,2560,128]{2,1,0:T(8,128)(2,1)} %get-tuple-element.15), calls=%async_computation.2 | async-start | bytes 5242880 | tf_op jit(solution)/shard_map/all_to_all | solution.py:173
  152.5 31.7 %all-to-all-done.2.message = bf16[4,2560,128]{2,1,0:T(8,128)(2,1)S(1)} async-done(((bf16[4,2560,128]{2,1,0:T(8,128)(2,1)}), bf16[4,2560,128]{2,1,0:T(8,128)(2,1)S(1)}, u32[]{:S(2)}, u32[]{:S(2)}) %all-to-all-start.2) | async-done | bytes 2621472 | tf_op jit(solution)/shard_map/all_to_all | solution.py:173
  184.1 2.3 shard_map.61
  187.8 3.9 %copy.9 = bf16[8,256,512]{1,2,0:T(8,128)(2,1)} copy(bf16[8,256,512]{2,1,0:T(8,128)(2,1)} %bitcast.26) | data formatting | bytes 4194304 | tf_op jit(solution)/shard_map/reshape | solution.py:193
  191.7 4.7 %all-to-all-start.3 = ((bf16[8,256,512]{1,2,0:T(8,128)(2,1)}), bf16[8,256,512]{1,2,0:T(8,128)(2,1)}, u32[]{:S(2)}, u32[]{:S(2)}) async-start(bf16[8,256,512]{1,2,0:T(8,128)(2,1)} %copy.9), calls=%async_computation.3 | async-start | bytes 4194304 | tf_op jit(solution)/shard_map/all_to_all | solution.py:193
  196.4 5.3 %shard_map.64 = bf16[256,1792]{1,0:T(8,128)(2,1)S(1)} custom-call(bf16[4,256,512]{2,1,0:T(8,128)(2,1)S(1)} %bitcast.24, bf16[4,256,512]{2,1,0:T(8,128)(2,1)} %collective-permute-done.9.grad_o, bf16[512,1792]{1,0:T(8,128)(2,1)S(1)} %copy-done.3, bf16[512,1792]{1,0:T(8,128)(2,1)} %collective-permute-done.1.r1, bf16[512,1792]{1,0:T(8,128)(2,1)} %collective-permute-done.8.r2, ...), custom_call_target="tpu_custom_call" | custom-call | flops 1879048192 | bytes 10354688 | tf_op jit(solution)/shard_map/pallas_call | solution.py:32
  203.3 5.3 %shard_map.63 = f32[256,1792]{1,0:T(8,128)S(1)} custom-call(bf16[4,256,512]{2,1,0:T(8,128)(2,1)S(1)} %bitcast.25, bf16[4,256,512]{2,1,0:T(8,128)(2,1)} %collective-permute-done.9.grad_o, bf16[512,1792]{1,0:T(8,128)(2,1)S(1)} %copy-done.3, bf16[512,1792]{1,0:T(8,128)(2,1)} %collective-permute-done.1.r1, bf16[512,1792]{1,0:T(8,128)(2,1)} %collective-permute-done.8.r2, ...), custom_call_target="tpu_custom_call" | custom-call | flops 1879048192 | bytes 11272192 | tf_op jit(solution)/shard_map/pallas_call | solution.py:32
  208.5 32.4 %collective-permute-done.10 = bf16[256,1792]{1,0:T(8,128)(2,1)S(1)} collective-permute-done((bf16[256,1792]{1,0:T(8,128)(2,1)S(1)}, bf16[256,1792]{1,0:T(8,128)(2,1)S(1)}, u32[]{:S(2)}, u32[]{:S(2)}) %collective-permute-start.10) | collective-permute-done | bytes 917536 | tf_op jit(solution)/shard_map/ppermute | solution.py:23
  242.3 2.6 %multiply_bitcast_fusion = f32[512,256]{1,0:T(8,128)} fusion(bf16[8,256,512]{1,2,0:T(8,128)(2,1)} %all-to-all-done.3), kind=kLoop, calls=%fused_computation.10 | loop fusion | flops 2097152 | bytes 2621440 | tf_op jit(solution)/shard_map/transpose | solution.py:197
  (34 shorter events, 20.1 us)
Async XLA Ops:
  0.6 8.4 %copy-start.2 = (bf16[512,1792]{1,0:T(8,128)(2,1)S(1)}, bf16[512,1792]{1,0:T(8,128)(2,1)}, u32[]{:S(2)}) copy-start(bf16[512,1792]{1,0:T(8,128)(2,1)} %r0.3) | copy-start | bytes 5505028
  7.6 12.1 %collective-permute-start = (f32[2048,256]{0,1:T(8,128)}, f32[2048,256]{0,1:T(8,128)}, u32[]{:S(2)}, u32[]{:S(2)}) collective-permute-start(f32[2048,256]{0,1:T(8,128)} %convolution_bitcast_fusion), channel_id=1, source_target_pairs={{0,1},{1,0},{2,3},{3,2},{4,5},{5,4},{6,7},{7,6},{8,9},{9,8},{10,11... | collective-permute-start | bytes 6291464 | tf_op jit(solution)/shard_map/ppermute | solution.py:23
  9.0 43.0 %collective-permute-start.1 = (bf16[512,1792]{1,0:T(8,128)(2,1)S(1)}, bf16[512,1792]{1,0:T(8,128)(2,1)}, u32[]{:S(2)}, u32[]{:S(2)}) collective-permute-start(bf16[512,1792]{1,0:T(8,128)(2,1)S(1)} %copy-done.2), channel_id=1, source_target_pairs={{0,16},{16,32},{32,48},{48,0},{1,17},{17,33},{33,49},{49,1},{2,18}... | collective-permute-start | bytes 5505032 | tf_op jit(solution)/shard_map/ppermute | solution.py:23
  10.3 41.7 %collective-permute-start.2 = (bf16[512,1792]{1,0:T(8,128)(2,1)S(1)}, bf16[512,1792]{1,0:T(8,128)(2,1)}, u32[]{:S(2)}, u32[]{:S(2)}) collective-permute-start(bf16[512,1792]{1,0:T(8,128)(2,1)S(1)} %copy-done.2), channel_id=1, source_target_pairs={{0,48},{16,0},{32,16},{48,32},{1,49},{17,1},{33,17},{49,33},{2,50}... | collective-permute-start | bytes 5505032 | tf_op jit(solution)/shard_map/ppermute | solution.py:23
  11.7 65.3 %collective-permute-start.3 = (bf16[512,2048]{1,0:T(8,128)(2,1)}, bf16[512,2048]{1,0:T(8,128)(2,1)}, u32[]{:S(2)}, u32[]{:S(2)}) collective-permute-start(bf16[512,2048]{1,0:T(8,128)(2,1)} %a0.1), channel_id=1, source_target_pairs={{0,66},{66,0},{2,64},{64,2},{1,67},{67,1},{3,65},{65,3},{4,70},{70... | collective-permute-start | bytes 6291464 | tf_op jit(solution)/shard_map/ppermute | solution.py:145
  22.9 54.1 %all-to-all-start = ((bf16[8,512,128]{2,1,0:T(8,128)(2,1)}), bf16[8,512,128]{2,1,0:T(8,128)(2,1)S(1)}, u32[]{:S(2)}, u32[]{:S(2)}) async-start(bf16[8,512,128]{2,1,0:T(8,128)(2,1)} %bitcast.30), calls=%async_computation | async-start | bytes 2097152 | tf_op jit(solution)/shard_map/all_to_all | solution.py:157
  29.9 2.6 %collective-permute-start.4 = (bf16[512,256]{1,0:T(8,128)(2,1)}, bf16[512,256]{1,0:T(8,128)(2,1)}, u32[]{:S(2)}, u32[]{:S(2)}) collective-permute-start(bf16[512,256]{1,0:T(8,128)(2,1)} %bitcast.32), channel_id=1, source_target_pairs={{0,1},{1,0},{2,3},{3,2},{4,5},{5,4},{6,7},{7,6},{8,9},{9,8},{10,11... | collective-permute-start | bytes 786440 | tf_op jit(solution)/shard_map/ppermute | solution.py:23
  33.5 14.1 %collective-permute-start.5 = (bf16[2,512,128]{2,1,0:T(8,128)(2,1)S(1)}, bf16[2,512,128]{2,1,0:T(8,128)(2,1)S(1)}, u32[]{:S(2)}, u32[]{:S(2)}) collective-permute-start(bf16[2,512,128]{2,1,0:T(8,128)(2,1)S(1)} %get-tuple-element.23), channel_id=1, source_target_pairs={{0,2},{2,0},{1,3},{3,1},{4,6},{6,4},{5,7},{7,5},{8,10},{10,8},{9,1... | collective-permute-start | bytes 786440 | tf_op jit(solution)/shard_map/ppermute | solution.py:23
  36.9 48.9 %collective-permute-start.6 = (bf16[512,2048]{1,0:T(8,128)(2,1)}, bf16[512,2048]{1,0:T(8,128)(2,1)}, u32[]{:S(2)}, u32[]{:S(2)}) collective-permute-start(bf16[512,2048]{1,0:T(8,128)(2,1)} %a0.1), channel_id=1, source_target_pairs={{0,1},{1,0},{2,3},{3,2},{4,5},{5,4},{6,7},{7,6},{8,9},{9,8},{10,11... | collective-permute-start | bytes 6291464 | tf_op jit(solution)/shard_map/ppermute | solution.py:23
  77.0 17.9 %collective-permute-start.7 = (bf16[512,2048]{1,0:T(8,128)(2,1)}, bf16[512,2048]{1,0:T(8,128)(2,1)}, u32[]{:S(2)}, u32[]{:S(2)}) collective-permute-start(bf16[512,2048]{1,0:T(8,128)(2,1)} %collective-permute-done.3.a2), channel_id=1, source_target_pairs={{0,1},{1,0},{2,3},{3,2},{4,5},{5,4},{6,7},{7,6},{8,9},{9,8},{10,11... | collective-permute-start | bytes 6291464 | tf_op jit(solution)/shard_map/ppermute | solution.py:23
  78.2 43.3 %collective-permute-start.8 = (bf16[512,1792]{1,0:T(8,128)(2,1)S(1)}, bf16[512,1792]{1,0:T(8,128)(2,1)}, u32[]{:S(2)}, u32[]{:S(2)}) collective-permute-start(bf16[512,1792]{1,0:T(8,128)(2,1)S(1)} %copy-done.2), channel_id=1, source_target_pairs={{0,32},{16,48},{32,0},{48,16},{1,33},{17,49},{33,1},{49,17},{2,34}... | collective-permute-start | bytes 5505032 | tf_op jit(solution)/shard_map/ppermute | solution.py:23
  80.7 14.1 %all-to-all-start.1 = ((bf16[4,512,128]{2,1,0:T(8,128)(2,1)}), bf16[4,512,128]{2,1,0:T(8,128)(2,1)S(1)}, u32[]{:S(2)}, u32[]{:S(2)}) async-start(bf16[4,512,128]{2,1,0:T(8,128)(2,1)} %shard_map.59), calls=%async_computation.1 | async-start | bytes 1048576 | tf_op jit(solution)/shard_map/all_to_all | solution.py:162
  105.2 16.3 %all-to-all-start.4 = ((bf16[4,32,2048]{2,1,0:T(8,128)(2,1)}), bf16[4,32,2048]{2,1,0:T(8,128)(2,1)S(1)}, u32[]{:S(2)}, u32[]{:S(2)}) async-start(bf16[4,32,2048]{2,1,0:T(8,128)(2,1)} %get-tuple-element.16), calls=%async_computation.4 | async-start | bytes 1048576 | tf_op jit(solution)/shard_map/all_to_all | solution.py:171
  145.7 38.4 %all-to-all-start.2 = ((bf16[4,2560,128]{2,1,0:T(8,128)(2,1)}), bf16[4,2560,128]{2,1,0:T(8,128)(2,1)S(1)}, u32[]{:S(2)}, u32[]{:S(2)}) async-start(bf16[4,2560,128]{2,1,0:T(8,128)(2,1)} %get-tuple-element.15), calls=%async_computation.2 | async-start | bytes 5242880 | tf_op jit(solution)/shard_map/all_to_all | solution.py:173
  152.2 44.2 %collective-permute-start.9 = (bf16[4,256,512]{2,1,0:T(8,128)(2,1)}, bf16[4,256,512]{2,1,0:T(8,128)(2,1)}, u32[]{:S(2)}, u32[]{:S(2)}) collective-permute-start(bf16[4,256,512]{2,1,0:T(8,128)(2,1)} %bitcast.23), channel_id=1, source_target_pairs={{0,1},{1,0},{2,3},{3,2},{4,5},{5,4},{6,7},{7,6},{8,9},{9,8},{10,11... | collective-permute-start | bytes 3145736 | tf_op jit(solution)/shard_map/ppermute | solution.py:23
  186.5 1.3 copy-start.1
  191.7 4.7 %copy-start = (bf16[32,32,512]{2,1,0:T(8,128)(2,1)S(1)}, bf16[32,32,512]{2,1,0:T(8,128)(2,1)}, u32[]{:S(2)}) copy-start(bf16[32,32,512]{2,1,0:T(8,128)(2,1)} %all_to_all.30) | copy-start | bytes 3145732
  191.7 4.7 %copy-start.3 = (bf16[512,1792]{1,0:T(8,128)(2,1)S(1)}, bf16[512,1792]{1,0:T(8,128)(2,1)}, u32[]{:S(2)}) copy-start(bf16[512,1792]{1,0:T(8,128)(2,1)} %r0.3) | copy-start | bytes 5505028
  191.7 50.6 %all-to-all-start.3 = ((bf16[8,256,512]{1,2,0:T(8,128)(2,1)}), bf16[8,256,512]{1,2,0:T(8,128)(2,1)}, u32[]{:S(2)}, u32[]{:S(2)}) async-start(bf16[8,256,512]{1,2,0:T(8,128)(2,1)} %copy.9), calls=%async_computation.3 | async-start | bytes 4194304 | tf_op jit(solution)/shard_map/all_to_all | solution.py:193
  201.7 39.2 %collective-permute-start.10 = (bf16[256,1792]{1,0:T(8,128)(2,1)S(1)}, bf16[256,1792]{1,0:T(8,128)(2,1)S(1)}, u32[]{:S(2)}, u32[]{:S(2)}) collective-permute-start(bf16[256,1792]{1,0:T(8,128)(2,1)S(1)} %shard_map.64), channel_id=1, source_target_pairs={{0,64},{64,0},{1,65},{65,1},{2,66},{66,2},{3,67},{67,3},{4,68},{68... | collective-permute-start | bytes 2752520 | tf_op jit(solution)/shard_map/ppermute | solution.py:23

commit v4 on v3

v4 whole, which is shorter than its diff:
```python
import functools

import jax
import jax.numpy as jnp
import numpy as np
from jax import lax
from jax.experimental import pallas as pl
from jax.experimental.pallas import tpu as pltpu
from jax.sharding import Mesh, PartitionSpec as P

BF, F32 = jnp.bfloat16, jnp.float32
TOK, CHAN, ZY = ("y_lo", "x"), ("z", "y_hi", "core"), ("z", "y_hi")
VMEM = pl.BlockSpec(memory_space=pltpu.VMEM)


def dot(left, right, left_dim=1, right_dim=0):
    return lax.dot_general(
        left, right, (((left_dim,), (right_dim,)), ((), ())), preferred_element_type=F32
    )


def shift(array, axis, size, step):
    return lax.ppermute(array, axis, [(i, (i + step) % size) for i in range(size)])


def swap(array, axis):
    return shift(array, axis, 2, 1)


def call(body, outs, *args, scratch=(), flops=0):
    moved = sum(a.size * a.dtype.itemsize for a in list(args) + list(outs))
    return pl.pallas_call(
        body,
        out_shape=outs if len(outs) > 1 else outs[0],
        in_specs=[VMEM] * len(args),
        out_specs=[VMEM] * len(outs) if len(outs) > 1 else VMEM,
        scratch_shapes=scratch,
        compiler_params=pltpu.CompilerParams(vmem_limit_bytes=48 * 1024 * 1024),
        cost_estimate=pl.CostEstimate(flops=flops, bytes_accessed=moved, transcendentals=0),
    )(*args)


def like(shape, dtype=BF):
    return jax.ShapeDtypeStruct(shape, dtype)


def total(ref, at=slice(None)):
    out = ref[0, at].astype(F32)
    for i in range(1, ref.shape[0]):
        out = out + ref[i, at].astype(F32)
    return out


def codes_kernel(other, acts, b, out, turned):
    core, half = lax.axis_index("core"), turned.shape[1]

    @pl.when(pl.program_id(0) == 0)
    def _():
        which = 1 - core if other else core
        turned[...] = acts[pl.ds(pl.multiple_of(which * half, half), half), :].T

    out[...] = dot(b[...], turned[...])


def codes_call(other, acts, proj_b):
    (tokens, wide), rank = acts.shape, proj_b.shape[0]
    half, step = tokens // 2, 512
    return pl.pallas_call(
        functools.partial(codes_kernel, other),
        grid=(rank // step,),
        out_shape=like((rank, half), F32),
        in_specs=[
            pl.BlockSpec((tokens, wide), lambda i: (0, 0)),
            pl.BlockSpec((step, wide), lambda i: (i, 0)),
        ],
        out_specs=pl.BlockSpec((step, half), lambda i: (i, 0)),
        scratch_shapes=[pltpu.VMEM((wide, half), BF)],
        compiler_params=pltpu.CompilerParams(vmem_limit_bytes=32 * 1024 * 1024),
        cost_estimate=pl.CostEstimate(
            flops=2 * rank * wide * half, bytes_accessed=2 * rank * wide, transcendentals=0
        ),
    )(acts, proj_b)


def sum_and_copy(blocks, out):
    value = total(blocks).astype(BF)
    for i in range(out.shape[0]):
        out[i] = value


def residual_kernel(codes, near, far, a0, a1, own, message, partial, held):
    rank, outs = codes.shape[0], a0.shape[0]
    step = 256
    for j, (target, a) in enumerate(((near, a0), (far, a1))):
        for at in range(0, outs, step):
            rows = slice(at, at + step)
            left = target[rows].astype(F32) - dot(a[rows], codes[...])
            left = left.astype(BF).T
            held[:, j * outs + at : j * outs + at + step] = left
            if j == 0:
                own[:, rows] = left
            else:
                message[rank + at : rank + at + step] = left
    message[:rank] = codes[...]
    sub = partial.shape[1]
    for at in range(0, rank, 512):
        cols = slice(at, at + 512)
        term = dot(held[:, :outs], a0[:, cols]) + dot(held[:, outs:], a1[:, cols])
        for i in range(partial.shape[0]):
            partial[i, :, cols] = term[i * sub : (i + 1) * sub].astype(BF)


def spread_kernel(blocks, out, held):
    y_lo = lax.axis_index("y_lo")
    held[...] = total(blocks).astype(BF)
    rank = held.shape[1]
    width = rank // 8
    for x in range(4):
        for side in range(2):
            start = (y_lo if side == 0 else 1 - y_lo) * (rank // 2) + x * width
            piece = held[:, pl.ds(pl.multiple_of(start, width), width)]
            for i in range(out.shape[1]):
                out[x, i, :, side * width : (side + 1) * width] = piece


def last_kernel(side, cuts, grad_m, grad_o, *refs):
    parts, out, turned = refs[:-2], refs[-2], refs[-1]
    core, x = lax.axis_index("core"), lax.axis_index("x")
    half, width = grad_m.shape[1], out.shape[0]
    at = slice(side * width, (side + 1) * width)
    for k in range(4):
        row = lax.rem(x + 4 - k, 4)
        first = pl.multiple_of(core * half, half)
        other = pl.multiple_of((1 - core) * half, half)
        turned[k, :, pl.ds(first, half)] = grad_m[row, :, at].T
        turned[k, :, pl.ds(other, half)] = grad_o[row, :, at].T
    step = 256
    for c in range(0, out.shape[1], step):
        acc = None
        for ref, (k, start) in zip(parts, cuts):
            if start <= c < start + ref.shape[1]:
                term = dot(turned[k], ref[:, c - start : c - start + step])
                acc = term if acc is None else acc + term
        out[:, c : c + step] = acc.astype(out.dtype)


def term_kernel(codes, own, message, out):
    rank, outs = out.shape
    for at in range(0, rank, 512):
        rows = slice(at, at + 512)
        for c in range(0, outs, 256):
            acc = dot(codes[rows], own[:, c : c + 256])
            acc = acc + dot(message[rows], message[rank + c : rank + c + 256])
            out[rows, c : c + 256] = acc.astype(BF)


def local(acts, target, proj_b, proj_a):
    core = lax.axis_index("core")
    tokens, rank = acts.shape[0], proj_b.shape[0]
    outs, wide = target.shape[1], acts.shape[1]
    half, sub, width = tokens // 2, tokens // 16, rank // 8
    scale = -2.0 / (tokens * 8)
    barrier = lax.optimization_barrier

    def part_of(array, which, size, axis):
        return lax.dynamic_slice_in_dim(array, which * size, size, axis)

    cut, low = 1280, 512
    plus_a, minus_a = shift(acts[:, :cut], "x", 4, 1), shift(acts[:, :cut], "x", 4, 3)
    pair_a = swap(proj_a, "core")
    target_t = target.T
    near_t = part_of(target_t, core, half, 1)
    pair_t = swap(part_of(target_t, 1 - core, half, 1), "core")

    theirs = codes_call(True, acts, proj_b)
    arrived = swap(theirs, "core")
    mine = codes_call(False, acts, proj_b)
    mine = (mine + arrived).astype(BF).reshape(8, width, half)
    blocks = lax.all_to_all(mine, ZY, 0, 0)
    blocks, plus_a, minus_a, acts_2 = barrier((blocks, plus_a, minus_a, acts))
    plus_b, minus_b = shift(acts_2[:, cut:], "x", 4, 1), shift(acts_2[:, cut:], "x", 4, 3)
    far_a = shift(acts_2[:, :low], "x", 4, 2)
    codes = call(sum_and_copy, [like((8, width, half))], blocks)
    codes = lax.all_to_all(codes, ZY, 0, 0).reshape(rank, half)

    own, message, partial = call(
        residual_kernel,
        [like((half, outs)), like((rank + outs, half)), like((8, sub, rank))],
        codes, near_t, pair_t, proj_a, pair_a,
        scratch=[pltpu.VMEM((half, 2 * outs), BF)],
        flops=8 * half * rank * outs,
    )
    partial, plus_b, minus_b, far_a, acts_3 = barrier((partial, plus_b, minus_b, far_a, acts_2))
    far_b = shift(acts_3[:, low:], "x", 4, 2)
    blocks = lax.all_to_all(partial, ZY, 0, 0)

    term = call(
        term_kernel, [like((rank, outs))], codes, own, swap(message, "core"), flops=2 * tokens * rank * outs
    )
    term = lax.all_to_all(term.reshape(8, width, outs), TOK, 0, 0)

    split = call(spread_kernel, [like((4, 8, sub, 2 * width))], blocks, scratch=[pltpu.VMEM((sub, rank), BF)])
    split = split.reshape(32, sub, 2 * width)
    grad_m = lax.all_to_all(split, ("x", "z", "y_hi"), 0, 0).reshape(4, half, 2 * width)
    grad_m, far_b, term = barrier((grad_m, far_b, term))
    grad_o = swap(grad_m, "core")
    parts = [acts, plus_a, plus_b, far_a, far_b, minus_a, minus_b]
    cuts = ((0, 0), (1, 0), (1, cut), (2, 0), (2, low), (3, 0), (3, cut))

    def last(side, dtype):
        return call(
            functools.partial(last_kernel, side, cuts),
            [like((width, wide), dtype)],
            grad_m, grad_o, *parts,
            scratch=[pltpu.VMEM((4, width, tokens), BF)],
            flops=8 * tokens * width * wide,
        )

    away = swap(last(1, BF), "y_lo")
    grad_b = (last(0, F32) + away.astype(F32)) * scale

    sums = term[0].astype(F32)
    for i in range(1, 8):
        sums = sums + term[i].astype(F32)
    grad_a = (sums * scale).T
    return (grad_a, grad_b)


def solution(mesh):
    fine = Mesh(np.reshape(mesh.devices, (2, 4, 4, 2, 2)), ("y_lo", "x", "z", "y_hi", "core"))
    return jax.shard_map(
        local,
        mesh=fine,
        in_specs=(P(TOK, CHAN), P(TOK, CHAN), P(None, CHAN), P(CHAN, None)),
        out_specs=(P(CHAN, TOK), P(TOK, CHAN)),
        check_vma=False,
    )
```

time: 246 us -> 223 us (0.907)
  blocking collectives: 24 us -> 0 us
  local copies, waits for them, and re-layouts: 8.55 us -> 27.2 us
  waiting for transfers between devices: 127 us -> 109 us
  matrix products: 12.1 us -> 0 us
  starting transfers between devices: 41.4 us -> 51.7 us
    ppermute x1 -> x0, waiting for transfers between devices: 25 us -> none  [local(): lax.ppermute(proj_a, ('y_lo', 'y_hi'), [(0, 3), (3, 0), (1, 2), (2, 1)])]
    all_to_all x1 -> x0, blocking collectives: 24 us -> none  [local(): lax.all_to_all(split, ('x', 'y_hi', 'z'), 0, 0).reshape(4, half, 2 * width)]
    ppermute x10 -> x12, waiting for transfers between devices: 61 us -> 83.4 us  [shift(): lax.ppermute(array, axis, [(i, (i + step) % size) for i in range(size)])]
    unnamed x10 -> x40, local copies, waits for them, and re-layouts: 2.27 us -> 20.2 us
    all_to_all x4, waiting for transfers between devices: 40.8 us -> 25.4 us  [the longest x1 11 us: local(): blocks = lax.all_to_all(partial, ZY, 0, 0)]
    dot_general x2 -> x0, matrix products: 12.1 us -> none  [dot(): lax.dot_general(left, right, (((left_dim,), (right_dim,)), ((), ())), pre...]
    all_to_all x4, starting transfers between devices: 20.1 us -> 28.2 us  [the longest x1 7.66 us: local(): codes = lax.all_to_all(codes, ZY, 0, 0).reshape(rank, half)]
    pallas_call x0 -> x2, Pallas kernels: none -> 5.82 us  [codes_call(): pl.pallas_call(functools.partial(codes_kernel, other), grid=(rank // step...]
  transfers between devices with their start and end apart: 16 -> 17, of which waited for: 8 -> 9; matrix products, arithmetic and copies ran while one was open for 7% -> 6% of each run, Pallas kernels for 10% -> 9%
where the time goes in v4:
time: 223 us; the launch traced here: 222 us
  waiting for transfers between devices  109 us (49%)
  starting transfers between devices  51.7 us (23%)
  local copies, waits for them, and re-layouts  27.2 us (12%)
  Pallas kernels  26.4 us (12%)
  other arithmetic  6.68 us (3%)
    ppermute x12, waiting for transfers between devices, shift(): lax.ppermute(array, axis, [(i, (i + step) % size) for i in range(size)])  83.4 us
    pallas_call x6, Pallas kernels, call(): pl.pallas_call(body, out_shape=outs if len(outs) > 1 else outs[0], in_spe...  20.6 us
    unnamed x40, local copies, waits for them, and re-layouts  20.2 us
    ppermute x12, starting transfers between devices, shift(): lax.ppermute(array, axis, [(i, (i + step) % size) for i in range(size)])  19.1 us
    all_to_all x1, waiting for transfers between devices, local(): blocks = lax.all_to_all(partial, ZY, 0, 0)  11 us
    all_to_all x1, waiting for transfers between devices, local(): lax.all_to_all(split, ('x', 'z', 'y_hi'), 0, 0).reshape(4, half, 2 * width)  7.69 us
    all_to_all x1, starting transfers between devices, local(): codes = lax.all_to_all(codes, ZY, 0, 0).reshape(rank, half)  7.66 us
    all_to_all x1, starting transfers between devices, local(): blocks = lax.all_to_all(mine, ZY, 0, 0)  7.66 us
  transfers between devices with their start and end apart: 17, of which 9 were waited for; matrix products, arithmetic and copies ran while one was open for 6% of the time, Pallas kernels for 9%

profile of v4, /device:TPU:1, one launch (start us, length us, event | category | flops | bytes accessed | tf_op | source)
XLA Modules:
  0.0 221.7 jit_solution(17011556590673017433)
XLA Ops:
  2.1 3.1 %copy-done.2 = bf16[2048,1792]{1,0:T(8,128)(2,1)S(1)} copy-done((bf16[2048,1792]{1,0:T(8,128)(2,1)S(1)}, bf16[2048,1792]{1,0:T(8,128)(2,1)}, u32[]{:S(2)}) %copy-start.2) | copy-done | bytes 7340056
  5.2 2.9 %shard_map.60 = f32[2048,256]{1,0:T(8,128)S(1)} custom-call(bf16[512,1792]{1,0:T(8,128)(2,1)S(1)} %copy-done, bf16[2048,1792]{1,0:T(8,128)(2,1)S(1)} %copy-done.2), custom_call_target="tpu_custom_call" | custom-call | flops 1879048192 | bytes 7340032 | tf_op jit(solution)/shard_map/pallas_call | solution.py:68
  13.6 2.9 %shard_map.59 = f32[2048,256]{1,0:T(8,128)S(1)} custom-call(bf16[512,1792]{1,0:T(8,128)(2,1)S(1)} %copy-done, bf16[2048,1792]{1,0:T(8,128)(2,1)S(1)} %copy-done.2), custom_call_target="tpu_custom_call" | custom-call | flops 1879048192 | bytes 7340032 | tf_op jit(solution)/shard_map/pallas_call | solution.py:68
  17.8 7.7 %all-to-all-start = ((bf16[8,256,256]{2,1,0:T(8,128)(2,1)}), bf16[8,256,256]{2,1,0:T(8,128)(2,1)}, u32[]{:S(2)}, u32[]{:S(2)}) async-start(bf16[8,256,256]{2,1,0:T(8,128)(2,1)} %bitcast), calls=%async_computation | async-start | bytes 2097152 | tf_op jit(solution)/shard_map/all_to_all | solution.py:179
  25.4 16.4 %collective-permute-done.2.refs_5_ = bf16[512,1280]{1,0:T(8,128)(2,1)} collective-permute-done((bf16[512,1280]{1,0:T(8,128)(2,1)}, bf16[512,1280]{1,0:T(8,128)(2,1)}, u32[]{:S(2)}, u32[]{:S(2)}) %collective-permute-start.2) | collective-permute-done | bytes 1310752 | tf_op jit(solution)/shard_map/ppermute | solution.py:23
  41.8 3.0 %collective-permute-done.1.refs_1_ = bf16[512,1280]{1,0:T(8,128)(2,1)S(1)} collective-permute-done((bf16[512,1280]{1,0:T(8,128)(2,1)}, bf16[512,1280]{1,0:T(8,128)(2,1)S(1)}, u32[]{:S(2)}, u32[]{:S(2)}) %collective-permute-start.1) | collective-permute-done | bytes 1310752 | tf_op jit(solution)/shard_map/ppermute | solution.py:23
  47.7 7.7 %all-to-all-start.1 = ((bf16[8,256,256]{2,1,0:T(8,128)(2,1)}), bf16[8,256,256]{2,1,0:T(8,128)(2,1)}, u32[]{:S(2)}, u32[]{:S(2)}) async-start(bf16[8,256,256]{2,1,0:T(8,128)(2,1)} %copy-done.6), calls=%async_computation.1 | async-start | bytes 2097152 | tf_op jit(solution)/shard_map/all_to_all | solution.py:184
  64.2 6.7 %all-to-all-done.1 = bf16[8,256,256]{2,1,0:T(8,128)(2,1)} async-done(((bf16[8,256,256]{2,1,0:T(8,128)(2,1)}), bf16[8,256,256]{2,1,0:T(8,128)(2,1)}, u32[]{:S(2)}, u32[]{:S(2)}) %all-to-all-start.1) | async-done | bytes 1048608 | tf_op jit(solution)/shard_map/all_to_all | solution.py:184
  71.9 5.2 %shard_map.62 = (bf16[256,512]{1,0:T(8,128)(2,1)S(1)}, bf16[2560,256]{1,0:T(8,128)(2,1)S(1)}, bf16[8,32,2048]{2,1,0:T(8,128)(2,1)S(1)}) custom-call(bf16[2048,256]{1,0:T(8,128)(2,1)} %bitcast.1.codes, bf16[512,256]{1,0:T(8,128)(2,1)S(1)} %bitcast.16, bf16[512,256]{1,0:T(8,128)(2,1)} %collective-permute-done.3.far, bf16[512,2048]{1,0:T(8,128)(2,1)} %a0.1, ...), custom_call_target="tpu_custom_call" | custom-call | flops 2147483648 | bytes 8388608 | tf_op jit(solution)/shard_map/pallas_call | solution.py:32
  82.0 6.4 %all-to-all-start.2 = ((bf16[8,32,2048]{2,1,0:T(8,128)(2,1)}), bf16[8,32,2048]{2,1,0:T(8,128)(2,1)S(1)}, u32[]{:S(2)}, u32[]{:S(2)}) async-start(bf16[8,32,2048]{2,1,0:T(8,128)(2,1)} %copy-done.12), calls=%async_computation.2 | async-start | bytes 2097152 | tf_op jit(solution)/shard_map/all_to_all | solution.py:195
  88.4 3.1 %collective-permute-start.9 = (bf16[2560,256]{1,0:T(8,128)(2,1)}, bf16[2560,256]{1,0:T(8,128)(2,1)}, u32[]{:S(2)}, u32[]{:S(2)}) collective-permute-start(bf16[2560,256]{1,0:T(8,128)(2,1)} %copy-done.16), channel_id=1, source_target_pairs={{0,1},{1,0},{2,3},{3,2},{4,5},{5,4},{6,7},{7,6},{8,9},{9,8},{10,11... | collective-permute-start | bytes 3932168 | tf_op jit(solution)/shard_map/ppermute | solution.py:23
  91.5 11.0 %all-to-all-done.2.blocks = bf16[8,32,2048]{2,1,0:T(8,128)(2,1)S(1)} async-done(((bf16[8,32,2048]{2,1,0:T(8,128)(2,1)}), bf16[8,32,2048]{2,1,0:T(8,128)(2,1)S(1)}, u32[]{:S(2)}, u32[]{:S(2)}) %all-to-all-start.2) | async-done | bytes 1048608 | tf_op jit(solution)/shard_map/all_to_all | solution.py:195
  103.8 6.5 %all-to-all-start.3 = ((bf16[32,32,512]{2,1,0:T(8,128)(2,1)}), bf16[32,32,512]{2,1,0:T(8,128)(2,1)S(1)}, u32[]{:S(2)}, u32[]{:S(2)}) async-start(bf16[32,32,512]{2,1,0:T(8,128)(2,1)} %bitcast.15), calls=%async_computation.3 | async-start | bytes 2097152 | tf_op jit(solution)/shard_map/all_to_all | solution.py:204
  111.3 2.9 %shard_map.64 = bf16[2048,512]{1,0:T(8,128)(2,1)S(1)} custom-call(bf16[2048,256]{1,0:T(8,128)(2,1)} %bitcast.1.codes, bf16[256,512]{1,0:T(8,128)(2,1)S(1)} %copy-done.14, bf16[2560,256]{1,0:T(8,128)(2,1)} %collective-permute-done.9.message), custom_call_target="tpu_custom_call" | custom-call | flops 1073741824 | bytes 4718592 | tf_op jit(solution)/shard_map/pallas_call | solution.py:32
  115.6 3.9 %copy.8 = bf16[8,256,512]{1,2,0:T(8,128)(2,1)} copy(bf16[8,256,512]{2,1,0:T(8,128)(2,1)} %bitcast.14) | data formatting | bytes 4194304 | tf_op jit(solution)/shard_map/reshape | solution.py:200
  119.5 7.7 %all-to-all-done.3 = bf16[32,32,512]{2,1,0:T(8,128)(2,1)S(1)} async-done(((bf16[32,32,512]{2,1,0:T(8,128)(2,1)}), bf16[32,32,512]{2,1,0:T(8,128)(2,1)S(1)}, u32[]{:S(2)}, u32[]{:S(2)}) %all-to-all-start.3) | async-done | bytes 1048608 | tf_op jit(solution)/shard_map/all_to_all | solution.py:204
  127.2 4.3 %all-to-all-start.4 = ((bf16[8,256,512]{1,2,0:T(8,128)(2,1)}), bf16[8,256,512]{1,2,0:T(8,128)(2,1)}, u32[]{:S(2)}, u32[]{:S(2)}) async-start(bf16[8,256,512]{1,2,0:T(8,128)(2,1)} %copy.8), calls=%async_computation.4 | async-start | bytes 4194304 | tf_op jit(solution)/shard_map/all_to_all | solution.py:200
  131.6 2.9 %collective-permute-start.8 = (bf16[512,1280]{1,0:T(8,128)(2,1)S(1)}, bf16[512,1280]{1,0:T(8,128)(2,1)S(1)}, u32[]{:S(2)}, u32[]{:S(2)}) collective-permute-start(bf16[512,1280]{1,0:T(8,128)(2,1)S(1)} %slice.41), channel_id=1, source_target_pairs={{0,32},{16,48},{32,0},{48,16},{1,33},{17,49},{33,1},{49,17},{2,34}... | collective-permute-start | bytes 3932168 | tf_op jit(solution)/shard_map/ppermute | solution.py:23
  134.5 48.3 %collective-permute-done.8.refs_4_ = bf16[512,1280]{1,0:T(8,128)(2,1)S(1)} collective-permute-done((bf16[512,1280]{1,0:T(8,128)(2,1)S(1)}, bf16[512,1280]{1,0:T(8,128)(2,1)S(1)}, u32[]{:S(2)}, u32[]{:S(2)}) %collective-permute-start.8) | collective-permute-done | bytes 1310752 | tf_op jit(solution)/shard_map/ppermute | solution.py:23
  182.8 4.0 %collective-permute-start.10 = (bf16[4,256,512]{2,1,0:T(8,128)(2,1)S(1)}, bf16[4,256,512]{2,1,0:T(8,128)(2,1)S(1)}, u32[]{:S(2)}, u32[]{:S(2)}) collective-permute-start(bf16[4,256,512]{2,1,0:T(8,128)(2,1)S(1)} %bitcast.11), channel_id=1, source_target_pairs={{0,1},{1,0},{2,3},{3,2},{4,5},{5,4},{6,7},{7,6},{8,9},{9,8},{10,11... | collective-permute-start | bytes 3145736 | tf_op jit(solution)/shard_map/ppermute | solution.py:23
  192.5 4.6 %shard_map.66 = bf16[256,1792]{1,0:T(8,128)(2,1)S(1)} custom-call(bf16[4,256,512]{2,1,0:T(8,128)(2,1)S(1)} %bitcast.12, bf16[4,256,512]{2,1,0:T(8,128)(2,1)S(1)} %collective-permute-done.10.grad_o, bf16[512,1792]{1,0:T(8,128)(2,1)} %refs_0_.3, bf16[512,1280]{1,0:T(8,128)(2,1)S(1)} %copy-done.5, bf16[512,512]{1,0:T(8,128)(2,1)S(1)} %copy-done.9, ...), custom_call_target="tpu_custom_call" | custom-call | flops 1879048192 | bytes 10354688 | tf_op jit(solution)/shard_map/pallas_call | solution.py:32
  201.0 5.8 %shard_map.65 = f32[256,1792]{1,0:T(8,128)} custom-call(bf16[4,256,512]{2,1,0:T(8,128)(2,1)S(1)} %bitcast.13, bf16[4,256,512]{2,1,0:T(8,128)(2,1)S(1)} %collective-permute-done.10.grad_o, bf16[512,1792]{1,0:T(8,128)(2,1)} %refs_0_.3, bf16[512,1280]{1,0:T(8,128)(2,1)S(1)} %copy-done.5, bf16[512,512]{1,0:T(8,128)(2,1)S(1)} %copy-done.9, ...), custom_call_target="tpu_custom_call" | custom-call | flops 1879048192 | bytes 11272192 | tf_op jit(solution)/shard_map/pallas_call | solution.py:32
  206.8 12.0 %collective-permute-done.11 = bf16[256,1792]{1,0:T(8,128)(2,1)S(1)} collective-permute-done((bf16[256,1792]{1,0:T(8,128)(2,1)S(1)}, bf16[256,1792]{1,0:T(8,128)(2,1)S(1)}, u32[]{:S(2)}, u32[]{:S(2)}) %collective-permute-start.11) | collective-permute-done | bytes 917536 | tf_op jit(solution)/shard_map/ppermute | solution.py:23
  218.8 2.9 %add_multiply_fusion = f32[256,1792]{1,0:T(8,128)} fusion(f32[256,1792]{1,0:T(8,128)} %shard_map.65, bf16[256,1792]{1,0:T(8,128)(2,1)S(1)} %collective-permute-done.11), kind=kLoop, calls=%fused_computation.1 | loop fusion | flops 1376256 | bytes 4587520 | tf_op jit(solution)/shard_map/mul | solution.py:220
  (66 shorter events, 39.0 us)
Async XLA Ops:
  0.6 1.5 copy-start
  2.1 3.1 %copy-start.2 = (bf16[2048,1792]{1,0:T(8,128)(2,1)S(1)}, bf16[2048,1792]{1,0:T(8,128)(2,1)}, u32[]{:S(2)}) copy-start(bf16[2048,1792]{1,0:T(8,128)(2,1)} %b.3) | copy-start | bytes 22020100
  8.1 8.4 %collective-permute-start = (f32[2048,256]{1,0:T(8,128)S(1)}, f32[2048,256]{1,0:T(8,128)S(1)}, u32[]{:S(2)}, u32[]{:S(2)}) collective-permute-start(f32[2048,256]{1,0:T(8,128)S(1)} %shard_map.60), channel_id=1, source_target_pairs={{0,1},{1,0},{2,3},{3,2},{4,5},{5,4},{6,7},{7,6},{8,9},{9,8},{10,11... | collective-permute-start | bytes 6291464 | tf_op jit(solution)/shard_map/ppermute | solution.py:23
  10.8 31.1 %collective-permute-start.2 = (bf16[512,1280]{1,0:T(8,128)(2,1)}, bf16[512,1280]{1,0:T(8,128)(2,1)}, u32[]{:S(2)}, u32[]{:S(2)}) collective-permute-start(bf16[512,1280]{1,0:T(8,128)(2,1)} %slice.38), channel_id=1, source_target_pairs={{0,48},{16,0},{32,16},{48,32},{1,49},{17,1},{33,17},{49,33},{2,50}... | collective-permute-start | bytes 3932168 | tf_op jit(solution)/shard_map/ppermute | solution.py:23
  13.3 31.5 %collective-permute-start.1 = (bf16[512,1280]{1,0:T(8,128)(2,1)}, bf16[512,1280]{1,0:T(8,128)(2,1)S(1)}, u32[]{:S(2)}, u32[]{:S(2)}) collective-permute-start(bf16[512,1280]{1,0:T(8,128)(2,1)} %slice.38), channel_id=1, source_target_pairs={{0,16},{16,32},{32,48},{48,0},{1,17},{17,33},{33,49},{49,1},{2,18}... | collective-permute-start | bytes 3932168 | tf_op jit(solution)/shard_map/ppermute | solution.py:23
  13.3 50.9 %collective-permute-start.4 = (bf16[512,2048]{1,0:T(8,128)(2,1)}, bf16[512,2048]{1,0:T(8,128)(2,1)}, u32[]{:S(2)}, u32[]{:S(2)}) collective-permute-start(bf16[512,2048]{1,0:T(8,128)(2,1)} %a0.1), channel_id=1, source_target_pairs={{0,1},{1,0},{2,3},{3,2},{4,5},{5,4},{6,7},{7,6},{8,9},{9,8},{10,11... | collective-permute-start | bytes 6291464 | tf_op jit(solution)/shard_map/ppermute | solution.py:23
  17.8 27.1 %all-to-all-start = ((bf16[8,256,256]{2,1,0:T(8,128)(2,1)}), bf16[8,256,256]{2,1,0:T(8,128)(2,1)}, u32[]{:S(2)}, u32[]{:S(2)}) async-start(bf16[8,256,256]{2,1,0:T(8,128)(2,1)} %bitcast), calls=%async_computation | async-start | bytes 2097152 | tf_op jit(solution)/shard_map/all_to_all | solution.py:179
  25.4 29.9 %copy-start.1 = (bf16[512,1792]{1,0:T(8,128)(2,1)S(1)}, bf16[512,1792]{1,0:T(8,128)(2,1)}, u32[]{:S(2)}) copy-start(bf16[512,1792]{1,0:T(8,128)(2,1)} %refs_0_.3) | copy-start | bytes 5505028
  44.8 2.8 %copy-start.4 = (bf16[512,1280]{1,0:T(8,128)(2,1)}, bf16[512,1280]{1,0:T(8,128)(2,1)S(1)}, u32[]{:S(2)}) copy-start(bf16[512,1280]{1,0:T(8,128)(2,1)S(1)} %collective-permute-done.1.refs_1_) | copy-start | bytes 3932164
  47.7 23.3 %all-to-all-start.1 = ((bf16[8,256,256]{2,1,0:T(8,128)(2,1)}), bf16[8,256,256]{2,1,0:T(8,128)(2,1)}, u32[]{:S(2)}, u32[]{:S(2)}) async-start(bf16[8,256,256]{2,1,0:T(8,128)(2,1)} %copy-done.6), calls=%async_computation.1 | async-start | bytes 2097152 | tf_op jit(solution)/shard_map/all_to_all | solution.py:184
  55.3 2.7 %copy-start.18 = (bf16[512,512]{1,0:T(8,128)(2,1)S(1)}, bf16[512,512]{1,0:T(8,128)(2,1)}, u32[]{:S(2)}) copy-start(bf16[512,512]{1,0:T(8,128)(2,1)} %param.5) | copy-start | bytes 1572868
  56.4 24.9 %collective-permute-start.6 = (bf16[512,512]{1,0:T(8,128)(2,1)}, bf16[512,512]{1,0:T(8,128)(2,1)S(1)}, u32[]{:S(2)}, u32[]{:S(2)}) collective-permute-start(bf16[512,512]{1,0:T(8,128)(2,1)} %get-tuple-element.33), channel_id=1, source_target_pairs={{0,48},{16,0},{32,16},{48,32},{1,49},{17,1},{33,17},{49,33},{2,50}... | collective-permute-start | bytes 1572872 | tf_op jit(solution)/shard_map/ppermute | solution.py:23
  56.8 24.4 %collective-permute-start.5 = (bf16[512,512]{1,0:T(8,128)(2,1)}, bf16[512,512]{1,0:T(8,128)(2,1)S(1)}, u32[]{:S(2)}, u32[]{:S(2)}) collective-permute-start(bf16[512,512]{1,0:T(8,128)(2,1)} %get-tuple-element.33), channel_id=1, source_target_pairs={{0,16},{16,32},{32,48},{48,0},{1,17},{17,33},{33,49},{49,1},{2,18}... | collective-permute-start | bytes 1572872 | tf_op jit(solution)/shard_map/ppermute | solution.py:23
  57.9 22.5 %collective-permute-start.7 = (bf16[512,512]{1,0:T(8,128)(2,1)}, bf16[512,512]{1,0:T(8,128)(2,1)S(1)}, u32[]{:S(2)}, u32[]{:S(2)}) collective-permute-start(bf16[512,512]{1,0:T(8,128)(2,1)} %get-tuple-element.32), channel_id=1, source_target_pairs={{0,32},{16,48},{32,0},{48,16},{1,33},{17,49},{33,1},{49,17},{2,34}... | collective-permute-start | bytes 1572872 | tf_op jit(solution)/shard_map/ppermute | solution.py:23
  60.6 3.6 %collective-permute-start.3 = (bf16[512,256]{1,0:T(8,128)(2,1)}, bf16[512,256]{1,0:T(8,128)(2,1)}, u32[]{:S(2)}, u32[]{:S(2)}) collective-permute-start(bf16[512,256]{1,0:T(8,128)(2,1)} %bitcast.17), channel_id=1, source_target_pairs={{0,1},{1,0},{2,3},{3,2},{4,5},{5,4},{6,7},{7,6},{8,9},{9,8},{10,11... | collective-permute-start | bytes 786440 | tf_op jit(solution)/shard_map/ppermute | solution.py:23
  78.9 2.3 %copy-start.12 = (bf16[8,32,2048]{2,1,0:T(8,128)(2,1)}, bf16[8,32,2048]{2,1,0:T(8,128)(2,1)S(1)}, u32[]{:S(2)}) copy-start(bf16[8,32,2048]{2,1,0:T(8,128)(2,1)S(1)} %get-tuple-element.20) | copy-start | bytes 3145732
  82.0 20.5 %all-to-all-start.2 = ((bf16[8,32,2048]{2,1,0:T(8,128)(2,1)}), bf16[8,32,2048]{2,1,0:T(8,128)(2,1)S(1)}, u32[]{:S(2)}, u32[]{:S(2)}) async-start(bf16[8,32,2048]{2,1,0:T(8,128)(2,1)} %copy-done.12), calls=%async_computation.2 | async-start | bytes 2097152 | tf_op jit(solution)/shard_map/all_to_all | solution.py:195
  88.4 22.0 %collective-permute-start.9 = (bf16[2560,256]{1,0:T(8,128)(2,1)}, bf16[2560,256]{1,0:T(8,128)(2,1)}, u32[]{:S(2)}, u32[]{:S(2)}) collective-permute-start(bf16[2560,256]{1,0:T(8,128)(2,1)} %copy-done.16), channel_id=1, source_target_pairs={{0,1},{1,0},{2,3},{3,2},{4,5},{5,4},{6,7},{7,6},{8,9},{9,8},{10,11... | collective-permute-start | bytes 3932168 | tf_op jit(solution)/shard_map/ppermute | solution.py:23
  103.8 23.4 %all-to-all-start.3 = ((bf16[32,32,512]{2,1,0:T(8,128)(2,1)}), bf16[32,32,512]{2,1,0:T(8,128)(2,1)S(1)}, u32[]{:S(2)}, u32[]{:S(2)}) async-start(bf16[32,32,512]{2,1,0:T(8,128)(2,1)} %bitcast.15), calls=%async_computation.3 | async-start | bytes 2097152 | tf_op jit(solution)/shard_map/all_to_all | solution.py:204
  127.2 55.7 %all-to-all-start.4 = ((bf16[8,256,512]{1,2,0:T(8,128)(2,1)}), bf16[8,256,512]{1,2,0:T(8,128)(2,1)}, u32[]{:S(2)}, u32[]{:S(2)}) async-start(bf16[8,256,512]{1,2,0:T(8,128)(2,1)} %copy.8), calls=%async_computation.4 | async-start | bytes 4194304 | tf_op jit(solution)/shard_map/all_to_all | solution.py:200
  131.6 51.2 %collective-permute-start.8 = (bf16[512,1280]{1,0:T(8,128)(2,1)S(1)}, bf16[512,1280]{1,0:T(8,128)(2,1)S(1)}, u32[]{:S(2)}, u32[]{:S(2)}) collective-permute-start(bf16[512,1280]{1,0:T(8,128)(2,1)S(1)} %slice.41), channel_id=1, source_target_pairs={{0,32},{16,48},{32,0},{48,16},{1,33},{17,49},{33,1},{49,17},{2,34}... | collective-permute-start | bytes 3932168 | tf_op jit(solution)/shard_map/ppermute | solution.py:23
  182.8 4.0 %copy-start.17 = (bf16[512,1280]{1,0:T(8,128)(2,1)}, bf16[512,1280]{1,0:T(8,128)(2,1)S(1)}, u32[]{:S(2)}) copy-start(bf16[512,1280]{1,0:T(8,128)(2,1)S(1)} %collective-permute-done.8.refs_4_) | copy-start | bytes 3932164
  182.8 6.3 %collective-permute-start.10 = (bf16[4,256,512]{2,1,0:T(8,128)(2,1)S(1)}, bf16[4,256,512]{2,1,0:T(8,128)(2,1)S(1)}, u32[]{:S(2)}, u32[]{:S(2)}) collective-permute-start(bf16[4,256,512]{2,1,0:T(8,128)(2,1)S(1)} %bitcast.11), channel_id=1, source_target_pairs={{0,1},{1,0},{2,3},{3,2},{4,5},{5,4},{6,7},{7,6},{8,9},{9,8},{10,11... | collective-permute-start | bytes 3145736 | tf_op jit(solution)/shard_map/ppermute | solution.py:23
  197.1 21.6 %collective-permute-start.11 = (bf16[256,1792]{1,0:T(8,128)(2,1)S(1)}, bf16[256,1792]{1,0:T(8,128)(2,1)S(1)}, u32[]{:S(2)}, u32[]{:S(2)}) collective-permute-start(bf16[256,1792]{1,0:T(8,128)(2,1)S(1)} %shard_map.66), channel_id=1, source_target_pairs={{0,64},{64,0},{1,65},{65,1},{2,66},{66,2},{3,67},{67,3},{4,68},{68... | collective-permute-start | bytes 2752520 | tf_op jit(solution)/shard_map/ppermute | solution.py:23
  (12 other events, 12.1 us)

commit v5 on v4

--- a/solution.py
+++ b/solution.py
@@ -35,7 +35,7 @@
         in_specs=[VMEM] * len(args),
         out_specs=[VMEM] * len(outs) if len(outs) > 1 else VMEM,
         scratch_shapes=scratch,
-        compiler_params=pltpu.CompilerParams(vmem_limit_bytes=48 * 1024 * 1024),
+        compiler_params=pltpu.CompilerParams(vmem_limit_bytes=16 * 1024 * 1024),
         cost_estimate=pl.CostEstimate(flops=flops, bytes_accessed=moved, transcendentals=0),
     )(*args)
 
@@ -75,7 +75,7 @@
         ],
         out_specs=pl.BlockSpec((step, half), lambda i: (i, 0)),
         scratch_shapes=[pltpu.VMEM((wide, half), BF)],
-        compiler_params=pltpu.CompilerParams(vmem_limit_bytes=32 * 1024 * 1024),
+        compiler_params=pltpu.CompilerParams(vmem_limit_bytes=60 * 1024 * 1024),
         cost_estimate=pl.CostEstimate(
             flops=2 * rank * wide * half, bytes_accessed=2 * rank * wide, transcendentals=0
         ),
@@ -123,35 +123,37 @@
                 out[x, i, :, side * width : (side + 1) * width] = piece
 
 
-def last_kernel(side, cuts, grad_m, grad_o, *refs):
-    parts, out, turned = refs[:-2], refs[-2], refs[-1]
+def last_kernel(side, cuts, other, more, grad, *refs):
+    parts = refs[: len(cuts)]
+    before = refs[len(cuts) : len(cuts) + more]
+    out, turned = refs[-2:]
     core, x = lax.axis_index("core"), lax.axis_index("x")
-    half, width = grad_m.shape[1], out.shape[0]
-    at = slice(side * width, (side + 1) * width)
+    half, width = grad.shape[1], out.shape[0]
+    which = 1 - core if other else core
+    rows = pl.ds(pl.multiple_of(which * half, half), half)
     for k in range(4):
-        row = lax.rem(x + 4 - k, 4)
-        first = pl.multiple_of(core * half, half)
-        other = pl.multiple_of((1 - core) * half, half)
-        turned[k, :, pl.ds(first, half)] = grad_m[row, :, at].T
-        turned[k, :, pl.ds(other, half)] = grad_o[row, :, at].T
+        turned[k] = grad[lax.rem(x + 4 - k, 4), :, side * width : (side + 1) * width].T
     step = 256
     for c in range(0, out.shape[1], step):
-        acc = None
+        acc = before[0][:, c : c + step] if more else None
         for ref, (k, start) in zip(parts, cuts):
             if start <= c < start + ref.shape[1]:
-                term = dot(turned[k], ref[:, c - start : c - start + step])
+                term = dot(turned[k], ref[rows, c - start : c - start + step])
                 acc = term if acc is None else acc + term
         out[:, c : c + step] = acc.astype(out.dtype)
 
 
-def term_kernel(codes, own, message, out):
-    rank, outs = out.shape
-    for at in range(0, rank, 512):
-        rows = slice(at, at + 512)
-        for c in range(0, outs, 256):
-            acc = dot(codes[rows], own[:, c : c + 256])
-            acc = acc + dot(message[rows], message[rank + c : rank + c + 256])
-            out[rows, c : c + 256] = acc.astype(BF)
+def term_kernel(codes, own, message, keep, send):
+    y_lo = lax.axis_index("y_lo")
+    rank, outs = codes.shape[0], keep.shape[1]
+    for out, which in ((send, 1 - y_lo), (keep, y_lo)):
+        for at in range(0, rank // 2, 512):
+            rows = pl.ds(pl.multiple_of(which * (rank // 2) + at, 512), 512)
+            left, right = codes[rows, :], message[rows, :]
+            for c in range(0, outs, 256):
+                acc = dot(left, own[:, c : c + 256])
+                acc = acc + dot(right, message[rank + c : rank + c + 256])
+                out[at : at + 512, c : c + 256] = acc.astype(out.dtype)
 
 
 def local(acts, target, proj_b, proj_a):
@@ -165,7 +167,7 @@
     def part_of(array, which, size, axis):
         return lax.dynamic_slice_in_dim(array, which * size, size, axis)
 
-    cut, low = 1280, 512
+    cut, low = 1024, 1024
     plus_a, minus_a = shift(acts[:, :cut], "x", 4, 1), shift(acts[:, :cut], "x", 4, 3)
     pair_a = swap(proj_a, "core")
     target_t = target.T
@@ -194,33 +196,40 @@
     far_b = shift(acts_3[:, low:], "x", 4, 2)
     blocks = lax.all_to_all(partial, ZY, 0, 0)
 
-    term = call(
-        term_kernel, [like((rank, outs))], codes, own, swap(message, "core"), flops=2 * tokens * rank * outs
-    )
-    term = lax.all_to_all(term.reshape(8, width, outs), TOK, 0, 0)
+    keep, send = call(
+        term_kernel,
+        [like((rank // 2, outs), F32), like((rank // 2, outs))],
+        codes, own, swap(message, "core"),
+        flops=2 * tokens * rank * outs,
+    )
+    blocks, far_b, keep, send = barrier((blocks, far_b, keep, send))
+    send = swap(send, "y_lo")
 
     split = call(spread_kernel, [like((4, 8, sub, 2 * width))], blocks, scratch=[pltpu.VMEM((sub, rank), BF)])
     split = split.reshape(32, sub, 2 * width)
     grad_m = lax.all_to_all(split, ("x", "z", "y_hi"), 0, 0).reshape(4, half, 2 * width)
-    grad_m, far_b, term = barrier((grad_m, far_b, term))
+    grad_m, send = barrier((grad_m, send))
+    term = (keep + send.astype(F32)).astype(BF).reshape(4, width, outs)
     grad_o = swap(grad_m, "core")
     parts = [acts, plus_a, plus_b, far_a, far_b, minus_a, minus_b]
     cuts = ((0, 0), (1, 0), (1, cut), (2, 0), (2, low), (3, 0), (3, cut))
 
-    def last(side, dtype):
+    def last(side, other, dtype, *before):
         return call(
-            functools.partial(last_kernel, side, cuts),
+            functools.partial(last_kernel, side, cuts, other, len(before)),
             [like((width, wide), dtype)],
-            grad_m, grad_o, *parts,
-            scratch=[pltpu.VMEM((4, width, tokens), BF)],
-            flops=8 * tokens * width * wide,
+            grad_o if other else grad_m, *parts, *before,
+            scratch=[pltpu.VMEM((4, width, half), BF)],
+            flops=8 * half * width * wide,
         )
 
-    away = swap(last(1, BF), "y_lo")
-    grad_b = (last(0, F32) + away.astype(F32)) * scale
-
+    away = swap(last(1, True, BF, last(1, False, F32)), "y_lo")
+    here = last(0, True, F32, last(0, False, F32))
+    grad_b = (here + away.astype(F32)) * scale
+
+    term = lax.all_to_all(term, "x", 0, 0)
     sums = term[0].astype(F32)
-    for i in range(1, 8):
+    for i in range(1, 4):
         sums = sums + term[i].astype(F32)
     grad_a = (sums * scale).T
     return (grad_a, grad_b)

time: 223 us -> 211 us (0.946)
  waiting for transfers between devices: 109 us -> 60.9 us
  blocking collectives: 0 us -> 34.9 us
  Pallas kernels: 26.4 us -> 40.5 us
  starting transfers between devices: 51.7 us -> 43.1 us
  local copies, waits for them, and re-layouts: 27.2 us -> 20.6 us
  other arithmetic: 6.68 us -> 9.53 us
    ppermute x12 -> x13, waiting for transfers between devices: 83.4 us -> 45.8 us  [shift(): lax.ppermute(array, axis, [(i, (i + step) % size) for i in range(size)])]
    all_to_all x0 -> x1, blocking collectives: none -> 34.9 us  [local(): lax.all_to_all(split, ('x', 'z', 'y_hi'), 0, 0).reshape(4, half, 2 * width)]
    all_to_all x1, waiting for transfers between devices: 11 us -> 0.01 us  [local(): blocks = lax.all_to_all(partial, ZY, 0, 0)]
    all_to_all x1, waiting for transfers between devices: 0.01 us -> 9.28 us  [local(): blocks = lax.all_to_all(mine, ZY, 0, 0)]
    pallas_call x2, Pallas kernels: 5.82 us -> 14.1 us  [codes_call(): pl.pallas_call(functools.partial(codes_kernel, other), grid=(rank // step...]
    unnamed x40 -> x32, local copies, waits for them, and re-layouts: 20.2 us -> 13.3 us
    all_to_all x2 -> x1, waiting for transfers between devices: 7.7 us -> 1.29 us  [local(): term = lax.all_to_all(term, 'x', 0, 0)]
    pallas_call x6 -> x8, Pallas kernels: 20.6 us -> 26.4 us  [call(): pl.pallas_call(body, out_shape=outs if len(outs) > 1 else outs[0], in_spe...]
  transfers between devices with their start and end apart: 17 -> 17, of which waited for: 9 -> 9; matrix products, arithmetic and copies ran while one was open for 6% -> 8% of each run, Pallas kernels for 9% -> 16%
where the time goes in v5:
time: 211 us; the launch traced here: 210 us
  waiting for transfers between devices  60.9 us (29%)
  starting transfers between devices  43.1 us (20%)
  Pallas kernels  40.5 us (19%)
  blocking collectives  34.9 us (17%)
  local copies, waits for them, and re-layouts  20.6 us (10%)
  other arithmetic  9.53 us (5%)
    ppermute x13, waiting for transfers between devices, shift(): lax.ppermute(array, axis, [(i, (i + step) % size) for i in range(size)])  45.8 us
    all_to_all x1, blocking collectives, local(): lax.all_to_all(split, ('x', 'z', 'y_hi'), 0, 0).reshape(4, half, 2 * width)  34.9 us
    pallas_call x8, Pallas kernels, call(): pl.pallas_call(body, out_shape=outs if len(outs) > 1 else outs[0], in_spe...  26.4 us
    ppermute x13, starting transfers between devices, shift(): lax.ppermute(array, axis, [(i, (i + step) % size) for i in range(size)])  19.3 us
    pallas_call x2, Pallas kernels, codes_call(): pl.pallas_call(functools.partial(codes_kernel, other), grid=(rank // step...  14.1 us
    unnamed x32, local copies, waits for them, and re-layouts  13.3 us
    all_to_all x1, waiting for transfers between devices, local(): blocks = lax.all_to_all(mine, ZY, 0, 0)  9.28 us
    all_to_all x1, starting transfers between devices, local(): blocks = lax.all_to_all(mine, ZY, 0, 0)  7.66 us
  transfers between devices with their start and end apart: 17, of which 9 were waited for; matrix products, arithmetic and copies ran while one was open for 8% of the time, Pallas kernels for 16%

profile of v5, /device:TPU:1, one launch (start us, length us, event | category | flops | bytes accessed | tf_op | source)
XLA Modules:
  0.0 210.3 jit_solution(3695297566144096977)
XLA Ops:
  0.6 7.1 %shard_map.60 = f32[2048,256]{1,0:T(8,128)} custom-call(bf16[512,1792]{1,0:T(8,128)(2,1)} %refs_0_.7, bf16[2048,1792]{1,0:T(8,128)(2,1)} %b.3), custom_call_target="tpu_custom_call" | custom-call | flops 1879048192 | bytes 7340032 | tf_op jit(solution)/shard_map/pallas_call | solution.py:68
  13.2 7.0 %shard_map.59 = f32[2048,256]{1,0:T(8,128)} custom-call(bf16[512,1792]{1,0:T(8,128)(2,1)} %refs_0_.7, bf16[2048,1792]{1,0:T(8,128)(2,1)} %b.3), custom_call_target="tpu_custom_call" | custom-call | flops 1879048192 | bytes 7340032 | tf_op jit(solution)/shard_map/pallas_call | solution.py:68
  20.2 3.4 %add_convert_fusion.1 = bf16[2048,256]{1,0:T(8,128)(2,1)} fusion(f32[2048,256]{1,0:T(8,128)} %shard_map.59, f32[2048,256]{1,0:T(8,128)} %collective-permute-done), kind=kLoop, calls=%fused_computation.1 | loop fusion | flops 1048576 | bytes 5242880 | tf_op jit(solution)/shard_map/convert_element_type | solution.py:180
  23.6 7.7 %all-to-all-start = ((bf16[8,256,256]{2,1,0:T(8,128)(2,1)}), bf16[8,256,256]{2,1,0:T(8,128)(2,1)}, u32[]{:S(2)}, u32[]{:S(2)}) async-start(bf16[8,256,256]{2,1,0:T(8,128)(2,1)} %bitcast), calls=%async_computation | async-start | bytes 2097152 | tf_op jit(solution)/shard_map/all_to_all | solution.py:181
  31.3 4.5 %collective-permute-done.2.refs_5_ = bf16[512,1024]{1,0:T(8,128)(2,1)S(1)} collective-permute-done((bf16[512,1024]{1,0:T(8,128)(2,1)}, bf16[512,1024]{1,0:T(8,128)(2,1)S(1)}, u32[]{:S(2)}, u32[]{:S(2)}) %collective-permute-start.2) | collective-permute-done | bytes 1048608 | tf_op jit(solution)/shard_map/ppermute | solution.py:23
  35.8 3.1 %collective-permute-done.1.refs_1_ = bf16[512,1024]{1,0:T(8,128)(2,1)} collective-permute-done((bf16[512,1024]{1,0:T(8,128)(2,1)}, bf16[512,1024]{1,0:T(8,128)(2,1)}, u32[]{:S(2)}, u32[]{:S(2)}) %collective-permute-start.1) | collective-permute-done | bytes 1048608 | tf_op jit(solution)/shard_map/ppermute | solution.py:23
  38.9 9.3 %all-to-all-done.blocks = bf16[8,256,256]{2,1,0:T(8,128)(2,1)} async-done(((bf16[8,256,256]{2,1,0:T(8,128)(2,1)}), bf16[8,256,256]{2,1,0:T(8,128)(2,1)}, u32[]{:S(2)}, u32[]{:S(2)}) %all-to-all-start) | async-done | bytes 1048608 | tf_op jit(solution)/shard_map/all_to_all | solution.py:181
  50.5 4.2 %all-to-all-start.1 = ((bf16[8,256,256]{2,1,0:T(8,128)(2,1)}), bf16[8,256,256]{2,1,0:T(8,128)(2,1)}, u32[]{:S(2)}, u32[]{:S(2)}) async-start(bf16[8,256,256]{2,1,0:T(8,128)(2,1)} %copy-done.7), calls=%async_computation.1 | async-start | bytes 2097152 | tf_op jit(solution)/shard_map/all_to_all | solution.py:186
  65.8 4.5 %all-to-all-done.1 = bf16[8,256,256]{2,1,0:T(8,128)(2,1)} async-done(((bf16[8,256,256]{2,1,0:T(8,128)(2,1)}), bf16[8,256,256]{2,1,0:T(8,128)(2,1)}, u32[]{:S(2)}, u32[]{:S(2)}) %all-to-all-start.1) | async-done | bytes 1048608 | tf_op jit(solution)/shard_map/all_to_all | solution.py:186
  71.9 5.5 %shard_map.62 = (bf16[256,512]{1,0:T(8,128)(2,1)S(1)}, bf16[2560,256]{1,0:T(8,128)(2,1)}, bf16[8,32,2048]{2,1,0:T(8,128)(2,1)S(1)}) custom-call(bf16[2048,256]{1,0:T(8,128)(2,1)} %bitcast.1.codes, bf16[512,256]{1,0:T(8,128)(2,1)S(1)} %bitcast.12, bf16[512,256]{1,0:T(8,128)(2,1)S(1)} %collective-permute-done.3.far, bf16[512,2048]{1,0:T(8,128)(2,1)S(1)} %copy-done.11, ...), custom_call_target="tpu_custom_call" | custom-call | flops 2147483648 | bytes 8388608 | tf_op jit(solution)/shard_map/pallas_call | solution.py:32
  79.1 2.6 %collective-permute-start.9 = (bf16[2560,256]{1,0:T(8,128)(2,1)}, bf16[2560,256]{1,0:T(8,128)(2,1)}, u32[]{:S(2)}, u32[]{:S(2)}) collective-permute-start(bf16[2560,256]{1,0:T(8,128)(2,1)} %get-tuple-element.28), channel_id=1, source_target_pairs={{0,1},{1,0},{2,3},{3,2},{4,5},{5,4},{6,7},{7,6},{8,9},{9,8},{10,11... | collective-permute-start | bytes 3932168 | tf_op jit(solution)/shard_map/ppermute | solution.py:23
  81.7 17.8 %collective-permute-done.6.refs_6_ = bf16[512,768]{1,0:T(8,128)(2,1)} collective-permute-done((bf16[512,768]{1,0:T(8,128)(2,1)}, bf16[512,768]{1,0:T(8,128)(2,1)}, u32[]{:S(2)}, u32[]{:S(2)}) %collective-permute-start.6) | collective-permute-done | bytes 786464 | tf_op jit(solution)/shard_map/ppermute | solution.py:23
  99.7 6.5 %all-to-all-start.2 = ((bf16[8,32,2048]{2,1,0:T(8,128)(2,1)}), bf16[8,32,2048]{2,1,0:T(8,128)(2,1)}, u32[]{:S(2)}, u32[]{:S(2)}) async-start(bf16[8,32,2048]{2,1,0:T(8,128)(2,1)} %copy-done.10), calls=%async_computation.2 | async-start | bytes 2097152 | tf_op jit(solution)/shard_map/all_to_all | solution.py:197
  108.7 2.9 %shard_map.63 = (f32[1024,512]{1,0:T(8,128)S(1)}, bf16[1024,512]{1,0:T(8,128)(2,1)S(1)}) custom-call(bf16[2048,256]{1,0:T(8,128)(2,1)} %bitcast.1.codes, bf16[256,512]{1,0:T(8,128)(2,1)S(1)} %copy-done.14, bf16[2560,256]{1,0:T(8,128)(2,1)} %collective-permute-done.9.message), custom_call_target="tpu_custom_call" | custom-call | flops 1073741824 | bytes 5767168 | tf_op jit(solution)/shard_map/pallas_call | solution.py:32
  113.9 11.4 %collective-permute-done.8.refs_4_ = bf16[512,768]{1,0:T(8,128)(2,1)S(1)} collective-permute-done((bf16[512,768]{1,0:T(8,128)(2,1)S(1)}, bf16[512,768]{1,0:T(8,128)(2,1)S(1)}, u32[]{:S(2)}, u32[]{:S(2)}) %collective-permute-start.8) | collective-permute-done | bytes 786464 | tf_op jit(solution)/shard_map/ppermute | solution.py:23
  128.3 34.9 %all_to_all.25 = bf16[32,32,512]{2,1,0:T(8,128)(2,1)} all-to-all(bf16[32,32,512]{2,1,0:T(8,128)(2,1)S(1)} %bitcast.11), channel_id=1, replica_groups=mesh['y_lo'=2,'x'=4,'z'=4,'y_hi'=2,'core'=2] {'x','z','y_hi'}, dimensions={0} | all-to-all | bytes 2097152 | tf_op jit(solution)/shard_map/all_to_all | solution.py:210
  163.2 4.4 %collective-permute-start.11 = (bf16[4,256,512]{2,1,0:T(8,128)(2,1)}, bf16[4,256,512]{2,1,0:T(8,128)(2,1)}, u32[]{:S(2)}, u32[]{:S(2)}) collective-permute-start(bf16[4,256,512]{2,1,0:T(8,128)(2,1)} %bitcast.5.grad), channel_id=1, source_target_pairs={{0,1},{1,0},{2,3},{3,2},{4,5},{5,4},{6,7},{7,6},{8,9},{9,8},{10,11... | collective-permute-start | bytes 3145736 | tf_op jit(solution)/shard_map/ppermute | solution.py:23
  171.3 5.4 %all-to-all-start.4 = ((bf16[4,256,512]{1,2,0:T(8,128)(2,1)}), bf16[4,256,512]{1,2,0:T(8,128)(2,1)}, u32[]{:S(2)}, u32[]{:S(2)}) async-start(bf16[4,256,512]{1,2,0:T(8,128)(2,1)} %copy.8), calls=%async_computation.4 | async-start | bytes 2097152 | tf_op jit(solution)/shard_map/all_to_all | solution.py:230
  177.8 3.5 %shard_map.67.refs_7_ = f32[256,1792]{1,0:T(8,128)S(1)} custom-call(bf16[4,256,512]{2,1,0:T(8,128)(2,1)} %bitcast.5.grad, bf16[512,1792]{1,0:T(8,128)(2,1)S(1)} %copy-done.1, bf16[512,1024]{1,0:T(8,128)(2,1)} %collective-permute-done.1.refs_1_, bf16[512,768]{1,0:T(8,128)(2,1)} %collective-permute-done.5.refs_2_, ...), custom_call_target="tpu_custom_call" | custom-call | flops 939524096 | bytes 10223616 | tf_op jit(solution)/shard_map/pallas_call | solution.py:32
  181.3 4.4 %shard_map.68 = bf16[256,1792]{1,0:T(8,128)(2,1)} custom-call(bf16[4,256,512]{2,1,0:T(8,128)(2,1)} %collective-permute-done.11.grad, bf16[512,1792]{1,0:T(8,128)(2,1)S(1)} %copy-done.1, bf16[512,1024]{1,0:T(8,128)(2,1)} %collective-permute-done.1.refs_1_, bf16[512,768]{1,0:T(8,128)(2,1)} %collective-permute-done.5.refs_2_, ...), custom_call_target="tpu_custom_call" | custom-call | flops 939524096 | bytes 11141120 | tf_op jit(solution)/shard_map/pallas_call | solution.py:32
  185.8 3.5 %shard_map.65.refs_7_ = f32[256,1792]{1,0:T(8,128)S(1)} custom-call(bf16[4,256,512]{2,1,0:T(8,128)(2,1)} %bitcast.5.grad, bf16[512,1792]{1,0:T(8,128)(2,1)S(1)} %copy-done.1, bf16[512,1024]{1,0:T(8,128)(2,1)} %collective-permute-done.1.refs_1_, bf16[512,768]{1,0:T(8,128)(2,1)} %collective-permute-done.5.refs_2_, ...), custom_call_target="tpu_custom_call" | custom-call | flops 939524096 | bytes 10223616 | tf_op jit(solution)/shard_map/pallas_call | solution.py:32
  195.5 3.5 %shard_map.66 = f32[256,1792]{1,0:T(8,128)S(1)} custom-call(bf16[4,256,512]{2,1,0:T(8,128)(2,1)} %collective-permute-done.11.grad, bf16[512,1792]{1,0:T(8,128)(2,1)S(1)} %copy-done.1, bf16[512,1024]{1,0:T(8,128)(2,1)} %collective-permute-done.1.refs_1_, bf16[512,768]{1,0:T(8,128)(2,1)} %collective-permute-done.5.refs_2_, ...), custom_call_target="tpu_custom_call" | custom-call | flops 939524096 | bytes 12058624 | tf_op jit(solution)/shard_map/pallas_call | solution.py:32
  199.0 8.7 %collective-permute-done.12 = bf16[256,1792]{1,0:T(8,128)(2,1)} collective-permute-done((bf16[256,1792]{1,0:T(8,128)(2,1)}, bf16[256,1792]{1,0:T(8,128)(2,1)}, u32[]{:S(2)}, u32[]{:S(2)}) %collective-permute-start.12) | collective-permute-done | bytes 917536 | tf_op jit(solution)/shard_map/ppermute | solution.py:23
  207.7 2.6 %add_multiply_fusion = f32[256,1792]{1,0:T(8,128)} fusion(f32[256,1792]{1,0:T(8,128)S(1)} %shard_map.66, bf16[256,1792]{1,0:T(8,128)(2,1)} %collective-permute-done.12), kind=kLoop, calls=%fused_computation.2 | loop fusion | flops 1376256 | bytes 4587520 | tf_op jit(solution)/shard_map/mul | solution.py:228
  (63 shorter events, 40.9 us)
Async XLA Ops:
  0.6 8.6 %copy-start = (bf16[512,1792]{1,0:T(8,128)(2,1)S(1)}, bf16[512,1792]{1,0:T(8,128)(2,1)}, u32[]{:S(2)}) copy-start(bf16[512,1792]{1,0:T(8,128)(2,1)} %refs_0_.7) | copy-start | bytes 5505028
  7.8 12.4 %collective-permute-start = (f32[2048,256]{1,0:T(8,128)}, f32[2048,256]{1,0:T(8,128)}, u32[]{:S(2)}, u32[]{:S(2)}) collective-permute-start(f32[2048,256]{1,0:T(8,128)} %shard_map.60), channel_id=1, source_target_pairs={{0,1},{1,0},{2,3},{3,2},{4,5},{5,4},{6,7},{7,6},{8,9},{9,8},{10,11... | collective-permute-start | bytes 6291464 | tf_op jit(solution)/shard_map/ppermute | solution.py:23
  10.3 25.5 %collective-permute-start.2 = (bf16[512,1024]{1,0:T(8,128)(2,1)}, bf16[512,1024]{1,0:T(8,128)(2,1)S(1)}, u32[]{:S(2)}, u32[]{:S(2)}) collective-permute-start(bf16[512,1024]{1,0:T(8,128)(2,1)} %slice.26), channel_id=1, source_target_pairs={{0,48},{16,0},{32,16},{48,32},{1,49},{17,1},{33,17},{49,33},{2,50}... | collective-permute-start | bytes 3145736 | tf_op jit(solution)/shard_map/ppermute | solution.py:23
  12.9 26.0 %collective-permute-start.1 = (bf16[512,1024]{1,0:T(8,128)(2,1)}, bf16[512,1024]{1,0:T(8,128)(2,1)}, u32[]{:S(2)}, u32[]{:S(2)}) collective-permute-start(bf16[512,1024]{1,0:T(8,128)(2,1)} %slice.26), channel_id=1, source_target_pairs={{0,16},{16,32},{32,48},{48,0},{1,17},{17,33},{33,49},{49,1},{2,18}... | collective-permute-start | bytes 3145736 | tf_op jit(solution)/shard_map/ppermute | solution.py:23
  12.9 52.9 %collective-permute-start.4 = (bf16[512,2048]{1,0:T(8,128)(2,1)}, bf16[512,2048]{1,0:T(8,128)(2,1)}, u32[]{:S(2)}, u32[]{:S(2)}) collective-permute-start(bf16[512,2048]{1,0:T(8,128)(2,1)} %a0.1), channel_id=1, source_target_pairs={{0,1},{1,0},{2,3},{3,2},{4,5},{5,4},{6,7},{7,6},{8,9},{9,8},{10,11... | collective-permute-start | bytes 6291464 | tf_op jit(solution)/shard_map/ppermute | solution.py:23
  23.6 24.6 %all-to-all-start = ((bf16[8,256,256]{2,1,0:T(8,128)(2,1)}), bf16[8,256,256]{2,1,0:T(8,128)(2,1)}, u32[]{:S(2)}, u32[]{:S(2)}) async-start(bf16[8,256,256]{2,1,0:T(8,128)(2,1)} %bitcast), calls=%async_computation | async-start | bytes 2097152 | tf_op jit(solution)/shard_map/all_to_all | solution.py:181
  31.3 23.5 %copy-start.1 = (bf16[512,1792]{1,0:T(8,128)(2,1)S(1)}, bf16[512,1792]{1,0:T(8,128)(2,1)}, u32[]{:S(2)}) copy-start(bf16[512,1792]{1,0:T(8,128)(2,1)} %refs_0_.7) | copy-start | bytes 5505028
  50.5 19.8 %all-to-all-start.1 = ((bf16[8,256,256]{2,1,0:T(8,128)(2,1)}), bf16[8,256,256]{2,1,0:T(8,128)(2,1)}, u32[]{:S(2)}, u32[]{:S(2)}) async-start(bf16[8,256,256]{2,1,0:T(8,128)(2,1)} %copy-done.7), calls=%async_computation.1 | async-start | bytes 2097152 | tf_op jit(solution)/shard_map/all_to_all | solution.py:186
  55.9 43.8 %collective-permute-start.7 = (bf16[512,1024]{1,0:T(8,128)(2,1)}, bf16[512,1024]{1,0:T(8,128)(2,1)}, u32[]{:S(2)}, u32[]{:S(2)}) collective-permute-start(bf16[512,1024]{1,0:T(8,128)(2,1)} %slice.28), channel_id=1, source_target_pairs={{0,32},{16,48},{32,0},{48,16},{1,33},{17,49},{33,1},{49,17},{2,34}... | collective-permute-start | bytes 3145736 | tf_op jit(solution)/shard_map/ppermute | solution.py:23
  60.8 5.0 %collective-permute-start.3 = (bf16[512,256]{1,0:T(8,128)(2,1)}, bf16[512,256]{1,0:T(8,128)(2,1)S(1)}, u32[]{:S(2)}, u32[]{:S(2)}) collective-permute-start(bf16[512,256]{1,0:T(8,128)(2,1)} %bitcast.14), channel_id=1, source_target_pairs={{0,1},{1,0},{2,3},{3,2},{4,5},{5,4},{6,7},{7,6},{8,9},{9,8},{10,11... | collective-permute-start | bytes 786440 | tf_op jit(solution)/shard_map/ppermute | solution.py:23
  63.2 36.4 %collective-permute-start.6 = (bf16[512,768]{1,0:T(8,128)(2,1)}, bf16[512,768]{1,0:T(8,128)(2,1)}, u32[]{:S(2)}, u32[]{:S(2)}) collective-permute-start(bf16[512,768]{1,0:T(8,128)(2,1)} %slice.27), channel_id=1, source_target_pairs={{0,48},{16,0},{32,16},{48,32},{1,49},{17,1},{33,17},{49,33},{2,50}... | collective-permute-start | bytes 2359304 | tf_op jit(solution)/shard_map/ppermute | solution.py:23
  64.0 35.7 %collective-permute-start.5 = (bf16[512,768]{1,0:T(8,128)(2,1)}, bf16[512,768]{1,0:T(8,128)(2,1)}, u32[]{:S(2)}, u32[]{:S(2)}) collective-permute-start(bf16[512,768]{1,0:T(8,128)(2,1)} %slice.27), channel_id=1, source_target_pairs={{0,16},{16,32},{32,48},{48,0},{1,17},{17,33},{33,49},{49,1},{2,18}... | collective-permute-start | bytes 2359304 | tf_op jit(solution)/shard_map/ppermute | solution.py:23
  70.3 1.6 copy-start.11
  79.1 29.6 %copy-start.14 = (bf16[256,512]{1,0:T(8,128)(2,1)S(1)}, bf16[256,512]{1,0:T(8,128)(2,1)}, u32[]{:S(2)}) copy-start(bf16[256,512]{1,0:T(8,128)(2,1)} %copy-done.13) | copy-start | bytes 786436
  79.1 29.6 %collective-permute-start.9 = (bf16[2560,256]{1,0:T(8,128)(2,1)}, bf16[2560,256]{1,0:T(8,128)(2,1)}, u32[]{:S(2)}, u32[]{:S(2)}) collective-permute-start(bf16[2560,256]{1,0:T(8,128)(2,1)} %get-tuple-element.28), channel_id=1, source_target_pairs={{0,1},{1,0},{2,3},{3,2},{4,5},{5,4},{6,7},{7,6},{8,9},{9,8},{10,11... | collective-permute-start | bytes 3932168 | tf_op jit(solution)/shard_map/ppermute | solution.py:23
  99.7 26.5 %all-to-all-start.2 = ((bf16[8,32,2048]{2,1,0:T(8,128)(2,1)}), bf16[8,32,2048]{2,1,0:T(8,128)(2,1)}, u32[]{:S(2)}, u32[]{:S(2)}) async-start(bf16[8,32,2048]{2,1,0:T(8,128)(2,1)} %copy-done.10), calls=%async_computation.2 | async-start | bytes 2097152 | tf_op jit(solution)/shard_map/all_to_all | solution.py:197
  106.3 19.0 %collective-permute-start.8 = (bf16[512,768]{1,0:T(8,128)(2,1)S(1)}, bf16[512,768]{1,0:T(8,128)(2,1)S(1)}, u32[]{:S(2)}, u32[]{:S(2)}) collective-permute-start(bf16[512,768]{1,0:T(8,128)(2,1)S(1)} %slice.29), channel_id=1, source_target_pairs={{0,32},{16,48},{32,0},{48,16},{1,33},{17,49},{33,1},{49,17},{2,34}... | collective-permute-start | bytes 2359304 | tf_op jit(solution)/shard_map/ppermute | solution.py:23
  126.2 41.5 %copy-start.9 = (f32[1024,512]{1,0:T(8,128)S(1)}, f32[1024,512]{1,0:T(8,128)}, u32[]{:S(2)}) copy-start(f32[1024,512]{1,0:T(8,128)} %copy-done.8) | copy-start | bytes 6291460
  126.2 37.0 %collective-permute-start.10 = (bf16[1024,512]{1,0:T(8,128)(2,1)}, bf16[1024,512]{1,0:T(8,128)(2,1)S(1)}, u32[]{:S(2)}, u32[]{:S(2)}) collective-permute-start(bf16[1024,512]{1,0:T(8,128)(2,1)} %copy-done.12), channel_id=1, source_target_pairs={{0,64},{64,0},{1,65},{65,1},{2,66},{66,2},{3,67},{67,3},{4,68},{68... | collective-permute-start | bytes 3145736 | tf_op jit(solution)/shard_map/ppermute | solution.py:23
  163.2 18.1 %collective-permute-start.11 = (bf16[4,256,512]{2,1,0:T(8,128)(2,1)}, bf16[4,256,512]{2,1,0:T(8,128)(2,1)}, u32[]{:S(2)}, u32[]{:S(2)}) collective-permute-start(bf16[4,256,512]{2,1,0:T(8,128)(2,1)} %bitcast.5.grad), channel_id=1, source_target_pairs={{0,1},{1,0},{2,3},{3,2},{4,5},{5,4},{6,7},{7,6},{8,9},{9,8},{10,11... | collective-permute-start | bytes 3145736 | tf_op jit(solution)/shard_map/ppermute | solution.py:23
  171.3 20.5 %all-to-all-start.4 = ((bf16[4,256,512]{1,2,0:T(8,128)(2,1)}), bf16[4,256,512]{1,2,0:T(8,128)(2,1)}, u32[]{:S(2)}, u32[]{:S(2)}) async-start(bf16[4,256,512]{1,2,0:T(8,128)(2,1)} %copy.8), calls=%async_computation.4 | async-start | bytes 2097152 | tf_op jit(solution)/shard_map/all_to_all | solution.py:230
  185.7 22.0 %collective-permute-start.12 = (bf16[256,1792]{1,0:T(8,128)(2,1)}, bf16[256,1792]{1,0:T(8,128)(2,1)}, u32[]{:S(2)}, u32[]{:S(2)}) collective-permute-start(bf16[256,1792]{1,0:T(8,128)(2,1)} %shard_map.68), channel_id=1, source_target_pairs={{0,64},{64,0},{1,65},{65,1},{2,66},{66,2},{3,67},{67,3},{4,68},{68... | collective-permute-start | bytes 2752520 | tf_op jit(solution)/shard_map/ppermute | solution.py:23
  191.8 2.2 %copy-start.4 = (bf16[512,768]{1,0:T(8,128)(2,1)S(1)}, bf16[512,768]{1,0:T(8,128)(2,1)}, u32[]{:S(2)}) copy-start(bf16[512,768]{1,0:T(8,128)(2,1)} %copy-done.2) | copy-start | bytes 2359300
  194.0 1.5 copy-start.6
  (8 other events, 8.3 us)

commit v6 on v4

--- a/solution.py
+++ b/solution.py
@@ -35,7 +35,7 @@
         in_specs=[VMEM] * len(args),
         out_specs=[VMEM] * len(outs) if len(outs) > 1 else VMEM,
         scratch_shapes=scratch,
-        compiler_params=pltpu.CompilerParams(vmem_limit_bytes=48 * 1024 * 1024),
+        compiler_params=pltpu.CompilerParams(vmem_limit_bytes=16 * 1024 * 1024),
         cost_estimate=pl.CostEstimate(flops=flops, bytes_accessed=moved, transcendentals=0),
     )(*args)
 
@@ -123,25 +123,22 @@
                 out[x, i, :, side * width : (side + 1) * width] = piece
 
 
-def last_kernel(side, cuts, grad_m, grad_o, *refs):
-    parts, out, turned = refs[:-2], refs[-2], refs[-1]
-    core, x = lax.axis_index("core"), lax.axis_index("x")
-    half, width = grad_m.shape[1], out.shape[0]
-    at = slice(side * width, (side + 1) * width)
+def last_kernel(side, other, more, grad, acts, *refs):
+    out, turned = refs[-2:]
+    core = lax.axis_index("core")
+    half, width = grad.shape[1], out.shape[0]
+    which = 1 - core if other else core
+    rows = pl.ds(pl.multiple_of(which * half, half), half)
     for k in range(4):
-        row = lax.rem(x + 4 - k, 4)
-        first = pl.multiple_of(core * half, half)
-        other = pl.multiple_of((1 - core) * half, half)
-        turned[k, :, pl.ds(first, half)] = grad_m[row, :, at].T
-        turned[k, :, pl.ds(other, half)] = grad_o[row, :, at].T
-    step = 256
-    for c in range(0, out.shape[1], step):
-        acc = None
-        for ref, (k, start) in zip(parts, cuts):
-            if start <= c < start + ref.shape[1]:
-                term = dot(turned[k], ref[:, c - start : c - start + step])
-                acc = term if acc is None else acc + term
-        out[:, c : c + step] = acc.astype(out.dtype)
+        turned[k] = grad[k, :, side * width : (side + 1) * width].T
+    for c in range(0, out.shape[1], 256):
+        cols = slice(c, c + 256)
+        acc = dot(turned[0], acts[0, rows, cols])
+        for k in range(1, 4):
+            acc = acc + dot(turned[k], acts[k, rows, cols])
+        if more:
+            acc = acc + refs[0][:, cols]
+        out[:, cols] = acc.astype(out.dtype)
 
 
 def term_kernel(codes, own, message, out):
@@ -150,8 +147,7 @@
         rows = slice(at, at + 512)
         for c in range(0, outs, 256):
             acc = dot(codes[rows], own[:, c : c + 256])
-            acc = acc + dot(message[rows], message[rank + c : rank + c + 256])
-            out[rows, c : c + 256] = acc.astype(BF)
+            out[rows, c : c + 256] = acc + dot(message[rows], message[rank + c : rank + c + 256])
 
 
 def local(acts, target, proj_b, proj_a):
@@ -160,26 +156,19 @@
     outs, wide = target.shape[1], acts.shape[1]
     half, sub, width = tokens // 2, tokens // 16, rank // 8
     scale = -2.0 / (tokens * 8)
-    barrier = lax.optimization_barrier
 
     def part_of(array, which, size, axis):
         return lax.dynamic_slice_in_dim(array, which * size, size, axis)
 
-    cut, low = 1280, 512
-    plus_a, minus_a = shift(acts[:, :cut], "x", 4, 1), shift(acts[:, :cut], "x", 4, 3)
+    row = lax.all_gather(acts, "x")
     pair_a = swap(proj_a, "core")
     target_t = target.T
     near_t = part_of(target_t, core, half, 1)
     pair_t = swap(part_of(target_t, 1 - core, half, 1), "core")
 
-    theirs = codes_call(True, acts, proj_b)
-    arrived = swap(theirs, "core")
-    mine = codes_call(False, acts, proj_b)
-    mine = (mine + arrived).astype(BF).reshape(8, width, half)
+    arrived = swap(codes_call(True, acts, proj_b), "core")
+    mine = (codes_call(False, acts, proj_b) + arrived).astype(BF).reshape(8, width, half)
     blocks = lax.all_to_all(mine, ZY, 0, 0)
-    blocks, plus_a, minus_a, acts_2 = barrier((blocks, plus_a, minus_a, acts))
-    plus_b, minus_b = shift(acts_2[:, cut:], "x", 4, 1), shift(acts_2[:, cut:], "x", 4, 3)
-    far_a = shift(acts_2[:, :low], "x", 4, 2)
     codes = call(sum_and_copy, [like((8, width, half))], blocks)
     codes = lax.all_to_all(codes, ZY, 0, 0).reshape(rank, half)
 
@@ -190,39 +179,31 @@
         scratch=[pltpu.VMEM((half, 2 * outs), BF)],
         flops=8 * half * rank * outs,
     )
-    partial, plus_b, minus_b, far_a, acts_3 = barrier((partial, plus_b, minus_b, far_a, acts_2))
-    far_b = shift(acts_3[:, low:], "x", 4, 2)
     blocks = lax.all_to_all(partial, ZY, 0, 0)
 
     term = call(
-        term_kernel, [like((rank, outs))], codes, own, swap(message, "core"), flops=2 * tokens * rank * outs
-    )
-    term = lax.all_to_all(term.reshape(8, width, outs), TOK, 0, 0)
+        term_kernel, [like((rank, outs), F32)], codes, own, swap(message, "core"), flops=2 * tokens * rank * outs
+    )
+    blocks, term = lax.optimization_barrier((blocks, term))
+    grad_a = (lax.psum_scatter(term, TOK, scatter_dimension=0, tiled=True) * scale).T
 
     split = call(spread_kernel, [like((4, 8, sub, 2 * width))], blocks, scratch=[pltpu.VMEM((sub, rank), BF)])
     split = split.reshape(32, sub, 2 * width)
     grad_m = lax.all_to_all(split, ("x", "z", "y_hi"), 0, 0).reshape(4, half, 2 * width)
-    grad_m, far_b, term = barrier((grad_m, far_b, term))
     grad_o = swap(grad_m, "core")
-    parts = [acts, plus_a, plus_b, far_a, far_b, minus_a, minus_b]
-    cuts = ((0, 0), (1, 0), (1, cut), (2, 0), (2, low), (3, 0), (3, cut))
-
-    def last(side, dtype):
+
+    def last(side, other, dtype, *before):
         return call(
-            functools.partial(last_kernel, side, cuts),
+            functools.partial(last_kernel, side, other, len(before)),
             [like((width, wide), dtype)],
-            grad_m, grad_o, *parts,
-            scratch=[pltpu.VMEM((4, width, tokens), BF)],
-            flops=8 * tokens * width * wide,
+            grad_o if other else grad_m, row, *before,
+            scratch=[pltpu.VMEM((4, width, half), BF)],
+            flops=8 * half * width * wide,
         )
 
-    away = swap(last(1, BF), "y_lo")
-    grad_b = (last(0, F32) + away.astype(F32)) * scale
-
-    sums = term[0].astype(F32)
-    for i in range(1, 8):
-        sums = sums + term[i].astype(F32)
-    grad_a = (sums * scale).T
+    away = swap(last(1, True, BF, last(1, False, F32)), "y_lo")
+    here = last(0, True, F32, last(0, False, F32))
+    grad_b = (here + away.astype(F32)) * scale
     return (grad_a, grad_b)
 
 

time: 223 us -> 198 us (0.89)
  the two profiles are of different devices: /device:TPU:1 before, /device:TPU:110 now
where the time goes in v6:
time: 198 us; the launch traced here: 197 us
  blocking collectives  82.9 us (42%)
  waiting for transfers between devices  49.6 us (25%)
  Pallas kernels  18.9 us (10%)
  between operations  15.6 us (8%)
  local copies, waits for them, and re-layouts  14.8 us (7%)
  starting transfers between devices  12.8 us (6%)
  other arithmetic  2.82 us (1%)
    all_to_all x1, blocking collectives, local(): lax.all_to_all(split, ('x', 'z', 'y_hi'), 0, 0).reshape(4, half, 2 * width)  61.7 us
    ppermute x6, waiting for transfers between devices, shift(): lax.ppermute(array, axis, [(i, (i + step) % size) for i in range(size)])  24.6 us
    all_to_all x1, blocking collectives, local(): blocks = lax.all_to_all(mine, ZY, 0, 0)  21.2 us
    unnamed x21, local copies, waits for them, and re-layouts  14.8 us
    pallas_call x8, Pallas kernels, call(): pl.pallas_call(body, out_shape=outs if len(outs) > 1 else outs[0], in_spe...  13.1 us
    all_to_all x1, waiting for transfers between devices, local(): codes = lax.all_to_all(codes, ZY, 0, 0).reshape(rank, half)  12.2 us
    all_to_all x1, waiting for transfers between devices, local(): blocks = lax.all_to_all(partial, ZY, 0, 0)  12.2 us
    all_to_all x1, starting transfers between devices, local(): blocks = lax.all_to_all(partial, ZY, 0, 0)  5.93 us
  transfers between devices with their start and end apart: 10, of which 5 were waited for; matrix products, arithmetic and copies ran while one was open for 1% of the time, Pallas kernels for 10%

profile of v6, /device:TPU:110, one launch (start us, length us, event | category | flops | bytes accessed | tf_op | source)
XLA Modules:
  0.0 197.5 jit_solution(2922239972646919376)
XLA Ops:
  9.5 3.1 %copy-done.2 = bf16[2048,1792]{1,0:T(8,128)(2,1)S(1)} copy-done((bf16[2048,1792]{1,0:T(8,128)(2,1)S(1)}, bf16[2048,1792]{1,0:T(8,128)(2,1)}, u32[]{:S(2)}) %copy-start.2) | copy-done | bytes 7340056
  12.6 2.9 %shard_map.60 = f32[2048,256]{1,0:T(8,128)S(1)} custom-call(bf16[512,1792]{1,0:T(8,128)(2,1)S(1)} %copy-done.4, bf16[2048,1792]{1,0:T(8,128)(2,1)S(1)} %copy-done.2), custom_call_target="tpu_custom_call" | custom-call | flops 1879048192 | bytes 7340032 | tf_op jit(solution)/shard_map/pallas_call | solution.py:68
  16.1 2.9 %shard_map.59 = f32[2048,256]{1,0:T(8,128)S(1)} custom-call(bf16[512,1792]{1,0:T(8,128)(2,1)S(1)} %copy-done.4, bf16[2048,1792]{1,0:T(8,128)(2,1)S(1)} %copy-done.2), custom_call_target="tpu_custom_call" | custom-call | flops 1879048192 | bytes 7340032 | tf_op jit(solution)/shard_map/pallas_call | solution.py:68
  19.0 2.8 %collective-permute-done = f32[2048,256]{1,0:T(8,128)S(1)} collective-permute-done((f32[2048,256]{1,0:T(8,128)S(1)}, f32[2048,256]{1,0:T(8,128)S(1)}, u32[]{:S(2)}, u32[]{:S(2)}) %collective-permute-start) | collective-permute-done | bytes 2097184 | tf_op jit(solution)/shard_map/ppermute | solution.py:23
  22.1 21.2 %all_to_all.20.blocks = bf16[8,256,256]{2,1,0:T(8,128)(2,1)S(1)} all-to-all(bf16[8,256,256]{2,1,0:T(8,128)(2,1)S(1)} %bitcast.20), channel_id=1, replica_groups=mesh['y_lo'=2,'x'=4,'z'=4,'y_hi'=2,'core'=2] {'z','y_hi'}, dimensions={0} | all-to-all | bytes 2097152 | tf_op jit(solution)/shard_map/all_to_all | solution.py:171
  43.3 1.1 shard_map.61
  44.4 5.9 %all-to-all-start.1 = ((bf16[8,256,256]{2,1,0:T(8,128)(2,1)}), bf16[8,256,256]{2,1,0:T(8,128)(2,1)S(1)}, u32[]{:S(2)}, u32[]{:S(2)}) async-start(bf16[8,256,256]{2,1,0:T(8,128)(2,1)} %shard_map.61), calls=%async_computation.1 | async-start | bytes 2097152 | tf_op jit(solution)/shard_map/all_to_all | solution.py:173
  50.7 1.4 collective-permute-done.1.far
  52.1 12.2 %all-to-all-done.1 = bf16[8,256,256]{2,1,0:T(8,128)(2,1)S(1)} async-done(((bf16[8,256,256]{2,1,0:T(8,128)(2,1)}), bf16[8,256,256]{2,1,0:T(8,128)(2,1)S(1)}, u32[]{:S(2)}, u32[]{:S(2)}) %all-to-all-start.1) | async-done | bytes 1048608 | tf_op jit(solution)/shard_map/all_to_all | solution.py:173
  64.3 5.8 %shard_map.62 = (bf16[256,512]{1,0:T(8,128)(2,1)S(1)}, bf16[2560,256]{1,0:T(8,128)(2,1)}, bf16[8,32,2048]{2,1,0:T(8,128)(2,1)S(1)}) custom-call(bf16[2048,256]{1,0:T(8,128)(2,1)S(1)} %bitcast.17, bf16[512,256]{1,0:T(8,128)(2,1)S(1)} %bitcast.19, bf16[512,256]{1,0:T(8,128)(2,1)S(1)} %collective-permute-done.1.far, bf16[512,2048]{1,0:T(8,128)(2,1)} %a0.1, ...), custom_call_target="tpu_custom_call" | custom-call | flops 2147483648 | bytes 8388608 | tf_op jit(solution)/shard_map/pallas_call | solution.py:32
  71.8 5.9 %all-to-all-start.2 = ((bf16[8,32,2048]{2,1,0:T(8,128)(2,1)}), bf16[8,32,2048]{2,1,0:T(8,128)(2,1)S(1)}, u32[]{:S(2)}, u32[]{:S(2)}) async-start(bf16[8,32,2048]{2,1,0:T(8,128)(2,1)} %copy-done.5), calls=%async_computation.2 | async-start | bytes 2097152 | tf_op jit(solution)/shard_map/all_to_all | solution.py:182
  78.7 1.3 shard_map.63
  79.9 2.0 %copy-done.3 = f32[2048,512]{1,0:T(8,128)} copy-done((f32[2048,512]{1,0:T(8,128)}, f32[2048,512]{1,0:T(8,128)S(1)}, u32[]{:S(2)}) %copy-start.3) | copy-done | bytes 4194328
  82.0 12.2 %all-to-all-done.2.blocks = bf16[8,32,2048]{2,1,0:T(8,128)(2,1)S(1)} async-done(((bf16[8,32,2048]{2,1,0:T(8,128)(2,1)}), bf16[8,32,2048]{2,1,0:T(8,128)(2,1)S(1)}, u32[]{:S(2)}, u32[]{:S(2)}) %all-to-all-start.2) | async-done | bytes 1048608 | tf_op jit(solution)/shard_map/all_to_all | solution.py:182
  94.5 61.7 %all_to_all.21 = bf16[32,32,512]{2,1,0:T(8,128)(2,1)S(1)} all-to-all(bf16[32,32,512]{2,1,0:T(8,128)(2,1)S(1)} %bitcast.16), channel_id=1, replica_groups=mesh['y_lo'=2,'x'=4,'z'=4,'y_hi'=2,'core'=2] {'x','z','y_hi'}, dimensions={0} | all-to-all | bytes 2097152 | tf_op jit(solution)/shard_map/all_to_all | solution.py:192
  156.2 3.1 %copy-done = bf16[2048,1792]{1,0:T(8,128)(2,1)S(1)} copy-done((bf16[2048,1792]{1,0:T(8,128)(2,1)S(1)}, bf16[2048,1792]{1,0:T(8,128)(2,1)}, u32[]{:S(2)}) %copy-start) | copy-done | bytes 7340056
  159.3 1.2 shard_map.67.refs_0_
  160.4 1.9 copy-done.1
  162.3 1.2 shard_map.68
  163.8 1.2 shard_map.65.refs_0_
  164.9 1.2 shard_map.66
  166.1 20.4 %collective-permute-done.5 = bf16[256,1792]{1,0:T(8,128)(2,1)S(1)} collective-permute-done((bf16[256,1792]{1,0:T(8,128)(2,1)S(1)}, bf16[256,1792]{1,0:T(8,128)(2,1)S(1)}, u32[]{:S(2)}, u32[]{:S(2)}) %collective-permute-start.5) | collective-permute-done | bytes 917536 | tf_op jit(solution)/shard_map/ppermute | solution.py:23
  186.5 1.4 add_multiply_fusion
  187.9 1.1 multiply_bitcast_fusion
  (35 shorter events, 7.0 us)
Async XLA Ops:
  8.0 1.5 copy-start.4
  8.0 148.2 %all-gather.3.cloned.1.call-start = ((), (), s32[]{:S(2)}) async-start(), calls=%async_computation.6 | async-start | bytes 9175040 | tf_op jit(solution)/shard_map/all_gather | solution.py:163
  9.5 3.1 %copy-start.2 = (bf16[2048,1792]{1,0:T(8,128)(2,1)S(1)}, bf16[2048,1792]{1,0:T(8,128)(2,1)}, u32[]{:S(2)}) copy-start(bf16[2048,1792]{1,0:T(8,128)(2,1)} %b.3) | copy-start | bytes 22020100
  15.5 6.3 %collective-permute-start = (f32[2048,256]{1,0:T(8,128)S(1)}, f32[2048,256]{1,0:T(8,128)S(1)}, u32[]{:S(2)}, u32[]{:S(2)}) collective-permute-start(f32[2048,256]{1,0:T(8,128)S(1)} %shard_map.60), channel_id=1, source_target_pairs={{0,1},{1,0},{2,3},{3,2},{4,5},{5,4},{6,7},{7,6},{8,9},{9,8},{10,11... | collective-permute-start | bytes 6291464 | tf_op jit(solution)/shard_map/ppermute | solution.py:23
  15.6 36.5 %collective-permute-start.2 = (bf16[512,2048]{1,0:T(8,128)(2,1)}, bf16[512,2048]{1,0:T(8,128)(2,1)}, u32[]{:S(2)}, u32[]{:S(2)}) collective-permute-start(bf16[512,2048]{1,0:T(8,128)(2,1)} %a0.1), channel_id=1, source_target_pairs={{0,1},{1,0},{2,3},{3,2},{4,5},{5,4},{6,7},{7,6},{8,9},{9,8},{10,11... | collective-permute-start | bytes 6291464 | tf_op jit(solution)/shard_map/ppermute | solution.py:23
  43.3 7.0 %copy-start.8 = (bf16[512,512]{1,0:T(8,128)(2,1)S(1)}, bf16[512,512]{1,0:T(8,128)(2,1)}, u32[]{:S(2)}) copy-start(bf16[512,512]{1,0:T(8,128)(2,1)} %param.5) | copy-start | bytes 1572868
  44.4 19.8 %all-to-all-start.1 = ((bf16[8,256,256]{2,1,0:T(8,128)(2,1)}), bf16[8,256,256]{2,1,0:T(8,128)(2,1)S(1)}, u32[]{:S(2)}, u32[]{:S(2)}) async-start(bf16[8,256,256]{2,1,0:T(8,128)(2,1)} %shard_map.61), calls=%async_computation.1 | async-start | bytes 2097152 | tf_op jit(solution)/shard_map/all_to_all | solution.py:173
  50.5 1.6 collective-permute-start.1
  70.1 1.0 copy-start.5
  71.1 0.7 copy-start.6
  71.8 5.9 %collective-permute-start.3 = (bf16[2560,256]{1,0:T(8,128)(2,1)}, bf16[2560,256]{1,0:T(8,128)(2,1)S(1)}, u32[]{:S(2)}, u32[]{:S(2)}) collective-permute-start(bf16[2560,256]{1,0:T(8,128)(2,1)} %get-tuple-element.9), channel_id=1, source_target_pairs={{0,1},{1,0},{2,3},{3,2},{4,5},{5,4},{6,7},{7,6},{8,9},{9,8},{10,11... | collective-permute-start | bytes 3932168 | tf_op jit(solution)/shard_map/ppermute | solution.py:23
  71.8 22.4 %all-to-all-start.2 = ((bf16[8,32,2048]{2,1,0:T(8,128)(2,1)}), bf16[8,32,2048]{2,1,0:T(8,128)(2,1)S(1)}, u32[]{:S(2)}, u32[]{:S(2)}) async-start(bf16[8,32,2048]{2,1,0:T(8,128)(2,1)} %copy-done.5), calls=%async_computation.2 | async-start | bytes 2097152 | tf_op jit(solution)/shard_map/all_to_all | solution.py:182
  77.7 110.2 %reduce-scatter.2.cloned.1.call-start = ((), (), s32[]{:S(2)}) async-start(), calls=%async_computation.5 | async-start | bytes 4718592 | tf_op jit(solution)/shard_map/reduce_scatter | solution.py:188
  77.7 1.0 copy-start.7
  79.9 2.1 %copy-start.3 = (f32[2048,512]{1,0:T(8,128)}, f32[2048,512]{1,0:T(8,128)S(1)}, u32[]{:S(2)}) copy-start(f32[2048,512]{1,0:T(8,128)S(1)} %shard_map.63) | copy-start | bytes 12582916
  156.2 4.3 %collective-permute-start.4 = (bf16[4,256,512]{2,1,0:T(8,128)(2,1)S(1)}, bf16[4,256,512]{2,1,0:T(8,128)(2,1)S(1)}, u32[]{:S(2)}, u32[]{:S(2)}) collective-permute-start(bf16[4,256,512]{2,1,0:T(8,128)(2,1)S(1)} %bitcast.13), channel_id=1, source_target_pairs={{0,1},{1,0},{2,3},{3,2},{4,5},{5,4},{6,7},{7,6},{8,9},{9,8},{10,11... | collective-permute-start | bytes 3145736 | tf_op jit(solution)/shard_map/ppermute | solution.py:23
  156.2 3.1 %copy-start = (bf16[2048,1792]{1,0:T(8,128)(2,1)S(1)}, bf16[2048,1792]{1,0:T(8,128)(2,1)}, u32[]{:S(2)}) copy-start(bf16[2048,1792]{1,0:T(8,128)(2,1)} %all-gather.3.cloned.1.call-done) | copy-start | bytes 22020100
  159.3 3.1 %copy-start.1 = (bf16[2048,1792]{1,0:T(8,128)(2,1)S(1)}, bf16[2048,1792]{1,0:T(8,128)(2,1)}, u32[]{:S(2)}) copy-start(bf16[2048,1792]{1,0:T(8,128)(2,1)} %all-gather.3.cloned.1.call-done) | copy-start | bytes 22020100
  163.5 23.0 %collective-permute-start.5 = (bf16[256,1792]{1,0:T(8,128)(2,1)S(1)}, bf16[256,1792]{1,0:T(8,128)(2,1)S(1)}, u32[]{:S(2)}, u32[]{:S(2)}) collective-permute-start(bf16[256,1792]{1,0:T(8,128)(2,1)S(1)} %shard_map.68), channel_id=1, source_target_pairs={{0,64},{64,0},{1,65},{65,1},{2,66},{66,2},{3,67},{67,3},{4,68},{68... | collective-permute-start | bytes 2752520 | tf_op jit(solution)/shard_map/ppermute | solution.py:23
Sparse Core Ops, SparseCore 0:
  10.5 74.4 all-gather.2
Sparse Core Ops, SparseCore 1:
  94.3 60.5 reduce-scatter.1

commit v7 on v6

--- a/solution.py
+++ b/solution.py
@@ -90,7 +90,7 @@
 
 def residual_kernel(codes, near, far, a0, a1, own, message, partial, held):
     rank, outs = codes.shape[0], a0.shape[0]
-    step = 256
+    step = 512
     for j, (target, a) in enumerate(((near, a0), (far, a1))):
         for at in range(0, outs, step):
             rows = slice(at, at + step)
@@ -100,7 +100,8 @@
             if j == 0:
                 own[:, rows] = left
             else:
-                message[rank + at : rank + at + step] = left
+                for c in range(0, step, 256):
+                    message[rank + at + c : rank + at + c + 256] = left[:, c : c + 256]
     message[:rank] = codes[...]
     sub = partial.shape[1]
     for at in range(0, rank, 512):
@@ -110,27 +111,27 @@
             partial[i, :, cols] = term[i * sub : (i + 1) * sub].astype(BF)
 
 
-def spread_kernel(blocks, out, held):
+def spread_kernel(blocks, away, own, held):
     y_lo = lax.axis_index("y_lo")
     held[...] = total(blocks).astype(BF)
     rank = held.shape[1]
     width = rank // 8
-    for x in range(4):
-        for side in range(2):
-            start = (y_lo if side == 0 else 1 - y_lo) * (rank // 2) + x * width
-            piece = held[:, pl.ds(pl.multiple_of(start, width), width)]
+    for out, side in ((away, 1 - y_lo), (own, y_lo)):
+        for x in range(4):
+            start = pl.multiple_of(side * (rank // 2) + x * width, width)
+            piece = held[:, pl.ds(start, width)]
             for i in range(out.shape[1]):
-                out[x, i, :, side * width : (side + 1) * width] = piece
-
-
-def last_kernel(side, other, more, grad, acts, *refs):
+                out[x, i] = piece
+
+
+def last_kernel(other, more, grad, acts, *refs):
     out, turned = refs[-2:]
     core = lax.axis_index("core")
     half, width = grad.shape[1], out.shape[0]
     which = 1 - core if other else core
     rows = pl.ds(pl.multiple_of(which * half, half), half)
     for k in range(4):
-        turned[k] = grad[k, :, side * width : (side + 1) * width].T
+        turned[k] = grad[k].T
     for c in range(0, out.shape[1], 256):
         cols = slice(c, c + 256)
         acc = dot(turned[0], acts[0, rows, cols])
@@ -147,7 +148,8 @@
         rows = slice(at, at + 512)
         for c in range(0, outs, 256):
             acc = dot(codes[rows], own[:, c : c + 256])
-            out[rows, c : c + 256] = acc + dot(message[rows], message[rank + c : rank + c + 256])
+            acc = acc + dot(message[rows], message[rank + c : rank + c + 256])
+            out[rows, c : c + 256] = acc.astype(BF)
 
 
 def local(acts, target, proj_b, proj_a):
@@ -182,29 +184,43 @@
     blocks = lax.all_to_all(partial, ZY, 0, 0)
 
     term = call(
-        term_kernel, [like((rank, outs), F32)], codes, own, swap(message, "core"), flops=2 * tokens * rank * outs
-    )
-    blocks, term = lax.optimization_barrier((blocks, term))
-    grad_a = (lax.psum_scatter(term, TOK, scatter_dimension=0, tiled=True) * scale).T
-
-    split = call(spread_kernel, [like((4, 8, sub, 2 * width))], blocks, scratch=[pltpu.VMEM((sub, rank), BF)])
-    split = split.reshape(32, sub, 2 * width)
-    grad_m = lax.all_to_all(split, ("x", "z", "y_hi"), 0, 0).reshape(4, half, 2 * width)
-    grad_o = swap(grad_m, "core")
-
-    def last(side, other, dtype, *before):
+        term_kernel, [like((rank, outs))], codes, own, swap(message, "core"), flops=2 * tokens * rank * outs
+    )
+    term = term.reshape(2, 4, width, outs).transpose(1, 0, 2, 3)
+    term = lax.all_to_all(term, "x", 0, 0)
+
+    blocks, row = lax.optimization_barrier((blocks, row))
+    spread = like((4, 8, sub, width))
+    split_a, split_o = call(spread_kernel, [spread, spread], blocks, scratch=[pltpu.VMEM((sub, rank), BF)])
+
+    def gather(split):
+        split = lax.all_to_all(split.reshape(32, sub, width), ("x", "z", "y_hi"), 0, 0)
+        return split.reshape(4, half, width)
+
+    def last(grad, other, dtype, *before):
         return call(
-            functools.partial(last_kernel, side, other, len(before)),
+            functools.partial(last_kernel, other, len(before)),
             [like((width, wide), dtype)],
-            grad_o if other else grad_m, row, *before,
+            grad, row, *before,
             scratch=[pltpu.VMEM((4, width, half), BF)],
             flops=8 * half * width * wide,
         )
 
-    away = swap(last(1, True, BF, last(1, False, F32)), "y_lo")
-    here = last(0, True, F32, last(0, False, F32))
+    grad = gather(split_a)
+    grad, split_o, term = lax.optimization_barrier((grad, split_o, term))
+    away = last(swap(grad, "core"), True, BF, last(grad, False, F32))
+    away = swap(away, "y_lo")
+    grad = gather(split_o)
+    here = last(swap(grad, "core"), True, F32, last(grad, False, F32))
     grad_b = (here + away.astype(F32)) * scale
-    return (grad_a, grad_b)
+
+    sums = term[0].astype(F32)
+    for i in range(1, 4):
+        sums = sums + term[i].astype(F32)
+    y_lo = lax.axis_index("y_lo")
+    pick = functools.partial(lax.dynamic_index_in_dim, sums, axis=0, keepdims=False)
+    grad_a = pick(y_lo) + swap(pick(1 - y_lo).astype(BF), "y_lo").astype(F32)
+    return ((grad_a * scale).T, grad_b)
 
 
 def solution(mesh):

time: 198 us -> 203 us (1.025)
  the two profiles are of different devices: /device:TPU:110 before, /device:TPU:1 now
where the time goes in v7:
time: 203 us; the launch traced here: 202 us
  waiting for transfers between devices  74.6 us (37%)
  blocking collectives  39.5 us (19%)
  starting transfers between devices  28.1 us (14%)
  Pallas kernels  20.5 us (10%)
  local copies, waits for them, and re-layouts  19.4 us (10%)
  between operations  14.3 us (7%)
  other arithmetic  5.54 us (3%)
    all_to_all x1, waiting for transfers between devices, local(): term = lax.all_to_all(term, 'x', 0, 0)  24.5 us
    all_to_all x1, blocking collectives, local(): blocks = lax.all_to_all(mine, ZY, 0, 0)  23.9 us
    ppermute x8, waiting for transfers between devices, shift(): lax.ppermute(array, axis, [(i, (i + step) % size) for i in range(size)])  23.4 us
    unnamed x22, local copies, waits for them, and re-layouts  16.9 us
    all_to_all x1, blocking collectives, gather(): lax.all_to_all(split.reshape(32, sub, width), ('x', 'z', 'y_hi'), 0, 0)  15.6 us
    pallas_call x8, Pallas kernels, call(): pl.pallas_call(body, out_shape=outs if len(outs) > 1 else outs[0], in_spe...  14.7 us
    ppermute x8, starting transfers between devices, shift(): lax.ppermute(array, axis, [(i, (i + step) % size) for i in range(size)])  12.6 us
    all_to_all x1, waiting for transfers between devices, local(): codes = lax.all_to_all(codes, ZY, 0, 0).reshape(rank, half)  11.8 us
  transfers between devices with their start and end apart: 13, of which 7 were waited for; matrix products, arithmetic and copies ran while one was open for 3% of the time, Pallas kernels for 10%

profile of v7, /device:TPU:1, one launch (start us, length us, event | category | flops | bytes accessed | tf_op | source)
XLA Modules:
  0.0 201.8 jit_solution(8697465568873087183)
XLA Ops:
  8.7 3.1 %copy-done.3 = bf16[2048,1792]{1,0:T(8,128)(2,1)S(1)} copy-done((bf16[2048,1792]{1,0:T(8,128)(2,1)S(1)}, bf16[2048,1792]{1,0:T(8,128)(2,1)}, u32[]{:S(2)}) %copy-start.3) | copy-done | bytes 7340056
  11.7 2.9 %shard_map.60 = f32[2048,256]{1,0:T(8,128)S(1)} custom-call(bf16[512,1792]{1,0:T(8,128)(2,1)S(1)} %copy-done.4, bf16[2048,1792]{1,0:T(8,128)(2,1)S(1)} %copy-done.3), custom_call_target="tpu_custom_call" | custom-call | flops 1879048192 | bytes 7340032 | tf_op jit(solution)/shard_map/pallas_call | solution.py:68
  16.3 2.9 %shard_map.59 = f32[2048,256]{1,0:T(8,128)S(1)} custom-call(bf16[512,1792]{1,0:T(8,128)(2,1)S(1)} %copy-done.4, bf16[2048,1792]{1,0:T(8,128)(2,1)S(1)} %copy-done.3), custom_call_target="tpu_custom_call" | custom-call | flops 1879048192 | bytes 7340032 | tf_op jit(solution)/shard_map/pallas_call | solution.py:68
  19.2 2.8 %collective-permute-done = f32[2048,256]{1,0:T(8,128)S(1)} collective-permute-done((f32[2048,256]{1,0:T(8,128)S(1)}, f32[2048,256]{1,0:T(8,128)S(1)}, u32[]{:S(2)}, u32[]{:S(2)}) %collective-permute-start) | collective-permute-done | bytes 2097184 | tf_op jit(solution)/shard_map/ppermute | solution.py:23
  22.4 23.9 %all_to_all.30.blocks = bf16[8,256,256]{2,1,0:T(8,128)(2,1)S(1)} all-to-all(bf16[8,256,256]{2,1,0:T(8,128)(2,1)S(1)} %bitcast.35), channel_id=1, replica_groups=mesh['y_lo'=2,'x'=4,'z'=4,'y_hi'=2,'core'=2] {'z','y_hi'}, dimensions={0} | all-to-all | bytes 2097152 | tf_op jit(solution)/shard_map/all_to_all | solution.py:173
  47.3 3.6 %all-to-all-start.1 = ((bf16[8,256,256]{2,1,0:T(8,128)(2,1)}), bf16[8,256,256]{2,1,0:T(8,128)(2,1)S(1)}, u32[]{:S(2)}, u32[]{:S(2)}) async-start(bf16[8,256,256]{2,1,0:T(8,128)(2,1)} %shard_map.61), calls=%async_computation.1 | async-start | bytes 2097152 | tf_op jit(solution)/shard_map/all_to_all | solution.py:175
  51.1 1.9 collective-permute-start.1
  54.2 11.8 %all-to-all-done.1 = bf16[8,256,256]{2,1,0:T(8,128)(2,1)S(1)} async-done(((bf16[8,256,256]{2,1,0:T(8,128)(2,1)}), bf16[8,256,256]{2,1,0:T(8,128)(2,1)S(1)}, u32[]{:S(2)}, u32[]{:S(2)}) %all-to-all-start.1) | async-done | bytes 1048608 | tf_op jit(solution)/shard_map/all_to_all | solution.py:175
  66.0 6.6 %shard_map.62 = (bf16[256,512]{1,0:T(8,128)(2,1)S(1)}, bf16[2560,256]{1,0:T(8,128)(2,1)}, bf16[8,32,2048]{2,1,0:T(8,128)(2,1)}) custom-call(bf16[2048,256]{1,0:T(8,128)(2,1)S(1)} %bitcast.26, bf16[512,256]{1,0:T(8,128)(2,1)S(1)} %bitcast.33, bf16[512,256]{1,0:T(8,128)(2,1)S(1)} %collective-permute-done.1.far, bf16[512,2048]{1,0:T(8,128)(2,1)} %a0.1, ...), custom_call_target="tpu_custom_call" | custom-call | flops 2147483648 | bytes 8388608 | tf_op jit(solution)/shard_map/pallas_call | solution.py:32
  72.5 3.1 %collective-permute-start.3 = (bf16[2560,256]{1,0:T(8,128)(2,1)}, bf16[2560,256]{1,0:T(8,128)(2,1)S(1)}, u32[]{:S(2)}, u32[]{:S(2)}) collective-permute-start(bf16[2560,256]{1,0:T(8,128)(2,1)} %get-tuple-element.17), channel_id=1, source_target_pairs={{0,1},{1,0},{2,3},{3,2},{4,5},{5,4},{6,7},{7,6},{8,9},{9,8},{10,11... | collective-permute-start | bytes 3932168 | tf_op jit(solution)/shard_map/ppermute | solution.py:23
  75.7 3.6 %all-to-all-start.2 = ((bf16[8,32,2048]{2,1,0:T(8,128)(2,1)}), bf16[8,32,2048]{2,1,0:T(8,128)(2,1)S(1)}, u32[]{:S(2)}, u32[]{:S(2)}) async-start(bf16[8,32,2048]{2,1,0:T(8,128)(2,1)} %get-tuple-element.12), calls=%async_computation.2 | async-start | bytes 2097152 | tf_op jit(solution)/shard_map/all_to_all | solution.py:184
  84.1 2.4 %copy.8 = bf16[2,4,256,512]{2,3,0,1:T(8,128)(2,1)} copy(bf16[2,4,256,512]{3,2,1,0:T(8,128)(2,1)S(1)} %bitcast.25) | data formatting | bytes 4194304 | tf_op jit(solution)/shard_map/reshape | solution.py:189
  86.5 10.1 %all-to-all-done.2.blocks = bf16[8,32,2048]{2,1,0:T(8,128)(2,1)S(1)} async-done(((bf16[8,32,2048]{2,1,0:T(8,128)(2,1)}), bf16[8,32,2048]{2,1,0:T(8,128)(2,1)S(1)}, u32[]{:S(2)}, u32[]{:S(2)}) %all-to-all-start.2) | async-done | bytes 1048608 | tf_op jit(solution)/shard_map/all_to_all | solution.py:184
  96.5 4.5 %all-to-all-start.4 = ((bf16[4,2,256,512]{2,3,1,0:T(8,128)(2,1)}), bf16[4,2,256,512]{2,3,1,0:T(8,128)(2,1)}, u32[]{:S(2)}, u32[]{:S(2)}) async-start(bf16[4,2,256,512]{2,3,1,0:T(8,128)(2,1)} %bitcast.34), calls=%async_computation.4 | async-start | bytes 4194304 | tf_op jit(solution)/shard_map/all_to_all | solution.py:190
  102.1 24.5 %all-to-all-done.4 = bf16[4,2,256,512]{2,3,1,0:T(8,128)(2,1)} async-done(((bf16[4,2,256,512]{2,3,1,0:T(8,128)(2,1)}), bf16[4,2,256,512]{2,3,1,0:T(8,128)(2,1)}, u32[]{:S(2)}, u32[]{:S(2)}) %all-to-all-start.4) | async-done | bytes 2097184 | tf_op jit(solution)/shard_map/all_to_all | solution.py:190
  126.6 15.6 %all_to_all.31 = bf16[32,32,256]{2,1,0:T(8,128)(2,1)S(1)} all-to-all(bf16[32,32,256]{2,1,0:T(8,128)(2,1)S(1)} %bitcast.32), channel_id=1, replica_groups=mesh['y_lo'=2,'x'=4,'z'=4,'y_hi'=2,'core'=2] {'x','z','y_hi'}, dimensions={0} | all-to-all | bytes 1048576 | tf_op jit(solution)/shard_map/all_to_all | solution.py:197
  142.2 2.9 %collective-permute-start.6 = (bf16[4,256,256]{2,1,0:T(8,128)(2,1)S(1)}, bf16[4,256,256]{2,1,0:T(8,128)(2,1)S(1)}, u32[]{:S(2)}, u32[]{:S(2)}) collective-permute-start(bf16[4,256,256]{2,1,0:T(8,128)(2,1)S(1)} %bitcast.30), channel_id=1, source_target_pairs={{0,1},{1,0},{2,3},{3,2},{4,5},{5,4},{6,7},{7,6},{8,9},{9,8},{10,11... | collective-permute-start | bytes 1572872 | tf_op jit(solution)/shard_map/ppermute | solution.py:23
  145.1 3.9 %all-to-all-start.5 = ((bf16[32,32,256]{2,1,0:T(8,128)(2,1)}), bf16[32,32,256]{2,1,0:T(8,128)(2,1)S(1)}, u32[]{:S(2)}, u32[]{:S(2)}) async-start(bf16[32,32,256]{2,1,0:T(8,128)(2,1)} %bitcast.12), calls=%async_computation.5 | async-start | bytes 1048576 | tf_op jit(solution)/shard_map/all_to_all | solution.py:197
  149.0 3.1 %copy-done = bf16[2048,1792]{1,0:T(8,128)(2,1)S(1)} copy-done((bf16[2048,1792]{1,0:T(8,128)(2,1)S(1)}, bf16[2048,1792]{1,0:T(8,128)(2,1)}, u32[]{:S(2)}) %copy-start) | copy-done | bytes 7340056
  157.9 4.2 %all-to-all-done.5 = bf16[32,32,256]{2,1,0:T(8,128)(2,1)S(1)} async-done(((bf16[32,32,256]{2,1,0:T(8,128)(2,1)}), bf16[32,32,256]{2,1,0:T(8,128)(2,1)S(1)}, u32[]{:S(2)}, u32[]{:S(2)}) %all-to-all-start.5) | async-done | bytes 524320 | tf_op jit(solution)/shard_map/all_to_all | solution.py:197
  163.5 19.5 %collective-permute-done.4 = bf16[256,512]{0,1:T(8,128)(2,1)S(1)} collective-permute-done((bf16[256,512]{0,1:T(8,128)(2,1)S(1)}, bf16[256,512]{0,1:T(8,128)(2,1)S(1)}, u32[]{:S(2)}, u32[]{:S(2)}) %collective-permute-start.4) | collective-permute-done | bytes 262176 | tf_op jit(solution)/shard_map/ppermute | solution.py:23
  183.8 3.1 %copy-done.1 = bf16[2048,1792]{1,0:T(8,128)(2,1)S(1)} copy-done((bf16[2048,1792]{1,0:T(8,128)(2,1)S(1)}, bf16[2048,1792]{1,0:T(8,128)(2,1)}, u32[]{:S(2)}) %copy-start.1) | copy-done | bytes 7340056
  188.1 3.1 %copy-done.2 = bf16[2048,1792]{1,0:T(8,128)(2,1)S(1)} copy-done((bf16[2048,1792]{1,0:T(8,128)(2,1)S(1)}, bf16[2048,1792]{1,0:T(8,128)(2,1)}, u32[]{:S(2)}) %copy-start.2) | copy-done | bytes 7340056
  192.4 2.6 %add_multiply_fusion = f32[256,1792]{1,0:T(8,128)} fusion(f32[256,1792]{1,0:T(8,128)S(1)} %shard_map.66, bf16[256,1792]{1,0:T(8,128)(2,1)} %collective-permute-done.7), kind=kLoop, calls=%fused_computation.1 | loop fusion | flops 1376256 | bytes 4587520 | tf_op jit(solution)/shard_map/mul | solution.py:215
  (44 shorter events, 22.2 us)
Async XLA Ops:
  7.2 1.5 copy-start.4
  7.2 93.9 %all-gather.3.cloned.1.call-start = ((), (), s32[]{:S(2)}) async-start(), calls=%async_computation.6 | async-start | bytes 9175040 | tf_op jit(solution)/shard_map/all_gather | solution.py:165
  8.7 3.1 %copy-start.3 = (bf16[2048,1792]{1,0:T(8,128)(2,1)S(1)}, bf16[2048,1792]{1,0:T(8,128)(2,1)}, u32[]{:S(2)}) copy-start(bf16[2048,1792]{1,0:T(8,128)(2,1)} %b.3) | copy-start | bytes 22020100
  14.7 7.4 %collective-permute-start = (f32[2048,256]{1,0:T(8,128)S(1)}, f32[2048,256]{1,0:T(8,128)S(1)}, u32[]{:S(2)}, u32[]{:S(2)}) collective-permute-start(f32[2048,256]{1,0:T(8,128)S(1)} %shard_map.60), channel_id=1, source_target_pairs={{0,1},{1,0},{2,3},{3,2},{4,5},{5,4},{6,7},{7,6},{8,9},{9,8},{10,11... | collective-permute-start | bytes 6291464 | tf_op jit(solution)/shard_map/ppermute | solution.py:23
  16.2 38.0 %collective-permute-start.2 = (bf16[512,2048]{1,0:T(8,128)(2,1)}, bf16[512,2048]{1,0:T(8,128)(2,1)}, u32[]{:S(2)}, u32[]{:S(2)}) collective-permute-start(bf16[512,2048]{1,0:T(8,128)(2,1)} %a0.1), channel_id=1, source_target_pairs={{0,1},{1,0},{2,3},{3,2},{4,5},{5,4},{6,7},{7,6},{8,9},{9,8},{10,11... | collective-permute-start | bytes 6291464 | tf_op jit(solution)/shard_map/ppermute | solution.py:23
  46.2 4.7 %copy-start.9 = (bf16[512,512]{1,0:T(8,128)(2,1)S(1)}, bf16[512,512]{1,0:T(8,128)(2,1)}, u32[]{:S(2)}) copy-start(bf16[512,512]{1,0:T(8,128)(2,1)} %param.5) | copy-start | bytes 1572868
  47.3 18.6 %all-to-all-start.1 = ((bf16[8,256,256]{2,1,0:T(8,128)(2,1)}), bf16[8,256,256]{2,1,0:T(8,128)(2,1)S(1)}, u32[]{:S(2)}, u32[]{:S(2)}) async-start(bf16[8,256,256]{2,1,0:T(8,128)(2,1)} %shard_map.61), calls=%async_computation.1 | async-start | bytes 2097152 | tf_op jit(solution)/shard_map/all_to_all | solution.py:175
  51.1 3.1 %collective-permute-start.1 = (bf16[512,256]{1,0:T(8,128)(2,1)S(1)}, bf16[512,256]{1,0:T(8,128)(2,1)S(1)}, u32[]{:S(2)}, u32[]{:S(2)}) collective-permute-start(bf16[512,256]{1,0:T(8,128)(2,1)S(1)} %bitcast.36), channel_id=1, source_target_pairs={{0,1},{1,0},{2,3},{3,2},{4,5},{5,4},{6,7},{7,6},{8,9},{9,8},{10,11... | collective-permute-start | bytes 786440 | tf_op jit(solution)/shard_map/ppermute | solution.py:23
  66.0 6.6 %copy-start.5 = (bf16[8,256,256]{2,1,0:T(8,128)(2,1)}, bf16[8,256,256]{2,1,0:T(8,128)(2,1)S(1)}, u32[]{:S(2)}) copy-start(bf16[8,256,256]{2,1,0:T(8,128)(2,1)S(1)} %all-to-all-done.1) | copy-start | bytes 3145732
  72.5 6.7 %collective-permute-start.3 = (bf16[2560,256]{1,0:T(8,128)(2,1)}, bf16[2560,256]{1,0:T(8,128)(2,1)S(1)}, u32[]{:S(2)}, u32[]{:S(2)}) collective-permute-start(bf16[2560,256]{1,0:T(8,128)(2,1)} %get-tuple-element.17), channel_id=1, source_target_pairs={{0,1},{1,0},{2,3},{3,2},{4,5},{5,4},{6,7},{7,6},{8,9},{9,8},{10,11... | collective-permute-start | bytes 3932168 | tf_op jit(solution)/shard_map/ppermute | solution.py:23
  75.7 20.9 %all-to-all-start.2 = ((bf16[8,32,2048]{2,1,0:T(8,128)(2,1)}), bf16[8,32,2048]{2,1,0:T(8,128)(2,1)S(1)}, u32[]{:S(2)}, u32[]{:S(2)}) async-start(bf16[8,32,2048]{2,1,0:T(8,128)(2,1)} %get-tuple-element.12), calls=%async_computation.2 | async-start | bytes 2097152 | tf_op jit(solution)/shard_map/all_to_all | solution.py:184
  79.2 1.1 copy-start.7
  80.3 1.2 copy-start.6
  81.5 1.3 copy-start.8
  96.5 30.1 %all-to-all-start.4 = ((bf16[4,2,256,512]{2,3,1,0:T(8,128)(2,1)}), bf16[4,2,256,512]{2,3,1,0:T(8,128)(2,1)}, u32[]{:S(2)}, u32[]{:S(2)}) async-start(bf16[4,2,256,512]{2,3,1,0:T(8,128)(2,1)} %bitcast.34), calls=%async_computation.4 | async-start | bytes 4194304 | tf_op jit(solution)/shard_map/all_to_all | solution.py:190
  142.2 11.0 %collective-permute-start.6 = (bf16[4,256,256]{2,1,0:T(8,128)(2,1)S(1)}, bf16[4,256,256]{2,1,0:T(8,128)(2,1)S(1)}, u32[]{:S(2)}, u32[]{:S(2)}) collective-permute-start(bf16[4,256,256]{2,1,0:T(8,128)(2,1)S(1)} %bitcast.30), channel_id=1, source_target_pairs={{0,1},{1,0},{2,3},{3,2},{4,5},{5,4},{6,7},{7,6},{8,9},{9,8},{10,11... | collective-permute-start | bytes 1572872 | tf_op jit(solution)/shard_map/ppermute | solution.py:23
  145.1 16.9 %all-to-all-start.5 = ((bf16[32,32,256]{2,1,0:T(8,128)(2,1)}), bf16[32,32,256]{2,1,0:T(8,128)(2,1)S(1)}, u32[]{:S(2)}, u32[]{:S(2)}) async-start(bf16[32,32,256]{2,1,0:T(8,128)(2,1)} %bitcast.12), calls=%async_computation.5 | async-start | bytes 1048576 | tf_op jit(solution)/shard_map/all_to_all | solution.py:197
  149.0 3.1 %copy-start = (bf16[2048,1792]{1,0:T(8,128)(2,1)S(1)}, bf16[2048,1792]{1,0:T(8,128)(2,1)}, u32[]{:S(2)}) copy-start(bf16[2048,1792]{1,0:T(8,128)(2,1)} %all-gather.3.cloned.1.call-done) | copy-start | bytes 22020100
  154.5 37.9 %collective-permute-start.7 = (bf16[256,1792]{1,0:T(8,128)(2,1)S(1)}, bf16[256,1792]{1,0:T(8,128)(2,1)}, u32[]{:S(2)}, u32[]{:S(2)}) collective-permute-start(bf16[256,1792]{1,0:T(8,128)(2,1)S(1)} %shard_map.68), channel_id=1, source_target_pairs={{0,64},{64,0},{1,65},{65,1},{2,66},{66,2},{3,67},{67,3},{4,68},{68... | collective-permute-start | bytes 2752520 | tf_op jit(solution)/shard_map/ppermute | solution.py:23
  156.7 26.2 %collective-permute-start.4 = (bf16[256,512]{0,1:T(8,128)(2,1)S(1)}, bf16[256,512]{0,1:T(8,128)(2,1)S(1)}, u32[]{:S(2)}, u32[]{:S(2)}) collective-permute-start(bf16[256,512]{0,1:T(8,128)(2,1)S(1)} %fusion.2), channel_id=1, source_target_pairs={{0,64},{64,0},{1,65},{65,1},{2,66},{66,2},{3,67},{67,3},{4,68},{68... | collective-permute-start | bytes 786440 | tf_op jit(solution)/shard_map/ppermute | solution.py:23
  162.1 26.0 %collective-permute-start.5 = (bf16[4,256,256]{2,1,0:T(8,128)(2,1)S(1)}, bf16[4,256,256]{2,1,0:T(8,128)(2,1)S(1)}, u32[]{:S(2)}, u32[]{:S(2)}) collective-permute-start(bf16[4,256,256]{2,1,0:T(8,128)(2,1)S(1)} %bitcast.28), channel_id=1, source_target_pairs={{0,1},{1,0},{2,3},{3,2},{4,5},{5,4},{6,7},{7,6},{8,9},{9,8},{10,11... | collective-permute-start | bytes 1572872 | tf_op jit(solution)/shard_map/ppermute | solution.py:23
  183.8 3.1 %copy-start.1 = (bf16[2048,1792]{1,0:T(8,128)(2,1)S(1)}, bf16[2048,1792]{1,0:T(8,128)(2,1)}, u32[]{:S(2)}) copy-start(bf16[2048,1792]{1,0:T(8,128)(2,1)} %all-gather.3.cloned.1.call-done) | copy-start | bytes 22020100
  188.1 3.1 %copy-start.2 = (bf16[2048,1792]{1,0:T(8,128)(2,1)S(1)}, bf16[2048,1792]{1,0:T(8,128)(2,1)}, u32[]{:S(2)}) copy-start(bf16[2048,1792]{1,0:T(8,128)(2,1)} %all-gather.3.cloned.1.call-done) | copy-start | bytes 22020100
Sparse Core Ops, SparseCore 0:
  9.7 77.5 all-gather.2

commit v8 on v7

--- a/solution.py
+++ b/solution.py
@@ -90,7 +90,7 @@
 
 def residual_kernel(codes, near, far, a0, a1, own, message, partial, held):
     rank, outs = codes.shape[0], a0.shape[0]
-    step = 512
+    step = 256
     for j, (target, a) in enumerate(((near, a0), (far, a1))):
         for at in range(0, outs, step):
             rows = slice(at, at + step)
@@ -124,32 +124,80 @@
                 out[x, i] = piece
 
 
-def last_kernel(other, more, grad, acts, *refs):
+def last_kernel(joined, grad_m, grad_o, acts, *refs):
     out, turned = refs[-2:]
-    core = lax.axis_index("core")
-    half, width = grad.shape[1], out.shape[0]
-    which = 1 - core if other else core
-    rows = pl.ds(pl.multiple_of(which * half, half), half)
-    for k in range(4):
-        turned[k] = grad[k].T
-    for c in range(0, out.shape[1], 256):
-        cols = slice(c, c + 256)
-        acc = dot(turned[0], acts[0, rows, cols])
+    core, step = lax.axis_index("core"), pl.program_id(0)
+    half = grad_m.shape[1]
+    steps = pl.num_programs(0) - (2 if joined else 0)
+
+    @pl.when(step == 0)
+    def _():
+        for k in range(4):
+            turned[k, :, pl.ds(pl.multiple_of(core * half, half), half)] = grad_m[k].T
+            turned[k, :, pl.ds(pl.multiple_of((1 - core) * half, half), half)] = grad_o[k].T
+
+    @pl.when(step < steps)
+    def _():
+        acc = dot(turned[0], acts[0])
         for k in range(1, 4):
-            acc = acc + dot(turned[k], acts[k, rows, cols])
-        if more:
-            acc = acc + refs[0][:, cols]
-        out[:, cols] = acc.astype(out.dtype)
-
-
-def term_kernel(codes, own, message, out):
-    rank, outs = out.shape
-    for at in range(0, rank, 512):
-        rows = slice(at, at + 512)
-        for c in range(0, outs, 256):
-            acc = dot(codes[rows], own[:, c : c + 256])
-            acc = acc + dot(message[rows], message[rank + c : rank + c + 256])
-            out[rows, c : c + 256] = acc.astype(BF)
+            acc = acc + dot(turned[k], acts[k])
+        out[...] = acc.astype(out.dtype)
+
+    if joined:
+
+        @pl.when(step >= steps)
+        def _():
+            out[...] = refs[0][...]
+
+
+def last_call(grad_m, grad_o, row, dtype, *joined):
+    _, tokens, wide = row.shape
+    half, width = grad_m.shape[1:]
+    block = 256
+    steps = wide // block
+    more = 2 if joined else 0
+    whole = pl.BlockSpec((4, half, width), lambda i: (0, 0, 0))
+    return pl.pallas_call(
+        functools.partial(last_kernel, bool(joined)),
+        grid=(steps + more,),
+        out_shape=like((width, wide + more * block), dtype),
+        in_specs=[
+            whole,
+            whole,
+            pl.BlockSpec((4, tokens, block), lambda i: (0, 0, jnp.minimum(i, steps - 1))),
+        ]
+        + [pl.BlockSpec((width, block), lambda i: (0, jnp.maximum(i - steps, 0)))] * len(joined),
+        out_specs=pl.BlockSpec((width, block), lambda i: (0, i)),
+        scratch_shapes=[pltpu.VMEM((4, width, tokens), BF)],
+        compiler_params=pltpu.CompilerParams(vmem_limit_bytes=48 * 1024 * 1024),
+        cost_estimate=pl.CostEstimate(
+            flops=8 * tokens * width * wide, bytes_accessed=8 * tokens * wide, transcendentals=0
+        ),
+    )(grad_m, grad_o, row, *joined)
+
+
+def term_kernel(codes, own, message, keep, s1, s2, s3):
+    x = lax.axis_index("x")
+    rank, outs = codes.shape[0], own.shape[1]
+    width = rank // 8
+    for k, out in enumerate((keep, s1, s2, s3)):
+        for side in range(2):
+            start = side * (rank // 2) + lax.rem(x + k, 4) * width
+            rows = pl.ds(pl.multiple_of(start, width), width)
+            left, right = codes[rows, :], message[rows, :]
+            for c in range(0, outs, 256):
+                acc = dot(left, own[:, c : c + 256])
+                acc = acc + dot(right, message[rank + c : rank + c + 256])
+                out[side, :, c : c + 256] = acc.astype(out.dtype)
+
+
+def term_sum_kernel(keep, r1, r2, r3, own, away):
+    y_lo = lax.axis_index("y_lo")
+    for out, side in ((own, y_lo), (away, 1 - y_lo)):
+        value = keep[side]
+        for r in (r1, r2, r3):
+            value = value + r[side].astype(F32)
+        out[...] = value.astype(out.dtype)
 
 
 def local(acts, target, proj_b, proj_a):
@@ -183,44 +231,31 @@
     )
     blocks = lax.all_to_all(partial, ZY, 0, 0)
 
-    term = call(
-        term_kernel, [like((rank, outs))], codes, own, swap(message, "core"), flops=2 * tokens * rank * outs
-    )
-    term = term.reshape(2, 4, width, outs).transpose(1, 0, 2, 3)
-    term = lax.all_to_all(term, "x", 0, 0)
-
-    blocks, row = lax.optimization_barrier((blocks, row))
+    piece = like((2, width, outs))
+    terms = call(
+        term_kernel,
+        [like(piece.shape, F32), piece, piece, piece],
+        codes, own, swap(message, "core"),
+        flops=2 * tokens * rank * outs,
+    )
+    terms = [terms[0]] + [shift(terms[k], "x", 4, k) for k in (1, 2, 3)]
+
+    blocks, row, *terms = lax.optimization_barrier((blocks, row, *terms))
     spread = like((4, 8, sub, width))
     split_a, split_o = call(spread_kernel, [spread, spread], blocks, scratch=[pltpu.VMEM((sub, rank), BF)])
+    term_o, term_a = call(term_sum_kernel, [like((width, outs), F32), like((width, outs))], *terms)
 
     def gather(split):
         split = lax.all_to_all(split.reshape(32, sub, width), ("x", "z", "y_hi"), 0, 0)
         return split.reshape(4, half, width)
 
-    def last(grad, other, dtype, *before):
-        return call(
-            functools.partial(last_kernel, other, len(before)),
-            [like((width, wide), dtype)],
-            grad, row, *before,
-            scratch=[pltpu.VMEM((4, width, half), BF)],
-            flops=8 * half * width * wide,
-        )
-
     grad = gather(split_a)
-    grad, split_o, term = lax.optimization_barrier((grad, split_o, term))
-    away = last(swap(grad, "core"), True, BF, last(grad, False, F32))
-    away = swap(away, "y_lo")
+    grad, split_o = lax.optimization_barrier((grad, split_o))
+    away = swap(last_call(grad, swap(grad, "core"), row, BF, term_a), "y_lo").astype(F32)
     grad = gather(split_o)
-    here = last(swap(grad, "core"), True, F32, last(grad, False, F32))
-    grad_b = (here + away.astype(F32)) * scale
-
-    sums = term[0].astype(F32)
-    for i in range(1, 4):
-        sums = sums + term[i].astype(F32)
-    y_lo = lax.axis_index("y_lo")
-    pick = functools.partial(lax.dynamic_index_in_dim, sums, axis=0, keepdims=False)
-    grad_a = pick(y_lo) + swap(pick(1 - y_lo).astype(BF), "y_lo").astype(F32)
-    return ((grad_a * scale).T, grad_b)
+    here = last_call(grad, swap(grad, "core"), row, F32)
+    here, term_o = lax.optimization_barrier((here, term_o))
+    return (((term_o + away[:, wide:]) * scale).T, (here + away[:, :wide]) * scale)
 
 
 def solution(mesh):

time: 203 us -> 186 us (0.916)
  waiting for transfers between devices: 74.6 us -> 57.6 us
  local copies, waits for them, and re-layouts: 19.4 us -> 5.94 us
  Pallas kernels: 20.5 us -> 33.5 us
  blocking collectives: 39.5 us -> 44.7 us
  other arithmetic: 5.54 us -> 2.14 us
    all_to_all x1 -> x0, waiting for transfers between devices: 24.5 us -> none  [local(): term = lax.all_to_all(term, 'x', 0, 0)]
    pallas_call x0 -> x2, Pallas kernels: none -> 14.7 us  [last_call(): pl.pallas_call(functools.partial(last_kernel, bool(joined)), grid=(steps...]
    unnamed x22 -> x13, local copies, waits for them, and re-layouts: 16.9 us -> 5.9 us
    ppermute x8 -> x10, waiting for transfers between devices: 23.4 us -> 31 us  [shift(): lax.ppermute(array, axis, [(i, (i + step) % size) for i in range(size)])]
    all_to_all x1, blocking collectives: 15.6 us -> 20.8 us  [gather(): lax.all_to_all(split.reshape(32, sub, width), ('x', 'z', 'y_hi'), 0, 0)]
    all_to_all x1 -> x0, starting transfers between devices: 4.46 us -> none  [local(): term = lax.all_to_all(term, 'x', 0, 0)]
    ppermute x8 -> x10, starting transfers between devices: 12.6 us -> 15.7 us  [shift(): lax.ppermute(array, axis, [(i, (i + step) % size) for i in range(size)])]
    reshape x1 -> x0, local copies, waits for them, and re-layouts: 2.37 us -> none  [local(): term = term.reshape(2, 4, width, outs).transpose(1, 0, 2, 3)]
  transfers between devices with their start and end apart: 13 -> 14, of which waited for: 7 -> 9; matrix products, arithmetic and copies ran while one was open for 3% -> 0% of each run, Pallas kernels for 10% -> 18%
where the time goes in v8:
time: 186 us; the launch traced here: 185 us
  waiting for transfers between devices  57.6 us (31%)
  blocking collectives  44.7 us (24%)
  Pallas kernels  33.5 us (18%)
  starting transfers between devices  26.7 us (14%)
  between operations  14.2 us (8%)
  local copies, waits for them, and re-layouts  5.94 us (3%)
  other arithmetic  2.14 us (1%)
    ppermute x10, waiting for transfers between devices, shift(): lax.ppermute(array, axis, [(i, (i + step) % size) for i in range(size)])  31 us
    all_to_all x1, blocking collectives, local(): blocks = lax.all_to_all(mine, ZY, 0, 0)  23.9 us
    all_to_all x1, blocking collectives, gather(): lax.all_to_all(split.reshape(32, sub, width), ('x', 'z', 'y_hi'), 0, 0)  20.8 us
    ppermute x10, starting transfers between devices, shift(): lax.ppermute(array, axis, [(i, (i + step) % size) for i in range(size)])  15.7 us
    pallas_call x2, Pallas kernels, last_call(): pl.pallas_call(functools.partial(last_kernel, bool(joined)), grid=(steps...  14.7 us
    pallas_call x5, Pallas kernels, call(): pl.pallas_call(body, out_shape=outs if len(outs) > 1 else outs[0], in_spe...  13 us
    all_to_all x1, waiting for transfers between devices, local(): codes = lax.all_to_all(codes, ZY, 0, 0).reshape(rank, half)  11.8 us
    all_to_all x1, waiting for transfers between devices, local(): blocks = lax.all_to_all(partial, ZY, 0, 0)  9.12 us
  transfers between devices with their start and end apart: 14, of which 9 were waited for; matrix products, arithmetic and copies ran while one was open for 0% of the time, Pallas kernels for 18%

profile of v8, /device:TPU:1, one launch (start us, length us, event | category | flops | bytes accessed | tf_op | source)
XLA Modules:
  0.0 184.8 jit_solution(14992906250994789173)
XLA Ops:
  8.7 3.1 %copy-done = bf16[2048,1792]{1,0:T(8,128)(2,1)S(1)} copy-done((bf16[2048,1792]{1,0:T(8,128)(2,1)S(1)}, bf16[2048,1792]{1,0:T(8,128)(2,1)}, u32[]{:S(2)}) %copy-start) | copy-done | bytes 7340056
  11.7 2.9 %shard_map.60 = f32[2048,256]{1,0:T(8,128)S(1)} custom-call(bf16[512,1792]{1,0:T(8,128)(2,1)S(1)} %copy-done.1, bf16[2048,1792]{1,0:T(8,128)(2,1)S(1)} %copy-done), custom_call_target="tpu_custom_call" | custom-call | flops 1879048192 | bytes 7340032 | tf_op jit(solution)/shard_map/pallas_call | solution.py:68
  16.3 2.9 %shard_map.59 = f32[2048,256]{1,0:T(8,128)S(1)} custom-call(bf16[512,1792]{1,0:T(8,128)(2,1)S(1)} %copy-done.1, bf16[2048,1792]{1,0:T(8,128)(2,1)S(1)} %copy-done), custom_call_target="tpu_custom_call" | custom-call | flops 1879048192 | bytes 7340032 | tf_op jit(solution)/shard_map/pallas_call | solution.py:68
  19.2 2.8 %collective-permute-done = f32[2048,256]{1,0:T(8,128)S(1)} collective-permute-done((f32[2048,256]{1,0:T(8,128)S(1)}, f32[2048,256]{1,0:T(8,128)S(1)}, u32[]{:S(2)}, u32[]{:S(2)}) %collective-permute-start) | collective-permute-done | bytes 2097184 | tf_op jit(solution)/shard_map/ppermute | solution.py:23
  22.4 23.9 %all_to_all.25.blocks = bf16[8,256,256]{2,1,0:T(8,128)(2,1)S(1)} all-to-all(bf16[8,256,256]{2,1,0:T(8,128)(2,1)S(1)} %bitcast.21), channel_id=1, replica_groups=mesh['y_lo'=2,'x'=4,'z'=4,'y_hi'=2,'core'=2] {'z','y_hi'}, dimensions={0} | all-to-all | bytes 2097152 | tf_op jit(solution)/shard_map/all_to_all | solution.py:221
  47.3 3.6 %all-to-all-start.1 = ((bf16[8,256,256]{2,1,0:T(8,128)(2,1)}), bf16[8,256,256]{2,1,0:T(8,128)(2,1)S(1)}, u32[]{:S(2)}, u32[]{:S(2)}) async-start(bf16[8,256,256]{2,1,0:T(8,128)(2,1)} %shard_map.61), calls=%async_computation.1 | async-start | bytes 2097152 | tf_op jit(solution)/shard_map/all_to_all | solution.py:223
  51.1 1.9 %collective-permute-start.1 = (bf16[512,256]{1,0:T(8,128)(2,1)S(1)}, bf16[512,256]{1,0:T(8,128)(2,1)S(1)}, u32[]{:S(2)}, u32[]{:S(2)}) collective-permute-start(bf16[512,256]{1,0:T(8,128)(2,1)S(1)} %bitcast.22), channel_id=1, source_target_pairs={{0,1},{1,0},{2,3},{3,2},{4,5},{5,4},{6,7},{7,6},{8,9},{9,8},{10,11... | collective-permute-start | bytes 786440 | tf_op jit(solution)/shard_map/ppermute | solution.py:23
  54.2 11.8 %all-to-all-done.1 = bf16[8,256,256]{2,1,0:T(8,128)(2,1)S(1)} async-done(((bf16[8,256,256]{2,1,0:T(8,128)(2,1)}), bf16[8,256,256]{2,1,0:T(8,128)(2,1)S(1)}, u32[]{:S(2)}, u32[]{:S(2)}) %all-to-all-start.1) | async-done | bytes 1048608 | tf_op jit(solution)/shard_map/all_to_all | solution.py:223
  66.0 6.2 %shard_map.62 = (bf16[256,512]{1,0:T(8,128)(2,1)S(1)}, bf16[2560,256]{1,0:T(8,128)(2,1)}, bf16[8,32,2048]{2,1,0:T(8,128)(2,1)}) custom-call(bf16[2048,256]{1,0:T(8,128)(2,1)S(1)} %bitcast.15, bf16[512,256]{1,0:T(8,128)(2,1)S(1)} %bitcast.18, bf16[512,256]{1,0:T(8,128)(2,1)S(1)} %collective-permute-done.1.far, bf16[512,2048]{1,0:T(8,128)(2,1)} %a0.1, ...), custom_call_target="tpu_custom_call" | custom-call | flops 2147483648 | bytes 8388608 | tf_op jit(solution)/shard_map/pallas_call | solution.py:32
  72.1 3.1 %collective-permute-start.3 = (bf16[2560,256]{1,0:T(8,128)(2,1)}, bf16[2560,256]{1,0:T(8,128)(2,1)}, u32[]{:S(2)}, u32[]{:S(2)}) collective-permute-start(bf16[2560,256]{1,0:T(8,128)(2,1)} %get-tuple-element.25), channel_id=1, source_target_pairs={{0,1},{1,0},{2,3},{3,2},{4,5},{5,4},{6,7},{7,6},{8,9},{9,8},{10,11... | collective-permute-start | bytes 3932168 | tf_op jit(solution)/shard_map/ppermute | solution.py:23
  75.3 3.6 %all-to-all-start.2 = ((bf16[8,32,2048]{2,1,0:T(8,128)(2,1)}), bf16[8,32,2048]{2,1,0:T(8,128)(2,1)S(1)}, u32[]{:S(2)}, u32[]{:S(2)}) async-start(bf16[8,32,2048]{2,1,0:T(8,128)(2,1)} %get-tuple-element.23), calls=%async_computation.2 | async-start | bytes 2097152 | tf_op jit(solution)/shard_map/all_to_all | solution.py:232
  78.8 3.4 %shard_map.63 = (f32[2,256,512]{2,1,0:T(8,128)S(1)}, bf16[2,256,512]{2,1,0:T(8,128)(2,1)}, bf16[2,256,512]{2,1,0:T(8,128)(2,1)}, bf16[2,256,512]{2,1,0:T(8,128)(2,1)}) custom-call(bf16[2048,256]{1,0:T(8,128)(2,1)S(1)} %bitcast.16, bf16[256,512]{1,0:T(8,128)(2,1)S(1)} %get-tuple-element.24.own, bf16[2560,256]{1,0:T(8,128)(2,1)} %collective-permute-done.3.message), custom_call_target="tpu_custom_call" | custom-call | flops 1073741824 | bytes 5242880 | tf_op jit(solution)/shard_map/pallas_call | solution.py:32
  83.4 2.4 %collective-permute-start.5 = (bf16[2,256,512]{2,1,0:T(8,128)(2,1)}, bf16[2,256,512]{2,1,0:T(8,128)(2,1)S(1)}, u32[]{:S(2)}, u32[]{:S(2)}) collective-permute-start(bf16[2,256,512]{2,1,0:T(8,128)(2,1)} %get-tuple-element.28), channel_id=1, source_target_pairs={{0,32},{16,48},{32,0},{48,16},{1,33},{17,49},{33,1},{49,17},{2,34}... | collective-permute-start | bytes 1572872 | tf_op jit(solution)/shard_map/ppermute | solution.py:23
  87.0 9.1 %all-to-all-done.2.blocks = bf16[8,32,2048]{2,1,0:T(8,128)(2,1)S(1)} async-done(((bf16[8,32,2048]{2,1,0:T(8,128)(2,1)}), bf16[8,32,2048]{2,1,0:T(8,128)(2,1)S(1)}, u32[]{:S(2)}, u32[]{:S(2)}) %all-to-all-start.2) | async-done | bytes 1048608 | tf_op jit(solution)/shard_map/all_to_all | solution.py:232
  96.1 2.1 %collective-permute-done.4.r1 = bf16[2,256,512]{2,1,0:T(8,128)(2,1)S(1)} collective-permute-done((bf16[2,256,512]{2,1,0:T(8,128)(2,1)}, bf16[2,256,512]{2,1,0:T(8,128)(2,1)S(1)}, u32[]{:S(2)}, u32[]{:S(2)}) %collective-permute-start.4) | collective-permute-done | bytes 524320 | tf_op jit(solution)/shard_map/ppermute | solution.py:23
  98.3 11.4 %collective-permute-done.5.r2 = bf16[2,256,512]{2,1,0:T(8,128)(2,1)S(1)} collective-permute-done((bf16[2,256,512]{2,1,0:T(8,128)(2,1)}, bf16[2,256,512]{2,1,0:T(8,128)(2,1)S(1)}, u32[]{:S(2)}, u32[]{:S(2)}) %collective-permute-start.5) | collective-permute-done | bytes 524320 | tf_op jit(solution)/shard_map/ppermute | solution.py:23
  110.7 20.8 %all_to_all.26 = bf16[32,32,256]{2,1,0:T(8,128)(2,1)S(1)} all-to-all(bf16[32,32,256]{2,1,0:T(8,128)(2,1)S(1)} %bitcast.17), channel_id=1, replica_groups=mesh['y_lo'=2,'x'=4,'z'=4,'y_hi'=2,'core'=2] {'x','z','y_hi'}, dimensions={0} | all-to-all | bytes 1048576 | tf_op jit(solution)/shard_map/all_to_all | solution.py:249
  131.5 2.4 %collective-permute-start.8 = (bf16[4,256,256]{2,1,0:T(8,128)(2,1)S(1)}, bf16[4,256,256]{2,1,0:T(8,128)(2,1)}, u32[]{:S(2)}, u32[]{:S(2)}) collective-permute-start(bf16[4,256,256]{2,1,0:T(8,128)(2,1)S(1)} %bitcast.13), channel_id=1, source_target_pairs={{0,1},{1,0},{2,3},{3,2},{4,5},{5,4},{6,7},{7,6},{8,9},{9,8},{10,11... | collective-permute-start | bytes 1572872 | tf_op jit(solution)/shard_map/ppermute | solution.py:23
  136.0 3.9 %all-to-all-start.4 = ((bf16[32,32,256]{2,1,0:T(8,128)(2,1)}), bf16[32,32,256]{2,1,0:T(8,128)(2,1)S(1)}, u32[]{:S(2)}, u32[]{:S(2)}) async-start(bf16[32,32,256]{2,1,0:T(8,128)(2,1)} %bitcast.7), calls=%async_computation.4 | async-start | bytes 1048576 | tf_op jit(solution)/shard_map/all_to_all | solution.py:249
  140.0 7.5 %shard_map.67 = bf16[256,2304]{1,0:T(8,128)(2,1)S(1)} custom-call(bf16[4,256,256]{2,1,0:T(8,128)(2,1)S(1)} %bitcast.14, bf16[4,256,256]{2,1,0:T(8,128)(2,1)} %collective-permute-done.8.grad_o, bf16[4,512,1792]{2,1,0:T(8,128)(2,1)} %bitcast.19, bf16[256,512]{1,0:T(8,128)(2,1)S(1)} %get-tuple-element.42.refs_0_), custom_call_target="tpu_custom_call" | custom-call | flops 1879048192 | bytes 7340032 | tf_op jit(solution)/shard_map/pallas_call | solution.py:160
  147.9 5.1 %all-to-all-done.4 = bf16[32,32,256]{2,1,0:T(8,128)(2,1)S(1)} async-done(((bf16[32,32,256]{2,1,0:T(8,128)(2,1)}), bf16[32,32,256]{2,1,0:T(8,128)(2,1)S(1)}, u32[]{:S(2)}, u32[]{:S(2)}) %all-to-all-start.4) | async-done | bytes 524320 | tf_op jit(solution)/shard_map/all_to_all | solution.py:249
  156.0 7.2 %shard_map.65 = f32[256,1792]{1,0:T(8,128)S(1)} custom-call(bf16[4,256,256]{2,1,0:T(8,128)(2,1)S(1)} %bitcast.12, bf16[4,256,256]{2,1,0:T(8,128)(2,1)S(1)} %collective-permute-done.7.grad_o, bf16[4,512,1792]{2,1,0:T(8,128)(2,1)} %bitcast.20), custom_call_target="tpu_custom_call" | custom-call | flops 1879048192 | bytes 7340032 | tf_op jit(solution)/shard_map/pallas_call | solution.py:160
  163.1 12.0 %collective-permute-done.9 = bf16[256,2304]{1,0:T(8,128)(2,1)S(1)} collective-permute-done((bf16[256,2304]{1,0:T(8,128)(2,1)S(1)}, bf16[256,2304]{1,0:T(8,128)(2,1)S(1)}, u32[]{:S(2)}, u32[]{:S(2)}) %collective-permute-start.9) | collective-permute-done | bytes 1179680 | tf_op jit(solution)/shard_map/ppermute | solution.py:23
  175.3 1.6 fusion
  (34 shorter events, 15.9 us)
Async XLA Ops:
  7.2 1.5 copy-start.1
  7.2 102.5 %all-gather.3.cloned.1.call-start = ((), (), s32[]{:S(2)}) async-start(), calls=%async_computation.5 | async-start | bytes 9175040 | tf_op jit(solution)/shard_map/all_gather | solution.py:213
  8.7 3.1 %copy-start = (bf16[2048,1792]{1,0:T(8,128)(2,1)S(1)}, bf16[2048,1792]{1,0:T(8,128)(2,1)}, u32[]{:S(2)}) copy-start(bf16[2048,1792]{1,0:T(8,128)(2,1)} %b.3) | copy-start | bytes 22020100
  14.7 7.4 %collective-permute-start = (f32[2048,256]{1,0:T(8,128)S(1)}, f32[2048,256]{1,0:T(8,128)S(1)}, u32[]{:S(2)}, u32[]{:S(2)}) collective-permute-start(f32[2048,256]{1,0:T(8,128)S(1)} %shard_map.60), channel_id=1, source_target_pairs={{0,1},{1,0},{2,3},{3,2},{4,5},{5,4},{6,7},{7,6},{8,9},{9,8},{10,11... | collective-permute-start | bytes 6291464 | tf_op jit(solution)/shard_map/ppermute | solution.py:23
  16.2 38.0 %collective-permute-start.2 = (bf16[512,2048]{1,0:T(8,128)(2,1)}, bf16[512,2048]{1,0:T(8,128)(2,1)}, u32[]{:S(2)}, u32[]{:S(2)}) collective-permute-start(bf16[512,2048]{1,0:T(8,128)(2,1)} %a0.1), channel_id=1, source_target_pairs={{0,1},{1,0},{2,3},{3,2},{4,5},{5,4},{6,7},{7,6},{8,9},{9,8},{10,11... | collective-permute-start | bytes 6291464 | tf_op jit(solution)/shard_map/ppermute | solution.py:23
  46.2 4.7 %copy-start.4 = (bf16[512,512]{1,0:T(8,128)(2,1)S(1)}, bf16[512,512]{1,0:T(8,128)(2,1)}, u32[]{:S(2)}) copy-start(bf16[512,512]{1,0:T(8,128)(2,1)} %param.5) | copy-start | bytes 1572868
  47.3 18.6 %all-to-all-start.1 = ((bf16[8,256,256]{2,1,0:T(8,128)(2,1)}), bf16[8,256,256]{2,1,0:T(8,128)(2,1)S(1)}, u32[]{:S(2)}, u32[]{:S(2)}) async-start(bf16[8,256,256]{2,1,0:T(8,128)(2,1)} %shard_map.61), calls=%async_computation.1 | async-start | bytes 2097152 | tf_op jit(solution)/shard_map/all_to_all | solution.py:223
  51.1 3.1 %collective-permute-start.1 = (bf16[512,256]{1,0:T(8,128)(2,1)S(1)}, bf16[512,256]{1,0:T(8,128)(2,1)S(1)}, u32[]{:S(2)}, u32[]{:S(2)}) collective-permute-start(bf16[512,256]{1,0:T(8,128)(2,1)S(1)} %bitcast.22), channel_id=1, source_target_pairs={{0,1},{1,0},{2,3},{3,2},{4,5},{5,4},{6,7},{7,6},{8,9},{9,8},{10,11... | collective-permute-start | bytes 786440 | tf_op jit(solution)/shard_map/ppermute | solution.py:23
  72.1 6.7 %collective-permute-start.3 = (bf16[2560,256]{1,0:T(8,128)(2,1)}, bf16[2560,256]{1,0:T(8,128)(2,1)}, u32[]{:S(2)}, u32[]{:S(2)}) collective-permute-start(bf16[2560,256]{1,0:T(8,128)(2,1)} %get-tuple-element.25), channel_id=1, source_target_pairs={{0,1},{1,0},{2,3},{3,2},{4,5},{5,4},{6,7},{7,6},{8,9},{9,8},{10,11... | collective-permute-start | bytes 3932168 | tf_op jit(solution)/shard_map/ppermute | solution.py:23
  75.3 20.9 %all-to-all-start.2 = ((bf16[8,32,2048]{2,1,0:T(8,128)(2,1)}), bf16[8,32,2048]{2,1,0:T(8,128)(2,1)S(1)}, u32[]{:S(2)}, u32[]{:S(2)}) async-start(bf16[8,32,2048]{2,1,0:T(8,128)(2,1)} %get-tuple-element.23), calls=%async_computation.2 | async-start | bytes 2097152 | tf_op jit(solution)/shard_map/all_to_all | solution.py:232
  82.2 16.0 %collective-permute-start.4 = (bf16[2,256,512]{2,1,0:T(8,128)(2,1)}, bf16[2,256,512]{2,1,0:T(8,128)(2,1)S(1)}, u32[]{:S(2)}, u32[]{:S(2)}) collective-permute-start(bf16[2,256,512]{2,1,0:T(8,128)(2,1)} %get-tuple-element.27), channel_id=1, source_target_pairs={{0,16},{16,32},{32,48},{48,0},{1,17},{17,33},{33,49},{49,1},{2,18}... | collective-permute-start | bytes 1572872 | tf_op jit(solution)/shard_map/ppermute | solution.py:23
  83.4 26.2 %collective-permute-start.5 = (bf16[2,256,512]{2,1,0:T(8,128)(2,1)}, bf16[2,256,512]{2,1,0:T(8,128)(2,1)S(1)}, u32[]{:S(2)}, u32[]{:S(2)}) collective-permute-start(bf16[2,256,512]{2,1,0:T(8,128)(2,1)} %get-tuple-element.28), channel_id=1, source_target_pairs={{0,32},{16,48},{32,0},{48,16},{1,33},{17,49},{33,1},{49,17},{2,34}... | collective-permute-start | bytes 1572872 | tf_op jit(solution)/shard_map/ppermute | solution.py:23
  85.9 23.8 %collective-permute-start.6 = (bf16[2,256,512]{2,1,0:T(8,128)(2,1)}, bf16[2,256,512]{2,1,0:T(8,128)(2,1)}, u32[]{:S(2)}, u32[]{:S(2)}) collective-permute-start(bf16[2,256,512]{2,1,0:T(8,128)(2,1)} %get-tuple-element.29), channel_id=1, source_target_pairs={{0,48},{16,0},{32,16},{48,32},{1,49},{17,1},{33,17},{49,33},{2,50}... | collective-permute-start | bytes 1572872 | tf_op jit(solution)/shard_map/ppermute | solution.py:23
  131.5 8.4 %collective-permute-start.8 = (bf16[4,256,256]{2,1,0:T(8,128)(2,1)S(1)}, bf16[4,256,256]{2,1,0:T(8,128)(2,1)}, u32[]{:S(2)}, u32[]{:S(2)}) collective-permute-start(bf16[4,256,256]{2,1,0:T(8,128)(2,1)S(1)} %bitcast.13), channel_id=1, source_target_pairs={{0,1},{1,0},{2,3},{3,2},{4,5},{5,4},{6,7},{7,6},{8,9},{9,8},{10,11... | collective-permute-start | bytes 1572872 | tf_op jit(solution)/shard_map/ppermute | solution.py:23
  135.3 0.8 copy-start.2
  136.0 16.9 %all-to-all-start.4 = ((bf16[32,32,256]{2,1,0:T(8,128)(2,1)}), bf16[32,32,256]{2,1,0:T(8,128)(2,1)S(1)}, u32[]{:S(2)}, u32[]{:S(2)}) async-start(bf16[32,32,256]{2,1,0:T(8,128)(2,1)} %bitcast.7), calls=%async_computation.4 | async-start | bytes 1048576 | tf_op jit(solution)/shard_map/all_to_all | solution.py:249
  147.5 27.7 %collective-permute-start.9 = (bf16[256,2304]{1,0:T(8,128)(2,1)S(1)}, bf16[256,2304]{1,0:T(8,128)(2,1)S(1)}, u32[]{:S(2)}, u32[]{:S(2)}) collective-permute-start(bf16[256,2304]{1,0:T(8,128)(2,1)S(1)} %shard_map.67), channel_id=1, source_target_pairs={{0,64},{64,0},{1,65},{65,1},{2,66},{66,2},{3,67},{67,3},{4,68},{68... | collective-permute-start | bytes 3538952 | tf_op jit(solution)/shard_map/ppermute | solution.py:23
  153.0 3.0 %collective-permute-start.7 = (bf16[4,256,256]{2,1,0:T(8,128)(2,1)S(1)}, bf16[4,256,256]{2,1,0:T(8,128)(2,1)S(1)}, u32[]{:S(2)}, u32[]{:S(2)}) collective-permute-start(bf16[4,256,256]{2,1,0:T(8,128)(2,1)S(1)} %bitcast.11), channel_id=1, source_target_pairs={{0,1},{1,0},{2,3},{3,2},{4,5},{5,4},{6,7},{7,6},{8,9},{9,8},{10,11... | collective-permute-start | bytes 1572872 | tf_op jit(solution)/shard_map/ppermute | solution.py:23
  175.3 1.6 copy-start.3
Sparse Core Ops, SparseCore 0:
  9.7 77.9 all-gather.2

commit v9 on v8

--- a/solution.py
+++ b/solution.py
@@ -11,6 +11,7 @@
 BF, F32 = jnp.bfloat16, jnp.float32
 TOK, CHAN, ZY = ("y_lo", "x"), ("z", "y_hi", "core"), ("z", "y_hi")
 VMEM = pl.BlockSpec(memory_space=pltpu.VMEM)
+ANY = pl.BlockSpec(memory_space=pl.ANY)
 
 
 def dot(left, right, left_dim=1, right_dim=0):
@@ -51,15 +52,22 @@
     return out
 
 
-def codes_kernel(other, acts, b, out, turned):
-    core, half = lax.axis_index("core"), turned.shape[1]
-
-    @pl.when(pl.program_id(0) == 0)
-    def _():
-        which = 1 - core if other else core
-        turned[...] = acts[pl.ds(pl.multiple_of(which * half, half), half), :].T
-
-    out[...] = dot(b[...], turned[...])
+def codes_kernel(other, acts, b, out, rows, turned, held, sems):
+    core, (parts, step), half = lax.axis_index("core"), held.shape[:2], rows.shape[0]
+    start = pl.multiple_of((1 - core if other else core) * half, half)
+    first = pltpu.make_async_copy(acts.at[pl.ds(start, half), :], rows, sems.at[parts])
+    first.start()
+    copies = [
+        pltpu.make_async_copy(b.at[pl.ds(i * step, step), :], held.at[i], sems.at[i])
+        for i in range(parts)
+    ]
+    for copy in copies:
+        copy.start()
+    first.wait()
+    turned[...] = rows[...].T
+    for i in range(parts):
+        copies[i].wait()
+        out[i * step : (i + 1) * step] = dot(held[i], turned[...])
 
 
 def codes_call(other, acts, proj_b):
@@ -67,15 +75,16 @@
     half, step = tokens // 2, 512
     return pl.pallas_call(
         functools.partial(codes_kernel, other),
-        grid=(rank // step,),
         out_shape=like((rank, half), F32),
-        in_specs=[
-            pl.BlockSpec((tokens, wide), lambda i: (0, 0)),
-            pl.BlockSpec((step, wide), lambda i: (i, 0)),
+        in_specs=[ANY, ANY],
+        out_specs=VMEM,
+        scratch_shapes=[
+            pltpu.VMEM((half, wide), BF),
+            pltpu.VMEM((wide, half), BF),
+            pltpu.VMEM((rank // step, step, wide), BF),
+            pltpu.SemaphoreType.DMA((rank // step + 1,)),
         ],
-        out_specs=pl.BlockSpec((step, half), lambda i: (i, 0)),
-        scratch_shapes=[pltpu.VMEM((wide, half), BF)],
-        compiler_params=pltpu.CompilerParams(vmem_limit_bytes=32 * 1024 * 1024),
+        compiler_params=pltpu.CompilerParams(vmem_limit_bytes=58 * 1024 * 1024),
         cost_estimate=pl.CostEstimate(
             flops=2 * rank * wide * half, bytes_accessed=2 * rank * wide, transcendentals=0
         ),
@@ -124,51 +133,42 @@
                 out[x, i] = piece
 
 
-def last_kernel(joined, grad_m, grad_o, acts, *refs):
-    out, turned = refs[-2:]
-    core, step = lax.axis_index("core"), pl.program_id(0)
-    half = grad_m.shape[1]
-    steps = pl.num_programs(0) - (2 if joined else 0)
-
-    @pl.when(step == 0)
-    def _():
-        for k in range(4):
-            turned[k, :, pl.ds(pl.multiple_of(core * half, half), half)] = grad_m[k].T
-            turned[k, :, pl.ds(pl.multiple_of((1 - core) * half, half), half)] = grad_o[k].T
-
-    @pl.when(step < steps)
-    def _():
-        acc = dot(turned[0], acts[0])
+def last_kernel(grad_m, grad_o, acts, *refs):
+    joined, (out, turned, held, sems) = refs[:-4], refs[-4:]
+    core = lax.axis_index("core")
+    half, wide, step = grad_m.shape[1], acts.shape[2], held.shape[3]
+    copies = [
+        pltpu.make_async_copy(acts.at[:, :, pl.ds(i * step, step)], held.at[i], sems.at[i])
+        for i in range(wide // step)
+    ]
+    for copy in copies:
+        copy.start()
+    for k in range(4):
+        turned[k, :, pl.ds(pl.multiple_of(core * half, half), half)] = grad_m[k].T
+        turned[k, :, pl.ds(pl.multiple_of((1 - core) * half, half), half)] = grad_o[k].T
+    for ref in joined:
+        out[:, wide:] = ref[...]
+    for i, copy in enumerate(copies):
+        copy.wait()
+        acc = dot(turned[0], held[i, 0])
         for k in range(1, 4):
-            acc = acc + dot(turned[k], acts[k])
-        out[...] = acc.astype(out.dtype)
-
-    if joined:
-
-        @pl.when(step >= steps)
-        def _():
-            out[...] = refs[0][...]
+            acc = acc + dot(turned[k], held[i, k])
+        out[:, i * step : (i + 1) * step] = acc.astype(out.dtype)
 
 
 def last_call(grad_m, grad_o, row, dtype, *joined):
     _, tokens, wide = row.shape
-    half, width = grad_m.shape[1:]
-    block = 256
-    steps = wide // block
-    more = 2 if joined else 0
-    whole = pl.BlockSpec((4, half, width), lambda i: (0, 0, 0))
+    width, step = grad_m.shape[2], 256
     return pl.pallas_call(
-        functools.partial(last_kernel, bool(joined)),
-        grid=(steps + more,),
-        out_shape=like((width, wide + more * block), dtype),
-        in_specs=[
-            whole,
-            whole,
-            pl.BlockSpec((4, tokens, block), lambda i: (0, 0, jnp.minimum(i, steps - 1))),
-        ]
-        + [pl.BlockSpec((width, block), lambda i: (0, jnp.maximum(i - steps, 0)))] * len(joined),
-        out_specs=pl.BlockSpec((width, block), lambda i: (0, i)),
-        scratch_shapes=[pltpu.VMEM((4, width, tokens), BF)],
+        last_kernel,
+        out_shape=like((width, wide + sum(j.shape[1] for j in joined)), dtype),
+        in_specs=[VMEM, VMEM, ANY] + [VMEM] * len(joined),
+        out_specs=VMEM,
+        scratch_shapes=[
+            pltpu.VMEM((4, width, tokens), BF),
+            pltpu.VMEM((wide // step, 4, tokens, step), BF),
+            pltpu.SemaphoreType.DMA((wide // step,)),
+        ],
         compiler_params=pltpu.CompilerParams(vmem_limit_bytes=48 * 1024 * 1024),
         cost_estimate=pl.CostEstimate(
             flops=8 * tokens * width * wide, bytes_accessed=8 * tokens * wide, transcendentals=0
@@ -240,18 +240,20 @@
     )
     terms = [terms[0]] + [shift(terms[k], "x", 4, k) for k in (1, 2, 3)]
 
-    blocks, row, *terms = lax.optimization_barrier((blocks, row, *terms))
+    blocks, row, terms[1], terms[3] = lax.optimization_barrier((blocks, row, terms[1], terms[3]))
     spread = like((4, 8, sub, width))
     split_a, split_o = call(spread_kernel, [spread, spread], blocks, scratch=[pltpu.VMEM((sub, rank), BF)])
-    term_o, term_a = call(term_sum_kernel, [like((width, outs), F32), like((width, outs))], *terms)
 
     def gather(split):
         split = lax.all_to_all(split.reshape(32, sub, width), ("x", "z", "y_hi"), 0, 0)
         return split.reshape(4, half, width)
 
     grad = gather(split_a)
-    grad, split_o = lax.optimization_barrier((grad, split_o))
-    away = swap(last_call(grad, swap(grad, "core"), row, BF, term_a), "y_lo").astype(F32)
+    grad, terms[2] = lax.optimization_barrier((grad, terms[2]))
+    term_o, term_a = call(term_sum_kernel, [like((width, outs), F32), like((width, outs))], *terms)
+    away = last_call(grad, swap(grad, "core"), row, BF, term_a)
+    away, split_o = lax.optimization_barrier((away, split_o))
+    away = swap(away, "y_lo").astype(F32)
     grad = gather(split_o)
     here = last_call(grad, swap(grad, "core"), row, F32)
     here, term_o = lax.optimization_barrier((here, term_o))

time: 186 us -> 192 us (1.032)
  blocking collectives: 44.7 us -> 23.9 us
  starting transfers between devices: 26.7 us -> 46.7 us
  Pallas kernels: 33.5 us -> 39.5 us
    all_to_all x1 -> x0, blocking collectives: 20.8 us -> none  [gather(): lax.all_to_all(split.reshape(32, sub, width), ('x', 'z', 'y_hi'), 0, 0)]
    all_to_all x1 -> x2, waiting for transfers between devices: 5.09 us -> 22.1 us  [gather(): lax.all_to_all(split.reshape(32, sub, width), ('x', 'z', 'y_hi'), 0, 0)]
    ppermute x10, waiting for transfers between devices: 31 us -> 15 us  [shift(): lax.ppermute(array, axis, [(i, (i + step) % size) for i in range(size)])]
    ppermute x10, starting transfers between devices: 15.7 us -> 26.7 us  [shift(): lax.ppermute(array, axis, [(i, (i + step) % size) for i in range(size)])]
    all_to_all x1 -> x2, starting transfers between devices: 3.89 us -> 12.9 us  [gather(): lax.all_to_all(split.reshape(32, sub, width), ('x', 'z', 'y_hi'), 0, 0)]
    pallas_call x4, Pallas kernels: 20.5 us -> 27 us  [the longest x2 15.2 us: codes_call(): pl.pallas_call(functools.partial(codes_kernel, other), out_shape=like((ra...]
    all_to_all x1, waiting for transfers between devices: 11.8 us -> 9.02 us  [local(): codes = lax.all_to_all(codes, ZY, 0, 0).reshape(rank, half)]
    unnamed x13 -> x15, local copies, waits for them, and re-layouts: 5.9 us -> 5.23 us
  transfers between devices with their start and end apart: 14 -> 15, of which waited for: 9 -> 9; matrix products, arithmetic and copies ran while one was open for 0% -> 3% of each run, Pallas kernels for 18% -> 18%
where the time goes in v9:
time: 192 us; the launch traced here: 191 us
  waiting for transfers between devices  56.3 us (29%)
  starting transfers between devices  46.7 us (24%)
  Pallas kernels  39.5 us (21%)
  blocking collectives  23.9 us (12%)
  between operations  14.2 us (7%)
  local copies, waits for them, and re-layouts  7 us (4%)
  other arithmetic  3.73 us (2%)
    ppermute x10, starting transfers between devices, shift(): lax.ppermute(array, axis, [(i, (i + step) % size) for i in range(size)])  26.7 us
    all_to_all x1, blocking collectives, local(): blocks = lax.all_to_all(mine, ZY, 0, 0)  23.9 us
    all_to_all x2, waiting for transfers between devices, gather(): lax.all_to_all(split.reshape(32, sub, width), ('x', 'z', 'y_hi'), 0, 0)  22.1 us
    pallas_call x2, Pallas kernels, codes_call(): pl.pallas_call(functools.partial(codes_kernel, other), out_shape=like((ra...  15.2 us
    ppermute x10, waiting for transfers between devices, shift(): lax.ppermute(array, axis, [(i, (i + step) % size) for i in range(size)])  15 us
    all_to_all x2, starting transfers between devices, gather(): lax.all_to_all(split.reshape(32, sub, width), ('x', 'z', 'y_hi'), 0, 0)  12.9 us
    pallas_call x5, Pallas kernels, call(): pl.pallas_call(body, out_shape=outs if len(outs) > 1 else outs[0], in_spe...  12.5 us
    pallas_call x2, Pallas kernels, last_call(): pl.pallas_call(last_kernel, out_shape=like((width, wide + sum((j.shape[1]...  11.8 us
  transfers between devices with their start and end apart: 15, of which 9 were waited for; matrix products, arithmetic and copies ran while one was open for 3% of the time, Pallas kernels for 18%

profile of v9, /device:TPU:1, one launch (start us, length us, event | category | flops | bytes accessed | tf_op | source)
XLA Modules:
  0.0 191.4 jit_solution(18107448251624933982)
XLA Ops:
  7.9 7.7 %shard_map.60 = f32[2048,256]{1,0:T(8,128)} custom-call(bf16[512,1792]{1,0:T(8,128)(2,1)} %acts.3, bf16[2048,1792]{1,0:T(8,128)(2,1)} %b.3), custom_call_target="tpu_custom_call" | custom-call | flops 1879048192 | bytes 7340032 | tf_op jit(solution)/shard_map/pallas_call | solution.py:76
  17.2 7.6 %shard_map.59 = f32[2048,256]{1,0:T(8,128)} custom-call(bf16[512,1792]{1,0:T(8,128)(2,1)} %acts.3, bf16[2048,1792]{1,0:T(8,128)(2,1)} %b.3), custom_call_target="tpu_custom_call" | custom-call | flops 1879048192 | bytes 7340032 | tf_op jit(solution)/shard_map/pallas_call | solution.py:76
  24.8 1.9 %add_convert_fusion = bf16[2048,256]{1,0:T(8,128)(2,1)S(1)} fusion(f32[2048,256]{1,0:T(8,128)} %shard_map.59, f32[2048,256]{1,0:T(8,128)S(1)} %collective-permute-done), kind=kLoop, calls=%fused_computation | loop fusion | flops 1048576 | bytes 5242880 | tf_op jit(solution)/shard_map/convert_element_type | solution.py:220
  26.7 23.9 %all_to_all.25.blocks = bf16[8,256,256]{2,1,0:T(8,128)(2,1)S(1)} all-to-all(bf16[8,256,256]{2,1,0:T(8,128)(2,1)S(1)} %bitcast.21), channel_id=1, replica_groups=mesh['y_lo'=2,'x'=4,'z'=4,'y_hi'=2,'core'=2] {'z','y_hi'}, dimensions={0} | all-to-all | bytes 2097152 | tf_op jit(solution)/shard_map/all_to_all | solution.py:221
  51.8 3.6 %all-to-all-start.1 = ((bf16[8,256,256]{2,1,0:T(8,128)(2,1)}), bf16[8,256,256]{2,1,0:T(8,128)(2,1)S(1)}, u32[]{:S(2)}, u32[]{:S(2)}) async-start(bf16[8,256,256]{2,1,0:T(8,128)(2,1)} %shard_map.61), calls=%async_computation.1 | async-start | bytes 2097152 | tf_op jit(solution)/shard_map/all_to_all | solution.py:223
  55.3 1.8 constant_dynamic-slice_fusion
  58.0 1.9 collective-permute-start.1
  61.3 9.0 %all-to-all-done.1 = bf16[8,256,256]{2,1,0:T(8,128)(2,1)S(1)} async-done(((bf16[8,256,256]{2,1,0:T(8,128)(2,1)}), bf16[8,256,256]{2,1,0:T(8,128)(2,1)S(1)}, u32[]{:S(2)}, u32[]{:S(2)}) %all-to-all-start.1) | async-done | bytes 1048608 | tf_op jit(solution)/shard_map/all_to_all | solution.py:223
  70.3 5.6 %shard_map.62 = (bf16[256,512]{1,0:T(8,128)(2,1)S(1)}, bf16[2560,256]{1,0:T(8,128)(2,1)}, bf16[8,32,2048]{2,1,0:T(8,128)(2,1)}) custom-call(bf16[2048,256]{1,0:T(8,128)(2,1)S(1)} %bitcast.15, bf16[512,256]{1,0:T(8,128)(2,1)S(1)} %bitcast.18, bf16[512,256]{1,0:T(8,128)(2,1)} %collective-permute-done.1.far, bf16[512,2048]{1,0:T(8,128)(2,1)S(1)} %copy-done.3, ...), custom_call_target="tpu_custom_call" | custom-call | flops 2147483648 | bytes 8388608 | tf_op jit(solution)/shard_map/pallas_call | solution.py:33
  76.7 3.1 %collective-permute-start.3 = (bf16[2560,256]{1,0:T(8,128)(2,1)}, bf16[2560,256]{1,0:T(8,128)(2,1)}, u32[]{:S(2)}, u32[]{:S(2)}) collective-permute-start(bf16[2560,256]{1,0:T(8,128)(2,1)} %get-tuple-element.25), channel_id=1, source_target_pairs={{0,1},{1,0},{2,3},{3,2},{4,5},{5,4},{6,7},{7,6},{8,9},{9,8},{10,11... | collective-permute-start | bytes 3932168 | tf_op jit(solution)/shard_map/ppermute | solution.py:24
  79.8 3.6 %all-to-all-start.2 = ((bf16[8,32,2048]{2,1,0:T(8,128)(2,1)}), bf16[8,32,2048]{2,1,0:T(8,128)(2,1)S(1)}, u32[]{:S(2)}, u32[]{:S(2)}) async-start(bf16[8,32,2048]{2,1,0:T(8,128)(2,1)} %get-tuple-element.23), calls=%async_computation.2 | async-start | bytes 2097152 | tf_op jit(solution)/shard_map/all_to_all | solution.py:232
  83.4 3.4 %shard_map.63 = (f32[2,256,512]{2,1,0:T(8,128)S(1)}, bf16[2,256,512]{2,1,0:T(8,128)(2,1)}, bf16[2,256,512]{2,1,0:T(8,128)(2,1)}, bf16[2,256,512]{2,1,0:T(8,128)(2,1)}) custom-call(bf16[2048,256]{1,0:T(8,128)(2,1)S(1)} %bitcast.16, bf16[256,512]{1,0:T(8,128)(2,1)S(1)} %copy-done.5, bf16[2560,256]{1,0:T(8,128)(2,1)} %collective-permute-done.3.message), custom_call_target="tpu_custom_call" | custom-call | flops 1073741824 | bytes 5242880 | tf_op jit(solution)/shard_map/pallas_call | solution.py:33
  89.4 1.5 collective-permute-start.6
  91.0 9.5 %all-to-all-done.2.blocks = bf16[8,32,2048]{2,1,0:T(8,128)(2,1)S(1)} async-done(((bf16[8,32,2048]{2,1,0:T(8,128)(2,1)}), bf16[8,32,2048]{2,1,0:T(8,128)(2,1)S(1)}, u32[]{:S(2)}, u32[]{:S(2)}) %all-to-all-start.2) | async-done | bytes 1048608 | tf_op jit(solution)/shard_map/all_to_all | solution.py:232
  103.5 9.0 %all-to-all-start.3 = ((bf16[32,32,256]{2,1,0:T(8,128)(2,1)}), bf16[32,32,256]{2,1,0:T(8,128)(2,1)S(1)}, u32[]{:S(2)}, u32[]{:S(2)}) async-start(bf16[32,32,256]{2,1,0:T(8,128)(2,1)} %bitcast.17), calls=%async_computation.3 | async-start | bytes 1048576 | tf_op jit(solution)/shard_map/all_to_all | solution.py:248
  113.9 9.6 %all-to-all-done.3 = bf16[32,32,256]{2,1,0:T(8,128)(2,1)S(1)} async-done(((bf16[32,32,256]{2,1,0:T(8,128)(2,1)}), bf16[32,32,256]{2,1,0:T(8,128)(2,1)S(1)}, u32[]{:S(2)}, u32[]{:S(2)}) %all-to-all-start.3) | async-done | bytes 524320 | tf_op jit(solution)/shard_map/all_to_all | solution.py:248
  123.5 14.0 %collective-permute-start.7 = (bf16[4,256,256]{2,1,0:T(8,128)(2,1)S(1)}, bf16[4,256,256]{2,1,0:T(8,128)(2,1)S(1)}, u32[]{:S(2)}, u32[]{:S(2)}) collective-permute-start(bf16[4,256,256]{2,1,0:T(8,128)(2,1)S(1)} %bitcast.11), channel_id=1, source_target_pairs={{0,1},{1,0},{2,3},{3,2},{4,5},{5,4},{6,7},{7,6},{8,9},{9,8},{10,11... | collective-permute-start | bytes 1572872 | tf_op jit(solution)/shard_map/ppermute | solution.py:24
  139.5 5.9 %shard_map.66 = bf16[256,2304]{1,0:T(8,128)(2,1)S(1)} custom-call(bf16[4,256,256]{2,1,0:T(8,128)(2,1)S(1)} %bitcast.12, bf16[4,256,256]{2,1,0:T(8,128)(2,1)S(1)} %collective-permute-done.7.grad_o, bf16[4,512,1792]{2,1,0:T(8,128)(2,1)} %bitcast.19, bf16[256,512]{1,0:T(8,128)(2,1)S(1)} %get-tuple-element.37.refs_0_), custom_call_target="tpu_custom_call" | custom-call | flops 1879048192 | bytes 7340032 | tf_op jit(solution)/shard_map/pallas_call | solution.py:162
  145.4 3.9 %all-to-all-start.4 = ((bf16[32,32,256]{2,1,0:T(8,128)(2,1)}), bf16[32,32,256]{2,1,0:T(8,128)(2,1)S(1)}, u32[]{:S(2)}, u32[]{:S(2)}) async-start(bf16[32,32,256]{2,1,0:T(8,128)(2,1)} %bitcast.7), calls=%async_computation.4 | async-start | bytes 1048576 | tf_op jit(solution)/shard_map/all_to_all | solution.py:248
  149.8 12.5 %all-to-all-done.4 = bf16[32,32,256]{2,1,0:T(8,128)(2,1)S(1)} async-done(((bf16[32,32,256]{2,1,0:T(8,128)(2,1)}), bf16[32,32,256]{2,1,0:T(8,128)(2,1)S(1)}, u32[]{:S(2)}, u32[]{:S(2)}) %all-to-all-start.4) | async-done | bytes 524320 | tf_op jit(solution)/shard_map/all_to_all | solution.py:248
  163.8 1.5 collective-permute-done.8.grad_o
  165.3 5.9 %shard_map.67 = f32[256,1792]{1,0:T(8,128)S(1)} custom-call(bf16[4,256,256]{2,1,0:T(8,128)(2,1)S(1)} %bitcast.14, bf16[4,256,256]{2,1,0:T(8,128)(2,1)S(1)} %collective-permute-done.8.grad_o, bf16[4,512,1792]{2,1,0:T(8,128)(2,1)} %bitcast.20), custom_call_target="tpu_custom_call" | custom-call | flops 1879048192 | bytes 7340032 | tf_op jit(solution)/shard_map/pallas_call | solution.py:162
  171.2 10.5 %collective-permute-done.9 = bf16[256,2304]{1,0:T(8,128)(2,1)S(1)} collective-permute-done((bf16[256,2304]{1,0:T(8,128)(2,1)S(1)}, bf16[256,2304]{1,0:T(8,128)(2,1)S(1)}, u32[]{:S(2)}, u32[]{:S(2)}) %collective-permute-start.9) | collective-permute-done | bytes 1179680 | tf_op jit(solution)/shard_map/ppermute | solution.py:24
  181.9 1.6 fusion
  (37 shorter events, 18.8 us)
Async XLA Ops:
  7.2 94.4 %all-gather.3.cloned.1.call-start = ((), (), s32[]{:S(2)}) async-start(), calls=%async_computation.5 | async-start | bytes 9175040 | tf_op jit(solution)/shard_map/all_gather | solution.py:213
  7.9 9.2 %copy-start.3 = (bf16[512,2048]{1,0:T(8,128)(2,1)S(1)}, bf16[512,2048]{1,0:T(8,128)(2,1)}, u32[]{:S(2)}) copy-start(bf16[512,2048]{1,0:T(8,128)(2,1)} %a0.1) | copy-start | bytes 6291460
  15.6 9.2 %collective-permute-start = (f32[2048,256]{1,0:T(8,128)}, f32[2048,256]{1,0:T(8,128)S(1)}, u32[]{:S(2)}, u32[]{:S(2)}) collective-permute-start(f32[2048,256]{1,0:T(8,128)} %shard_map.60), channel_id=1, source_target_pairs={{0,1},{1,0},{2,3},{3,2},{4,5},{5,4},{6,7},{7,6},{8,9},{9,8},{10,11... | collective-permute-start | bytes 6291464 | tf_op jit(solution)/shard_map/ppermute | solution.py:24
  17.1 44.2 %collective-permute-start.2 = (bf16[512,2048]{1,0:T(8,128)(2,1)S(1)}, bf16[512,2048]{1,0:T(8,128)(2,1)}, u32[]{:S(2)}, u32[]{:S(2)}) collective-permute-start(bf16[512,2048]{1,0:T(8,128)(2,1)S(1)} %copy-done.3), channel_id=1, source_target_pairs={{0,1},{1,0},{2,3},{3,2},{4,5},{5,4},{6,7},{7,6},{8,9},{9,8},{10,11... | collective-permute-start | bytes 6291464 | tf_op jit(solution)/shard_map/ppermute | solution.py:24
  51.8 18.6 %all-to-all-start.1 = ((bf16[8,256,256]{2,1,0:T(8,128)(2,1)}), bf16[8,256,256]{2,1,0:T(8,128)(2,1)S(1)}, u32[]{:S(2)}, u32[]{:S(2)}) async-start(bf16[8,256,256]{2,1,0:T(8,128)(2,1)} %shard_map.61), calls=%async_computation.1 | async-start | bytes 2097152 | tf_op jit(solution)/shard_map/all_to_all | solution.py:223
  58.0 3.4 %collective-permute-start.1 = (bf16[512,256]{1,0:T(8,128)(2,1)}, bf16[512,256]{1,0:T(8,128)(2,1)}, u32[]{:S(2)}, u32[]{:S(2)}) collective-permute-start(bf16[512,256]{1,0:T(8,128)(2,1)} %bitcast.22), channel_id=1, source_target_pairs={{0,1},{1,0},{2,3},{3,2},{4,5},{5,4},{6,7},{7,6},{8,9},{9,8},{10,11... | collective-permute-start | bytes 786440 | tf_op jit(solution)/shard_map/ppermute | solution.py:24
  76.0 0.7 copy-start.4
  76.7 6.7 %copy-start.5 = (bf16[256,512]{1,0:T(8,128)(2,1)S(1)}, bf16[256,512]{1,0:T(8,128)(2,1)}, u32[]{:S(2)}) copy-start(bf16[256,512]{1,0:T(8,128)(2,1)} %copy-done.4) | copy-start | bytes 786436
  76.7 6.6 %collective-permute-start.3 = (bf16[2560,256]{1,0:T(8,128)(2,1)}, bf16[2560,256]{1,0:T(8,128)(2,1)}, u32[]{:S(2)}, u32[]{:S(2)}) collective-permute-start(bf16[2560,256]{1,0:T(8,128)(2,1)} %get-tuple-element.25), channel_id=1, source_target_pairs={{0,1},{1,0},{2,3},{3,2},{4,5},{5,4},{6,7},{7,6},{8,9},{9,8},{10,11... | collective-permute-start | bytes 3932168 | tf_op jit(solution)/shard_map/ppermute | solution.py:24
  79.8 20.7 %all-to-all-start.2 = ((bf16[8,32,2048]{2,1,0:T(8,128)(2,1)}), bf16[8,32,2048]{2,1,0:T(8,128)(2,1)S(1)}, u32[]{:S(2)}, u32[]{:S(2)}) async-start(bf16[8,32,2048]{2,1,0:T(8,128)(2,1)} %get-tuple-element.23), calls=%async_computation.2 | async-start | bytes 2097152 | tf_op jit(solution)/shard_map/all_to_all | solution.py:232
  86.7 14.8 %collective-permute-start.4 = (bf16[2,256,512]{2,1,0:T(8,128)(2,1)}, bf16[2,256,512]{2,1,0:T(8,128)(2,1)S(1)}, u32[]{:S(2)}, u32[]{:S(2)}) collective-permute-start(bf16[2,256,512]{2,1,0:T(8,128)(2,1)} %get-tuple-element.26), channel_id=1, source_target_pairs={{0,16},{16,32},{32,48},{48,0},{1,17},{17,33},{33,49},{49,1},{2,18}... | collective-permute-start | bytes 1572872 | tf_op jit(solution)/shard_map/ppermute | solution.py:24
  88.0 13.6 %collective-permute-start.5 = (bf16[2,256,512]{2,1,0:T(8,128)(2,1)}, bf16[2,256,512]{2,1,0:T(8,128)(2,1)S(1)}, u32[]{:S(2)}, u32[]{:S(2)}) collective-permute-start(bf16[2,256,512]{2,1,0:T(8,128)(2,1)} %get-tuple-element.27), channel_id=1, source_target_pairs={{0,48},{16,0},{32,16},{48,32},{1,49},{17,1},{33,17},{49,33},{2,50}... | collective-permute-start | bytes 1572872 | tf_op jit(solution)/shard_map/ppermute | solution.py:24
  89.4 24.5 %collective-permute-start.6 = (bf16[2,256,512]{2,1,0:T(8,128)(2,1)}, bf16[2,256,512]{2,1,0:T(8,128)(2,1)}, u32[]{:S(2)}, u32[]{:S(2)}) collective-permute-start(bf16[2,256,512]{2,1,0:T(8,128)(2,1)} %get-tuple-element.30), channel_id=1, source_target_pairs={{0,32},{16,48},{32,0},{48,16},{1,33},{17,49},{33,1},{49,17},{2,34}... | collective-permute-start | bytes 1572872 | tf_op jit(solution)/shard_map/ppermute | solution.py:24
  102.7 0.8 copy-start.2
  103.5 20.0 %all-to-all-start.3 = ((bf16[32,32,256]{2,1,0:T(8,128)(2,1)}), bf16[32,32,256]{2,1,0:T(8,128)(2,1)S(1)}, u32[]{:S(2)}, u32[]{:S(2)}) async-start(bf16[32,32,256]{2,1,0:T(8,128)(2,1)} %bitcast.17), calls=%async_computation.3 | async-start | bytes 1048576 | tf_op jit(solution)/shard_map/all_to_all | solution.py:248
  123.5 16.0 %collective-permute-start.7 = (bf16[4,256,256]{2,1,0:T(8,128)(2,1)S(1)}, bf16[4,256,256]{2,1,0:T(8,128)(2,1)S(1)}, u32[]{:S(2)}, u32[]{:S(2)}) collective-permute-start(bf16[4,256,256]{2,1,0:T(8,128)(2,1)S(1)} %bitcast.11), channel_id=1, source_target_pairs={{0,1},{1,0},{2,3},{3,2},{4,5},{5,4},{6,7},{7,6},{8,9},{9,8},{10,11... | collective-permute-start | bytes 1572872 | tf_op jit(solution)/shard_map/ppermute | solution.py:24
  138.7 0.8 copy-start
  145.4 16.9 %all-to-all-start.4 = ((bf16[32,32,256]{2,1,0:T(8,128)(2,1)}), bf16[32,32,256]{2,1,0:T(8,128)(2,1)S(1)}, u32[]{:S(2)}, u32[]{:S(2)}) async-start(bf16[32,32,256]{2,1,0:T(8,128)(2,1)} %bitcast.7), calls=%async_computation.4 | async-start | bytes 1048576 | tf_op jit(solution)/shard_map/all_to_all | solution.py:248
  149.3 32.4 %collective-permute-start.9 = (bf16[256,2304]{1,0:T(8,128)(2,1)S(1)}, bf16[256,2304]{1,0:T(8,128)(2,1)S(1)}, u32[]{:S(2)}, u32[]{:S(2)}) collective-permute-start(bf16[256,2304]{1,0:T(8,128)(2,1)S(1)} %shard_map.66), channel_id=1, source_target_pairs={{0,64},{64,0},{1,65},{65,1},{2,66},{66,2},{3,67},{67,3},{4,68},{68... | collective-permute-start | bytes 3538952 | tf_op jit(solution)/shard_map/ppermute | solution.py:24
  162.4 3.0 %collective-permute-start.8 = (bf16[4,256,256]{2,1,0:T(8,128)(2,1)S(1)}, bf16[4,256,256]{2,1,0:T(8,128)(2,1)S(1)}, u32[]{:S(2)}, u32[]{:S(2)}) collective-permute-start(bf16[4,256,256]{2,1,0:T(8,128)(2,1)S(1)} %bitcast.13), channel_id=1, source_target_pairs={{0,1},{1,0},{2,3},{3,2},{4,5},{5,4},{6,7},{7,6},{8,9},{9,8},{10,11... | collective-permute-start | bytes 1572872 | tf_op jit(solution)/shard_map/ppermute | solution.py:24
  181.9 1.6 copy-start.1
Sparse Core Ops, SparseCore 0:
  9.7 77.5 all-gather.2

commit v10 on v9

--- a/solution.py
+++ b/solution.py
@@ -52,22 +52,15 @@
     return out
 
 
-def codes_kernel(other, acts, b, out, rows, turned, held, sems):
-    core, (parts, step), half = lax.axis_index("core"), held.shape[:2], rows.shape[0]
-    start = pl.multiple_of((1 - core if other else core) * half, half)
-    first = pltpu.make_async_copy(acts.at[pl.ds(start, half), :], rows, sems.at[parts])
-    first.start()
-    copies = [
-        pltpu.make_async_copy(b.at[pl.ds(i * step, step), :], held.at[i], sems.at[i])
-        for i in range(parts)
-    ]
-    for copy in copies:
-        copy.start()
-    first.wait()
-    turned[...] = rows[...].T
-    for i in range(parts):
-        copies[i].wait()
-        out[i * step : (i + 1) * step] = dot(held[i], turned[...])
+def codes_kernel(other, acts, b, out, turned):
+    core, half = lax.axis_index("core"), turned.shape[1]
+
+    @pl.when(pl.program_id(0) == 0)
+    def _():
+        which = 1 - core if other else core
+        turned[...] = acts[pl.ds(pl.multiple_of(which * half, half), half), :].T
+
+    out[...] = dot(b[...], turned[...])
 
 
 def codes_call(other, acts, proj_b):
@@ -75,16 +68,15 @@
     half, step = tokens // 2, 512
     return pl.pallas_call(
         functools.partial(codes_kernel, other),
+        grid=(rank // step,),
         out_shape=like((rank, half), F32),
-        in_specs=[ANY, ANY],
-        out_specs=VMEM,
-        scratch_shapes=[
-            pltpu.VMEM((half, wide), BF),
-            pltpu.VMEM((wide, half), BF),
-            pltpu.VMEM((rank // step, step, wide), BF),
-            pltpu.SemaphoreType.DMA((rank // step + 1,)),
+        in_specs=[
+            pl.BlockSpec((tokens, wide), lambda i: (0, 0)),
+            pl.BlockSpec((step, wide), lambda i: (i, 0)),
         ],
-        compiler_params=pltpu.CompilerParams(vmem_limit_bytes=58 * 1024 * 1024),
+        out_specs=pl.BlockSpec((step, half), lambda i: (i, 0)),
+        scratch_shapes=[pltpu.VMEM((wide, half), BF)],
+        compiler_params=pltpu.CompilerParams(vmem_limit_bytes=32 * 1024 * 1024),
         cost_estimate=pl.CostEstimate(
             flops=2 * rank * wide * half, bytes_accessed=2 * rank * wide, transcendentals=0
         ),
@@ -240,7 +232,7 @@
     )
     terms = [terms[0]] + [shift(terms[k], "x", 4, k) for k in (1, 2, 3)]
 
-    blocks, row, terms[1], terms[3] = lax.optimization_barrier((blocks, row, terms[1], terms[3]))
+    blocks, row = lax.optimization_barrier((blocks, row))
     spread = like((4, 8, sub, width))
     split_a, split_o = call(spread_kernel, [spread, spread], blocks, scratch=[pltpu.VMEM((sub, rank), BF)])
 
@@ -249,7 +241,7 @@
         return split.reshape(4, half, width)
 
     grad = gather(split_a)
-    grad, terms[2] = lax.optimization_barrier((grad, terms[2]))
+    grad, *terms = lax.optimization_barrier((grad, *terms))
     term_o, term_a = call(term_sum_kernel, [like((width, outs), F32), like((width, outs))], *terms)
     away = last_call(grad, swap(grad, "core"), row, BF, term_a)
     away, split_o = lax.optimization_barrier((away, split_o))

time: 192 us -> 176 us (0.917)
  starting transfers between devices: 46.7 us -> 31.6 us
  waiting for transfers between devices: 56.3 us -> 66.4 us
  Pallas kernels: 39.5 us -> 30.6 us
    ppermute x10, starting transfers between devices: 26.7 us -> 14.4 us  [shift(): lax.ppermute(array, axis, [(i, (i + step) % size) for i in range(size)])]
    pallas_call x2, Pallas kernels: 15.2 us -> 5.82 us  [codes_call(): pl.pallas_call(functools.partial(codes_kernel, other), grid=(rank // step...]
    ppermute x10, waiting for transfers between devices: 15 us -> 22.1 us  [shift(): lax.ppermute(array, axis, [(i, (i + step) % size) for i in range(size)])]
    all_to_all x2, starting transfers between devices: 12.9 us -> 10.1 us  [gather(): lax.all_to_all(split.reshape(32, sub, width), ('x', 'z', 'y_hi'), 0, 0)]
    all_to_all x1, waiting for transfers between devices: 9.02 us -> 11.8 us  [local(): codes = lax.all_to_all(codes, ZY, 0, 0).reshape(rank, half)]
  transfers between devices with their start and end apart: 15 -> 15, of which waited for: 9 -> 9; matrix products, arithmetic and copies ran while one was open for 3% -> 0% of each run, Pallas kernels for 18% -> 14%
where the time goes in v10:
time: 176 us
  waiting for transfers between devices  66.4 us (38%)
  starting transfers between devices  31.6 us (18%)
  Pallas kernels  30.6 us (17%)
  blocking collectives  23.9 us (14%)
  between operations  14.2 us (8%)
  local copies, waits for them, and re-layouts  6.74 us (4%)
  other arithmetic  2.14 us (1%)
    all_to_all x1, blocking collectives, local(): blocks = lax.all_to_all(mine, ZY, 0, 0)  23.9 us
    all_to_all x2, waiting for transfers between devices, gather(): lax.all_to_all(split.reshape(32, sub, width), ('x', 'z', 'y_hi'), 0, 0)  22.7 us
    ppermute x10, waiting for transfers between devices, shift(): lax.ppermute(array, axis, [(i, (i + step) % size) for i in range(size)])  22.1 us
    ppermute x10, starting transfers between devices, shift(): lax.ppermute(array, axis, [(i, (i + step) % size) for i in range(size)])  14.4 us
    pallas_call x5, Pallas kernels, call(): pl.pallas_call(body, out_shape=outs if len(outs) > 1 else outs[0], in_spe...  13.1 us
    all_to_all x1, waiting for transfers between devices, local(): codes = lax.all_to_all(codes, ZY, 0, 0).reshape(rank, half)  11.8 us
    pallas_call x2, Pallas kernels, last_call(): pl.pallas_call(last_kernel, out_shape=like((width, wide + sum((j.shape[1]...  11.8 us
    all_to_all x2, starting transfers between devices, gather(): lax.all_to_all(split.reshape(32, sub, width), ('x', 'z', 'y_hi'), 0, 0)  10.1 us
  transfers between devices with their start and end apart: 15, of which 9 were waited for; matrix products, arithmetic and copies ran while one was open for 0% of the time, Pallas kernels for 14%

profile of v10, /device:TPU:1, one launch (start us, length us, event | category | flops | bytes accessed | tf_op | source)
XLA Modules:
  0.0 175.6 jit_solution(15053651064134078281)
XLA Ops:
  8.7 3.1 %copy-done = bf16[2048,1792]{1,0:T(8,128)(2,1)S(1)} copy-done((bf16[2048,1792]{1,0:T(8,128)(2,1)S(1)}, bf16[2048,1792]{1,0:T(8,128)(2,1)}, u32[]{:S(2)}) %copy-start) | copy-done | bytes 7340056
  11.7 2.9 %shard_map.60 = f32[2048,256]{1,0:T(8,128)S(1)} custom-call(bf16[512,1792]{1,0:T(8,128)(2,1)S(1)} %copy-done.1, bf16[2048,1792]{1,0:T(8,128)(2,1)S(1)} %copy-done), custom_call_target="tpu_custom_call" | custom-call | flops 1879048192 | bytes 7340032 | tf_op jit(solution)/shard_map/pallas_call | solution.py:69
  16.3 2.9 %shard_map.59 = f32[2048,256]{1,0:T(8,128)S(1)} custom-call(bf16[512,1792]{1,0:T(8,128)(2,1)S(1)} %copy-done.1, bf16[2048,1792]{1,0:T(8,128)(2,1)S(1)} %copy-done), custom_call_target="tpu_custom_call" | custom-call | flops 1879048192 | bytes 7340032 | tf_op jit(solution)/shard_map/pallas_call | solution.py:69
  19.2 2.8 %collective-permute-done = f32[2048,256]{1,0:T(8,128)S(1)} collective-permute-done((f32[2048,256]{1,0:T(8,128)S(1)}, f32[2048,256]{1,0:T(8,128)S(1)}, u32[]{:S(2)}, u32[]{:S(2)}) %collective-permute-start) | collective-permute-done | bytes 2097184 | tf_op jit(solution)/shard_map/ppermute | solution.py:24
  22.4 23.9 %all_to_all.25.blocks = bf16[8,256,256]{2,1,0:T(8,128)(2,1)S(1)} all-to-all(bf16[8,256,256]{2,1,0:T(8,128)(2,1)S(1)} %bitcast.21), channel_id=1, replica_groups=mesh['y_lo'=2,'x'=4,'z'=4,'y_hi'=2,'core'=2] {'z','y_hi'}, dimensions={0} | all-to-all | bytes 2097152 | tf_op jit(solution)/shard_map/all_to_all | solution.py:213
  47.3 3.6 %all-to-all-start.1 = ((bf16[8,256,256]{2,1,0:T(8,128)(2,1)}), bf16[8,256,256]{2,1,0:T(8,128)(2,1)S(1)}, u32[]{:S(2)}, u32[]{:S(2)}) async-start(bf16[8,256,256]{2,1,0:T(8,128)(2,1)} %shard_map.61), calls=%async_computation.1 | async-start | bytes 2097152 | tf_op jit(solution)/shard_map/all_to_all | solution.py:215
  51.1 1.9 %collective-permute-start.1 = (bf16[512,256]{1,0:T(8,128)(2,1)S(1)}, bf16[512,256]{1,0:T(8,128)(2,1)S(1)}, u32[]{:S(2)}, u32[]{:S(2)}) collective-permute-start(bf16[512,256]{1,0:T(8,128)(2,1)S(1)} %bitcast.22), channel_id=1, source_target_pairs={{0,1},{1,0},{2,3},{3,2},{4,5},{5,4},{6,7},{7,6},{8,9},{9,8},{10,11... | collective-permute-start | bytes 786440 | tf_op jit(solution)/shard_map/ppermute | solution.py:24
  54.2 11.8 %all-to-all-done.1 = bf16[8,256,256]{2,1,0:T(8,128)(2,1)S(1)} async-done(((bf16[8,256,256]{2,1,0:T(8,128)(2,1)}), bf16[8,256,256]{2,1,0:T(8,128)(2,1)S(1)}, u32[]{:S(2)}, u32[]{:S(2)}) %all-to-all-start.1) | async-done | bytes 1048608 | tf_op jit(solution)/shard_map/all_to_all | solution.py:215
  66.0 6.2 %shard_map.62 = (bf16[256,512]{1,0:T(8,128)(2,1)S(1)}, bf16[2560,256]{1,0:T(8,128)(2,1)}, bf16[8,32,2048]{2,1,0:T(8,128)(2,1)}) custom-call(bf16[2048,256]{1,0:T(8,128)(2,1)S(1)} %bitcast.15, bf16[512,256]{1,0:T(8,128)(2,1)S(1)} %bitcast.18, bf16[512,256]{1,0:T(8,128)(2,1)S(1)} %collective-permute-done.1.far, bf16[512,2048]{1,0:T(8,128)(2,1)} %a0.1, ...), custom_call_target="tpu_custom_call" | custom-call | flops 2147483648 | bytes 8388608 | tf_op jit(solution)/shard_map/pallas_call | solution.py:33
  72.2 3.1 %collective-permute-start.3 = (bf16[2560,256]{1,0:T(8,128)(2,1)}, bf16[2560,256]{1,0:T(8,128)(2,1)}, u32[]{:S(2)}, u32[]{:S(2)}) collective-permute-start(bf16[2560,256]{1,0:T(8,128)(2,1)} %get-tuple-element.28), channel_id=1, source_target_pairs={{0,1},{1,0},{2,3},{3,2},{4,5},{5,4},{6,7},{7,6},{8,9},{9,8},{10,11... | collective-permute-start | bytes 3932168 | tf_op jit(solution)/shard_map/ppermute | solution.py:24
  75.3 3.6 %all-to-all-start.2 = ((bf16[8,32,2048]{2,1,0:T(8,128)(2,1)}), bf16[8,32,2048]{2,1,0:T(8,128)(2,1)S(1)}, u32[]{:S(2)}, u32[]{:S(2)}) async-start(bf16[8,32,2048]{2,1,0:T(8,128)(2,1)} %get-tuple-element.24), calls=%async_computation.2 | async-start | bytes 2097152 | tf_op jit(solution)/shard_map/all_to_all | solution.py:224
  78.8 3.4 %shard_map.64 = (f32[2,256,512]{2,1,0:T(8,128)S(1)}, bf16[2,256,512]{2,1,0:T(8,128)(2,1)}, bf16[2,256,512]{2,1,0:T(8,128)(2,1)}, bf16[2,256,512]{2,1,0:T(8,128)(2,1)}) custom-call(bf16[2048,256]{1,0:T(8,128)(2,1)S(1)} %bitcast.16, bf16[256,512]{1,0:T(8,128)(2,1)S(1)} %get-tuple-element.27.own, bf16[2560,256]{1,0:T(8,128)(2,1)} %collective-permute-done.3.message), custom_call_target="tpu_custom_call" | custom-call | flops 1073741824 | bytes 5242880 | tf_op jit(solution)/shard_map/pallas_call | solution.py:33
  83.4 2.4 %collective-permute-start.5 = (bf16[2,256,512]{2,1,0:T(8,128)(2,1)}, bf16[2,256,512]{2,1,0:T(8,128)(2,1)S(1)}, u32[]{:S(2)}, u32[]{:S(2)}) collective-permute-start(bf16[2,256,512]{2,1,0:T(8,128)(2,1)} %get-tuple-element.31), channel_id=1, source_target_pairs={{0,32},{16,48},{32,0},{48,16},{1,33},{17,49},{33,1},{49,17},{2,34}... | collective-permute-start | bytes 1572872 | tf_op jit(solution)/shard_map/ppermute | solution.py:24
  87.0 9.1 %all-to-all-done.2.blocks = bf16[8,32,2048]{2,1,0:T(8,128)(2,1)S(1)} async-done(((bf16[8,32,2048]{2,1,0:T(8,128)(2,1)}), bf16[8,32,2048]{2,1,0:T(8,128)(2,1)S(1)}, u32[]{:S(2)}, u32[]{:S(2)}) %all-to-all-start.2) | async-done | bytes 1048608 | tf_op jit(solution)/shard_map/all_to_all | solution.py:224
  98.1 5.6 %all-to-all-start.3 = ((bf16[32,32,256]{2,1,0:T(8,128)(2,1)}), bf16[32,32,256]{2,1,0:T(8,128)(2,1)S(1)}, u32[]{:S(2)}, u32[]{:S(2)}) async-start(bf16[32,32,256]{2,1,0:T(8,128)(2,1)} %bitcast.17), calls=%async_computation.3 | async-start | bytes 1048576 | tf_op jit(solution)/shard_map/all_to_all | solution.py:240
  103.7 6.0 %collective-permute-done.5.r2 = bf16[2,256,512]{2,1,0:T(8,128)(2,1)S(1)} collective-permute-done((bf16[2,256,512]{2,1,0:T(8,128)(2,1)}, bf16[2,256,512]{2,1,0:T(8,128)(2,1)S(1)}, u32[]{:S(2)}, u32[]{:S(2)}) %collective-permute-start.5) | collective-permute-done | bytes 524320 | tf_op jit(solution)/shard_map/ppermute | solution.py:24
  109.7 10.6 %all-to-all-done.3 = bf16[32,32,256]{2,1,0:T(8,128)(2,1)S(1)} async-done(((bf16[32,32,256]{2,1,0:T(8,128)(2,1)}), bf16[32,32,256]{2,1,0:T(8,128)(2,1)S(1)}, u32[]{:S(2)}, u32[]{:S(2)}) %all-to-all-start.3) | async-done | bytes 524320 | tf_op jit(solution)/shard_map/all_to_all | solution.py:240
  122.9 5.9 %shard_map.66 = bf16[256,2304]{1,0:T(8,128)(2,1)S(1)} custom-call(bf16[4,256,256]{2,1,0:T(8,128)(2,1)S(1)} %bitcast.12, bf16[4,256,256]{2,1,0:T(8,128)(2,1)S(1)} %collective-permute-done.7.grad_o, bf16[4,512,1792]{2,1,0:T(8,128)(2,1)} %bitcast.19, bf16[256,512]{1,0:T(8,128)(2,1)S(1)} %get-tuple-element.39.refs_0_), custom_call_target="tpu_custom_call" | custom-call | flops 1879048192 | bytes 7340032 | tf_op jit(solution)/shard_map/pallas_call | solution.py:154
  128.8 4.5 %all-to-all-start.4 = ((bf16[32,32,256]{2,1,0:T(8,128)(2,1)}), bf16[32,32,256]{2,1,0:T(8,128)(2,1)S(1)}, u32[]{:S(2)}, u32[]{:S(2)}) async-start(bf16[32,32,256]{2,1,0:T(8,128)(2,1)} %bitcast.7), calls=%async_computation.4 | async-start | bytes 1048576 | tf_op jit(solution)/shard_map/all_to_all | solution.py:240
  134.2 12.0 %all-to-all-done.4 = bf16[32,32,256]{2,1,0:T(8,128)(2,1)S(1)} async-done(((bf16[32,32,256]{2,1,0:T(8,128)(2,1)}), bf16[32,32,256]{2,1,0:T(8,128)(2,1)S(1)}, u32[]{:S(2)}, u32[]{:S(2)}) %all-to-all-start.4) | async-done | bytes 524320 | tf_op jit(solution)/shard_map/all_to_all | solution.py:240
  147.8 1.5 collective-permute-done.8.grad_o
  149.3 5.9 %shard_map.67 = f32[256,1792]{1,0:T(8,128)S(1)} custom-call(bf16[4,256,256]{2,1,0:T(8,128)(2,1)S(1)} %bitcast.14, bf16[4,256,256]{2,1,0:T(8,128)(2,1)S(1)} %collective-permute-done.8.grad_o, bf16[4,512,1792]{2,1,0:T(8,128)(2,1)} %bitcast.20), custom_call_target="tpu_custom_call" | custom-call | flops 1879048192 | bytes 7340032 | tf_op jit(solution)/shard_map/pallas_call | solution.py:154
  155.2 10.7 %collective-permute-done.9 = bf16[256,2304]{1,0:T(8,128)(2,1)S(1)} collective-permute-done((bf16[256,2304]{1,0:T(8,128)(2,1)S(1)}, bf16[256,2304]{1,0:T(8,128)(2,1)S(1)}, u32[]{:S(2)}, u32[]{:S(2)}) %collective-permute-start.9) | collective-permute-done | bytes 1179680 | tf_op jit(solution)/shard_map/ppermute | solution.py:24
  166.1 1.6 fusion
  (37 shorter events, 16.4 us)
Async XLA Ops:
  7.2 1.5 copy-start.1
  7.2 89.0 %all-gather.3.cloned.1.call-start = ((), (), s32[]{:S(2)}) async-start(), calls=%async_computation.5 | async-start | bytes 9175040 | tf_op jit(solution)/shard_map/all_gather | solution.py:205
  8.7 3.1 %copy-start = (bf16[2048,1792]{1,0:T(8,128)(2,1)S(1)}, bf16[2048,1792]{1,0:T(8,128)(2,1)}, u32[]{:S(2)}) copy-start(bf16[2048,1792]{1,0:T(8,128)(2,1)} %b.3) | copy-start | bytes 22020100
  14.7 7.4 %collective-permute-start = (f32[2048,256]{1,0:T(8,128)S(1)}, f32[2048,256]{1,0:T(8,128)S(1)}, u32[]{:S(2)}, u32[]{:S(2)}) collective-permute-start(f32[2048,256]{1,0:T(8,128)S(1)} %shard_map.60), channel_id=1, source_target_pairs={{0,1},{1,0},{2,3},{3,2},{4,5},{5,4},{6,7},{7,6},{8,9},{9,8},{10,11... | collective-permute-start | bytes 6291464 | tf_op jit(solution)/shard_map/ppermute | solution.py:24
  16.2 38.0 %collective-permute-start.2 = (bf16[512,2048]{1,0:T(8,128)(2,1)}, bf16[512,2048]{1,0:T(8,128)(2,1)}, u32[]{:S(2)}, u32[]{:S(2)}) collective-permute-start(bf16[512,2048]{1,0:T(8,128)(2,1)} %a0.1), channel_id=1, source_target_pairs={{0,1},{1,0},{2,3},{3,2},{4,5},{5,4},{6,7},{7,6},{8,9},{9,8},{10,11... | collective-permute-start | bytes 6291464 | tf_op jit(solution)/shard_map/ppermute | solution.py:24
  46.2 4.7 %copy-start.5 = (bf16[512,512]{1,0:T(8,128)(2,1)S(1)}, bf16[512,512]{1,0:T(8,128)(2,1)}, u32[]{:S(2)}) copy-start(bf16[512,512]{1,0:T(8,128)(2,1)} %param.5) | copy-start | bytes 1572868
  47.3 18.6 %all-to-all-start.1 = ((bf16[8,256,256]{2,1,0:T(8,128)(2,1)}), bf16[8,256,256]{2,1,0:T(8,128)(2,1)S(1)}, u32[]{:S(2)}, u32[]{:S(2)}) async-start(bf16[8,256,256]{2,1,0:T(8,128)(2,1)} %shard_map.61), calls=%async_computation.1 | async-start | bytes 2097152 | tf_op jit(solution)/shard_map/all_to_all | solution.py:215
  51.1 3.1 %collective-permute-start.1 = (bf16[512,256]{1,0:T(8,128)(2,1)S(1)}, bf16[512,256]{1,0:T(8,128)(2,1)S(1)}, u32[]{:S(2)}, u32[]{:S(2)}) collective-permute-start(bf16[512,256]{1,0:T(8,128)(2,1)S(1)} %bitcast.22), channel_id=1, source_target_pairs={{0,1},{1,0},{2,3},{3,2},{4,5},{5,4},{6,7},{7,6},{8,9},{9,8},{10,11... | collective-permute-start | bytes 786440 | tf_op jit(solution)/shard_map/ppermute | solution.py:24
  72.2 6.7 %collective-permute-start.3 = (bf16[2560,256]{1,0:T(8,128)(2,1)}, bf16[2560,256]{1,0:T(8,128)(2,1)}, u32[]{:S(2)}, u32[]{:S(2)}) collective-permute-start(bf16[2560,256]{1,0:T(8,128)(2,1)} %get-tuple-element.28), channel_id=1, source_target_pairs={{0,1},{1,0},{2,3},{3,2},{4,5},{5,4},{6,7},{7,6},{8,9},{9,8},{10,11... | collective-permute-start | bytes 3932168 | tf_op jit(solution)/shard_map/ppermute | solution.py:24
  75.3 20.9 %all-to-all-start.2 = ((bf16[8,32,2048]{2,1,0:T(8,128)(2,1)}), bf16[8,32,2048]{2,1,0:T(8,128)(2,1)S(1)}, u32[]{:S(2)}, u32[]{:S(2)}) async-start(bf16[8,32,2048]{2,1,0:T(8,128)(2,1)} %get-tuple-element.24), calls=%async_computation.2 | async-start | bytes 2097152 | tf_op jit(solution)/shard_map/all_to_all | solution.py:224
  82.2 21.4 %collective-permute-start.4 = (bf16[2,256,512]{2,1,0:T(8,128)(2,1)}, bf16[2,256,512]{2,1,0:T(8,128)(2,1)S(1)}, u32[]{:S(2)}, u32[]{:S(2)}) collective-permute-start(bf16[2,256,512]{2,1,0:T(8,128)(2,1)} %get-tuple-element.30), channel_id=1, source_target_pairs={{0,16},{16,32},{32,48},{48,0},{1,17},{17,33},{33,49},{49,1},{2,18}... | collective-permute-start | bytes 1572872 | tf_op jit(solution)/shard_map/ppermute | solution.py:24
  83.4 26.3 %collective-permute-start.5 = (bf16[2,256,512]{2,1,0:T(8,128)(2,1)}, bf16[2,256,512]{2,1,0:T(8,128)(2,1)S(1)}, u32[]{:S(2)}, u32[]{:S(2)}) collective-permute-start(bf16[2,256,512]{2,1,0:T(8,128)(2,1)} %get-tuple-element.31), channel_id=1, source_target_pairs={{0,32},{16,48},{32,0},{48,16},{1,33},{17,49},{33,1},{49,17},{2,34}... | collective-permute-start | bytes 1572872 | tf_op jit(solution)/shard_map/ppermute | solution.py:24
  85.8 23.9 %collective-permute-start.6 = (bf16[2,256,512]{2,1,0:T(8,128)(2,1)}, bf16[2,256,512]{2,1,0:T(8,128)(2,1)}, u32[]{:S(2)}, u32[]{:S(2)}) collective-permute-start(bf16[2,256,512]{2,1,0:T(8,128)(2,1)} %get-tuple-element.32), channel_id=1, source_target_pairs={{0,48},{16,0},{32,16},{48,32},{1,49},{17,1},{33,17},{49,33},{2,50}... | collective-permute-start | bytes 1572872 | tf_op jit(solution)/shard_map/ppermute | solution.py:24
  97.3 0.8 copy-start.4
  98.1 22.2 %all-to-all-start.3 = ((bf16[32,32,256]{2,1,0:T(8,128)(2,1)}), bf16[32,32,256]{2,1,0:T(8,128)(2,1)S(1)}, u32[]{:S(2)}, u32[]{:S(2)}) async-start(bf16[32,32,256]{2,1,0:T(8,128)(2,1)} %bitcast.17), calls=%async_computation.3 | async-start | bytes 1048576 | tf_op jit(solution)/shard_map/all_to_all | solution.py:240
  120.3 2.6 %collective-permute-start.7 = (bf16[4,256,256]{2,1,0:T(8,128)(2,1)S(1)}, bf16[4,256,256]{2,1,0:T(8,128)(2,1)S(1)}, u32[]{:S(2)}, u32[]{:S(2)}) collective-permute-start(bf16[4,256,256]{2,1,0:T(8,128)(2,1)S(1)} %bitcast.11), channel_id=1, source_target_pairs={{0,1},{1,0},{2,3},{3,2},{4,5},{5,4},{6,7},{7,6},{8,9},{9,8},{10,11... | collective-permute-start | bytes 1572872 | tf_op jit(solution)/shard_map/ppermute | solution.py:24
  122.1 0.8 copy-start.2
  128.8 17.5 %all-to-all-start.4 = ((bf16[32,32,256]{2,1,0:T(8,128)(2,1)}), bf16[32,32,256]{2,1,0:T(8,128)(2,1)S(1)}, u32[]{:S(2)}, u32[]{:S(2)}) async-start(bf16[32,32,256]{2,1,0:T(8,128)(2,1)} %bitcast.7), calls=%async_computation.4 | async-start | bytes 1048576 | tf_op jit(solution)/shard_map/all_to_all | solution.py:240
  133.3 32.6 %collective-permute-start.9 = (bf16[256,2304]{1,0:T(8,128)(2,1)S(1)}, bf16[256,2304]{1,0:T(8,128)(2,1)S(1)}, u32[]{:S(2)}, u32[]{:S(2)}) collective-permute-start(bf16[256,2304]{1,0:T(8,128)(2,1)S(1)} %shard_map.66), channel_id=1, source_target_pairs={{0,64},{64,0},{1,65},{65,1},{2,66},{66,2},{3,67},{67,3},{4,68},{68... | collective-permute-start | bytes 3538952 | tf_op jit(solution)/shard_map/ppermute | solution.py:24
  146.3 3.1 %collective-permute-start.8 = (bf16[4,256,256]{2,1,0:T(8,128)(2,1)S(1)}, bf16[4,256,256]{2,1,0:T(8,128)(2,1)S(1)}, u32[]{:S(2)}, u32[]{:S(2)}) collective-permute-start(bf16[4,256,256]{2,1,0:T(8,128)(2,1)S(1)} %bitcast.13), channel_id=1, source_target_pairs={{0,1},{1,0},{2,3},{3,2},{4,5},{5,4},{6,7},{7,6},{8,9},{9,8},{10,11... | collective-permute-start | bytes 1572872 | tf_op jit(solution)/shard_map/ppermute | solution.py:24
  166.0 1.6 copy-start.3
Sparse Core Ops, SparseCore 0:
  9.7 77.9 all-gather.2

commit v11 on v10

--- a/solution.py
+++ b/solution.py
@@ -125,47 +125,37 @@
                 out[x, i] = piece
 
 
-def last_kernel(grad_m, grad_o, acts, *refs):
-    joined, (out, turned, held, sems) = refs[:-4], refs[-4:]
-    core = lax.axis_index("core")
-    half, wide, step = grad_m.shape[1], acts.shape[2], held.shape[3]
-    copies = [
-        pltpu.make_async_copy(acts.at[:, :, pl.ds(i * step, step)], held.at[i], sems.at[i])
-        for i in range(wide // step)
-    ]
-    for copy in copies:
-        copy.start()
+def last_kernel(cuts, joined, grad_m, grad_o, *refs):
+    parts, more, (out, turned) = refs[: len(cuts)], refs[len(cuts) : -2], refs[-2:]
+    core, x = lax.axis_index("core"), lax.axis_index("x")
+    half = grad_m.shape[1]
+    wide = max(start + ref.shape[1] for ref, (_, start) in zip(parts, cuts))
     for k in range(4):
-        turned[k, :, pl.ds(pl.multiple_of(core * half, half), half)] = grad_m[k].T
-        turned[k, :, pl.ds(pl.multiple_of((1 - core) * half, half), half)] = grad_o[k].T
-    for ref in joined:
+        row = lax.rem(x + 4 - k, 4)
+        turned[k, :, pl.ds(pl.multiple_of(core * half, half), half)] = grad_m[row].T
+        turned[k, :, pl.ds(pl.multiple_of((1 - core) * half, half), half)] = grad_o[row].T
+    for ref in more:
         out[:, wide:] = ref[...]
-    for i, copy in enumerate(copies):
-        copy.wait()
-        acc = dot(turned[0], held[i, 0])
-        for k in range(1, 4):
-            acc = acc + dot(turned[k], held[i, k])
-        out[:, i * step : (i + 1) * step] = acc.astype(out.dtype)
-
-
-def last_call(grad_m, grad_o, row, dtype, *joined):
-    _, tokens, wide = row.shape
-    width, step = grad_m.shape[2], 256
-    return pl.pallas_call(
-        last_kernel,
-        out_shape=like((width, wide + sum(j.shape[1] for j in joined)), dtype),
-        in_specs=[VMEM, VMEM, ANY] + [VMEM] * len(joined),
-        out_specs=VMEM,
-        scratch_shapes=[
-            pltpu.VMEM((4, width, tokens), BF),
-            pltpu.VMEM((wide // step, 4, tokens, step), BF),
-            pltpu.SemaphoreType.DMA((wide // step,)),
-        ],
-        compiler_params=pltpu.CompilerParams(vmem_limit_bytes=48 * 1024 * 1024),
-        cost_estimate=pl.CostEstimate(
-            flops=8 * tokens * width * wide, bytes_accessed=8 * tokens * wide, transcendentals=0
-        ),
-    )(grad_m, grad_o, row, *joined)
+    edges = sorted({start for _, start in cuts} | {wide})
+    for low, high in zip(edges, edges[1:]):
+        acc = None
+        for ref, (k, start) in zip(parts, cuts):
+            if start <= low and high <= start + ref.shape[1]:
+                term = dot(turned[k], ref[:, low - start : high - start])
+                acc = term if acc is None else acc + term
+        out[:, low:high] = acc.astype(out.dtype)
+
+
+def last_call(grad_m, grad_o, cuts, parts, dtype, *joined):
+    tokens, wide = parts[0].shape
+    width = grad_m.shape[2]
+    return call(
+        functools.partial(last_kernel, cuts, bool(joined)),
+        [like((width, wide + sum(j.shape[1] for j in joined)), dtype)],
+        grad_m, grad_o, *parts, *joined,
+        scratch=[pltpu.VMEM((4, width, tokens), BF)],
+        flops=8 * tokens * width * wide if joined else 0,
+    )
 
 
 def term_kernel(codes, own, message, keep, s1, s2, s3):
@@ -202,7 +192,10 @@
     def part_of(array, which, size, axis):
         return lax.dynamic_slice_in_dim(array, which * size, size, axis)
 
-    row = lax.all_gather(acts, "x")
+    barrier = lax.optimization_barrier
+    c1, c2, c3 = 1152, 384, 896
+    plus_a = shift(acts[:, :c1], "x", 4, 1)
+    minus_a = shift(acts[:, wide - c1 :], "x", 4, 3)
     pair_a = swap(proj_a, "core")
     target_t = target.T
     near_t = part_of(target_t, core, half, 1)
@@ -211,6 +204,10 @@
     arrived = swap(codes_call(True, acts, proj_b), "core")
     mine = (codes_call(False, acts, proj_b) + arrived).astype(BF).reshape(8, width, half)
     blocks = lax.all_to_all(mine, ZY, 0, 0)
+    blocks, plus_a, minus_a, later = barrier((blocks, plus_a, minus_a, acts))
+    plus_b = shift(later[:, c1:], "x", 4, 1)
+    minus_b = shift(later[:, : wide - c1], "x", 4, 3)
+    far_a = shift(plus_a[:, :c2], "x", 4, 1), shift(minus_a[:, c1 - c2 :], "x", 4, 3)
     codes = call(sum_and_copy, [like((8, width, half))], blocks)
     codes = lax.all_to_all(codes, ZY, 0, 0).reshape(rank, half)
 
@@ -221,6 +218,11 @@
         scratch=[pltpu.VMEM((half, 2 * outs), BF)],
         flops=8 * half * rank * outs,
     )
+    partial, plus_a, minus_a, plus_b, minus_b, far_a = barrier((partial, plus_a, minus_a, plus_b, minus_b, far_a))
+    far_b = (
+        shift(plus_a[:, c2:c3], "x", 4, 1),
+        shift(minus_a[:, c1 - c3 : c1 - c2], "x", 4, 3),
+    )
     blocks = lax.all_to_all(partial, ZY, 0, 0)
 
     piece = like((2, width, outs))
@@ -232,7 +234,6 @@
     )
     terms = [terms[0]] + [shift(terms[k], "x", 4, k) for k in (1, 2, 3)]
 
-    blocks, row = lax.optimization_barrier((blocks, row))
     spread = like((4, 8, sub, width))
     split_a, split_o = call(spread_kernel, [spread, spread], blocks, scratch=[pltpu.VMEM((sub, rank), BF)])
 
@@ -241,14 +242,16 @@
         return split.reshape(4, half, width)
 
     grad = gather(split_a)
-    grad, *terms = lax.optimization_barrier((grad, *terms))
+    grad, far_b, *terms = barrier((grad, far_b, *terms))
     term_o, term_a = call(term_sum_kernel, [like((width, outs), F32), like((width, outs))], *terms)
-    away = last_call(grad, swap(grad, "core"), row, BF, term_a)
-    away, split_o = lax.optimization_barrier((away, split_o))
+    parts = [acts, plus_a, plus_b, far_a[0], far_b[0], far_b[1], far_a[1], minus_b, minus_a]
+    cuts = ((0, 0), (1, 0), (1, c1), (2, 0), (2, c2), (2, c3), (2, wide - c2), (3, 0), (3, wide - c1))
+    away = last_call(grad, swap(grad, "core"), cuts, parts, BF, term_a)
+    away, split_o = barrier((away, split_o))
     away = swap(away, "y_lo").astype(F32)
     grad = gather(split_o)
-    here = last_call(grad, swap(grad, "core"), row, F32)
-    here, term_o = lax.optimization_barrier((here, term_o))
+    here = last_call(grad, swap(grad, "core"), cuts, parts, F32)
+    here, term_o = barrier((here, term_o))
     return (((term_o + away[:, wide:]) * scale).T, (here + away[:, :wide]) * scale)
 
 

time: 176 us -> 197 us (1.12)
  starting transfers between devices: 31.6 us -> 49.7 us
  local copies, waits for them, and re-layouts: 6.74 us -> 22.3 us
  between operations: 14.2 us -> 0.88 us
  blocking collectives: 23.9 us -> 32.5 us
  waiting for transfers between devices: 66.4 us -> 61.3 us
  Pallas kernels: 30.6 us -> 27.1 us
    pallas_call x2 -> x0, Pallas kernels: 11.8 us -> none  [last_call(): pl.pallas_call(last_kernel, out_shape=like((width, wide + sum((j.shape[1]...]
    ppermute x10 -> x18, starting transfers between devices: 14.4 us -> 25.4 us  [shift(): lax.ppermute(array, axis, [(i, (i + step) % size) for i in range(size)])]
    all_to_all x1, blocking collectives: 23.9 us -> 32.5 us  [gather(): lax.all_to_all(split.reshape(32, sub, width), ('x', 'z', 'y_hi'), 0, 0)]
    pallas_call x5 -> x7, Pallas kernels: 13.1 us -> 21.3 us  [call(): pl.pallas_call(body, out_shape=outs if len(outs) > 1 else outs[0], in_spe...]
    all_to_all x0 -> x1, starting transfers between devices: none -> 7.75 us  [local(): blocks = lax.all_to_all(mine, ZY, 0, 0)]
    unnamed x15 -> x39, local copies, waits for them, and re-layouts: 6.7 us -> 13.8 us
    all_to_all x1, waiting for transfers between devices: 9.14 us -> 2.38 us  [local(): blocks = lax.all_to_all(partial, ZY, 0, 0)]
    slice x0 -> x6, local copies, waits for them, and re-layouts: none -> 6.71 us  [the longest x1 1.98 us: local(): minus_a[:, c1 - c3:c1 - c2]]
  transfers between devices with their start and end apart: 15 -> 22, of which waited for: 9 -> 7; matrix products, arithmetic and copies ran while one was open for 0% -> 6% of each run, Pallas kernels for 14% -> 10%
where the time goes in v11:
time: 197 us
  waiting for transfers between devices  61.3 us (31%)
  starting transfers between devices  49.7 us (25%)
  blocking collectives  32.5 us (16%)
  Pallas kernels  27.1 us (14%)
  local copies, waits for them, and re-layouts  22.3 us (11%)
  other arithmetic  2.83 us (1%)
    all_to_all x1, blocking collectives, gather(): lax.all_to_all(split.reshape(32, sub, width), ('x', 'z', 'y_hi'), 0, 0)  32.5 us
    ppermute x18, starting transfers between devices, shift(): lax.ppermute(array, axis, [(i, (i + step) % size) for i in range(size)])  25.4 us
    all_to_all x1, waiting for transfers between devices, gather(): lax.all_to_all(split.reshape(32, sub, width), ('x', 'z', 'y_hi'), 0, 0)  24.8 us
    ppermute x18, waiting for transfers between devices, shift(): lax.ppermute(array, axis, [(i, (i + step) % size) for i in range(size)])  23.6 us
    pallas_call x7, Pallas kernels, call(): pl.pallas_call(body, out_shape=outs if len(outs) > 1 else outs[0], in_spe...  21.3 us
    unnamed x39, local copies, waits for them, and re-layouts  13.8 us
    all_to_all x1, starting transfers between devices, local(): blocks = lax.all_to_all(mine, ZY, 0, 0)  7.75 us
    all_to_all x1, waiting for transfers between devices, local(): codes = lax.all_to_all(codes, ZY, 0, 0).reshape(rank, half)  7.33 us
  transfers between devices with their start and end apart: 22, of which 7 were waited for; matrix products, arithmetic and copies ran while one was open for 6% of the time, Pallas kernels for 10%

profile of v11, /device:TPU:1, one launch (start us, length us, event | category | flops | bytes accessed | tf_op | source)
XLA Modules:
  0.0 196.6 jit_solution(12396345113591415380)
XLA Ops:
  2.1 3.1 %copy-done.2 = bf16[2048,1792]{1,0:T(8,128)(2,1)S(1)} copy-done((bf16[2048,1792]{1,0:T(8,128)(2,1)S(1)}, bf16[2048,1792]{1,0:T(8,128)(2,1)}, u32[]{:S(2)}) %copy-start.2) | copy-done | bytes 7340056
  5.2 2.9 %shard_map.60 = f32[2048,256]{1,0:T(8,128)S(1)} custom-call(bf16[512,1792]{1,0:T(8,128)(2,1)S(1)} %copy-done, bf16[2048,1792]{1,0:T(8,128)(2,1)S(1)} %copy-done.2), custom_call_target="tpu_custom_call" | custom-call | flops 1879048192 | bytes 7340032 | tf_op jit(solution)/shard_map/pallas_call | solution.py:69
  14.5 2.9 %shard_map.59 = f32[2048,256]{1,0:T(8,128)S(1)} custom-call(bf16[512,1792]{1,0:T(8,128)(2,1)S(1)} %copy-done, bf16[2048,1792]{1,0:T(8,128)(2,1)S(1)} %copy-done.2), custom_call_target="tpu_custom_call" | custom-call | flops 1879048192 | bytes 7340032 | tf_op jit(solution)/shard_map/pallas_call | solution.py:69
  18.6 7.7 %all-to-all-start = ((bf16[8,256,256]{2,1,0:T(8,128)(2,1)}), bf16[8,256,256]{2,1,0:T(8,128)(2,1)S(1)}, u32[]{:S(2)}, u32[]{:S(2)}) async-start(bf16[8,256,256]{2,1,0:T(8,128)(2,1)} %bitcast.15), calls=%async_computation | async-start | bytes 2097152 | tf_op jit(solution)/shard_map/all_to_all | solution.py:206
  26.4 13.9 %collective-permute-done.1.refs_1_ = bf16[512,1152]{1,0:T(8,128)(2,1)S(1)} collective-permute-done((bf16[512,1152]{1,0:T(8,128)(2,1)}, bf16[512,1152]{1,0:T(8,128)(2,1)S(1)}, u32[]{:S(2)}, u32[]{:S(2)}) %collective-permute-start.1) | collective-permute-done | bytes 1179680 | tf_op jit(solution)/shard_map/ppermute | solution.py:24
  40.3 3.2 %all-to-all-done.blocks = bf16[8,256,256]{2,1,0:T(8,128)(2,1)S(1)} async-done(((bf16[8,256,256]{2,1,0:T(8,128)(2,1)}), bf16[8,256,256]{2,1,0:T(8,128)(2,1)S(1)}, u32[]{:S(2)}, u32[]{:S(2)}) %all-to-all-start) | async-done | bytes 1048608 | tf_op jit(solution)/shard_map/all_to_all | solution.py:206
  44.6 5.8 %all-to-all-start.1 = ((bf16[8,256,256]{2,1,0:T(8,128)(2,1)}), bf16[8,256,256]{2,1,0:T(8,128)(2,1)}, u32[]{:S(2)}, u32[]{:S(2)}) async-start(bf16[8,256,256]{2,1,0:T(8,128)(2,1)} %copy-done.5), calls=%async_computation.1 | async-start | bytes 2097152 | tf_op jit(solution)/shard_map/all_to_all | solution.py:212
  59.0 7.3 %all-to-all-done.1 = bf16[8,256,256]{2,1,0:T(8,128)(2,1)} async-done(((bf16[8,256,256]{2,1,0:T(8,128)(2,1)}), bf16[8,256,256]{2,1,0:T(8,128)(2,1)}, u32[]{:S(2)}, u32[]{:S(2)}) %all-to-all-start.1) | async-done | bytes 1048608 | tf_op jit(solution)/shard_map/all_to_all | solution.py:212
  66.3 6.1 %shard_map.62 = (bf16[256,512]{1,0:T(8,128)(2,1)S(1)}, bf16[2560,256]{1,0:T(8,128)(2,1)}, bf16[8,32,2048]{2,1,0:T(8,128)(2,1)S(1)}) custom-call(bf16[2048,256]{1,0:T(8,128)(2,1)} %bitcast.1.codes, bf16[512,256]{1,0:T(8,128)(2,1)S(1)} %bitcast.14, bf16[512,256]{1,0:T(8,128)(2,1)S(1)} %collective-permute-done.3.far, bf16[512,2048]{1,0:T(8,128)(2,1)} %a0.1, ...), custom_call_target="tpu_custom_call" | custom-call | flops 2147483648 | bytes 8388608 | tf_op jit(solution)/shard_map/pallas_call | solution.py:33
  72.4 2.3 %collective-permute-start.11 = (bf16[2560,256]{1,0:T(8,128)(2,1)}, bf16[2560,256]{1,0:T(8,128)(2,1)}, u32[]{:S(2)}, u32[]{:S(2)}) collective-permute-start(bf16[2560,256]{1,0:T(8,128)(2,1)} %get-tuple-element.45), channel_id=1, source_target_pairs={{0,1},{1,0},{2,3},{3,2},{4,5},{5,4},{6,7},{7,6},{8,9},{9,8},{10,11... | collective-permute-start | bytes 3932168 | tf_op jit(solution)/shard_map/ppermute | solution.py:24
  76.8 1.9 collective-permute-start.8
  78.6 8.2 %collective-permute-done.7.refs_3_ = bf16[512,384]{1,0:T(8,128)(2,1)S(1)} collective-permute-done((bf16[512,384]{1,0:T(8,128)(2,1)S(1)}, bf16[512,384]{1,0:T(8,128)(2,1)S(1)}, u32[]{:S(2)}, u32[]{:S(2)}) %collective-permute-start.7) | collective-permute-done | bytes 393248 | tf_op jit(solution)/shard_map/ppermute | solution.py:24
  88.3 4.3 %all-to-all-start.2 = ((bf16[8,32,2048]{2,1,0:T(8,128)(2,1)}), bf16[8,32,2048]{2,1,0:T(8,128)(2,1)}, u32[]{:S(2)}, u32[]{:S(2)}) async-start(bf16[8,32,2048]{2,1,0:T(8,128)(2,1)} %copy-done.10), calls=%async_computation.2 | async-start | bytes 2097152 | tf_op jit(solution)/shard_map/all_to_all | solution.py:226
  92.6 2.0 %slice.37 = bf16[512,512]{1,0:T(8,128)(2,1)} slice(bf16[512,1152]{1,0:T(8,128)(2,1)} %copy-done.3), slice={[0:512], [256:768]} | slice | bytes 1048576 | tf_op jit(solution)/shard_map/slice | solution.py:224
  94.6 2.7 %collective-permute-start.10 = (bf16[512,512]{1,0:T(8,128)(2,1)}, bf16[512,512]{1,0:T(8,128)(2,1)S(1)}, u32[]{:S(2)}, u32[]{:S(2)}) collective-permute-start(bf16[512,512]{1,0:T(8,128)(2,1)} %slice.37), channel_id=1, source_target_pairs={{0,48},{16,0},{32,16},{48,32},{1,49},{17,1},{33,17},{49,33},{2,50}... | collective-permute-start | bytes 1572872 | tf_op jit(solution)/shard_map/ppermute | solution.py:24
  98.1 3.7 %shard_map.64 = (f32[2,256,512]{2,1,0:T(8,128)S(1)}, bf16[2,256,512]{2,1,0:T(8,128)(2,1)}, bf16[2,256,512]{2,1,0:T(8,128)(2,1)}, bf16[2,256,512]{2,1,0:T(8,128)(2,1)}) custom-call(bf16[2048,256]{1,0:T(8,128)(2,1)} %bitcast.1.codes, bf16[256,512]{1,0:T(8,128)(2,1)S(1)} %copy-done.17, bf16[2560,256]{1,0:T(8,128)(2,1)} %collective-permute-done.11.message), custom_call_target="tpu_custom_call" | custom-call | flops 1073741824 | bytes 5242880 | tf_op jit(solution)/shard_map/pallas_call | solution.py:33
  102.8 3.8 %collective-permute-start.13 = (bf16[2,256,512]{2,1,0:T(8,128)(2,1)}, bf16[2,256,512]{2,1,0:T(8,128)(2,1)}, u32[]{:S(2)}, u32[]{:S(2)}) collective-permute-start(bf16[2,256,512]{2,1,0:T(8,128)(2,1)} %get-tuple-element.48), channel_id=1, source_target_pairs={{0,32},{16,48},{32,0},{48,16},{1,33},{17,49},{33,1},{49,17},{2,34}... | collective-permute-start | bytes 1572872 | tf_op jit(solution)/shard_map/ppermute | solution.py:24
  106.7 2.4 %all-to-all-done.2.blocks = bf16[8,32,2048]{2,1,0:T(8,128)(2,1)} async-done(((bf16[8,32,2048]{2,1,0:T(8,128)(2,1)}), bf16[8,32,2048]{2,1,0:T(8,128)(2,1)}, u32[]{:S(2)}, u32[]{:S(2)}) %all-to-all-start.2) | async-done | bytes 1048608 | tf_op jit(solution)/shard_map/all_to_all | solution.py:226
  112.2 6.5 %all-to-all-start.3 = ((bf16[32,32,256]{2,1,0:T(8,128)(2,1)}), bf16[32,32,256]{2,1,0:T(8,128)(2,1)}, u32[]{:S(2)}, u32[]{:S(2)}) async-start(bf16[32,32,256]{2,1,0:T(8,128)(2,1)} %bitcast.13), calls=%async_computation.3 | async-start | bytes 1048576 | tf_op jit(solution)/shard_map/all_to_all | solution.py:241
  118.7 24.8 %all-to-all-done.3 = bf16[32,32,256]{2,1,0:T(8,128)(2,1)} async-done(((bf16[32,32,256]{2,1,0:T(8,128)(2,1)}), bf16[32,32,256]{2,1,0:T(8,128)(2,1)}, u32[]{:S(2)}, u32[]{:S(2)}) %all-to-all-start.3) | async-done | bytes 524320 | tf_op jit(solution)/shard_map/all_to_all | solution.py:241
  143.5 3.6 %collective-permute-start.15 = (bf16[4,256,256]{2,1,0:T(8,128)(2,1)}, bf16[4,256,256]{2,1,0:T(8,128)(2,1)S(1)}, u32[]{:S(2)}, u32[]{:S(2)}) collective-permute-start(bf16[4,256,256]{2,1,0:T(8,128)(2,1)} %bitcast.5.grad_m), channel_id=1, source_target_pairs={{0,1},{1,0},{2,3},{3,2},{4,5},{5,4},{6,7},{7,6},{8,9},{9,8},{10,11... | collective-permute-start | bytes 1572872 | tf_op jit(solution)/shard_map/ppermute | solution.py:24
  150.0 4.2 %shard_map.66 = bf16[256,2304]{1,0:T(8,128)(2,1)S(1)} custom-call(bf16[4,256,256]{2,1,0:T(8,128)(2,1)} %bitcast.5.grad_m, bf16[4,256,256]{2,1,0:T(8,128)(2,1)S(1)} %collective-permute-done.15.grad_o, bf16[512,1792]{1,0:T(8,128)(2,1)S(1)} %copy-done.1, bf16[512,1152]{1,0:T(8,128)(2,1)S(1)} %collective-permute-done.1.refs_1_, ...), custom_call_target="tpu_custom_call" | custom-call | flops 1879048192 | bytes 9830400 | tf_op jit(solution)/shard_map/pallas_call | solution.py:33
  154.7 32.5 %all_to_all.25 = bf16[32,32,256]{2,1,0:T(8,128)(2,1)S(1)} all-to-all(bf16[32,32,256]{2,1,0:T(8,128)(2,1)S(1)} %bitcast.12), channel_id=1, replica_groups=mesh['y_lo'=2,'x'=4,'z'=4,'y_hi'=2,'core'=2] {'x','z','y_hi'}, dimensions={0} | all-to-all | bytes 1048576 | tf_op jit(solution)/shard_map/all_to_all | solution.py:241
  189.9 4.0 %shard_map.67 = f32[256,1792]{1,0:T(8,128)S(1)} custom-call(bf16[4,256,256]{2,1,0:T(8,128)(2,1)S(1)} %bitcast.11, bf16[4,256,256]{2,1,0:T(8,128)(2,1)S(1)} %collective-permute-done.16.grad_o, bf16[512,1792]{1,0:T(8,128)(2,1)S(1)} %copy-done.1, bf16[512,1152]{1,0:T(8,128)(2,1)S(1)} %collective-permute-done.1.refs_1_, ...), custom_call_target="tpu_custom_call" | custom-call | bytes 10223616 | tf_op jit(solution)/shard_map/pallas_call | solution.py:33
  (80 shorter events, 35.9 us)
Async XLA Ops:
  8.1 9.3 %collective-permute-start = (f32[2048,256]{1,0:T(8,128)S(1)}, f32[2048,256]{1,0:T(8,128)S(1)}, u32[]{:S(2)}, u32[]{:S(2)}) collective-permute-start(f32[2048,256]{1,0:T(8,128)S(1)} %shard_map.60), channel_id=1, source_target_pairs={{0,1},{1,0},{2,3},{3,2},{4,5},{5,4},{6,7},{7,6},{8,9},{9,8},{10,11... | collective-permute-start | bytes 6291464 | tf_op jit(solution)/shard_map/ppermute | solution.py:24
  11.3 29.0 %collective-permute-start.1 = (bf16[512,1152]{1,0:T(8,128)(2,1)}, bf16[512,1152]{1,0:T(8,128)(2,1)S(1)}, u32[]{:S(2)}, u32[]{:S(2)}) collective-permute-start(bf16[512,1152]{1,0:T(8,128)(2,1)} %get-tuple-element.73), channel_id=1, source_target_pairs={{0,16},{16,32},{32,48},{48,0},{1,17},{17,33},{33,49},{49,1},{2,18}... | collective-permute-start | bytes 3538952 | tf_op jit(solution)/shard_map/ppermute | solution.py:24
  12.6 27.7 %collective-permute-start.2 = (bf16[512,1152]{1,0:T(8,128)(2,1)}, bf16[512,1152]{1,0:T(8,128)(2,1)S(1)}, u32[]{:S(2)}, u32[]{:S(2)}) collective-permute-start(bf16[512,1152]{1,0:T(8,128)(2,1)} %get-tuple-element.72), channel_id=1, source_target_pairs={{0,48},{16,0},{32,16},{48,32},{1,49},{17,1},{33,17},{49,33},{2,50}... | collective-permute-start | bytes 3538952 | tf_op jit(solution)/shard_map/ppermute | solution.py:24
  13.9 45.0 %collective-permute-start.4 = (bf16[512,2048]{1,0:T(8,128)(2,1)}, bf16[512,2048]{1,0:T(8,128)(2,1)}, u32[]{:S(2)}, u32[]{:S(2)}) collective-permute-start(bf16[512,2048]{1,0:T(8,128)(2,1)} %a0.1), channel_id=1, source_target_pairs={{0,1},{1,0},{2,3},{3,2},{4,5},{5,4},{6,7},{7,6},{8,9},{9,8},{10,11... | collective-permute-start | bytes 6291464 | tf_op jit(solution)/shard_map/ppermute | solution.py:24
  18.6 24.8 %all-to-all-start = ((bf16[8,256,256]{2,1,0:T(8,128)(2,1)}), bf16[8,256,256]{2,1,0:T(8,128)(2,1)S(1)}, u32[]{:S(2)}, u32[]{:S(2)}) async-start(bf16[8,256,256]{2,1,0:T(8,128)(2,1)} %bitcast.15), calls=%async_computation | async-start | bytes 2097152 | tf_op jit(solution)/shard_map/all_to_all | solution.py:206
  44.6 21.8 %all-to-all-start.1 = ((bf16[8,256,256]{2,1,0:T(8,128)(2,1)}), bf16[8,256,256]{2,1,0:T(8,128)(2,1)}, u32[]{:S(2)}, u32[]{:S(2)}) async-start(bf16[8,256,256]{2,1,0:T(8,128)(2,1)} %copy-done.5), calls=%async_computation.1 | async-start | bytes 2097152 | tf_op jit(solution)/shard_map/all_to_all | solution.py:212
  52.9 6.0 %collective-permute-start.3 = (bf16[512,256]{1,0:T(8,128)(2,1)}, bf16[512,256]{1,0:T(8,128)(2,1)S(1)}, u32[]{:S(2)}, u32[]{:S(2)}) collective-permute-start(bf16[512,256]{1,0:T(8,128)(2,1)} %bitcast.16), channel_id=1, source_target_pairs={{0,1},{1,0},{2,3},{3,2},{4,5},{5,4},{6,7},{7,6},{8,9},{9,8},{10,11... | collective-permute-start | bytes 786440 | tf_op jit(solution)/shard_map/ppermute | solution.py:24
  56.3 32.0 %collective-permute-start.5 = (bf16[512,640]{1,0:T(8,128)(2,1)}, bf16[512,640]{1,0:T(8,128)(2,1)}, u32[]{:S(2)}, u32[]{:S(2)}) collective-permute-start(bf16[512,640]{1,0:T(8,128)(2,1)} %get-tuple-element.71), channel_id=1, source_target_pairs={{0,16},{16,32},{32,48},{48,0},{1,17},{17,33},{33,49},{49,1},{2,18}... | collective-permute-start | bytes 1966088 | tf_op jit(solution)/shard_map/ppermute | solution.py:24
  57.5 30.8 %collective-permute-start.6 = (bf16[512,640]{1,0:T(8,128)(2,1)}, bf16[512,640]{1,0:T(8,128)(2,1)}, u32[]{:S(2)}, u32[]{:S(2)}) collective-permute-start(bf16[512,640]{1,0:T(8,128)(2,1)} %get-tuple-element.70), channel_id=1, source_target_pairs={{0,48},{16,0},{32,16},{48,32},{1,49},{17,1},{33,17},{49,33},{2,50}... | collective-permute-start | bytes 1966088 | tf_op jit(solution)/shard_map/ppermute | solution.py:24
  72.4 15.1 %copy-start.16 = (bf16[256,512]{1,0:T(8,128)(2,1)}, bf16[256,512]{1,0:T(8,128)(2,1)S(1)}, u32[]{:S(2)}) copy-start(bf16[256,512]{1,0:T(8,128)(2,1)S(1)} %get-tuple-element.44.own) | copy-start | bytes 786436
  72.4 15.9 %copy-start.10 = (bf16[8,32,2048]{2,1,0:T(8,128)(2,1)}, bf16[8,32,2048]{2,1,0:T(8,128)(2,1)S(1)}, u32[]{:S(2)}) copy-start(bf16[8,32,2048]{2,1,0:T(8,128)(2,1)S(1)} %get-tuple-element.40) | copy-start | bytes 3145732
  72.4 25.7 %collective-permute-start.11 = (bf16[2560,256]{1,0:T(8,128)(2,1)}, bf16[2560,256]{1,0:T(8,128)(2,1)}, u32[]{:S(2)}, u32[]{:S(2)}) collective-permute-start(bf16[2560,256]{1,0:T(8,128)(2,1)} %get-tuple-element.45), channel_id=1, source_target_pairs={{0,1},{1,0},{2,3},{3,2},{4,5},{5,4},{6,7},{7,6},{8,9},{9,8},{10,11... | collective-permute-start | bytes 3932168 | tf_op jit(solution)/shard_map/ppermute | solution.py:24
  74.8 12.0 %collective-permute-start.7 = (bf16[512,384]{1,0:T(8,128)(2,1)S(1)}, bf16[512,384]{1,0:T(8,128)(2,1)S(1)}, u32[]{:S(2)}, u32[]{:S(2)}) collective-permute-start(bf16[512,384]{1,0:T(8,128)(2,1)S(1)} %slice.34), channel_id=1, source_target_pairs={{0,16},{16,32},{32,48},{48,0},{1,17},{17,33},{33,49},{49,1},{2,18}... | collective-permute-start | bytes 1179656 | tf_op jit(solution)/shard_map/ppermute | solution.py:24
  76.8 10.8 %collective-permute-start.8 = (bf16[512,384]{1,0:T(8,128)(2,1)S(1)}, bf16[512,384]{1,0:T(8,128)(2,1)S(1)}, u32[]{:S(2)}, u32[]{:S(2)}) collective-permute-start(bf16[512,384]{1,0:T(8,128)(2,1)S(1)} %slice.35), channel_id=1, source_target_pairs={{0,48},{16,0},{32,16},{48,32},{1,49},{17,1},{33,17},{49,33},{2,50}... | collective-permute-start | bytes 1179656 | tf_op jit(solution)/shard_map/ppermute | solution.py:24
  88.3 20.7 %all-to-all-start.2 = ((bf16[8,32,2048]{2,1,0:T(8,128)(2,1)}), bf16[8,32,2048]{2,1,0:T(8,128)(2,1)}, u32[]{:S(2)}, u32[]{:S(2)}) async-start(bf16[8,32,2048]{2,1,0:T(8,128)(2,1)} %copy-done.10), calls=%async_computation.2 | async-start | bytes 2097152 | tf_op jit(solution)/shard_map/all_to_all | solution.py:226
  94.6 24.1 %collective-permute-start.10 = (bf16[512,512]{1,0:T(8,128)(2,1)}, bf16[512,512]{1,0:T(8,128)(2,1)S(1)}, u32[]{:S(2)}, u32[]{:S(2)}) collective-permute-start(bf16[512,512]{1,0:T(8,128)(2,1)} %slice.37), channel_id=1, source_target_pairs={{0,48},{16,0},{32,16},{48,32},{1,49},{17,1},{33,17},{49,33},{2,50}... | collective-permute-start | bytes 1572872 | tf_op jit(solution)/shard_map/ppermute | solution.py:24
  98.1 20.6 %collective-permute-start.9 = (bf16[512,512]{1,0:T(8,128)(2,1)}, bf16[512,512]{1,0:T(8,128)(2,1)}, u32[]{:S(2)}, u32[]{:S(2)}) collective-permute-start(bf16[512,512]{1,0:T(8,128)(2,1)} %slice.36), channel_id=1, source_target_pairs={{0,16},{16,32},{32,48},{48,0},{1,17},{17,33},{33,49},{49,1},{2,18}... | collective-permute-start | bytes 1572872 | tf_op jit(solution)/shard_map/ppermute | solution.py:24
  102.8 40.7 %collective-permute-start.12 = (bf16[2,256,512]{2,1,0:T(8,128)(2,1)}, bf16[2,256,512]{2,1,0:T(8,128)(2,1)}, u32[]{:S(2)}, u32[]{:S(2)}) collective-permute-start(bf16[2,256,512]{2,1,0:T(8,128)(2,1)} %get-tuple-element.47), channel_id=1, source_target_pairs={{0,16},{16,32},{32,48},{48,0},{1,17},{17,33},{33,49},{49,1},{2,18}... | collective-permute-start | bytes 1572872 | tf_op jit(solution)/shard_map/ppermute | solution.py:24
  102.8 40.7 %collective-permute-start.13 = (bf16[2,256,512]{2,1,0:T(8,128)(2,1)}, bf16[2,256,512]{2,1,0:T(8,128)(2,1)}, u32[]{:S(2)}, u32[]{:S(2)}) collective-permute-start(bf16[2,256,512]{2,1,0:T(8,128)(2,1)} %get-tuple-element.48), channel_id=1, source_target_pairs={{0,32},{16,48},{32,0},{48,16},{1,33},{17,49},{33,1},{49,17},{2,34}... | collective-permute-start | bytes 1572872 | tf_op jit(solution)/shard_map/ppermute | solution.py:24
  106.6 36.9 %collective-permute-start.14 = (bf16[2,256,512]{2,1,0:T(8,128)(2,1)}, bf16[2,256,512]{2,1,0:T(8,128)(2,1)}, u32[]{:S(2)}, u32[]{:S(2)}) collective-permute-start(bf16[2,256,512]{2,1,0:T(8,128)(2,1)} %get-tuple-element.49), channel_id=1, source_target_pairs={{0,48},{16,0},{32,16},{48,32},{1,49},{17,1},{33,17},{49,33},{2,50}... | collective-permute-start | bytes 1572872 | tf_op jit(solution)/shard_map/ppermute | solution.py:24
  112.2 31.3 %all-to-all-start.3 = ((bf16[32,32,256]{2,1,0:T(8,128)(2,1)}), bf16[32,32,256]{2,1,0:T(8,128)(2,1)}, u32[]{:S(2)}, u32[]{:S(2)}) async-start(bf16[32,32,256]{2,1,0:T(8,128)(2,1)} %bitcast.13), calls=%async_computation.3 | async-start | bytes 1048576 | tf_op jit(solution)/shard_map/all_to_all | solution.py:241
  143.5 6.4 %collective-permute-start.15 = (bf16[4,256,256]{2,1,0:T(8,128)(2,1)}, bf16[4,256,256]{2,1,0:T(8,128)(2,1)S(1)}, u32[]{:S(2)}, u32[]{:S(2)}) collective-permute-start(bf16[4,256,256]{2,1,0:T(8,128)(2,1)} %bitcast.5.grad_m), channel_id=1, source_target_pairs={{0,1},{1,0},{2,3},{3,2},{4,5},{5,4},{6,7},{7,6},{8,9},{9,8},{10,11... | collective-permute-start | bytes 1572872 | tf_op jit(solution)/shard_map/ppermute | solution.py:24
  154.3 39.7 %collective-permute-start.17 = (bf16[256,2304]{1,0:T(8,128)(2,1)S(1)}, bf16[256,2304]{1,0:T(8,128)(2,1)S(1)}, u32[]{:S(2)}, u32[]{:S(2)}) collective-permute-start(bf16[256,2304]{1,0:T(8,128)(2,1)S(1)} %shard_map.66), channel_id=1, source_target_pairs={{0,64},{64,0},{1,65},{65,1},{2,66},{66,2},{3,67},{67,3},{4,68},{68... | collective-permute-start | bytes 3538952 | tf_op jit(solution)/shard_map/ppermute | solution.py:24
  187.3 2.7 %collective-permute-start.16 = (bf16[4,256,256]{2,1,0:T(8,128)(2,1)S(1)}, bf16[4,256,256]{2,1,0:T(8,128)(2,1)S(1)}, u32[]{:S(2)}, u32[]{:S(2)}) collective-permute-start(bf16[4,256,256]{2,1,0:T(8,128)(2,1)S(1)} %bitcast.10), channel_id=1, source_target_pairs={{0,1},{1,0},{2,3},{3,2},{4,5},{5,4},{6,7},{7,6},{8,9},{9,8},{10,11... | collective-permute-start | bytes 1572872 | tf_op jit(solution)/shard_map/ppermute | solution.py:24
  (16 other events, 54.4 us)

commit v12 on v11

--- a/solution.py
+++ b/solution.py
@@ -112,49 +112,53 @@
             partial[i, :, cols] = term[i * sub : (i + 1) * sub].astype(BF)
 
 
-def spread_kernel(blocks, away, own, held):
+def spread_kernel(blocks, out, held):
     y_lo = lax.axis_index("y_lo")
     held[...] = total(blocks).astype(BF)
     rank = held.shape[1]
     width = rank // 8
-    for out, side in ((away, 1 - y_lo), (own, y_lo)):
+    for at, side in ((0, 1 - y_lo), (width, y_lo)):
         for x in range(4):
             start = pl.multiple_of(side * (rank // 2) + x * width, width)
             piece = held[:, pl.ds(start, width)]
             for i in range(out.shape[1]):
-                out[x, i] = piece
-
-
-def last_kernel(cuts, joined, grad_m, grad_o, *refs):
-    parts, more, (out, turned) = refs[: len(cuts)], refs[len(cuts) : -2], refs[-2:]
+                out[x, i, :, at : at + width] = piece
+
+
+def last_kernel(cuts, side, other, more, grad, *refs):
+    parts, before, (out, turned) = refs[: len(cuts)], refs[len(cuts) : -2], refs[-2:]
     core, x = lax.axis_index("core"), lax.axis_index("x")
-    half = grad_m.shape[1]
+    half, width = grad.shape[1], out.shape[0]
     wide = max(start + ref.shape[1] for ref, (_, start) in zip(parts, cuts))
+    rows = pl.ds(pl.multiple_of((1 - core if other else core) * half, half), half)
     for k in range(4):
-        row = lax.rem(x + 4 - k, 4)
-        turned[k, :, pl.ds(pl.multiple_of(core * half, half), half)] = grad_m[row].T
-        turned[k, :, pl.ds(pl.multiple_of((1 - core) * half, half), half)] = grad_o[row].T
-    for ref in more:
+        turned[k] = grad[lax.rem(x + 4 - k, 4), :, side * width : (side + 1) * width].T
+    for ref in before[1:]:
         out[:, wide:] = ref[...]
     edges = sorted({start for _, start in cuts} | {wide})
     for low, high in zip(edges, edges[1:]):
-        acc = None
+        acc = before[0][:, low:high] if other else None
         for ref, (k, start) in zip(parts, cuts):
             if start <= low and high <= start + ref.shape[1]:
-                term = dot(turned[k], ref[:, low - start : high - start])
+                term = dot(turned[k], ref[rows, low - start : high - start])
                 acc = term if acc is None else acc + term
         out[:, low:high] = acc.astype(out.dtype)
 
 
-def last_call(grad_m, grad_o, cuts, parts, dtype, *joined):
+def last_call(grad_m, grad_o, cuts, parts, side, dtype, *joined):
     tokens, wide = parts[0].shape
-    width = grad_m.shape[2]
+    half, width = tokens // 2, grad_m.shape[2] // 2
+    scratch = [pltpu.VMEM((4, width, half), BF)]
+    flops = 4 * tokens * width * wide
+    first = call(
+        functools.partial(last_kernel, cuts, side, False, 0),
+        [like((width, wide), F32)],
+        grad_m, *parts, scratch=scratch, flops=flops,
+    )
     return call(
-        functools.partial(last_kernel, cuts, bool(joined)),
+        functools.partial(last_kernel, cuts, side, True, len(joined)),
         [like((width, wide + sum(j.shape[1] for j in joined)), dtype)],
-        grad_m, grad_o, *parts, *joined,
-        scratch=[pltpu.VMEM((4, width, tokens), BF)],
-        flops=8 * tokens * width * wide if joined else 0,
+        grad_o, *parts, first, *joined, scratch=scratch, flops=flops,
     )
 
 
@@ -204,7 +208,7 @@
     arrived = swap(codes_call(True, acts, proj_b), "core")
     mine = (codes_call(False, acts, proj_b) + arrived).astype(BF).reshape(8, width, half)
     blocks = lax.all_to_all(mine, ZY, 0, 0)
-    blocks, plus_a, minus_a, later = barrier((blocks, plus_a, minus_a, acts))
+    blocks, plus_a, minus_a, later, pair_a, pair_t = barrier((blocks, plus_a, minus_a, acts, pair_a, pair_t))
     plus_b = shift(later[:, c1:], "x", 4, 1)
     minus_b = shift(later[:, : wide - c1], "x", 4, 3)
     far_a = shift(plus_a[:, :c2], "x", 4, 1), shift(minus_a[:, c1 - c2 :], "x", 4, 3)
@@ -234,23 +238,17 @@
     )
     terms = [terms[0]] + [shift(terms[k], "x", 4, k) for k in (1, 2, 3)]
 
-    spread = like((4, 8, sub, width))
-    split_a, split_o = call(spread_kernel, [spread, spread], blocks, scratch=[pltpu.VMEM((sub, rank), BF)])
-
-    def gather(split):
-        split = lax.all_to_all(split.reshape(32, sub, width), ("x", "z", "y_hi"), 0, 0)
-        return split.reshape(4, half, width)
-
-    grad = gather(split_a)
+    split = call(spread_kernel, [like((4, 8, sub, 2 * width))], blocks, scratch=[pltpu.VMEM((sub, rank), BF)])
+    grad = lax.all_to_all(split.reshape(32, sub, 2 * width), ("x", "z", "y_hi"), 0, 0)
+    grad = grad.reshape(4, half, 2 * width)
     grad, far_b, *terms = barrier((grad, far_b, *terms))
+    grad_o = swap(grad, "core")
     term_o, term_a = call(term_sum_kernel, [like((width, outs), F32), like((width, outs))], *terms)
     parts = [acts, plus_a, plus_b, far_a[0], far_b[0], far_b[1], far_a[1], minus_b, minus_a]
     cuts = ((0, 0), (1, 0), (1, c1), (2, 0), (2, c2), (2, c3), (2, wide - c2), (3, 0), (3, wide - c1))
-    away = last_call(grad, swap(grad, "core"), cuts, parts, BF, term_a)
-    away, split_o = barrier((away, split_o))
+    away = last_call(grad, grad_o, cuts, parts, 0, BF, term_a)
     away = swap(away, "y_lo").astype(F32)
-    grad = gather(split_o)
-    here = last_call(grad, swap(grad, "core"), cuts, parts, F32)
+    here = last_call(grad, grad_o, cuts, parts, 1, F32)
     here, term_o = barrier((here, term_o))
     return (((term_o + away[:, wide:]) * scale).T, (here + away[:, :wide]) * scale)
 

time: 197 us -> 197 us (level)
  blocking collectives: 32.5 us -> 19.3 us
  waiting for transfers between devices: 61.3 us -> 71.9 us
  starting transfers between devices: 49.7 us -> 43.6 us
  local copies, waits for them, and re-layouts: 22.3 us -> 27.9 us
  Pallas kernels: 27.1 us -> 29.6 us
    ppermute x18 -> x17, waiting for transfers between devices: 23.6 us -> 65.3 us  [shift(): lax.ppermute(array, axis, [(i, (i + step) % size) for i in range(size)])]
    all_to_all x2 -> x1, waiting for transfers between devices: 27.2 us -> 0.01 us  [local(): lax.all_to_all(split.reshape(32, sub, 2 * width), ('x', 'z', 'y_hi'), 0, 0)]
    all_to_all x1, blocking collectives: 32.5 us -> 19.3 us  [local(): blocks = lax.all_to_all(partial, ZY, 0, 0)]
    unnamed x39 -> x49, local copies, waits for them, and re-layouts: 13.8 us -> 20.6 us
    all_to_all x2 -> x1, starting transfers between devices: 10.8 us -> 4.66 us  [local(): lax.all_to_all(split.reshape(32, sub, 2 * width), ('x', 'z', 'y_hi'), 0, 0)]
    all_to_all x1, waiting for transfers between devices: 3.15 us -> 0.01 us  [local(): blocks = lax.all_to_all(mine, ZY, 0, 0)]
    pallas_call x7 -> x9, Pallas kernels: 21.3 us -> 23.7 us  [call(): pl.pallas_call(body, out_shape=outs if len(outs) > 1 else outs[0], in_spe...]
    ppermute x18 -> x17, starting transfers between devices: 25.4 us -> 23.5 us  [shift(): lax.ppermute(array, axis, [(i, (i + step) % size) for i in range(size)])]
  transfers between devices with their start and end apart: 22 -> 20, of which waited for: 7 -> 9; matrix products, arithmetic and copies ran while one was open for 6% -> 5% of each run, Pallas kernels for 10% -> 11%
where the time goes in v12:
time: 197 us; the launch traced here: 196 us
  waiting for transfers between devices  71.9 us (36%)
  starting transfers between devices  43.6 us (22%)
  Pallas kernels  29.6 us (15%)
  local copies, waits for them, and re-layouts  27.9 us (14%)
  blocking collectives  19.3 us (10%)
  other arithmetic  3.05 us (2%)
    ppermute x17, waiting for transfers between devices, shift(): lax.ppermute(array, axis, [(i, (i + step) % size) for i in range(size)])  65.3 us
    pallas_call x9, Pallas kernels, call(): pl.pallas_call(body, out_shape=outs if len(outs) > 1 else outs[0], in_spe...  23.7 us
    ppermute x17, starting transfers between devices, shift(): lax.ppermute(array, axis, [(i, (i + step) % size) for i in range(size)])  23.5 us
    unnamed x49, local copies, waits for them, and re-layouts  20.6 us
    all_to_all x1, blocking collectives, local(): blocks = lax.all_to_all(partial, ZY, 0, 0)  19.3 us
    all_to_all x1, starting transfers between devices, local(): blocks = lax.all_to_all(mine, ZY, 0, 0)  7.8 us
    all_to_all x1, starting transfers between devices, local(): codes = lax.all_to_all(codes, ZY, 0, 0).reshape(rank, half)  7.66 us
    all_to_all x1, waiting for transfers between devices, local(): codes = lax.all_to_all(codes, ZY, 0, 0).reshape(rank, half)  6.67 us
  transfers between devices with their start and end apart: 20, of which 9 were waited for; matrix products, arithmetic and copies ran while one was open for 5% of the time, Pallas kernels for 11%

profile of v12, /device:TPU:1, one launch (start us, length us, event | category | flops | bytes accessed | tf_op | source)
XLA Modules:
  0.0 196.2 jit_solution(10915441244027006774)
XLA Ops:
  2.1 3.1 %copy-done.2 = bf16[2048,1792]{1,0:T(8,128)(2,1)S(1)} copy-done((bf16[2048,1792]{1,0:T(8,128)(2,1)S(1)}, bf16[2048,1792]{1,0:T(8,128)(2,1)}, u32[]{:S(2)}) %copy-start.2) | copy-done | bytes 7340056
  5.2 2.9 %shard_map.60 = f32[2048,256]{1,0:T(8,128)S(1)} custom-call(bf16[512,1792]{1,0:T(8,128)(2,1)S(1)} %copy-done, bf16[2048,1792]{1,0:T(8,128)(2,1)S(1)} %copy-done.2), custom_call_target="tpu_custom_call" | custom-call | flops 1879048192 | bytes 7340032 | tf_op jit(solution)/shard_map/pallas_call | solution.py:69
  13.9 2.9 %shard_map.59 = f32[2048,256]{1,0:T(8,128)S(1)} custom-call(bf16[512,1792]{1,0:T(8,128)(2,1)S(1)} %copy-done, bf16[2048,1792]{1,0:T(8,128)(2,1)S(1)} %copy-done.2), custom_call_target="tpu_custom_call" | custom-call | flops 1879048192 | bytes 7340032 | tf_op jit(solution)/shard_map/pallas_call | solution.py:69
  18.0 7.8 %all-to-all-start = ((bf16[8,256,256]{2,1,0:T(8,128)(2,1)}), bf16[8,256,256]{2,1,0:T(8,128)(2,1)}, u32[]{:S(2)}, u32[]{:S(2)}) async-start(bf16[8,256,256]{2,1,0:T(8,128)(2,1)} %bitcast), calls=%async_computation | async-start | bytes 2097152 | tf_op jit(solution)/shard_map/all_to_all | solution.py:210
  29.7 9.4 %collective-permute-done.2.refs_8_ = bf16[512,1152]{1,0:T(8,128)(2,1)S(1)} collective-permute-done((bf16[512,1152]{1,0:T(8,128)(2,1)}, bf16[512,1152]{1,0:T(8,128)(2,1)S(1)}, u32[]{:S(2)}, u32[]{:S(2)}) %collective-permute-start.2) | collective-permute-done | bytes 1179680 | tf_op jit(solution)/shard_map/ppermute | solution.py:24
  39.1 3.1 %collective-permute-done.1.refs_1_ = bf16[512,1152]{1,0:T(8,128)(2,1)} collective-permute-done((bf16[512,1152]{1,0:T(8,128)(2,1)}, bf16[512,1152]{1,0:T(8,128)(2,1)}, u32[]{:S(2)}, u32[]{:S(2)}) %collective-permute-start.1) | collective-permute-done | bytes 1179680 | tf_op jit(solution)/shard_map/ppermute | solution.py:24
  44.6 7.7 %all-to-all-start.1 = ((bf16[8,256,256]{2,1,0:T(8,128)(2,1)}), bf16[8,256,256]{2,1,0:T(8,128)(2,1)}, u32[]{:S(2)}, u32[]{:S(2)}) async-start(bf16[8,256,256]{2,1,0:T(8,128)(2,1)} %copy-done.8), calls=%async_computation.1 | async-start | bytes 2097152 | tf_op jit(solution)/shard_map/all_to_all | solution.py:216
  60.7 6.7 %all-to-all-done.1 = bf16[8,256,256]{2,1,0:T(8,128)(2,1)} async-done(((bf16[8,256,256]{2,1,0:T(8,128)(2,1)}), bf16[8,256,256]{2,1,0:T(8,128)(2,1)}, u32[]{:S(2)}, u32[]{:S(2)}) %all-to-all-start.1) | async-done | bytes 1048608 | tf_op jit(solution)/shard_map/all_to_all | solution.py:216
  69.3 6.1 %shard_map.62 = (bf16[256,512]{1,0:T(8,128)(2,1)S(1)}, bf16[2560,256]{1,0:T(8,128)(2,1)}, bf16[8,32,2048]{2,1,0:T(8,128)(2,1)S(1)}) custom-call(bf16[2048,256]{1,0:T(8,128)(2,1)} %bitcast.2.codes, bf16[512,256]{1,0:T(8,128)(2,1)S(1)} %bitcast.9, bf16[512,256]{1,0:T(8,128)(2,1)S(1)} %copy-done.19, bf16[512,2048]{1,0:T(8,128)(2,1)} %a0.1, ...), custom_call_target="tpu_custom_call" | custom-call | flops 2147483648 | bytes 8388608 | tf_op jit(solution)/shard_map/pallas_call | solution.py:33
  75.4 3.1 %collective-permute-start.11 = (bf16[2560,256]{1,0:T(8,128)(2,1)}, bf16[2560,256]{1,0:T(8,128)(2,1)}, u32[]{:S(2)}, u32[]{:S(2)}) collective-permute-start(bf16[2560,256]{1,0:T(8,128)(2,1)} %get-tuple-element.44), channel_id=1, source_target_pairs={{0,1},{1,0},{2,3},{3,2},{4,5},{5,4},{6,7},{7,6},{8,9},{9,8},{10,11... | collective-permute-start | bytes 3932168 | tf_op jit(solution)/shard_map/ppermute | solution.py:24
  78.5 19.3 %all_to_all.20.blocks = bf16[8,32,2048]{2,1,0:T(8,128)(2,1)S(1)} all-to-all(bf16[8,32,2048]{2,1,0:T(8,128)(2,1)S(1)} %get-tuple-element.40), channel_id=1, replica_groups=mesh['y_lo'=2,'x'=4,'z'=4,'y_hi'=2,'core'=2] {'z','y_hi'}, dimensions={0} | all-to-all | bytes 2097152 | tf_op jit(solution)/shard_map/all_to_all | solution.py:230
  99.1 4.7 %all-to-all-start.3 = ((bf16[32,32,512]{2,1,0:T(8,128)(2,1)}), bf16[32,32,512]{2,1,0:T(8,128)(2,1)}, u32[]{:S(2)}, u32[]{:S(2)}) async-start(bf16[32,32,512]{2,1,0:T(8,128)(2,1)} %bitcast.8), calls=%async_computation.3 | async-start | bytes 2097152 | tf_op jit(solution)/shard_map/all_to_all | solution.py:242
  107.5 2.9 %shard_map.64 = (f32[2,256,512]{2,1,0:T(8,128)S(1)}, bf16[2,256,512]{2,1,0:T(8,128)(2,1)S(1)}, bf16[2,256,512]{2,1,0:T(8,128)(2,1)S(1)}, bf16[2,256,512]{2,1,0:T(8,128)(2,1)S(1)}) custom-call(bf16[2048,256]{1,0:T(8,128)(2,1)} %bitcast.2.codes, bf16[256,512]{1,0:T(8,128)(2,1)S(1)} %copy-done.21, bf16[2560,256]{1,0:T(8,128)(2,1)} %collective-permute-done.11.message), custom_call_target="tpu_custom_call" | custom-call | flops 1073741824 | bytes 5242880 | tf_op jit(solution)/shard_map/pallas_call | solution.py:33
  111.5 3.7 %collective-permute-start.13 = (bf16[2,256,512]{2,1,0:T(8,128)(2,1)S(1)}, bf16[2,256,512]{2,1,0:T(8,128)(2,1)S(1)}, u32[]{:S(2)}, u32[]{:S(2)}) collective-permute-start(bf16[2,256,512]{2,1,0:T(8,128)(2,1)S(1)} %get-tuple-element.47), channel_id=1, source_target_pairs={{0,32},{16,48},{32,0},{48,16},{1,33},{17,49},{33,1},{49,17},{2,34}... | collective-permute-start | bytes 1572872 | tf_op jit(solution)/shard_map/ppermute | solution.py:24
  115.2 8.5 %collective-permute-done.10.refs_5_ = bf16[512,512]{1,0:T(8,128)(2,1)S(1)} collective-permute-done((bf16[512,512]{1,0:T(8,128)(2,1)S(1)}, bf16[512,512]{1,0:T(8,128)(2,1)S(1)}, u32[]{:S(2)}, u32[]{:S(2)}) %collective-permute-start.10) | collective-permute-done | bytes 524320 | tf_op jit(solution)/shard_map/ppermute | solution.py:24
  123.7 3.3 %collective-permute-done.9.refs_4_ = bf16[512,512]{1,0:T(8,128)(2,1)S(1)} collective-permute-done((bf16[512,512]{1,0:T(8,128)(2,1)S(1)}, bf16[512,512]{1,0:T(8,128)(2,1)S(1)}, u32[]{:S(2)}, u32[]{:S(2)}) %collective-permute-start.9) | collective-permute-done | bytes 524320 | tf_op jit(solution)/shard_map/ppermute | solution.py:24
  127.8 12.3 %collective-permute-done.12.r1 = bf16[2,256,512]{2,1,0:T(8,128)(2,1)S(1)} collective-permute-done((bf16[2,256,512]{2,1,0:T(8,128)(2,1)S(1)}, bf16[2,256,512]{2,1,0:T(8,128)(2,1)S(1)}, u32[]{:S(2)}, u32[]{:S(2)}) %collective-permute-start.12) | collective-permute-done | bytes 524320 | tf_op jit(solution)/shard_map/ppermute | solution.py:24
  140.9 6.7 %collective-permute-done.13.r2 = bf16[2,256,512]{2,1,0:T(8,128)(2,1)S(1)} collective-permute-done((bf16[2,256,512]{2,1,0:T(8,128)(2,1)S(1)}, bf16[2,256,512]{2,1,0:T(8,128)(2,1)S(1)}, u32[]{:S(2)}, u32[]{:S(2)}) %collective-permute-start.13) | collective-permute-done | bytes 524320 | tf_op jit(solution)/shard_map/ppermute | solution.py:24
  149.2 5.4 %collective-permute-start.15 = (bf16[4,256,512]{2,1,0:T(8,128)(2,1)}, bf16[4,256,512]{2,1,0:T(8,128)(2,1)S(1)}, u32[]{:S(2)}, u32[]{:S(2)}) collective-permute-start(bf16[4,256,512]{2,1,0:T(8,128)(2,1)} %bitcast.5.grad), channel_id=1, source_target_pairs={{0,1},{1,0},{2,3},{3,2},{4,5},{5,4},{6,7},{7,6},{8,9},{9,8},{10,11... | collective-permute-start | bytes 3145736 | tf_op jit(solution)/shard_map/ppermute | solution.py:24
  159.3 3.4 %shard_map.68.refs_9_ = f32[256,1792]{1,0:T(8,128)S(1)} custom-call(bf16[4,256,512]{2,1,0:T(8,128)(2,1)} %bitcast.5.grad, bf16[512,1792]{1,0:T(8,128)(2,1)S(1)} %copy-done.1, bf16[512,1152]{1,0:T(8,128)(2,1)} %collective-permute-done.1.refs_1_, bf16[512,640]{1,0:T(8,128)(2,1)} %collective-permute-done.5.refs_2_, ...), custom_call_target="tpu_custom_call" | custom-call | flops 939524096 | bytes 10223616 | tf_op jit(solution)/shard_map/pallas_call | solution.py:33
  162.7 3.1 %shard_map.69 = bf16[256,2304]{1,0:T(8,128)(2,1)S(1)} custom-call(bf16[4,256,512]{2,1,0:T(8,128)(2,1)S(1)} %collective-permute-done.15.grad, bf16[512,1792]{1,0:T(8,128)(2,1)S(1)} %copy-done.1, bf16[512,1152]{1,0:T(8,128)(2,1)} %collective-permute-done.1.refs_1_, bf16[512,640]{1,0:T(8,128)(2,1)} %collective-permute-done.5.refs_2_, ...), custom_call_target="tpu_custom_call" | custom-call | flops 939524096 | bytes 11665408 | tf_op jit(solution)/shard_map/pallas_call | solution.py:33
  166.2 3.4 %shard_map.65.refs_9_ = f32[256,1792]{1,0:T(8,128)S(1)} custom-call(bf16[4,256,512]{2,1,0:T(8,128)(2,1)} %bitcast.5.grad, bf16[512,1792]{1,0:T(8,128)(2,1)S(1)} %copy-done.1, bf16[512,1152]{1,0:T(8,128)(2,1)} %collective-permute-done.1.refs_1_, bf16[512,640]{1,0:T(8,128)(2,1)} %collective-permute-done.5.refs_2_, ...), custom_call_target="tpu_custom_call" | custom-call | flops 939524096 | bytes 10223616 | tf_op jit(solution)/shard_map/pallas_call | solution.py:33
  169.6 3.1 %shard_map.66 = f32[256,1792]{1,0:T(8,128)S(1)} custom-call(bf16[4,256,512]{2,1,0:T(8,128)(2,1)S(1)} %collective-permute-done.15.grad, bf16[512,1792]{1,0:T(8,128)(2,1)S(1)} %copy-done.1, bf16[512,1152]{1,0:T(8,128)(2,1)} %collective-permute-done.1.refs_1_, bf16[512,640]{1,0:T(8,128)(2,1)} %collective-permute-done.5.refs_2_, ...), custom_call_target="tpu_custom_call" | custom-call | flops 939524096 | bytes 12058624 | tf_op jit(solution)/shard_map/pallas_call | solution.py:33
  172.7 20.7 %collective-permute-done.16 = bf16[256,2304]{1,0:T(8,128)(2,1)S(1)} collective-permute-done((bf16[256,2304]{1,0:T(8,128)(2,1)S(1)}, bf16[256,2304]{1,0:T(8,128)(2,1)S(1)}, u32[]{:S(2)}, u32[]{:S(2)}) %collective-permute-start.16) | collective-permute-done | bytes 1179680 | tf_op jit(solution)/shard_map/ppermute | solution.py:24
  (88 shorter events, 42.2 us)
Async XLA Ops:
  8.1 8.7 %collective-permute-start = (f32[2048,256]{1,0:T(8,128)S(1)}, f32[2048,256]{1,0:T(8,128)S(1)}, u32[]{:S(2)}, u32[]{:S(2)}) collective-permute-start(f32[2048,256]{1,0:T(8,128)S(1)} %shard_map.60), channel_id=1, source_target_pairs={{0,1},{1,0},{2,3},{3,2},{4,5},{5,4},{6,7},{7,6},{8,9},{9,8},{10,11... | collective-permute-start | bytes 6291464 | tf_op jit(solution)/shard_map/ppermute | solution.py:24
  9.6 32.6 %collective-permute-start.3 = (bf16[512,2048]{1,0:T(8,128)(2,1)}, bf16[512,2048]{1,0:T(8,128)(2,1)}, u32[]{:S(2)}, u32[]{:S(2)}) collective-permute-start(bf16[512,2048]{1,0:T(8,128)(2,1)} %a0.1), channel_id=1, source_target_pairs={{0,1},{1,0},{2,3},{3,2},{4,5},{5,4},{6,7},{7,6},{8,9},{9,8},{10,11... | collective-permute-start | bytes 6291464 | tf_op jit(solution)/shard_map/ppermute | solution.py:24
  11.3 27.8 %collective-permute-start.2 = (bf16[512,1152]{1,0:T(8,128)(2,1)}, bf16[512,1152]{1,0:T(8,128)(2,1)S(1)}, u32[]{:S(2)}, u32[]{:S(2)}) collective-permute-start(bf16[512,1152]{1,0:T(8,128)(2,1)} %get-tuple-element.68), channel_id=1, source_target_pairs={{0,48},{16,0},{32,16},{48,32},{1,49},{17,1},{33,17},{49,33},{2,50}... | collective-permute-start | bytes 3538952 | tf_op jit(solution)/shard_map/ppermute | solution.py:24
  13.9 28.3 %collective-permute-start.1 = (bf16[512,1152]{1,0:T(8,128)(2,1)}, bf16[512,1152]{1,0:T(8,128)(2,1)}, u32[]{:S(2)}, u32[]{:S(2)}) collective-permute-start(bf16[512,1152]{1,0:T(8,128)(2,1)} %get-tuple-element.69), channel_id=1, source_target_pairs={{0,16},{16,32},{32,48},{48,0},{1,17},{17,33},{33,49},{49,1},{2,18}... | collective-permute-start | bytes 3538952 | tf_op jit(solution)/shard_map/ppermute | solution.py:24
  18.0 24.2 %all-to-all-start = ((bf16[8,256,256]{2,1,0:T(8,128)(2,1)}), bf16[8,256,256]{2,1,0:T(8,128)(2,1)}, u32[]{:S(2)}, u32[]{:S(2)}) async-start(bf16[8,256,256]{2,1,0:T(8,128)(2,1)} %bitcast), calls=%async_computation | async-start | bytes 2097152 | tf_op jit(solution)/shard_map/all_to_all | solution.py:210
  26.7 25.5 %copy-start.1 = (bf16[512,1792]{1,0:T(8,128)(2,1)S(1)}, bf16[512,1792]{1,0:T(8,128)(2,1)}, u32[]{:S(2)}) copy-start(bf16[512,1792]{1,0:T(8,128)(2,1)} %refs_0_.7) | copy-start | bytes 5505028
  26.7 2.2 %collective-permute-start.4 = (bf16[512,256]{1,0:T(8,128)(2,1)S(1)}, bf16[512,256]{1,0:T(8,128)(2,1)S(1)}, u32[]{:S(2)}, u32[]{:S(2)}) collective-permute-start(bf16[512,256]{1,0:T(8,128)(2,1)S(1)} %bitcast.10), channel_id=1, source_target_pairs={{0,1},{1,0},{2,3},{3,2},{4,5},{5,4},{6,7},{7,6},{8,9},{9,8},{10,11... | collective-permute-start | bytes 786440 | tf_op jit(solution)/shard_map/ppermute | solution.py:24
  44.6 22.9 %all-to-all-start.1 = ((bf16[8,256,256]{2,1,0:T(8,128)(2,1)}), bf16[8,256,256]{2,1,0:T(8,128)(2,1)}, u32[]{:S(2)}, u32[]{:S(2)}) async-start(bf16[8,256,256]{2,1,0:T(8,128)(2,1)} %copy-done.8), calls=%async_computation.1 | async-start | bytes 2097152 | tf_op jit(solution)/shard_map/all_to_all | solution.py:216
  53.4 25.1 %collective-permute-start.6 = (bf16[512,640]{1,0:T(8,128)(2,1)}, bf16[512,640]{1,0:T(8,128)(2,1)}, u32[]{:S(2)}, u32[]{:S(2)}) collective-permute-start(bf16[512,640]{1,0:T(8,128)(2,1)} %get-tuple-element.66), channel_id=1, source_target_pairs={{0,48},{16,0},{32,16},{48,32},{1,49},{17,1},{33,17},{49,33},{2,50}... | collective-permute-start | bytes 1966088 | tf_op jit(solution)/shard_map/ppermute | solution.py:24
  53.6 24.9 %collective-permute-start.5 = (bf16[512,640]{1,0:T(8,128)(2,1)}, bf16[512,640]{1,0:T(8,128)(2,1)}, u32[]{:S(2)}, u32[]{:S(2)}) collective-permute-start(bf16[512,640]{1,0:T(8,128)(2,1)} %get-tuple-element.67), channel_id=1, source_target_pairs={{0,16},{16,32},{32,48},{48,0},{1,17},{17,33},{33,49},{49,1},{2,18}... | collective-permute-start | bytes 1966088 | tf_op jit(solution)/shard_map/ppermute | solution.py:24
  57.5 21.0 %collective-permute-start.8 = (bf16[512,384]{1,0:T(8,128)(2,1)}, bf16[512,384]{1,0:T(8,128)(2,1)S(1)}, u32[]{:S(2)}, u32[]{:S(2)}) collective-permute-start(bf16[512,384]{1,0:T(8,128)(2,1)} %slice.35), channel_id=1, source_target_pairs={{0,48},{16,0},{32,16},{48,32},{1,49},{17,1},{33,17},{49,33},{2,50}... | collective-permute-start | bytes 1179656 | tf_op jit(solution)/shard_map/ppermute | solution.py:24
  58.9 19.6 %collective-permute-start.7 = (bf16[512,384]{1,0:T(8,128)(2,1)}, bf16[512,384]{1,0:T(8,128)(2,1)}, u32[]{:S(2)}, u32[]{:S(2)}) collective-permute-start(bf16[512,384]{1,0:T(8,128)(2,1)} %slice.34), channel_id=1, source_target_pairs={{0,16},{16,32},{32,48},{48,0},{1,17},{17,33},{33,49},{49,1},{2,18}... | collective-permute-start | bytes 1179656 | tf_op jit(solution)/shard_map/ppermute | solution.py:24
  75.4 22.7 %copy-start.20 = (bf16[256,512]{1,0:T(8,128)(2,1)}, bf16[256,512]{1,0:T(8,128)(2,1)S(1)}, u32[]{:S(2)}) copy-start(bf16[256,512]{1,0:T(8,128)(2,1)S(1)} %get-tuple-element.43.own) | copy-start | bytes 786436
  75.4 32.0 %collective-permute-start.11 = (bf16[2560,256]{1,0:T(8,128)(2,1)}, bf16[2560,256]{1,0:T(8,128)(2,1)}, u32[]{:S(2)}, u32[]{:S(2)}) collective-permute-start(bf16[2560,256]{1,0:T(8,128)(2,1)} %get-tuple-element.44), channel_id=1, source_target_pairs={{0,1},{1,0},{2,3},{3,2},{4,5},{5,4},{6,7},{7,6},{8,9},{9,8},{10,11... | collective-permute-start | bytes 3932168 | tf_op jit(solution)/shard_map/ppermute | solution.py:24
  78.5 19.6 %copy-start.5 = (bf16[512,384]{1,0:T(8,128)(2,1)}, bf16[512,384]{1,0:T(8,128)(2,1)S(1)}, u32[]{:S(2)}) copy-start(bf16[512,384]{1,0:T(8,128)(2,1)S(1)} %collective-permute-done.8.refs_6_) | copy-start | bytes 1179652
  99.1 50.1 %all-to-all-start.3 = ((bf16[32,32,512]{2,1,0:T(8,128)(2,1)}), bf16[32,32,512]{2,1,0:T(8,128)(2,1)}, u32[]{:S(2)}, u32[]{:S(2)}) async-start(bf16[32,32,512]{2,1,0:T(8,128)(2,1)} %bitcast.8), calls=%async_computation.3 | async-start | bytes 2097152 | tf_op jit(solution)/shard_map/all_to_all | solution.py:242
  105.0 18.8 %collective-permute-start.10 = (bf16[512,512]{1,0:T(8,128)(2,1)S(1)}, bf16[512,512]{1,0:T(8,128)(2,1)S(1)}, u32[]{:S(2)}, u32[]{:S(2)}) collective-permute-start(bf16[512,512]{1,0:T(8,128)(2,1)S(1)} %slice.37), channel_id=1, source_target_pairs={{0,48},{16,0},{32,16},{48,32},{1,49},{17,1},{33,17},{49,33},{2,50}... | collective-permute-start | bytes 1572872 | tf_op jit(solution)/shard_map/ppermute | solution.py:24
  107.4 19.6 %collective-permute-start.9 = (bf16[512,512]{1,0:T(8,128)(2,1)S(1)}, bf16[512,512]{1,0:T(8,128)(2,1)S(1)}, u32[]{:S(2)}, u32[]{:S(2)}) collective-permute-start(bf16[512,512]{1,0:T(8,128)(2,1)S(1)} %slice.36), channel_id=1, source_target_pairs={{0,16},{16,32},{32,48},{48,0},{1,17},{17,33},{33,49},{49,1},{2,18}... | collective-permute-start | bytes 1572872 | tf_op jit(solution)/shard_map/ppermute | solution.py:24
  111.3 28.8 %collective-permute-start.12 = (bf16[2,256,512]{2,1,0:T(8,128)(2,1)S(1)}, bf16[2,256,512]{2,1,0:T(8,128)(2,1)S(1)}, u32[]{:S(2)}, u32[]{:S(2)}) collective-permute-start(bf16[2,256,512]{2,1,0:T(8,128)(2,1)S(1)} %get-tuple-element.46), channel_id=1, source_target_pairs={{0,16},{16,32},{32,48},{48,0},{1,17},{17,33},{33,49},{49,1},{2,18}... | collective-permute-start | bytes 1572872 | tf_op jit(solution)/shard_map/ppermute | solution.py:24
  111.5 36.2 %collective-permute-start.13 = (bf16[2,256,512]{2,1,0:T(8,128)(2,1)S(1)}, bf16[2,256,512]{2,1,0:T(8,128)(2,1)S(1)}, u32[]{:S(2)}, u32[]{:S(2)}) collective-permute-start(bf16[2,256,512]{2,1,0:T(8,128)(2,1)S(1)} %get-tuple-element.47), channel_id=1, source_target_pairs={{0,32},{16,48},{32,0},{48,16},{1,33},{17,49},{33,1},{49,17},{2,34}... | collective-permute-start | bytes 1572872 | tf_op jit(solution)/shard_map/ppermute | solution.py:24
  115.2 33.3 %collective-permute-start.14 = (bf16[2,256,512]{2,1,0:T(8,128)(2,1)S(1)}, bf16[2,256,512]{2,1,0:T(8,128)(2,1)S(1)}, u32[]{:S(2)}, u32[]{:S(2)}) collective-permute-start(bf16[2,256,512]{2,1,0:T(8,128)(2,1)S(1)} %get-tuple-element.48), channel_id=1, source_target_pairs={{0,48},{16,0},{32,16},{48,32},{1,49},{17,1},{33,17},{49,33},{2,50}... | collective-permute-start | bytes 1572872 | tf_op jit(solution)/shard_map/ppermute | solution.py:24
  149.2 10.0 %copy-start.6 = (bf16[512,384]{1,0:T(8,128)(2,1)S(1)}, bf16[512,384]{1,0:T(8,128)(2,1)}, u32[]{:S(2)}) copy-start(bf16[512,384]{1,0:T(8,128)(2,1)} %copy-done.5) | copy-start | bytes 1179652
  149.2 13.4 %collective-permute-start.15 = (bf16[4,256,512]{2,1,0:T(8,128)(2,1)}, bf16[4,256,512]{2,1,0:T(8,128)(2,1)S(1)}, u32[]{:S(2)}, u32[]{:S(2)}) collective-permute-start(bf16[4,256,512]{2,1,0:T(8,128)(2,1)} %bitcast.5.grad), channel_id=1, source_target_pairs={{0,1},{1,0},{2,3},{3,2},{4,5},{5,4},{6,7},{7,6},{8,9},{9,8},{10,11... | collective-permute-start | bytes 3145736 | tf_op jit(solution)/shard_map/ppermute | solution.py:24
  165.7 27.6 %collective-permute-start.16 = (bf16[256,2304]{1,0:T(8,128)(2,1)S(1)}, bf16[256,2304]{1,0:T(8,128)(2,1)S(1)}, u32[]{:S(2)}, u32[]{:S(2)}) collective-permute-start(bf16[256,2304]{1,0:T(8,128)(2,1)S(1)} %shard_map.69), channel_id=1, source_target_pairs={{0,64},{64,0},{1,65},{65,1},{2,66},{66,2},{3,67},{67,3},{4,68},{68... | collective-permute-start | bytes 3538952 | tf_op jit(solution)/shard_map/ppermute | solution.py:24
  (19 other events, 39.2 us)

commit v13 on v12

--- a/solution.py
+++ b/solution.py
@@ -125,40 +125,60 @@
                 out[x, i, :, at : at + width] = piece
 
 
-def last_kernel(cuts, side, other, more, grad, *refs):
-    parts, before, (out, turned) = refs[: len(cuts)], refs[len(cuts) : -2], refs[-2:]
-    core, x = lax.axis_index("core"), lax.axis_index("x")
-    half, width = grad.shape[1], out.shape[0]
-    wide = max(start + ref.shape[1] for ref, (_, start) in zip(parts, cuts))
+def hold_kernel(row, out, sems):
+    parts = sems.shape[0]
+    copies = [pltpu.make_async_copy(row.at[i], out.at[i], sems.at[i]) for i in range(parts)]
+    for copy in copies:
+        copy.start()
+    for copy in copies:
+        copy.wait()
+
+
+def hold(row):
+    return pl.pallas_call(
+        hold_kernel,
+        out_shape=like(row.shape),
+        in_specs=[ANY],
+        out_specs=VMEM,
+        scratch_shapes=[pltpu.SemaphoreType.DMA((row.shape[0],))],
+        compiler_params=pltpu.CompilerParams(vmem_limit_bytes=16 * 1024 * 1024),
+        cost_estimate=pl.CostEstimate(flops=0, bytes_accessed=4 * row.size, transcendentals=0),
+    )(row)
+
+
+def last_kernel(side, other, grad, acts, *refs):
+    before, (out, turned) = refs[:-2], refs[-2:]
+    core = lax.axis_index("core")
+    half, wide, width = grad.shape[1], acts.shape[2], out.shape[0]
     rows = pl.ds(pl.multiple_of((1 - core if other else core) * half, half), half)
     for k in range(4):
-        turned[k] = grad[lax.rem(x + 4 - k, 4), :, side * width : (side + 1) * width].T
+        turned[k] = grad[k, :, side * width : (side + 1) * width].T
     for ref in before[1:]:
         out[:, wide:] = ref[...]
-    edges = sorted({start for _, start in cuts} | {wide})
-    for low, high in zip(edges, edges[1:]):
-        acc = before[0][:, low:high] if other else None
-        for ref, (k, start) in zip(parts, cuts):
-            if start <= low and high <= start + ref.shape[1]:
-                term = dot(turned[k], ref[rows, low - start : high - start])
-                acc = term if acc is None else acc + term
-        out[:, low:high] = acc.astype(out.dtype)
-
-
-def last_call(grad_m, grad_o, cuts, parts, side, dtype, *joined):
-    tokens, wide = parts[0].shape
+    for c in range(0, wide, 256):
+        cols = slice(c, c + 256)
+        acc = dot(turned[0], acts[0, rows, cols])
+        for k in range(1, 4):
+            acc = acc + dot(turned[k], acts[k, rows, cols])
+        if other:
+            acc = acc + before[0][:, cols]
+        out[:, cols] = acc.astype(out.dtype)
+
+
+def last_call(grad_m, grad_o, held, side, dtype, *joined):
+    _, tokens, wide = held.shape
     half, width = tokens // 2, grad_m.shape[2] // 2
     scratch = [pltpu.VMEM((4, width, half), BF)]
     flops = 4 * tokens * width * wide
     first = call(
-        functools.partial(last_kernel, cuts, side, False, 0),
+        functools.partial(last_kernel, side, False),
         [like((width, wide), F32)],
-        grad_m, *parts, scratch=scratch, flops=flops,
+        grad_m, held, scratch=scratch, flops=flops,
     )
     return call(
-        functools.partial(last_kernel, cuts, side, True, len(joined)),
+        functools.partial(last_kernel, side, True),
         [like((width, wide + sum(j.shape[1] for j in joined)), dtype)],
-        grad_o, *parts, first, *joined, scratch=scratch, flops=flops,
+        grad_o, held, first, *joined, scratch=scratch, flops=flops,
     )
 
 
@@ -196,10 +216,7 @@
     def part_of(array, which, size, axis):
         return lax.dynamic_slice_in_dim(array, which * size, size, axis)
 
-    barrier = lax.optimization_barrier
-    c1, c2, c3 = 1152, 384, 896
-    plus_a = shift(acts[:, :c1], "x", 4, 1)
-    minus_a = shift(acts[:, wide - c1 :], "x", 4, 3)
+    row = lax.all_gather(acts, "x")
     pair_a = swap(proj_a, "core")
     target_t = target.T
     near_t = part_of(target_t, core, half, 1)
@@ -208,10 +225,6 @@
     arrived = swap(codes_call(True, acts, proj_b), "core")
     mine = (codes_call(False, acts, proj_b) + arrived).astype(BF).reshape(8, width, half)
     blocks = lax.all_to_all(mine, ZY, 0, 0)
-    blocks, plus_a, minus_a, later, pair_a, pair_t = barrier((blocks, plus_a, minus_a, acts, pair_a, pair_t))
-    plus_b = shift(later[:, c1:], "x", 4, 1)
-    minus_b = shift(later[:, : wide - c1], "x", 4, 3)
-    far_a = shift(plus_a[:, :c2], "x", 4, 1), shift(minus_a[:, c1 - c2 :], "x", 4, 3)
     codes = call(sum_and_copy, [like((8, width, half))], blocks)
     codes = lax.all_to_all(codes, ZY, 0, 0).reshape(rank, half)
 
@@ -222,11 +235,6 @@
         scratch=[pltpu.VMEM((half, 2 * outs), BF)],
         flops=8 * half * rank * outs,
     )
-    partial, plus_a, minus_a, plus_b, minus_b, far_a = barrier((partial, plus_a, minus_a, plus_b, minus_b, far_a))
-    far_b = (
-        shift(plus_a[:, c2:c3], "x", 4, 1),
-        shift(minus_a[:, c1 - c3 : c1 - c2], "x", 4, 3),
-    )
     blocks = lax.all_to_all(partial, ZY, 0, 0)
 
     piece = like((2, width, outs))
@@ -238,17 +246,18 @@
     )
     terms = [terms[0]] + [shift(terms[k], "x", 4, k) for k in (1, 2, 3)]
 
+    barrier = lax.optimization_barrier
+    blocks, row = barrier((blocks, row))
     split = call(spread_kernel, [like((4, 8, sub, 2 * width))], blocks, scratch=[pltpu.VMEM((sub, rank), BF)])
+    split, row = barrier((split, row))
+    held = hold(row)
     grad = lax.all_to_all(split.reshape(32, sub, 2 * width), ("x", "z", "y_hi"), 0, 0)
     grad = grad.reshape(4, half, 2 * width)
-    grad, far_b, *terms = barrier((grad, far_b, *terms))
+    grad, held, *terms = barrier((grad, held, *terms))
     grad_o = swap(grad, "core")
     term_o, term_a = call(term_sum_kernel, [like((width, outs), F32), like((width, outs))], *terms)
-    parts = [acts, plus_a, plus_b, far_a[0], far_b[0], far_b[1], far_a[1], minus_b, minus_a]
-    cuts = ((0, 0), (1, 0), (1, c1), (2, 0), (2, c2), (2, c3), (2, wide - c2), (3, 0), (3, wide - c1))
-    away = last_call(grad, grad_o, cuts, parts, 0, BF, term_a)
-    away = swap(away, "y_lo").astype(F32)
-    here = last_call(grad, grad_o, cuts, parts, 1, F32)
+    away = swap(last_call(grad, grad_o, held, 0, BF, term_a), "y_lo").astype(F32)
+    here = last_call(grad, grad_o, held, 1, F32)
     here, term_o = barrier((here, term_o))
     return (((term_o + away[:, wide:]) * scale).T, (here + away[:, :wide]) * scale)
 

time: 197 us -> 188 us (0.954)
  blocking collectives: 19.3 us -> 43.4 us
  starting transfers between devices: 43.6 us -> 23.3 us
  between operations: 0.88 us -> 14.2 us
  waiting for transfers between devices: 71.9 us -> 61.6 us
  Pallas kernels: 29.6 us -> 20.7 us
  local copies, waits for them, and re-layouts: 27.9 us -> 22 us
    all_to_all x0 -> x1, blocking collectives: none -> 23.9 us  [local(): blocks = lax.all_to_all(mine, ZY, 0, 0)]
    ppermute x17 -> x9, waiting for transfers between devices: 65.3 us -> 49.1 us  [shift(): lax.ppermute(array, axis, [(i, (i + step) % size) for i in range(size)])]
    ppermute x17 -> x9, starting transfers between devices: 23.5 us -> 14 us  [shift(): lax.ppermute(array, axis, [(i, (i + step) % size) for i in range(size)])]
    pallas_call x9, Pallas kernels: 23.7 us -> 14.4 us  [call(): pl.pallas_call(body, out_shape=outs if len(outs) > 1 else outs[0], in_spe...]
    all_to_all x1 -> x0, starting transfers between devices: 7.8 us -> none  [local(): blocks = lax.all_to_all(mine, ZY, 0, 0)]
    slice x6 -> x0, local copies, waits for them, and re-layouts: 6.52 us -> none  [the longest x1 1.78 us: local(): plus_a[:, :c2]]
    all_to_all x1, waiting for transfers between devices: 6.67 us -> 11.8 us  [local(): codes = lax.all_to_all(codes, ZY, 0, 0).reshape(rank, half)]
    all_to_all x1, starting transfers between devices: 7.66 us -> 3.56 us  [local(): codes = lax.all_to_all(codes, ZY, 0, 0).reshape(rank, half)]
  transfers between devices with their start and end apart: 20 -> 12, of which waited for: 9 -> 6; matrix products, arithmetic and copies ran while one was open for 5% -> 0% of each run, Pallas kernels for 11% -> 10%
where the time goes in v13:
time: 188 us; the launch traced here: 187 us
  waiting for transfers between devices  61.6 us (33%)
  blocking collectives  43.4 us (23%)
  starting transfers between devices  23.3 us (12%)
  local copies, waits for them, and re-layouts  22 us (12%)
  Pallas kernels  20.7 us (11%)
  between operations  14.2 us (8%)
  other arithmetic  2.17 us (1%)
    ppermute x9, waiting for transfers between devices, shift(): lax.ppermute(array, axis, [(i, (i + step) % size) for i in range(size)])  49.1 us
    all_to_all x1, blocking collectives, local(): blocks = lax.all_to_all(mine, ZY, 0, 0)  23.9 us
    unnamed x29, local copies, waits for them, and re-layouts  21.9 us
    all_to_all x1, blocking collectives, local(): blocks = lax.all_to_all(partial, ZY, 0, 0)  19.5 us
    pallas_call x9, Pallas kernels, call(): pl.pallas_call(body, out_shape=outs if len(outs) > 1 else outs[0], in_spe...  14.4 us
    ppermute x9, starting transfers between devices, shift(): lax.ppermute(array, axis, [(i, (i + step) % size) for i in range(size)])  14 us
    all_to_all x1, waiting for transfers between devices, local(): codes = lax.all_to_all(codes, ZY, 0, 0).reshape(rank, half)  11.8 us
    pallas_call x2, Pallas kernels, codes_call(): pl.pallas_call(functools.partial(codes_kernel, other), grid=(rank // step...  5.82 us
  transfers between devices with their start and end apart: 12, of which 6 were waited for; matrix products, arithmetic and copies ran while one was open for 0% of the time, Pallas kernels for 10%

profile of v13, /device:TPU:1, one launch (start us, length us, event | category | flops | bytes accessed | tf_op | source)
XLA Modules:
  0.0 187.4 jit_solution(1542497455703122737)
XLA Ops:
  8.7 3.1 %copy-done.3 = bf16[2048,1792]{1,0:T(8,128)(2,1)S(1)} copy-done((bf16[2048,1792]{1,0:T(8,128)(2,1)S(1)}, bf16[2048,1792]{1,0:T(8,128)(2,1)}, u32[]{:S(2)}) %copy-start.3) | copy-done | bytes 7340056
  11.7 2.9 %shard_map.60 = f32[2048,256]{1,0:T(8,128)S(1)} custom-call(bf16[512,1792]{1,0:T(8,128)(2,1)S(1)} %copy-done.4, bf16[2048,1792]{1,0:T(8,128)(2,1)S(1)} %copy-done.3), custom_call_target="tpu_custom_call" | custom-call | flops 1879048192 | bytes 7340032 | tf_op jit(solution)/shard_map/pallas_call | solution.py:69
  14.7 1.5 collective-permute-start
  16.3 2.9 %shard_map.59 = f32[2048,256]{1,0:T(8,128)S(1)} custom-call(bf16[512,1792]{1,0:T(8,128)(2,1)S(1)} %copy-done.4, bf16[2048,1792]{1,0:T(8,128)(2,1)S(1)} %copy-done.3), custom_call_target="tpu_custom_call" | custom-call | flops 1879048192 | bytes 7340032 | tf_op jit(solution)/shard_map/pallas_call | solution.py:69
  19.2 2.8 %collective-permute-done = f32[2048,256]{1,0:T(8,128)S(1)} collective-permute-done((f32[2048,256]{1,0:T(8,128)S(1)}, f32[2048,256]{1,0:T(8,128)S(1)}, u32[]{:S(2)}, u32[]{:S(2)}) %collective-permute-start) | collective-permute-done | bytes 2097184 | tf_op jit(solution)/shard_map/ppermute | solution.py:24
  22.4 23.9 %all_to_all.20.blocks = bf16[8,256,256]{2,1,0:T(8,128)(2,1)S(1)} all-to-all(bf16[8,256,256]{2,1,0:T(8,128)(2,1)S(1)} %bitcast.16), channel_id=1, replica_groups=mesh['y_lo'=2,'x'=4,'z'=4,'y_hi'=2,'core'=2] {'z','y_hi'}, dimensions={0} | all-to-all | bytes 2097152 | tf_op jit(solution)/shard_map/all_to_all | solution.py:227
  47.3 3.6 %all-to-all-start.1 = ((bf16[8,256,256]{2,1,0:T(8,128)(2,1)}), bf16[8,256,256]{2,1,0:T(8,128)(2,1)S(1)}, u32[]{:S(2)}, u32[]{:S(2)}) async-start(bf16[8,256,256]{2,1,0:T(8,128)(2,1)} %shard_map.61), calls=%async_computation.1 | async-start | bytes 2097152 | tf_op jit(solution)/shard_map/all_to_all | solution.py:229
  51.1 1.9 %collective-permute-start.1 = (bf16[512,256]{1,0:T(8,128)(2,1)S(1)}, bf16[512,256]{1,0:T(8,128)(2,1)S(1)}, u32[]{:S(2)}, u32[]{:S(2)}) collective-permute-start(bf16[512,256]{1,0:T(8,128)(2,1)S(1)} %bitcast.17), channel_id=1, source_target_pairs={{0,1},{1,0},{2,3},{3,2},{4,5},{5,4},{6,7},{7,6},{8,9},{9,8},{10,11... | collective-permute-start | bytes 786440 | tf_op jit(solution)/shard_map/ppermute | solution.py:24
  54.2 11.8 %all-to-all-done.1 = bf16[8,256,256]{2,1,0:T(8,128)(2,1)S(1)} async-done(((bf16[8,256,256]{2,1,0:T(8,128)(2,1)}), bf16[8,256,256]{2,1,0:T(8,128)(2,1)S(1)}, u32[]{:S(2)}, u32[]{:S(2)}) %all-to-all-start.1) | async-done | bytes 1048608 | tf_op jit(solution)/shard_map/all_to_all | solution.py:229
  66.0 5.8 %shard_map.62 = (bf16[256,512]{1,0:T(8,128)(2,1)S(1)}, bf16[2560,256]{1,0:T(8,128)(2,1)}, bf16[8,32,2048]{2,1,0:T(8,128)(2,1)S(1)}) custom-call(bf16[2048,256]{1,0:T(8,128)(2,1)S(1)} %bitcast.13, bf16[512,256]{1,0:T(8,128)(2,1)S(1)} %bitcast.15, bf16[512,256]{1,0:T(8,128)(2,1)S(1)} %collective-permute-done.1.far, bf16[512,2048]{1,0:T(8,128)(2,1)} %a0.1, ...), custom_call_target="tpu_custom_call" | custom-call | flops 2147483648 | bytes 8388608 | tf_op jit(solution)/shard_map/pallas_call | solution.py:33
  72.5 3.1 %collective-permute-start.3 = (bf16[2560,256]{1,0:T(8,128)(2,1)}, bf16[2560,256]{1,0:T(8,128)(2,1)S(1)}, u32[]{:S(2)}, u32[]{:S(2)}) collective-permute-start(bf16[2560,256]{1,0:T(8,128)(2,1)} %get-tuple-element.29), channel_id=1, source_target_pairs={{0,1},{1,0},{2,3},{3,2},{4,5},{5,4},{6,7},{7,6},{8,9},{9,8},{10,11... | collective-permute-start | bytes 3932168 | tf_op jit(solution)/shard_map/ppermute | solution.py:24
  75.6 19.5 %all_to_all.21.blocks = bf16[8,32,2048]{2,1,0:T(8,128)(2,1)S(1)} all-to-all(bf16[8,32,2048]{2,1,0:T(8,128)(2,1)S(1)} %get-tuple-element.23), channel_id=1, replica_groups=mesh['y_lo'=2,'x'=4,'z'=4,'y_hi'=2,'core'=2] {'z','y_hi'}, dimensions={0} | all-to-all | bytes 2097152 | tf_op jit(solution)/shard_map/all_to_all | solution.py:238
  95.1 1.4 shard_map.63
  96.5 5.7 %all-to-all-start.3 = ((bf16[32,32,512]{2,1,0:T(8,128)(2,1)}), bf16[32,32,512]{2,1,0:T(8,128)(2,1)S(1)}, u32[]{:S(2)}, u32[]{:S(2)}) async-start(bf16[32,32,512]{2,1,0:T(8,128)(2,1)} %bitcast.5), calls=%async_computation.3 | async-start | bytes 2097152 | tf_op jit(solution)/shard_map/all_to_all | solution.py:254
  108.1 2.4 %collective-permute-start.5 = (bf16[2,256,512]{2,1,0:T(8,128)(2,1)S(1)}, bf16[2,256,512]{2,1,0:T(8,128)(2,1)S(1)}, u32[]{:S(2)}, u32[]{:S(2)}) collective-permute-start(bf16[2,256,512]{2,1,0:T(8,128)(2,1)S(1)} %get-tuple-element.32), channel_id=1, source_target_pairs={{0,32},{16,48},{32,0},{48,16},{1,33},{17,49},{33,1},{49,17},{2,34}... | collective-permute-start | bytes 1572872 | tf_op jit(solution)/shard_map/ppermute | solution.py:24
  111.7 3.1 %copy-done.5 = bf16[2048,1792]{1,0:T(8,128)(2,1)S(1)} copy-done((bf16[2048,1792]{1,0:T(8,128)(2,1)S(1)}, bf16[2048,1792]{1,0:T(8,128)(2,1)}, u32[]{:S(2)}) %copy-start.5) | copy-done | bytes 7340056
  115.3 2.9 %copy-done = bf16[4,512,1792]{2,1,0:T(8,128)(2,1)} copy-done((bf16[4,512,1792]{2,1,0:T(8,128)(2,1)}, bf16[4,512,1792]{2,1,0:T(8,128)(2,1)S(1)}, u32[]{:S(2)}) %copy-start) | copy-done | bytes 7340056
  118.2 9.3 %collective-permute-done.4.r1 = bf16[2,256,512]{2,1,0:T(8,128)(2,1)S(1)} collective-permute-done((bf16[2,256,512]{2,1,0:T(8,128)(2,1)S(1)}, bf16[2,256,512]{2,1,0:T(8,128)(2,1)S(1)}, u32[]{:S(2)}, u32[]{:S(2)}) %collective-permute-start.4) | collective-permute-done | bytes 524320 | tf_op jit(solution)/shard_map/ppermute | solution.py:24
  127.5 11.1 %collective-permute-done.5.r2 = bf16[2,256,512]{2,1,0:T(8,128)(2,1)S(1)} collective-permute-done((bf16[2,256,512]{2,1,0:T(8,128)(2,1)S(1)}, bf16[2,256,512]{2,1,0:T(8,128)(2,1)S(1)}, u32[]{:S(2)}, u32[]{:S(2)}) %collective-permute-start.5) | collective-permute-done | bytes 524320 | tf_op jit(solution)/shard_map/ppermute | solution.py:24
  139.5 1.8 collective-permute-start.7
  142.5 3.1 %copy-done.1 = bf16[4,512,1792]{2,1,0:T(8,128)(2,1)S(1)} copy-done((bf16[4,512,1792]{2,1,0:T(8,128)(2,1)S(1)}, bf16[4,512,1792]{2,1,0:T(8,128)(2,1)}, u32[]{:S(2)}) %copy-start.1) | copy-done | bytes 7340056
  146.7 1.9 %copy-done.2 = bf16[4,512,1792]{2,1,0:T(8,128)(2,1)S(1)} copy-done((bf16[4,512,1792]{2,1,0:T(8,128)(2,1)S(1)}, bf16[4,512,1792]{2,1,0:T(8,128)(2,1)}, u32[]{:S(2)}) %copy-start.2) | copy-done | bytes 7340056
  152.9 24.8 %collective-permute-done.8 = bf16[256,2304]{1,0:T(8,128)(2,1)S(1)} collective-permute-done((bf16[256,2304]{1,0:T(8,128)(2,1)S(1)}, bf16[256,2304]{1,0:T(8,128)(2,1)S(1)}, u32[]{:S(2)}, u32[]{:S(2)}) %collective-permute-start.8) | collective-permute-done | bytes 1179680 | tf_op jit(solution)/shard_map/ppermute | solution.py:24
  177.8 1.6 fusion
  (49 shorter events, 21.3 us)
Async XLA Ops:
  7.2 1.5 copy-start.4
  7.2 87.9 %all-gather.3.cloned.1.call-start = ((), (), s32[]{:S(2)}) async-start(), calls=%async_computation.4 | async-start | bytes 9175040 | tf_op jit(solution)/shard_map/all_gather | solution.py:219
  8.7 3.1 %copy-start.3 = (bf16[2048,1792]{1,0:T(8,128)(2,1)S(1)}, bf16[2048,1792]{1,0:T(8,128)(2,1)}, u32[]{:S(2)}) copy-start(bf16[2048,1792]{1,0:T(8,128)(2,1)} %b.3) | copy-start | bytes 22020100
  14.7 7.4 %collective-permute-start = (f32[2048,256]{1,0:T(8,128)S(1)}, f32[2048,256]{1,0:T(8,128)S(1)}, u32[]{:S(2)}, u32[]{:S(2)}) collective-permute-start(f32[2048,256]{1,0:T(8,128)S(1)} %shard_map.60), channel_id=1, source_target_pairs={{0,1},{1,0},{2,3},{3,2},{4,5},{5,4},{6,7},{7,6},{8,9},{9,8},{10,11... | collective-permute-start | bytes 6291464 | tf_op jit(solution)/shard_map/ppermute | solution.py:24
  16.2 38.0 %collective-permute-start.2 = (bf16[512,2048]{1,0:T(8,128)(2,1)}, bf16[512,2048]{1,0:T(8,128)(2,1)}, u32[]{:S(2)}, u32[]{:S(2)}) collective-permute-start(bf16[512,2048]{1,0:T(8,128)(2,1)} %a0.1), channel_id=1, source_target_pairs={{0,1},{1,0},{2,3},{3,2},{4,5},{5,4},{6,7},{7,6},{8,9},{9,8},{10,11... | collective-permute-start | bytes 6291464 | tf_op jit(solution)/shard_map/ppermute | solution.py:24
  46.2 4.7 %copy-start.12 = (bf16[512,512]{1,0:T(8,128)(2,1)S(1)}, bf16[512,512]{1,0:T(8,128)(2,1)}, u32[]{:S(2)}) copy-start(bf16[512,512]{1,0:T(8,128)(2,1)} %param.5) | copy-start | bytes 1572868
  47.3 18.6 %all-to-all-start.1 = ((bf16[8,256,256]{2,1,0:T(8,128)(2,1)}), bf16[8,256,256]{2,1,0:T(8,128)(2,1)S(1)}, u32[]{:S(2)}, u32[]{:S(2)}) async-start(bf16[8,256,256]{2,1,0:T(8,128)(2,1)} %shard_map.61), calls=%async_computation.1 | async-start | bytes 2097152 | tf_op jit(solution)/shard_map/all_to_all | solution.py:229
  51.1 3.1 %collective-permute-start.1 = (bf16[512,256]{1,0:T(8,128)(2,1)S(1)}, bf16[512,256]{1,0:T(8,128)(2,1)S(1)}, u32[]{:S(2)}, u32[]{:S(2)}) collective-permute-start(bf16[512,256]{1,0:T(8,128)(2,1)S(1)} %bitcast.17), channel_id=1, source_target_pairs={{0,1},{1,0},{2,3},{3,2},{4,5},{5,4},{6,7},{7,6},{8,9},{9,8},{10,11... | collective-permute-start | bytes 786440 | tf_op jit(solution)/shard_map/ppermute | solution.py:24
  72.5 29.7 %collective-permute-start.3 = (bf16[2560,256]{1,0:T(8,128)(2,1)}, bf16[2560,256]{1,0:T(8,128)(2,1)S(1)}, u32[]{:S(2)}, u32[]{:S(2)}) collective-permute-start(bf16[2560,256]{1,0:T(8,128)(2,1)} %get-tuple-element.29), channel_id=1, source_target_pairs={{0,1},{1,0},{2,3},{3,2},{4,5},{5,4},{6,7},{7,6},{8,9},{9,8},{10,11... | collective-permute-start | bytes 3932168 | tf_op jit(solution)/shard_map/ppermute | solution.py:24
  96.5 43.0 %all-to-all-start.3 = ((bf16[32,32,512]{2,1,0:T(8,128)(2,1)}), bf16[32,32,512]{2,1,0:T(8,128)(2,1)S(1)}, u32[]{:S(2)}, u32[]{:S(2)}) async-start(bf16[32,32,512]{2,1,0:T(8,128)(2,1)} %bitcast.5), calls=%async_computation.3 | async-start | bytes 2097152 | tf_op jit(solution)/shard_map/all_to_all | solution.py:254
  102.2 1.1 copy-start.8
  103.3 1.3 copy-start.9
  104.6 0.9 copy-start.11
  106.8 20.7 %collective-permute-start.4 = (bf16[2,256,512]{2,1,0:T(8,128)(2,1)S(1)}, bf16[2,256,512]{2,1,0:T(8,128)(2,1)S(1)}, u32[]{:S(2)}, u32[]{:S(2)}) collective-permute-start(bf16[2,256,512]{2,1,0:T(8,128)(2,1)S(1)} %get-tuple-element.31), channel_id=1, source_target_pairs={{0,16},{16,32},{32,48},{48,0},{1,17},{17,33},{33,49},{49,1},{2,18}... | collective-permute-start | bytes 1572872 | tf_op jit(solution)/shard_map/ppermute | solution.py:24
  108.1 30.6 %collective-permute-start.5 = (bf16[2,256,512]{2,1,0:T(8,128)(2,1)S(1)}, bf16[2,256,512]{2,1,0:T(8,128)(2,1)S(1)}, u32[]{:S(2)}, u32[]{:S(2)}) collective-permute-start(bf16[2,256,512]{2,1,0:T(8,128)(2,1)S(1)} %get-tuple-element.32), channel_id=1, source_target_pairs={{0,32},{16,48},{32,0},{48,16},{1,33},{17,49},{33,1},{49,17},{2,34}... | collective-permute-start | bytes 1572872 | tf_op jit(solution)/shard_map/ppermute | solution.py:24
  110.5 28.1 %collective-permute-start.6 = (bf16[2,256,512]{2,1,0:T(8,128)(2,1)S(1)}, bf16[2,256,512]{2,1,0:T(8,128)(2,1)S(1)}, u32[]{:S(2)}, u32[]{:S(2)}) collective-permute-start(bf16[2,256,512]{2,1,0:T(8,128)(2,1)S(1)} %get-tuple-element.33), channel_id=1, source_target_pairs={{0,48},{16,0},{32,16},{48,32},{1,49},{17,1},{33,17},{49,33},{2,50}... | collective-permute-start | bytes 1572872 | tf_op jit(solution)/shard_map/ppermute | solution.py:24
  111.7 3.1 %copy-start.5 = (bf16[2048,1792]{1,0:T(8,128)(2,1)S(1)}, bf16[2048,1792]{1,0:T(8,128)(2,1)}, u32[]{:S(2)}) copy-start(bf16[2048,1792]{1,0:T(8,128)(2,1)} %all-gather.3.cloned.1.call-done) | copy-start | bytes 22020100
  115.3 2.9 %copy-start = (bf16[4,512,1792]{2,1,0:T(8,128)(2,1)}, bf16[4,512,1792]{2,1,0:T(8,128)(2,1)S(1)}, u32[]{:S(2)}) copy-start(bf16[4,512,1792]{2,1,0:T(8,128)(2,1)S(1)} %shard_map.64.acts) | copy-start | bytes 22020100
  138.7 0.8 copy-start.6
  139.5 7.3 %collective-permute-start.7 = (bf16[4,256,512]{2,1,0:T(8,128)(2,1)S(1)}, bf16[4,256,512]{2,1,0:T(8,128)(2,1)S(1)}, u32[]{:S(2)}, u32[]{:S(2)}) collective-permute-start(bf16[4,256,512]{2,1,0:T(8,128)(2,1)S(1)} %bitcast.9), channel_id=1, source_target_pairs={{0,1},{1,0},{2,3},{3,2},{4,5},{5,4},{6,7},{7,6},{8,9},{9,8},{10,11... | collective-permute-start | bytes 3145736 | tf_op jit(solution)/shard_map/ppermute | solution.py:24
  141.2 1.0 copy-start.7
  142.5 3.1 %copy-start.1 = (bf16[4,512,1792]{2,1,0:T(8,128)(2,1)S(1)}, bf16[4,512,1792]{2,1,0:T(8,128)(2,1)}, u32[]{:S(2)}) copy-start(bf16[4,512,1792]{2,1,0:T(8,128)(2,1)} %copy-done) | copy-start | bytes 22020100
  145.6 3.1 %copy-start.2 = (bf16[4,512,1792]{2,1,0:T(8,128)(2,1)S(1)}, bf16[4,512,1792]{2,1,0:T(8,128)(2,1)}, u32[]{:S(2)}) copy-start(bf16[4,512,1792]{2,1,0:T(8,128)(2,1)} %copy-done) | copy-start | bytes 22020100
  149.8 27.9 %collective-permute-start.8 = (bf16[256,2304]{1,0:T(8,128)(2,1)S(1)}, bf16[256,2304]{1,0:T(8,128)(2,1)S(1)}, u32[]{:S(2)}, u32[]{:S(2)}) collective-permute-start(bf16[256,2304]{1,0:T(8,128)(2,1)S(1)} %shard_map.70), channel_id=1, source_target_pairs={{0,64},{64,0},{1,65},{65,1},{2,66},{66,2},{3,67},{67,3},{4,68},{68... | collective-permute-start | bytes 3538952 | tf_op jit(solution)/shard_map/ppermute | solution.py:24
  (1 other events, 0.7 us)
Sparse Core Ops, SparseCore 0:
  9.7 77.5 all-gather.2

commit v14 on v13

--- a/solution.py
+++ b/solution.py
@@ -125,61 +125,61 @@
                 out[x, i, :, at : at + width] = piece
 
 
-def hold_kernel(row, out, sems):
-    parts = sems.shape[0]
-    copies = [pltpu.make_async_copy(row.at[i], out.at[i], sems.at[i]) for i in range(parts)]
-    for copy in copies:
-        copy.start()
-    for copy in copies:
-        copy.wait()
-
-
-def hold(row):
-    return pl.pallas_call(
-        hold_kernel,
-        out_shape=like(row.shape),
-        in_specs=[ANY],
-        out_specs=VMEM,
-        scratch_shapes=[pltpu.SemaphoreType.DMA((row.shape[0],))],
-        compiler_params=pltpu.CompilerParams(vmem_limit_bytes=16 * 1024 * 1024),
-        cost_estimate=pl.CostEstimate(flops=0, bytes_accessed=4 * row.size, transcendentals=0),
-    )(row)
-
-
 def last_kernel(side, other, grad, acts, *refs):
-    before, (out, turned) = refs[:-2], refs[-2:]
+    before, (out, turned, held, sems) = refs[:-4], refs[-4:]
     core = lax.axis_index("core")
     half, wide, width = grad.shape[1], acts.shape[2], out.shape[0]
-    rows = pl.ds(pl.multiple_of((1 - core if other else core) * half, half), half)
+    step, flight = held.shape[3], 4
+    start = pl.multiple_of((1 - core if other else core) * half, half)
+    copies = [
+        pltpu.make_async_copy(
+            acts.at[:, pl.ds(start, half), pl.ds(i * step, step)], held.at[i], sems.at[i]
+        )
+        for i in range(wide // step)
+    ]
+    for copy in copies[:flight]:
+        copy.start()
     for k in range(4):
         turned[k] = grad[k, :, side * width : (side + 1) * width].T
     for ref in before[1:]:
         out[:, wide:] = ref[...]
-    for c in range(0, wide, 256):
-        cols = slice(c, c + 256)
-        acc = dot(turned[0], acts[0, rows, cols])
+    for i, copy in enumerate(copies):
+        copy.wait()
+        if i + flight < len(copies):
+            copies[i + flight].start()
+        cols = slice(i * step, (i + 1) * step)
+        acc = dot(turned[0], held[i, 0])
         for k in range(1, 4):
-            acc = acc + dot(turned[k], acts[k, rows, cols])
+            acc = acc + dot(turned[k], held[i, k])
         if other:
             acc = acc + before[0][:, cols]
         out[:, cols] = acc.astype(out.dtype)
 
 
-def last_call(grad_m, grad_o, held, side, dtype, *joined):
-    _, tokens, wide = held.shape
-    half, width = tokens // 2, grad_m.shape[2] // 2
-    scratch = [pltpu.VMEM((4, width, half), BF)]
-    flops = 4 * tokens * width * wide
-    first = call(
-        functools.partial(last_kernel, side, False),
-        [like((width, wide), F32)],
-        grad_m, held, scratch=scratch, flops=flops,
-    )
-    return call(
-        functools.partial(last_kernel, side, True),
-        [like((width, wide + sum(j.shape[1] for j in joined)), dtype)],
-        grad_o, held, first, *joined, scratch=scratch, flops=flops,
-    )
+def last_call(grad_m, grad_o, row, side, dtype, *joined):
+    _, tokens, wide = row.shape
+    half, width, step = tokens // 2, grad_m.shape[2] // 2, 256
+
+    def part(other, out, grad, *more):
+        return pl.pallas_call(
+            functools.partial(last_kernel, side, other),
+            out_shape=out,
+            in_specs=[VMEM, ANY] + [VMEM] * len(more),
+            out_specs=VMEM,
+            scratch_shapes=[
+                pltpu.VMEM((4, width, half), BF),
+                pltpu.VMEM((wide // step, 4, half, step), BF),
+                pltpu.SemaphoreType.DMA((wide // step,)),
+            ],
+            compiler_params=pltpu.CompilerParams(vmem_limit_bytes=32 * 1024 * 1024),
+            cost_estimate=pl.CostEstimate(
+                flops=4 * tokens * width * wide, bytes_accessed=4 * tokens * wide, transcendentals=0
+            ),
+        )(grad, row, *more)
+
+    first = part(False, like((width, wide), F32), grad_m)
+    shape = (width, wide + sum(j.shape[1] for j in joined))
+    return part(True, like(shape, dtype), grad_o, first, *joined)
 
 
 def term_kernel(codes, own, message, keep, s1, s2, s3):
@@ -247,17 +247,15 @@
     terms = [terms[0]] + [shift(terms[k], "x", 4, k) for k in (1, 2, 3)]
 
     barrier = lax.optimization_barrier
-    blocks, row = barrier((blocks, row))
+    blocks, row, terms[0] = barrier((blocks, row, terms[0]))
     split = call(spread_kernel, [like((4, 8, sub, 2 * width))], blocks, scratch=[pltpu.VMEM((sub, rank), BF)])
-    split, row = barrier((split, row))
-    held = hold(row)
     grad = lax.all_to_all(split.reshape(32, sub, 2 * width), ("x", "z", "y_hi"), 0, 0)
     grad = grad.reshape(4, half, 2 * width)
-    grad, held, *terms = barrier((grad, held, *terms))
+    grad, *terms = barrier((grad, *terms))
     grad_o = swap(grad, "core")
     term_o, term_a = call(term_sum_kernel, [like((width, outs), F32), like((width, outs))], *terms)
-    away = swap(last_call(grad, grad_o, held, 0, BF, term_a), "y_lo").astype(F32)
-    here = last_call(grad, grad_o, held, 1, F32)
+    away = swap(last_call(grad, grad_o, row, 0, BF, term_a), "y_lo").astype(F32)
+    here = last_call(grad, grad_o, row, 1, F32)
     here, term_o = barrier((here, term_o))
     return (((term_o + away[:, wide:]) * scale).T, (here + away[:, :wide]) * scale)
 

time: 188 us -> 200 us (1.064)
  blocking collectives: 43.4 us -> 23.9 us
  waiting for transfers between devices: 61.6 us -> 78.1 us
  Pallas kernels: 20.7 us -> 30.8 us
  starting transfers between devices: 23.3 us -> 26.6 us
    all_to_all x1 -> x0, blocking collectives: 19.5 us -> none  [local(): blocks = lax.all_to_all(partial, ZY, 0, 0)]
    pallas_call x1 -> x4, Pallas kernels: 0.53 us -> 15.9 us  [part(): pl.pallas_call(functools.partial(last_kernel, side, other), out_shape=out...]
    all_to_all x0 -> x1, waiting for transfers between devices: none -> 11.7 us  [local(): blocks = lax.all_to_all(partial, ZY, 0, 0)]
    pallas_call x9 -> x5, Pallas kernels: 14.4 us -> 9.08 us  [call(): pl.pallas_call(body, out_shape=outs if len(outs) > 1 else outs[0], in_spe...]
    ppermute x9, waiting for transfers between devices: 49.1 us -> 53.9 us  [shift(): lax.ppermute(array, axis, [(i, (i + step) % size) for i in range(size)])]
    all_to_all x0 -> x1, starting transfers between devices: none -> 3.56 us  [local(): blocks = lax.all_to_all(partial, ZY, 0, 0)]
    unnamed x29 -> x47, local copies, waits for them, and re-layouts: 21.9 us -> 23.2 us
  transfers between devices with their start and end apart: 12 -> 13, of which waited for: 6 -> 7; matrix products, arithmetic and copies ran while one was open for 0% -> 0% of each run, Pallas kernels for 10% -> 14%
where the time goes in v14:
time: 200 us; the launch traced here: 199 us
  waiting for transfers between devices  78.1 us (39%)
  Pallas kernels  30.8 us (15%)
  starting transfers between devices  26.6 us (13%)
  blocking collectives  23.9 us (12%)
  local copies, waits for them, and re-layouts  23.3 us (12%)
  between operations  14.3 us (7%)
  other arithmetic  2.17 us (1%)
    ppermute x9, waiting for transfers between devices, shift(): lax.ppermute(array, axis, [(i, (i + step) % size) for i in range(size)])  53.9 us
    all_to_all x1, blocking collectives, local(): blocks = lax.all_to_all(mine, ZY, 0, 0)  23.9 us
    unnamed x47, local copies, waits for them, and re-layouts  23.2 us
    pallas_call x4, Pallas kernels, part(): pl.pallas_call(functools.partial(last_kernel, side, other), out_shape=out...  15.9 us
    ppermute x9, starting transfers between devices, shift(): lax.ppermute(array, axis, [(i, (i + step) % size) for i in range(size)])  13.6 us
    all_to_all x1, waiting for transfers between devices, local(): codes = lax.all_to_all(codes, ZY, 0, 0).reshape(rank, half)  11.8 us
    all_to_all x1, waiting for transfers between devices, local(): blocks = lax.all_to_all(partial, ZY, 0, 0)  11.7 us
    pallas_call x5, Pallas kernels, call(): pl.pallas_call(body, out_shape=outs if len(outs) > 1 else outs[0], in_spe...  9.08 us
  transfers between devices with their start and end apart: 13, of which 7 were waited for; matrix products, arithmetic and copies ran while one was open for 0% of the time, Pallas kernels for 14%

profile of v14, /device:TPU:1, one launch (start us, length us, event | category | flops | bytes accessed | tf_op | source)
XLA Modules:
  0.0 199.1 jit_solution(15573513319743714506)
XLA Ops:
  8.7 3.1 %copy-done.1 = bf16[2048,1792]{1,0:T(8,128)(2,1)S(1)} copy-done((bf16[2048,1792]{1,0:T(8,128)(2,1)S(1)}, bf16[2048,1792]{1,0:T(8,128)(2,1)}, u32[]{:S(2)}) %copy-start.1) | copy-done | bytes 7340056
  11.7 2.9 %shard_map.60 = f32[2048,256]{1,0:T(8,128)S(1)} custom-call(bf16[512,1792]{1,0:T(8,128)(2,1)S(1)} %copy-done.2, bf16[2048,1792]{1,0:T(8,128)(2,1)S(1)} %copy-done.1), custom_call_target="tpu_custom_call" | custom-call | flops 1879048192 | bytes 7340032 | tf_op jit(solution)/shard_map/pallas_call | solution.py:69
  16.3 2.9 %shard_map.59 = f32[2048,256]{1,0:T(8,128)S(1)} custom-call(bf16[512,1792]{1,0:T(8,128)(2,1)S(1)} %copy-done.2, bf16[2048,1792]{1,0:T(8,128)(2,1)S(1)} %copy-done.1), custom_call_target="tpu_custom_call" | custom-call | flops 1879048192 | bytes 7340032 | tf_op jit(solution)/shard_map/pallas_call | solution.py:69
  19.2 2.8 %collective-permute-done = f32[2048,256]{1,0:T(8,128)S(1)} collective-permute-done((f32[2048,256]{1,0:T(8,128)S(1)}, f32[2048,256]{1,0:T(8,128)S(1)}, u32[]{:S(2)}, u32[]{:S(2)}) %collective-permute-start) | collective-permute-done | bytes 2097184 | tf_op jit(solution)/shard_map/ppermute | solution.py:24
  22.4 23.9 %all_to_all.20.blocks = bf16[8,256,256]{2,1,0:T(8,128)(2,1)S(1)} all-to-all(bf16[8,256,256]{2,1,0:T(8,128)(2,1)S(1)} %bitcast.19), channel_id=1, replica_groups=mesh['y_lo'=2,'x'=4,'z'=4,'y_hi'=2,'core'=2] {'z','y_hi'}, dimensions={0} | all-to-all | bytes 2097152 | tf_op jit(solution)/shard_map/all_to_all | solution.py:227
  47.3 3.6 %all-to-all-start.1 = ((bf16[8,256,256]{2,1,0:T(8,128)(2,1)}), bf16[8,256,256]{2,1,0:T(8,128)(2,1)S(1)}, u32[]{:S(2)}, u32[]{:S(2)}) async-start(bf16[8,256,256]{2,1,0:T(8,128)(2,1)} %shard_map.61), calls=%async_computation.1 | async-start | bytes 2097152 | tf_op jit(solution)/shard_map/all_to_all | solution.py:229
  51.1 1.9 collective-permute-start.1
  54.2 11.8 %all-to-all-done.1 = bf16[8,256,256]{2,1,0:T(8,128)(2,1)S(1)} async-done(((bf16[8,256,256]{2,1,0:T(8,128)(2,1)}), bf16[8,256,256]{2,1,0:T(8,128)(2,1)S(1)}, u32[]{:S(2)}, u32[]{:S(2)}) %all-to-all-start.1) | async-done | bytes 1048608 | tf_op jit(solution)/shard_map/all_to_all | solution.py:229
  66.0 6.2 %shard_map.62 = (bf16[256,512]{1,0:T(8,128)(2,1)S(1)}, bf16[2560,256]{1,0:T(8,128)(2,1)}, bf16[8,32,2048]{2,1,0:T(8,128)(2,1)}) custom-call(bf16[2048,256]{1,0:T(8,128)(2,1)S(1)} %bitcast.16, bf16[512,256]{1,0:T(8,128)(2,1)S(1)} %bitcast.18, bf16[512,256]{1,0:T(8,128)(2,1)S(1)} %collective-permute-done.1.far, bf16[512,2048]{1,0:T(8,128)(2,1)} %a0.1, ...), custom_call_target="tpu_custom_call" | custom-call | flops 2147483648 | bytes 8388608 | tf_op jit(solution)/shard_map/pallas_call | solution.py:33
  72.9 3.1 %collective-permute-start.3 = (bf16[2560,256]{1,0:T(8,128)(2,1)}, bf16[2560,256]{1,0:T(8,128)(2,1)S(1)}, u32[]{:S(2)}, u32[]{:S(2)}) collective-permute-start(bf16[2560,256]{1,0:T(8,128)(2,1)} %get-tuple-element.23), channel_id=1, source_target_pairs={{0,1},{1,0},{2,3},{3,2},{4,5},{5,4},{6,7},{7,6},{8,9},{9,8},{10,11... | collective-permute-start | bytes 3932168 | tf_op jit(solution)/shard_map/ppermute | solution.py:24
  76.0 3.6 %all-to-all-start.2 = ((bf16[8,32,2048]{2,1,0:T(8,128)(2,1)}), bf16[8,32,2048]{2,1,0:T(8,128)(2,1)S(1)}, u32[]{:S(2)}, u32[]{:S(2)}) async-start(bf16[8,32,2048]{2,1,0:T(8,128)(2,1)} %get-tuple-element.21), calls=%async_computation.2 | async-start | bytes 2097152 | tf_op jit(solution)/shard_map/all_to_all | solution.py:238
  85.2 11.7 %all-to-all-done.2.blocks = bf16[8,32,2048]{2,1,0:T(8,128)(2,1)S(1)} async-done(((bf16[8,32,2048]{2,1,0:T(8,128)(2,1)}), bf16[8,32,2048]{2,1,0:T(8,128)(2,1)S(1)}, u32[]{:S(2)}, u32[]{:S(2)}) %all-to-all-start.2) | async-done | bytes 1048608 | tf_op jit(solution)/shard_map/all_to_all | solution.py:238
  100.4 5.8 %all-to-all-start.3 = ((bf16[32,32,512]{2,1,0:T(8,128)(2,1)}), bf16[32,32,512]{2,1,0:T(8,128)(2,1)}, u32[]{:S(2)}, u32[]{:S(2)}) async-start(bf16[32,32,512]{2,1,0:T(8,128)(2,1)} %bitcast.15), calls=%async_computation.3 | async-start | bytes 2097152 | tf_op jit(solution)/shard_map/all_to_all | solution.py:252
  107.5 2.4 %collective-permute-start.5 = (bf16[2,256,512]{2,1,0:T(8,128)(2,1)}, bf16[2,256,512]{2,1,0:T(8,128)(2,1)S(1)}, u32[]{:S(2)}, u32[]{:S(2)}) collective-permute-start(bf16[2,256,512]{2,1,0:T(8,128)(2,1)} %copy-done.15), channel_id=1, source_target_pairs={{0,32},{16,48},{32,0},{48,16},{1,33},{17,49},{33,1},{49,17},{2,34}... | collective-permute-start | bytes 1572872 | tf_op jit(solution)/shard_map/ppermute | solution.py:24
  111.1 20.6 %collective-permute-done.4.r1 = bf16[2,256,512]{2,1,0:T(8,128)(2,1)S(1)} collective-permute-done((bf16[2,256,512]{2,1,0:T(8,128)(2,1)}, bf16[2,256,512]{2,1,0:T(8,128)(2,1)S(1)}, u32[]{:S(2)}, u32[]{:S(2)}) %collective-permute-start.4) | collective-permute-done | bytes 524320 | tf_op jit(solution)/shard_map/ppermute | solution.py:24
  132.5 10.3 %collective-permute-done.5.r2 = bf16[2,256,512]{2,1,0:T(8,128)(2,1)S(1)} collective-permute-done((bf16[2,256,512]{2,1,0:T(8,128)(2,1)}, bf16[2,256,512]{2,1,0:T(8,128)(2,1)S(1)}, u32[]{:S(2)}, u32[]{:S(2)}) %collective-permute-start.5) | collective-permute-done | bytes 524320 | tf_op jit(solution)/shard_map/ppermute | solution.py:24
  144.4 1.6 collective-permute-start.7
  150.5 3.1 %copy-done = bf16[2048,1792]{1,0:T(8,128)(2,1)S(1)} copy-done((bf16[2048,1792]{1,0:T(8,128)(2,1)S(1)}, bf16[2048,1792]{1,0:T(8,128)(2,1)}, u32[]{:S(2)}) %copy-start) | copy-done | bytes 7340056
  153.6 4.7 %shard_map.68.refs_0_ = f32[256,1792]{1,0:T(8,128)S(1)} custom-call(bf16[4,256,512]{2,1,0:T(8,128)(2,1)} %bitcast.6.grad, bf16[4,512,1792]{2,1,0:T(8,128)(2,1)S(1)} %bitcast.9), custom_call_target="tpu_custom_call" | custom-call | flops 939524096 | bytes 3670016 | tf_op jit(solution)/shard_map/pallas_call | solution.py:164
  158.4 3.3 %shard_map.69 = bf16[256,2304]{1,0:T(8,128)(2,1)S(1)} custom-call(bf16[4,256,512]{2,1,0:T(8,128)(2,1)S(1)} %collective-permute-done.7.grad, bf16[4,512,1792]{2,1,0:T(8,128)(2,1)S(1)} %bitcast.12, f32[256,1792]{1,0:T(8,128)S(1)} %shard_map.68.refs_0_, bf16[256,512]{1,0:T(8,128)(2,1)S(1)} %get-tuple-element.38.refs_1_), custom_call_target="tpu_custom_call" | custom-call | flops 939524096 | bytes 3670016 | tf_op jit(solution)/shard_map/pallas_call | solution.py:164
  162.3 4.5 %shard_map.65.refs_0_ = f32[256,1792]{1,0:T(8,128)S(1)} custom-call(bf16[4,256,512]{2,1,0:T(8,128)(2,1)} %bitcast.6.grad, bf16[4,512,1792]{2,1,0:T(8,128)(2,1)S(1)} %bitcast.13), custom_call_target="tpu_custom_call" | custom-call | flops 939524096 | bytes 3670016 | tf_op jit(solution)/shard_map/pallas_call | solution.py:164
  166.8 3.3 %shard_map.66 = f32[256,1792]{1,0:T(8,128)S(1)} custom-call(bf16[4,256,512]{2,1,0:T(8,128)(2,1)S(1)} %collective-permute-done.7.grad, bf16[4,512,1792]{2,1,0:T(8,128)(2,1)S(1)} %bitcast.14, f32[256,1792]{1,0:T(8,128)S(1)} %shard_map.65.refs_0_), custom_call_target="tpu_custom_call" | custom-call | flops 939524096 | bytes 3670016 | tf_op jit(solution)/shard_map/pallas_call | solution.py:164
  170.2 19.2 %collective-permute-done.8 = bf16[256,2304]{1,0:T(8,128)(2,1)S(1)} collective-permute-done((bf16[256,2304]{1,0:T(8,128)(2,1)S(1)}, bf16[256,2304]{1,0:T(8,128)(2,1)S(1)}, u32[]{:S(2)}, u32[]{:S(2)}) %collective-permute-start.8) | collective-permute-done | bytes 1179680 | tf_op jit(solution)/shard_map/ppermute | solution.py:24
  189.6 1.6 fusion
  (68 shorter events, 26.8 us)
Async XLA Ops:
  7.2 1.5 copy-start.2
  7.2 90.8 %all-gather.3.cloned.1.call-start = ((), (), s32[]{:S(2)}) async-start(), calls=%async_computation.4 | async-start | bytes 9175040 | tf_op jit(solution)/shard_map/all_gather | solution.py:219
  8.7 3.1 %copy-start.1 = (bf16[2048,1792]{1,0:T(8,128)(2,1)S(1)}, bf16[2048,1792]{1,0:T(8,128)(2,1)}, u32[]{:S(2)}) copy-start(bf16[2048,1792]{1,0:T(8,128)(2,1)} %b.3) | copy-start | bytes 22020100
  14.7 7.4 %collective-permute-start = (f32[2048,256]{1,0:T(8,128)S(1)}, f32[2048,256]{1,0:T(8,128)S(1)}, u32[]{:S(2)}, u32[]{:S(2)}) collective-permute-start(f32[2048,256]{1,0:T(8,128)S(1)} %shard_map.60), channel_id=1, source_target_pairs={{0,1},{1,0},{2,3},{3,2},{4,5},{5,4},{6,7},{7,6},{8,9},{9,8},{10,11... | collective-permute-start | bytes 6291464 | tf_op jit(solution)/shard_map/ppermute | solution.py:24
  16.2 38.0 %collective-permute-start.2 = (bf16[512,2048]{1,0:T(8,128)(2,1)}, bf16[512,2048]{1,0:T(8,128)(2,1)}, u32[]{:S(2)}, u32[]{:S(2)}) collective-permute-start(bf16[512,2048]{1,0:T(8,128)(2,1)} %a0.1), channel_id=1, source_target_pairs={{0,1},{1,0},{2,3},{3,2},{4,5},{5,4},{6,7},{7,6},{8,9},{9,8},{10,11... | collective-permute-start | bytes 6291464 | tf_op jit(solution)/shard_map/ppermute | solution.py:24
  46.2 4.7 %copy-start.19 = (bf16[512,512]{1,0:T(8,128)(2,1)S(1)}, bf16[512,512]{1,0:T(8,128)(2,1)}, u32[]{:S(2)}) copy-start(bf16[512,512]{1,0:T(8,128)(2,1)} %param.5) | copy-start | bytes 1572868
  47.3 18.6 %all-to-all-start.1 = ((bf16[8,256,256]{2,1,0:T(8,128)(2,1)}), bf16[8,256,256]{2,1,0:T(8,128)(2,1)S(1)}, u32[]{:S(2)}, u32[]{:S(2)}) async-start(bf16[8,256,256]{2,1,0:T(8,128)(2,1)} %shard_map.61), calls=%async_computation.1 | async-start | bytes 2097152 | tf_op jit(solution)/shard_map/all_to_all | solution.py:229
  51.1 3.1 %collective-permute-start.1 = (bf16[512,256]{1,0:T(8,128)(2,1)S(1)}, bf16[512,256]{1,0:T(8,128)(2,1)S(1)}, u32[]{:S(2)}, u32[]{:S(2)}) collective-permute-start(bf16[512,256]{1,0:T(8,128)(2,1)S(1)} %bitcast.20), channel_id=1, source_target_pairs={{0,1},{1,0},{2,3},{3,2},{4,5},{5,4},{6,7},{7,6},{8,9},{9,8},{10,11... | collective-permute-start | bytes 786440 | tf_op jit(solution)/shard_map/ppermute | solution.py:24
  72.9 6.7 %collective-permute-start.3 = (bf16[2560,256]{1,0:T(8,128)(2,1)}, bf16[2560,256]{1,0:T(8,128)(2,1)S(1)}, u32[]{:S(2)}, u32[]{:S(2)}) collective-permute-start(bf16[2560,256]{1,0:T(8,128)(2,1)} %get-tuple-element.23), channel_id=1, source_target_pairs={{0,1},{1,0},{2,3},{3,2},{4,5},{5,4},{6,7},{7,6},{8,9},{9,8},{10,11... | collective-permute-start | bytes 3932168 | tf_op jit(solution)/shard_map/ppermute | solution.py:24
  76.0 20.9 %all-to-all-start.2 = ((bf16[8,32,2048]{2,1,0:T(8,128)(2,1)}), bf16[8,32,2048]{2,1,0:T(8,128)(2,1)S(1)}, u32[]{:S(2)}, u32[]{:S(2)}) async-start(bf16[8,32,2048]{2,1,0:T(8,128)(2,1)} %get-tuple-element.21), calls=%async_computation.2 | async-start | bytes 2097152 | tf_op jit(solution)/shard_map/all_to_all | solution.py:238
  96.9 1.1 copy-start.4
  98.0 1.2 copy-start.5
  99.2 59.2 %slice-start = ((s8[7340032]{0:T(1024)(128)(4,1)}), s8[3145728]{0:T(1024)(128)(4,1)S(1)}, s32[]{:S(2)}) async-start(s8[7340032]{0:T(1024)(128)(4,1)} %bitcast.10), calls=%async_computation.5 | async-start | bytes 6291456
  100.4 43.9 %all-to-all-start.3 = ((bf16[32,32,512]{2,1,0:T(8,128)(2,1)}), bf16[32,32,512]{2,1,0:T(8,128)(2,1)}, u32[]{:S(2)}, u32[]{:S(2)}) async-start(bf16[32,32,512]{2,1,0:T(8,128)(2,1)} %bitcast.15), calls=%async_computation.3 | async-start | bytes 2097152 | tf_op jit(solution)/shard_map/all_to_all | solution.py:252
  106.3 25.4 %collective-permute-start.4 = (bf16[2,256,512]{2,1,0:T(8,128)(2,1)}, bf16[2,256,512]{2,1,0:T(8,128)(2,1)S(1)}, u32[]{:S(2)}, u32[]{:S(2)}) collective-permute-start(bf16[2,256,512]{2,1,0:T(8,128)(2,1)} %copy-done.16), channel_id=1, source_target_pairs={{0,16},{16,32},{32,48},{48,0},{1,17},{17,33},{33,49},{49,1},{2,18}... | collective-permute-start | bytes 1572872 | tf_op jit(solution)/shard_map/ppermute | solution.py:24
  107.5 35.2 %collective-permute-start.5 = (bf16[2,256,512]{2,1,0:T(8,128)(2,1)}, bf16[2,256,512]{2,1,0:T(8,128)(2,1)S(1)}, u32[]{:S(2)}, u32[]{:S(2)}) collective-permute-start(bf16[2,256,512]{2,1,0:T(8,128)(2,1)} %copy-done.15), channel_id=1, source_target_pairs={{0,32},{16,48},{32,0},{48,16},{1,33},{17,49},{33,1},{49,17},{2,34}... | collective-permute-start | bytes 1572872 | tf_op jit(solution)/shard_map/ppermute | solution.py:24
  109.9 33.6 %collective-permute-start.6 = (bf16[2,256,512]{2,1,0:T(8,128)(2,1)}, bf16[2,256,512]{2,1,0:T(8,128)(2,1)S(1)}, u32[]{:S(2)}, u32[]{:S(2)}) collective-permute-start(bf16[2,256,512]{2,1,0:T(8,128)(2,1)} %copy-done.14), channel_id=1, source_target_pairs={{0,48},{16,0},{32,16},{48,32},{1,49},{17,1},{33,17},{49,33},{2,50}... | collective-permute-start | bytes 1572872 | tf_op jit(solution)/shard_map/ppermute | solution.py:24
  144.4 14.0 %collective-permute-start.7 = (bf16[4,256,512]{2,1,0:T(8,128)(2,1)}, bf16[4,256,512]{2,1,0:T(8,128)(2,1)S(1)}, u32[]{:S(2)}, u32[]{:S(2)}) collective-permute-start(bf16[4,256,512]{2,1,0:T(8,128)(2,1)} %bitcast.6.grad), channel_id=1, source_target_pairs={{0,1},{1,0},{2,3},{3,2},{4,5},{5,4},{6,7},{7,6},{8,9},{9,8},{10,11... | collective-permute-start | bytes 3145736 | tf_op jit(solution)/shard_map/ppermute | solution.py:24
  146.0 1.2 copy-start.7
  147.2 1.0 copy-start.9
  148.2 1.0 copy-start.11
  150.5 3.1 %copy-start = (bf16[2048,1792]{1,0:T(8,128)(2,1)S(1)}, bf16[2048,1792]{1,0:T(8,128)(2,1)}, u32[]{:S(2)}) copy-start(bf16[2048,1792]{1,0:T(8,128)(2,1)} %all-gather.3.cloned.1.call-done) | copy-start | bytes 22020100
  153.6 4.7 %slice-start.1 = ((s8[7340032]{0:T(1024)(128)(4,1)}), s8[4194304]{0:T(1024)(128)(4,1)S(1)}, s32[]{:S(2)}) async-start(s8[7340032]{0:T(1024)(128)(4,1)} %bitcast.10), calls=%async_computation.6 | async-start | bytes 8388608
  161.7 27.7 %collective-permute-start.8 = (bf16[256,2304]{1,0:T(8,128)(2,1)S(1)}, bf16[256,2304]{1,0:T(8,128)(2,1)S(1)}, u32[]{:S(2)}, u32[]{:S(2)}) collective-permute-start(bf16[256,2304]{1,0:T(8,128)(2,1)S(1)} %shard_map.69), channel_id=1, source_target_pairs={{0,64},{64,0},{1,65},{65,1},{2,66},{66,2},{3,67},{67,3},{4,68},{68... | collective-permute-start | bytes 3538952 | tf_op jit(solution)/shard_map/ppermute | solution.py:24
  (11 other events, 9.5 us)
Sparse Core Ops, SparseCore 0:
  9.7 77.5 all-gather.2

commit v15 on v10

--- a/solution.py
+++ b/solution.py
@@ -112,47 +112,51 @@
             partial[i, :, cols] = term[i * sub : (i + 1) * sub].astype(BF)
 
 
-def spread_kernel(blocks, away, own, held):
+def spread_kernel(blocks, out, held):
     y_lo = lax.axis_index("y_lo")
     held[...] = total(blocks).astype(BF)
     rank = held.shape[1]
     width = rank // 8
-    for out, side in ((away, 1 - y_lo), (own, y_lo)):
+    for at, side in ((0, 1 - y_lo), (width, y_lo)):
         for x in range(4):
             start = pl.multiple_of(side * (rank // 2) + x * width, width)
             piece = held[:, pl.ds(start, width)]
             for i in range(out.shape[1]):
-                out[x, i] = piece
-
-
-def last_kernel(grad_m, grad_o, acts, *refs):
+                out[x, i, :, at : at + width] = piece
+
+
+def last_kernel(side, grad_m, grad_o, acts, *refs):
     joined, (out, turned, held, sems) = refs[:-4], refs[-4:]
     core = lax.axis_index("core")
-    half, wide, step = grad_m.shape[1], acts.shape[2], held.shape[3]
+    half, wide, width = grad_m.shape[1], acts.shape[2], out.shape[0]
+    step, flight = held.shape[3], 4
     copies = [
         pltpu.make_async_copy(acts.at[:, :, pl.ds(i * step, step)], held.at[i], sems.at[i])
         for i in range(wide // step)
     ]
-    for copy in copies:
+    for copy in copies[:flight]:
         copy.start()
+    at = slice(side * width, (side + 1) * width)
     for k in range(4):
-        turned[k, :, pl.ds(pl.multiple_of(core * half, half), half)] = grad_m[k].T
-        turned[k, :, pl.ds(pl.multiple_of((1 - core) * half, half), half)] = grad_o[k].T
+        turned[k, :, pl.ds(pl.multiple_of(core * half, half), half)] = grad_m[k, :, at].T
+        turned[k, :, pl.ds(pl.multiple_of((1 - core) * half, half), half)] = grad_o[k, :, at].T
     for ref in joined:
         out[:, wide:] = ref[...]
     for i, copy in enumerate(copies):
         copy.wait()
+        if i + flight < len(copies):
+            copies[i + flight].start()
         acc = dot(turned[0], held[i, 0])
         for k in range(1, 4):
             acc = acc + dot(turned[k], held[i, k])
         out[:, i * step : (i + 1) * step] = acc.astype(out.dtype)
 
 
-def last_call(grad_m, grad_o, row, dtype, *joined):
+def last_call(grad_m, grad_o, row, side, dtype, *joined):
     _, tokens, wide = row.shape
-    width, step = grad_m.shape[2], 256
+    width, step = grad_m.shape[2] // 2, 256
     return pl.pallas_call(
-        last_kernel,
+        functools.partial(last_kernel, side),
         out_shape=like((width, wide + sum(j.shape[1] for j in joined)), dtype),
         in_specs=[VMEM, VMEM, ANY] + [VMEM] * len(joined),
         out_specs=VMEM,
@@ -230,25 +234,20 @@
         codes, own, swap(message, "core"),
         flops=2 * tokens * rank * outs,
     )
-    terms = [terms[0]] + [shift(terms[k], "x", 4, k) for k in (1, 2, 3)]
-
-    blocks, row = lax.optimization_barrier((blocks, row))
-    spread = like((4, 8, sub, width))
-    split_a, split_o = call(spread_kernel, [spread, spread], blocks, scratch=[pltpu.VMEM((sub, rank), BF)])
-
-    def gather(split):
-        split = lax.all_to_all(split.reshape(32, sub, width), ("x", "z", "y_hi"), 0, 0)
-        return split.reshape(4, half, width)
-
-    grad = gather(split_a)
-    grad, *terms = lax.optimization_barrier((grad, *terms))
+    near = [shift(terms[k], "x", 4, k) for k in (1, 3)]
+
+    barrier = lax.optimization_barrier
+    blocks, row, near, later = barrier((blocks, row, near, terms[2]))
+    terms = [terms[0], shift(later, "x", 4, 2)] + near
+    split = call(spread_kernel, [like((4, 8, sub, 2 * width))], blocks, scratch=[pltpu.VMEM((sub, rank), BF)])
+    grad = lax.all_to_all(split.reshape(32, sub, 2 * width), ("x", "z", "y_hi"), 0, 0)
+    grad = grad.reshape(4, half, 2 * width)
+    grad, *terms = barrier((grad, *terms))
+    grad_o = swap(grad, "core")
     term_o, term_a = call(term_sum_kernel, [like((width, outs), F32), like((width, outs))], *terms)
-    away = last_call(grad, swap(grad, "core"), row, BF, term_a)
-    away, split_o = lax.optimization_barrier((away, split_o))
-    away = swap(away, "y_lo").astype(F32)
-    grad = gather(split_o)
-    here = last_call(grad, swap(grad, "core"), row, F32)
-    here, term_o = lax.optimization_barrier((here, term_o))
+    away = swap(last_call(grad, grad_o, row, 0, BF, term_a), "y_lo").astype(F32)
+    here = last_call(grad, grad_o, row, 1, F32)
+    here, term_o = barrier((here, term_o))
     return (((term_o + away[:, wide:]) * scale).T, (here + away[:, :wide]) * scale)
 
 

time: 176 us -> 184 us (1.045)
  waiting for transfers between devices: 66.4 us -> 71.8 us
  local copies, waits for them, and re-layouts: 6.74 us -> 11 us
  Pallas kernels: 30.6 us -> 28.4 us
    ppermute x10 -> x9, waiting for transfers between devices: 22.1 us -> 50.6 us  [shift(): lax.ppermute(array, axis, [(i, (i + step) % size) for i in range(size)])]
    all_to_all x2 -> x1, waiting for transfers between devices: 22.7 us -> 0.01 us  [local(): lax.all_to_all(split.reshape(32, sub, 2 * width), ('x', 'z', 'y_hi'), 0, 0)]
    unnamed x15 -> x23, local copies, waits for them, and re-layouts: 6.7 us -> 11 us
    pallas_call x5, Pallas kernels: 13.1 us -> 10.8 us  [call(): pl.pallas_call(body, out_shape=outs if len(outs) > 1 else outs[0], in_spe...]
    ppermute x10 -> x9, starting transfers between devices: 14.4 us -> 15.7 us  [shift(): lax.ppermute(array, axis, [(i, (i + step) % size) for i in range(size)])]
    all_to_all x2 -> x1, starting transfers between devices: 10.1 us -> 9.57 us  [local(): lax.all_to_all(split.reshape(32, sub, 2 * width), ('x', 'z', 'y_hi'), 0, 0)]
  transfers between devices with their start and end apart: 15 -> 13, of which waited for: 9 -> 8; matrix products, arithmetic and copies ran while one was open for 0% -> 0% of each run, Pallas kernels for 14% -> 12%
where the time goes in v15:
time: 184 us
  waiting for transfers between devices  71.8 us (39%)
  starting transfers between devices  32.4 us (18%)
  Pallas kernels  28.4 us (15%)
  blocking collectives  23.9 us (13%)
  between operations  14.2 us (8%)
  local copies, waits for them, and re-layouts  11 us (6%)
  other arithmetic  2.17 us (1%)
    ppermute x9, waiting for transfers between devices, shift(): lax.ppermute(array, axis, [(i, (i + step) % size) for i in range(size)])  50.6 us
    all_to_all x1, blocking collectives, local(): blocks = lax.all_to_all(mine, ZY, 0, 0)  23.9 us
    ppermute x9, starting transfers between devices, shift(): lax.ppermute(array, axis, [(i, (i + step) % size) for i in range(size)])  15.7 us
    all_to_all x1, waiting for transfers between devices, local(): codes = lax.all_to_all(codes, ZY, 0, 0).reshape(rank, half)  11.8 us
    pallas_call x2, Pallas kernels, last_call(): pl.pallas_call(functools.partial(last_kernel, side), out_shape=like((widt...  11.8 us
    unnamed x23, local copies, waits for them, and re-layouts  11 us
    pallas_call x5, Pallas kernels, call(): pl.pallas_call(body, out_shape=outs if len(outs) > 1 else outs[0], in_spe...  10.8 us
    all_to_all x1, starting transfers between devices, local(): lax.all_to_all(split.reshape(32, sub, 2 * width), ('x', 'z', 'y_hi'), 0, 0)  9.57 us
  transfers between devices with their start and end apart: 13, of which 8 were waited for; matrix products, arithmetic and copies ran while one was open for 0% of the time, Pallas kernels for 12%

profile of v15, /device:TPU:1, one launch (start us, length us, event | category | flops | bytes accessed | tf_op | source)
XLA Modules:
  0.0 183.8 jit_solution(10538907126657074722)
XLA Ops:
  8.7 3.1 %copy-done = bf16[2048,1792]{1,0:T(8,128)(2,1)S(1)} copy-done((bf16[2048,1792]{1,0:T(8,128)(2,1)S(1)}, bf16[2048,1792]{1,0:T(8,128)(2,1)}, u32[]{:S(2)}) %copy-start) | copy-done | bytes 7340056
  11.7 2.9 %shard_map.60 = f32[2048,256]{1,0:T(8,128)S(1)} custom-call(bf16[512,1792]{1,0:T(8,128)(2,1)S(1)} %copy-done.1, bf16[2048,1792]{1,0:T(8,128)(2,1)S(1)} %copy-done), custom_call_target="tpu_custom_call" | custom-call | flops 1879048192 | bytes 7340032 | tf_op jit(solution)/shard_map/pallas_call | solution.py:69
  14.7 1.5 collective-permute-start
  16.3 2.9 %shard_map.59 = f32[2048,256]{1,0:T(8,128)S(1)} custom-call(bf16[512,1792]{1,0:T(8,128)(2,1)S(1)} %copy-done.1, bf16[2048,1792]{1,0:T(8,128)(2,1)S(1)} %copy-done), custom_call_target="tpu_custom_call" | custom-call | flops 1879048192 | bytes 7340032 | tf_op jit(solution)/shard_map/pallas_call | solution.py:69
  19.2 2.8 %collective-permute-done = f32[2048,256]{1,0:T(8,128)S(1)} collective-permute-done((f32[2048,256]{1,0:T(8,128)S(1)}, f32[2048,256]{1,0:T(8,128)S(1)}, u32[]{:S(2)}, u32[]{:S(2)}) %collective-permute-start) | collective-permute-done | bytes 2097184 | tf_op jit(solution)/shard_map/ppermute | solution.py:24
  22.4 23.9 %all_to_all.20.blocks = bf16[8,256,256]{2,1,0:T(8,128)(2,1)S(1)} all-to-all(bf16[8,256,256]{2,1,0:T(8,128)(2,1)S(1)} %bitcast.17), channel_id=1, replica_groups=mesh['y_lo'=2,'x'=4,'z'=4,'y_hi'=2,'core'=2] {'z','y_hi'}, dimensions={0} | all-to-all | bytes 2097152 | tf_op jit(solution)/shard_map/all_to_all | solution.py:217
  47.3 3.6 %all-to-all-start.1 = ((bf16[8,256,256]{2,1,0:T(8,128)(2,1)}), bf16[8,256,256]{2,1,0:T(8,128)(2,1)S(1)}, u32[]{:S(2)}, u32[]{:S(2)}) async-start(bf16[8,256,256]{2,1,0:T(8,128)(2,1)} %shard_map.61), calls=%async_computation.1 | async-start | bytes 2097152 | tf_op jit(solution)/shard_map/all_to_all | solution.py:219
  51.1 1.9 %collective-permute-start.1 = (bf16[512,256]{1,0:T(8,128)(2,1)S(1)}, bf16[512,256]{1,0:T(8,128)(2,1)S(1)}, u32[]{:S(2)}, u32[]{:S(2)}) collective-permute-start(bf16[512,256]{1,0:T(8,128)(2,1)S(1)} %bitcast.18), channel_id=1, source_target_pairs={{0,1},{1,0},{2,3},{3,2},{4,5},{5,4},{6,7},{7,6},{8,9},{9,8},{10,11... | collective-permute-start | bytes 786440 | tf_op jit(solution)/shard_map/ppermute | solution.py:24
  54.2 11.8 %all-to-all-done.1 = bf16[8,256,256]{2,1,0:T(8,128)(2,1)S(1)} async-done(((bf16[8,256,256]{2,1,0:T(8,128)(2,1)}), bf16[8,256,256]{2,1,0:T(8,128)(2,1)S(1)}, u32[]{:S(2)}, u32[]{:S(2)}) %all-to-all-start.1) | async-done | bytes 1048608 | tf_op jit(solution)/shard_map/all_to_all | solution.py:219
  66.0 6.2 %shard_map.62 = (bf16[256,512]{1,0:T(8,128)(2,1)S(1)}, bf16[2560,256]{1,0:T(8,128)(2,1)}, bf16[8,32,2048]{2,1,0:T(8,128)(2,1)}) custom-call(bf16[2048,256]{1,0:T(8,128)(2,1)S(1)} %bitcast.12, bf16[512,256]{1,0:T(8,128)(2,1)S(1)} %bitcast.14, bf16[512,256]{1,0:T(8,128)(2,1)S(1)} %collective-permute-done.1.far, bf16[512,2048]{1,0:T(8,128)(2,1)} %a0.1, ...), custom_call_target="tpu_custom_call" | custom-call | flops 2147483648 | bytes 8388608 | tf_op jit(solution)/shard_map/pallas_call | solution.py:33
  72.9 3.1 %collective-permute-start.3 = (bf16[2560,256]{1,0:T(8,128)(2,1)}, bf16[2560,256]{1,0:T(8,128)(2,1)S(1)}, u32[]{:S(2)}, u32[]{:S(2)}) collective-permute-start(bf16[2560,256]{1,0:T(8,128)(2,1)} %get-tuple-element.25), channel_id=1, source_target_pairs={{0,1},{1,0},{2,3},{3,2},{4,5},{5,4},{6,7},{7,6},{8,9},{9,8},{10,11... | collective-permute-start | bytes 3932168 | tf_op jit(solution)/shard_map/ppermute | solution.py:24
  76.0 3.6 %all-to-all-start.2 = ((bf16[8,32,2048]{2,1,0:T(8,128)(2,1)}), bf16[8,32,2048]{2,1,0:T(8,128)(2,1)S(1)}, u32[]{:S(2)}, u32[]{:S(2)}) async-start(bf16[8,32,2048]{2,1,0:T(8,128)(2,1)} %get-tuple-element.23), calls=%async_computation.2 | async-start | bytes 2097152 | tf_op jit(solution)/shard_map/all_to_all | solution.py:228
  82.9 2.1 %shard_map.63 = (f32[2,256,512]{2,1,0:T(8,128)S(1)}, bf16[2,256,512]{2,1,0:T(8,128)(2,1)}, bf16[2,256,512]{2,1,0:T(8,128)(2,1)S(1)}, bf16[2,256,512]{2,1,0:T(8,128)(2,1)}) custom-call(bf16[2048,256]{1,0:T(8,128)(2,1)S(1)} %bitcast.13, bf16[256,512]{1,0:T(8,128)(2,1)S(1)} %copy-done.8, bf16[2560,256]{1,0:T(8,128)(2,1)S(1)} %copy-done.5), custom_call_target="tpu_custom_call" | custom-call | flops 1073741824 | bytes 5242880 | tf_op jit(solution)/shard_map/pallas_call | solution.py:33
  86.1 2.1 %collective-permute-start.5 = (bf16[2,256,512]{2,1,0:T(8,128)(2,1)}, bf16[2,256,512]{2,1,0:T(8,128)(2,1)S(1)}, u32[]{:S(2)}, u32[]{:S(2)}) collective-permute-start(bf16[2,256,512]{2,1,0:T(8,128)(2,1)} %get-tuple-element.27), channel_id=1, source_target_pairs={{0,48},{16,0},{32,16},{48,32},{1,49},{17,1},{33,17},{49,33},{2,50}... | collective-permute-start | bytes 1572872 | tf_op jit(solution)/shard_map/ppermute | solution.py:24
  88.2 8.7 %all-to-all-done.2.blocks = bf16[8,32,2048]{2,1,0:T(8,128)(2,1)S(1)} async-done(((bf16[8,32,2048]{2,1,0:T(8,128)(2,1)}), bf16[8,32,2048]{2,1,0:T(8,128)(2,1)S(1)}, u32[]{:S(2)}, u32[]{:S(2)}) %all-to-all-start.2) | async-done | bytes 1048608 | tf_op jit(solution)/shard_map/all_to_all | solution.py:228
  96.9 3.1 %collective-permute-done.4.r2 = bf16[2,256,512]{2,1,0:T(8,128)(2,1)S(1)} collective-permute-done((bf16[2,256,512]{2,1,0:T(8,128)(2,1)}, bf16[2,256,512]{2,1,0:T(8,128)(2,1)S(1)}, u32[]{:S(2)}, u32[]{:S(2)}) %collective-permute-start.4) | collective-permute-done | bytes 524320 | tf_op jit(solution)/shard_map/ppermute | solution.py:24
  101.2 9.6 %all-to-all-start.3 = ((bf16[32,32,512]{2,1,0:T(8,128)(2,1)}), bf16[32,32,512]{2,1,0:T(8,128)(2,1)S(1)}, u32[]{:S(2)}, u32[]{:S(2)}) async-start(bf16[32,32,512]{2,1,0:T(8,128)(2,1)} %bitcast.5), calls=%async_computation.3 | async-start | bytes 2097152 | tf_op jit(solution)/shard_map/all_to_all | solution.py:243
  110.7 2.8 %collective-permute-start.6 = (bf16[2,256,512]{2,1,0:T(8,128)(2,1)}, bf16[2,256,512]{2,1,0:T(8,128)(2,1)S(1)}, u32[]{:S(2)}, u32[]{:S(2)}) collective-permute-start(bf16[2,256,512]{2,1,0:T(8,128)(2,1)} %copy-done.6), channel_id=1, source_target_pairs={{0,32},{16,48},{32,0},{48,16},{1,33},{17,49},{33,1},{49,17},{2,34}... | collective-permute-start | bytes 1572872 | tf_op jit(solution)/shard_map/ppermute | solution.py:24
  113.6 21.8 %collective-permute-done.6.r1 = bf16[2,256,512]{2,1,0:T(8,128)(2,1)S(1)} collective-permute-done((bf16[2,256,512]{2,1,0:T(8,128)(2,1)}, bf16[2,256,512]{2,1,0:T(8,128)(2,1)S(1)}, u32[]{:S(2)}, u32[]{:S(2)}) %collective-permute-start.6) | collective-permute-done | bytes 524320 | tf_op jit(solution)/shard_map/ppermute | solution.py:24
  136.2 2.3 %collective-permute-start.7 = (bf16[4,256,512]{2,1,0:T(8,128)(2,1)S(1)}, bf16[4,256,512]{2,1,0:T(8,128)(2,1)S(1)}, u32[]{:S(2)}, u32[]{:S(2)}) collective-permute-start(bf16[4,256,512]{2,1,0:T(8,128)(2,1)S(1)} %bitcast.9), channel_id=1, source_target_pairs={{0,1},{1,0},{2,3},{3,2},{4,5},{5,4},{6,7},{7,6},{8,9},{9,8},{10,11... | collective-permute-start | bytes 3145736 | tf_op jit(solution)/shard_map/ppermute | solution.py:24
  140.8 5.9 %shard_map.67 = bf16[256,2304]{1,0:T(8,128)(2,1)S(1)} custom-call(bf16[4,256,512]{2,1,0:T(8,128)(2,1)S(1)} %bitcast.10, bf16[4,256,512]{2,1,0:T(8,128)(2,1)S(1)} %collective-permute-done.7.grad_o, bf16[4,512,1792]{2,1,0:T(8,128)(2,1)} %bitcast.15, bf16[256,512]{1,0:T(8,128)(2,1)S(1)} %get-tuple-element.42.refs_0_), custom_call_target="tpu_custom_call" | custom-call | flops 1879048192 | bytes 7340032 | tf_op jit(solution)/shard_map/pallas_call | solution.py:158
  147.4 5.9 %shard_map.65 = f32[256,1792]{1,0:T(8,128)S(1)} custom-call(bf16[4,256,512]{2,1,0:T(8,128)(2,1)S(1)} %bitcast.11, bf16[4,256,512]{2,1,0:T(8,128)(2,1)S(1)} %collective-permute-done.7.grad_o, bf16[4,512,1792]{2,1,0:T(8,128)(2,1)} %bitcast.16), custom_call_target="tpu_custom_call" | custom-call | flops 1879048192 | bytes 7340032 | tf_op jit(solution)/shard_map/pallas_call | solution.py:158
  153.3 20.8 %collective-permute-done.8 = bf16[256,2304]{1,0:T(8,128)(2,1)S(1)} collective-permute-done((bf16[256,2304]{1,0:T(8,128)(2,1)S(1)}, bf16[256,2304]{1,0:T(8,128)(2,1)S(1)}, u32[]{:S(2)}, u32[]{:S(2)}) %collective-permute-start.8) | collective-permute-done | bytes 1179680 | tf_op jit(solution)/shard_map/ppermute | solution.py:24
  174.3 1.6 fusion
  (41 shorter events, 15.8 us)
Async XLA Ops:
  7.2 1.5 copy-start.1
  7.2 92.7 %all-gather.3.cloned.1.call-start = ((), (), s32[]{:S(2)}) async-start(), calls=%async_computation.4 | async-start | bytes 9175040 | tf_op jit(solution)/shard_map/all_gather | solution.py:209
  8.7 3.1 %copy-start = (bf16[2048,1792]{1,0:T(8,128)(2,1)S(1)}, bf16[2048,1792]{1,0:T(8,128)(2,1)}, u32[]{:S(2)}) copy-start(bf16[2048,1792]{1,0:T(8,128)(2,1)} %b.3) | copy-start | bytes 22020100
  14.7 7.4 %collective-permute-start = (f32[2048,256]{1,0:T(8,128)S(1)}, f32[2048,256]{1,0:T(8,128)S(1)}, u32[]{:S(2)}, u32[]{:S(2)}) collective-permute-start(f32[2048,256]{1,0:T(8,128)S(1)} %shard_map.60), channel_id=1, source_target_pairs={{0,1},{1,0},{2,3},{3,2},{4,5},{5,4},{6,7},{7,6},{8,9},{9,8},{10,11... | collective-permute-start | bytes 6291464 | tf_op jit(solution)/shard_map/ppermute | solution.py:24
  16.2 38.0 %collective-permute-start.2 = (bf16[512,2048]{1,0:T(8,128)(2,1)}, bf16[512,2048]{1,0:T(8,128)(2,1)}, u32[]{:S(2)}, u32[]{:S(2)}) collective-permute-start(bf16[512,2048]{1,0:T(8,128)(2,1)} %a0.1), channel_id=1, source_target_pairs={{0,1},{1,0},{2,3},{3,2},{4,5},{5,4},{6,7},{7,6},{8,9},{9,8},{10,11... | collective-permute-start | bytes 6291464 | tf_op jit(solution)/shard_map/ppermute | solution.py:24
  46.2 4.7 %copy-start.9 = (bf16[512,512]{1,0:T(8,128)(2,1)S(1)}, bf16[512,512]{1,0:T(8,128)(2,1)}, u32[]{:S(2)}) copy-start(bf16[512,512]{1,0:T(8,128)(2,1)} %param.5) | copy-start | bytes 1572868
  47.3 18.6 %all-to-all-start.1 = ((bf16[8,256,256]{2,1,0:T(8,128)(2,1)}), bf16[8,256,256]{2,1,0:T(8,128)(2,1)S(1)}, u32[]{:S(2)}, u32[]{:S(2)}) async-start(bf16[8,256,256]{2,1,0:T(8,128)(2,1)} %shard_map.61), calls=%async_computation.1 | async-start | bytes 2097152 | tf_op jit(solution)/shard_map/all_to_all | solution.py:219
  51.1 3.1 %collective-permute-start.1 = (bf16[512,256]{1,0:T(8,128)(2,1)S(1)}, bf16[512,256]{1,0:T(8,128)(2,1)S(1)}, u32[]{:S(2)}, u32[]{:S(2)}) collective-permute-start(bf16[512,256]{1,0:T(8,128)(2,1)S(1)} %bitcast.18), channel_id=1, source_target_pairs={{0,1},{1,0},{2,3},{3,2},{4,5},{5,4},{6,7},{7,6},{8,9},{9,8},{10,11... | collective-permute-start | bytes 786440 | tf_op jit(solution)/shard_map/ppermute | solution.py:24
  72.2 0.7 copy-start.7
  72.9 6.7 %collective-permute-start.3 = (bf16[2560,256]{1,0:T(8,128)(2,1)}, bf16[2560,256]{1,0:T(8,128)(2,1)S(1)}, u32[]{:S(2)}, u32[]{:S(2)}) collective-permute-start(bf16[2560,256]{1,0:T(8,128)(2,1)} %get-tuple-element.25), channel_id=1, source_target_pairs={{0,1},{1,0},{2,3},{3,2},{4,5},{5,4},{6,7},{7,6},{8,9},{9,8},{10,11... | collective-permute-start | bytes 3932168 | tf_op jit(solution)/shard_map/ppermute | solution.py:24
  76.0 20.9 %all-to-all-start.2 = ((bf16[8,32,2048]{2,1,0:T(8,128)(2,1)}), bf16[8,32,2048]{2,1,0:T(8,128)(2,1)S(1)}, u32[]{:S(2)}, u32[]{:S(2)}) async-start(bf16[8,32,2048]{2,1,0:T(8,128)(2,1)} %get-tuple-element.23), calls=%async_computation.2 | async-start | bytes 2097152 | tf_op jit(solution)/shard_map/all_to_all | solution.py:228
  79.5 1.1 copy-start.4
  80.6 1.3 copy-start.5
  81.9 0.9 copy-start.8
  84.9 1.2 copy-start.6
  84.9 15.0 %collective-permute-start.4 = (bf16[2,256,512]{2,1,0:T(8,128)(2,1)}, bf16[2,256,512]{2,1,0:T(8,128)(2,1)S(1)}, u32[]{:S(2)}, u32[]{:S(2)}) collective-permute-start(bf16[2,256,512]{2,1,0:T(8,128)(2,1)} %get-tuple-element.26), channel_id=1, source_target_pairs={{0,16},{16,32},{32,48},{48,0},{1,17},{17,33},{33,49},{49,1},{2,18}... | collective-permute-start | bytes 1572872 | tf_op jit(solution)/shard_map/ppermute | solution.py:24
  86.1 13.8 %collective-permute-start.5 = (bf16[2,256,512]{2,1,0:T(8,128)(2,1)}, bf16[2,256,512]{2,1,0:T(8,128)(2,1)S(1)}, u32[]{:S(2)}, u32[]{:S(2)}) collective-permute-start(bf16[2,256,512]{2,1,0:T(8,128)(2,1)} %get-tuple-element.27), channel_id=1, source_target_pairs={{0,48},{16,0},{32,16},{48,32},{1,49},{17,1},{33,17},{49,33},{2,50}... | collective-permute-start | bytes 1572872 | tf_op jit(solution)/shard_map/ppermute | solution.py:24
  101.2 35.0 %all-to-all-start.3 = ((bf16[32,32,512]{2,1,0:T(8,128)(2,1)}), bf16[32,32,512]{2,1,0:T(8,128)(2,1)S(1)}, u32[]{:S(2)}, u32[]{:S(2)}) async-start(bf16[32,32,512]{2,1,0:T(8,128)(2,1)} %bitcast.5), calls=%async_computation.3 | async-start | bytes 2097152 | tf_op jit(solution)/shard_map/all_to_all | solution.py:243
  110.7 24.6 %collective-permute-start.6 = (bf16[2,256,512]{2,1,0:T(8,128)(2,1)}, bf16[2,256,512]{2,1,0:T(8,128)(2,1)S(1)}, u32[]{:S(2)}, u32[]{:S(2)}) collective-permute-start(bf16[2,256,512]{2,1,0:T(8,128)(2,1)} %copy-done.6), channel_id=1, source_target_pairs={{0,32},{16,48},{32,0},{48,16},{1,33},{17,49},{33,1},{49,17},{2,34}... | collective-permute-start | bytes 1572872 | tf_op jit(solution)/shard_map/ppermute | solution.py:24
  135.4 0.8 copy-start.2
  136.2 4.6 %collective-permute-start.7 = (bf16[4,256,512]{2,1,0:T(8,128)(2,1)S(1)}, bf16[4,256,512]{2,1,0:T(8,128)(2,1)S(1)}, u32[]{:S(2)}, u32[]{:S(2)}) collective-permute-start(bf16[4,256,512]{2,1,0:T(8,128)(2,1)S(1)} %bitcast.9), channel_id=1, source_target_pairs={{0,1},{1,0},{2,3},{3,2},{4,5},{5,4},{6,7},{7,6},{8,9},{9,8},{10,11... | collective-permute-start | bytes 3145736 | tf_op jit(solution)/shard_map/ppermute | solution.py:24
  138.5 1.0 copy-start.3
  146.7 27.4 %collective-permute-start.8 = (bf16[256,2304]{1,0:T(8,128)(2,1)S(1)}, bf16[256,2304]{1,0:T(8,128)(2,1)S(1)}, u32[]{:S(2)}, u32[]{:S(2)}) collective-permute-start(bf16[256,2304]{1,0:T(8,128)(2,1)S(1)} %shard_map.67), channel_id=1, source_target_pairs={{0,64},{64,0},{1,65},{65,1},{2,66},{66,2},{3,67},{67,3},{4,68},{68... | collective-permute-start | bytes 3538952 | tf_op jit(solution)/shard_map/ppermute | solution.py:24
Sparse Core Ops, SparseCore 0:
  9.7 77.5 all-gather.2

commit v16 on v11

--- a/solution.py
+++ b/solution.py
@@ -125,36 +125,37 @@
                 out[x, i] = piece
 
 
-def last_kernel(cuts, joined, grad_m, grad_o, *refs):
-    parts, more, (out, turned) = refs[: len(cuts)], refs[len(cuts) : -2], refs[-2:]
+def last_kernel(grad_m, grad_o, r0, r1, r2, r3, *refs):
+    joined, (out, picked, turned) = refs[:-3], refs[-3:]
     core, x = lax.axis_index("core"), lax.axis_index("x")
-    half = grad_m.shape[1]
-    wide = max(start + ref.shape[1] for ref, (_, start) in zip(parts, cuts))
-    for k in range(4):
-        row = lax.rem(x + 4 - k, 4)
-        turned[k, :, pl.ds(pl.multiple_of(core * half, half), half)] = grad_m[row].T
-        turned[k, :, pl.ds(pl.multiple_of((1 - core) * half, half), half)] = grad_o[row].T
-    for ref in more:
+    half, wide = grad_m.shape[1], r0.shape[1]
+    starts = [pl.multiple_of(which * half, half) for which in (core, 1 - core)]
+    for h, grad in enumerate((grad_m, grad_o)):
+        for k in range(4):
+            picked[h, k] = grad[lax.rem(x + 4 - k, 4)]
+    for h in range(2):
+        for k in range(4):
+            turned[h, k] = picked[h, k].T
+    for ref in joined:
         out[:, wide:] = ref[...]
-    edges = sorted({start for _, start in cuts} | {wide})
-    for low, high in zip(edges, edges[1:]):
+    for c in range(0, wide, 256):
+        cols = slice(c, c + 256)
         acc = None
-        for ref, (k, start) in zip(parts, cuts):
-            if start <= low and high <= start + ref.shape[1]:
-                term = dot(turned[k], ref[:, low - start : high - start])
+        for h in range(2):
+            for k, r in enumerate((r0, r1, r2, r3)):
+                term = dot(turned[h, k], r[pl.ds(starts[h], half), cols])
                 acc = term if acc is None else acc + term
-        out[:, low:high] = acc.astype(out.dtype)
-
-
-def last_call(grad_m, grad_o, cuts, parts, dtype, *joined):
-    tokens, wide = parts[0].shape
-    width = grad_m.shape[2]
+        out[:, cols] = acc.astype(out.dtype)
+
+
+def last_call(grad_m, grad_o, row, dtype, *joined):
+    (tokens, wide), (_, half, width) = row[0].shape, grad_m.shape
     return call(
-        functools.partial(last_kernel, cuts, bool(joined)),
+        last_kernel,
         [like((width, wide + sum(j.shape[1] for j in joined)), dtype)],
-        grad_m, grad_o, *parts, *joined,
-        scratch=[pltpu.VMEM((4, width, tokens), BF)],
-        flops=8 * tokens * width * wide if joined else 0,
+        grad_m, grad_o, *row, *joined,
+        scratch=[pltpu.VMEM((2, 4, half, width), BF), pltpu.VMEM((2, 4, width, half), BF)],
+        flops=8 * tokens * width * wide,
     )
 
 
@@ -179,7 +180,11 @@
         value = keep[side]
         for r in (r1, r2, r3):
             value = value + r[side].astype(F32)
-        out[...] = value.astype(out.dtype)
+        value = value.T
+        rows = out.shape[0]
+        for i in range(value.shape[0] // rows):
+            piece = value[i * rows : (i + 1) * rows].astype(out.dtype)
+            out[:, i * value.shape[1] : (i + 1) * value.shape[1]] = piece
 
 
 def local(acts, target, proj_b, proj_a):
@@ -193,9 +198,7 @@
         return lax.dynamic_slice_in_dim(array, which * size, size, axis)
 
     barrier = lax.optimization_barrier
-    c1, c2, c3 = 1152, 384, 896
-    plus_a = shift(acts[:, :c1], "x", 4, 1)
-    minus_a = shift(acts[:, wide - c1 :], "x", 4, 3)
+    plus, minus = shift(acts, "x", 4, 1), shift(acts, "x", 4, 3)
     pair_a = swap(proj_a, "core")
     target_t = target.T
     near_t = part_of(target_t, core, half, 1)
@@ -204,10 +207,8 @@
     arrived = swap(codes_call(True, acts, proj_b), "core")
     mine = (codes_call(False, acts, proj_b) + arrived).astype(BF).reshape(8, width, half)
     blocks = lax.all_to_all(mine, ZY, 0, 0)
-    blocks, plus_a, minus_a, later = barrier((blocks, plus_a, minus_a, acts))
-    plus_b = shift(later[:, c1:], "x", 4, 1)
-    minus_b = shift(later[:, : wide - c1], "x", 4, 3)
-    far_a = shift(plus_a[:, :c2], "x", 4, 1), shift(minus_a[:, c1 - c2 :], "x", 4, 3)
+    blocks, plus, minus, later, pair_a, pair_t = barrier((blocks, plus, minus, acts, pair_a, pair_t))
+    far = shift(later, "x", 4, 2)
     codes = call(sum_and_copy, [like((8, width, half))], blocks)
     codes = lax.all_to_all(codes, ZY, 0, 0).reshape(rank, half)
 
@@ -218,11 +219,6 @@
         scratch=[pltpu.VMEM((half, 2 * outs), BF)],
         flops=8 * half * rank * outs,
     )
-    partial, plus_a, minus_a, plus_b, minus_b, far_a = barrier((partial, plus_a, minus_a, plus_b, minus_b, far_a))
-    far_b = (
-        shift(plus_a[:, c2:c3], "x", 4, 1),
-        shift(minus_a[:, c1 - c3 : c1 - c2], "x", 4, 3),
-    )
     blocks = lax.all_to_all(partial, ZY, 0, 0)
 
     piece = like((2, width, outs))
@@ -234,6 +230,8 @@
     )
     terms = [terms[0]] + [shift(terms[k], "x", 4, k) for k in (1, 2, 3)]
 
+    blocks, far = barrier((blocks, far))
+    row = [acts, plus, far, minus]
     spread = like((4, 8, sub, width))
     split_a, split_o = call(spread_kernel, [spread, spread], blocks, scratch=[pltpu.VMEM((sub, rank), BF)])
 
@@ -242,17 +240,16 @@
         return split.reshape(4, half, width)
 
     grad = gather(split_a)
-    grad, far_b, *terms = barrier((grad, far_b, *terms))
-    term_o, term_a = call(term_sum_kernel, [like((width, outs), F32), like((width, outs))], *terms)
-    parts = [acts, plus_a, plus_b, far_a[0], far_b[0], far_b[1], far_a[1], minus_b, minus_a]
-    cuts = ((0, 0), (1, 0), (1, c1), (2, 0), (2, c2), (2, c3), (2, wide - c2), (3, 0), (3, wide - c1))
-    away = last_call(grad, swap(grad, "core"), cuts, parts, BF, term_a)
+    term_o, term_a = call(term_sum_kernel, [like((outs, width), F32), like((width, outs))], *terms)
+    grad, split_o, term_o, term_a = barrier((grad, split_o, term_o, term_a))
+    away = last_call(grad, swap(grad, "core"), row, BF, term_a)
     away, split_o = barrier((away, split_o))
     away = swap(away, "y_lo").astype(F32)
     grad = gather(split_o)
-    here = last_call(grad, swap(grad, "core"), cuts, parts, F32)
+    here = last_call(grad, swap(grad, "core"), row, F32)
     here, term_o = barrier((here, term_o))
-    return (((term_o + away[:, wide:]) * scale).T, (here + away[:, :wide]) * scale)
+    term_a = away[:, wide:].reshape(width, outs // width, width).transpose(1, 0, 2).reshape(outs, width)
+    return ((term_o + term_a) * scale, (here + away[:, :wide]) * scale)
 
 
 def solution(mesh):

time: 197 us -> 191 us (0.970)
  blocking collectives: 32.5 us -> 0 us
  waiting for transfers between devices: 61.3 us -> 93.6 us
  starting transfers between devices: 49.7 us -> 40.7 us
  Pallas kernels: 27.1 us -> 29.8 us
  local copies, waits for them, and re-layouts: 22.3 us -> 19.8 us
  other arithmetic: 2.83 us -> 5.19 us
    all_to_all x1 -> x0, blocking collectives: 32.5 us -> none  [gather(): lax.all_to_all(split.reshape(32, sub, width), ('x', 'z', 'y_hi'), 0, 0)]
    ppermute x18 -> x13, waiting for transfers between devices: 23.6 us -> 53.9 us  [shift(): lax.ppermute(array, axis, [(i, (i + step) % size) for i in range(size)])]
    ppermute x18 -> x13, starting transfers between devices: 25.4 us -> 13.9 us  [shift(): lax.ppermute(array, axis, [(i, (i + step) % size) for i in range(size)])]
    all_to_all x1, waiting for transfers between devices: 7.33 us -> 14 us  [local(): codes = lax.all_to_all(codes, ZY, 0, 0).reshape(rank, half)]
    slice x6 -> x1, local copies, waits for them, and re-layouts: 6.71 us -> 1 us  [local(): away[:, wide:].reshape(width, outs // width, width).transpose(1, 0, 2)]
    all_to_all x1 -> x2, waiting for transfers between devices: 24.8 us -> 20.4 us  [gather(): lax.all_to_all(split.reshape(32, sub, width), ('x', 'z', 'y_hi'), 0, 0)]
    all_to_all x1, waiting for transfers between devices: 3.15 us -> 0.01 us  [local(): blocks = lax.all_to_all(mine, ZY, 0, 0)]
    pallas_call x2, Pallas kernels: 5.82 us -> 8.9 us  [codes_call(): pl.pallas_call(functools.partial(codes_kernel, other), grid=(rank // step...]
  transfers between devices with their start and end apart: 22 -> 18, of which waited for: 7 -> 13; matrix products, arithmetic and copies ran while one was open for 6% -> 3% of each run, Pallas kernels for 10% -> 11%
where the time goes in v16:
time: 191 us; the launch traced here: 190 us
  waiting for transfers between devices  93.6 us (49%)
  starting transfers between devices  40.7 us (21%)
  Pallas kernels  29.8 us (16%)
  local copies, waits for them, and re-layouts  19.8 us (10%)
  other arithmetic  5.19 us (3%)
    ppermute x13, waiting for transfers between devices, shift(): lax.ppermute(array, axis, [(i, (i + step) % size) for i in range(size)])  53.9 us
    pallas_call x7, Pallas kernels, call(): pl.pallas_call(body, out_shape=outs if len(outs) > 1 else outs[0], in_spe...  20.9 us
    all_to_all x2, waiting for transfers between devices, gather(): lax.all_to_all(split.reshape(32, sub, width), ('x', 'z', 'y_hi'), 0, 0)  20.4 us
    unnamed x36, local copies, waits for them, and re-layouts  16.6 us
    all_to_all x1, waiting for transfers between devices, local(): codes = lax.all_to_all(codes, ZY, 0, 0).reshape(rank, half)  14 us
    ppermute x13, starting transfers between devices, shift(): lax.ppermute(array, axis, [(i, (i + step) % size) for i in range(size)])  13.9 us
    pallas_call x2, Pallas kernels, codes_call(): pl.pallas_call(functools.partial(codes_kernel, other), grid=(rank // step...  8.9 us
    all_to_all x2, starting transfers between devices, gather(): lax.all_to_all(split.reshape(32, sub, width), ('x', 'z', 'y_hi'), 0, 0)  7.97 us
  transfers between devices with their start and end apart: 18, of which 13 were waited for; matrix products, arithmetic and copies ran while one was open for 3% of the time, Pallas kernels for 11%

profile of v16, /device:TPU:1, one launch (start us, length us, event | category | flops | bytes accessed | tf_op | source)
XLA Modules:
  0.0 189.9 jit_solution(2785757614652640813)
XLA Ops:
  0.6 3.1 %copy-done = bf16[2048,1792]{1,0:T(8,128)(2,1)S(1)} copy-done((bf16[2048,1792]{1,0:T(8,128)(2,1)S(1)}, bf16[2048,1792]{1,0:T(8,128)(2,1)}, u32[]{:S(2)}) %copy-start) | copy-done | bytes 7340056
  3.7 4.4 %shard_map.60 = f32[2048,256]{1,0:T(8,128)S(1)} custom-call(bf16[512,1792]{1,0:T(8,128)(2,1)} %r0.3, bf16[2048,1792]{1,0:T(8,128)(2,1)S(1)} %copy-done), custom_call_target="tpu_custom_call" | custom-call | flops 1879048192 | bytes 7340032 | tf_op jit(solution)/shard_map/pallas_call | solution.py:69
  9.7 2.6 %collective-permute-start.2 = (bf16[512,1792]{1,0:T(8,128)(2,1)}, bf16[512,1792]{1,0:T(8,128)(2,1)S(1)}, u32[]{:S(2)}, u32[]{:S(2)}) collective-permute-start(bf16[512,1792]{1,0:T(8,128)(2,1)} %r0.3), channel_id=1, source_target_pairs={{0,48},{16,0},{32,16},{48,32},{1,49},{17,1},{33,17},{49,33},{2,50}... | collective-permute-start | bytes 5505032 | tf_op jit(solution)/shard_map/ppermute | solution.py:24
  12.3 4.5 %shard_map.59 = f32[2048,256]{1,0:T(8,128)S(1)} custom-call(bf16[512,1792]{1,0:T(8,128)(2,1)} %r0.3, bf16[2048,1792]{1,0:T(8,128)(2,1)S(1)} %copy-done), custom_call_target="tpu_custom_call" | custom-call | flops 1879048192 | bytes 7340032 | tf_op jit(solution)/shard_map/pallas_call | solution.py:69
  18.0 7.7 %all-to-all-start = ((bf16[8,256,256]{2,1,0:T(8,128)(2,1)}), bf16[8,256,256]{2,1,0:T(8,128)(2,1)S(1)}, u32[]{:S(2)}, u32[]{:S(2)}) async-start(bf16[8,256,256]{2,1,0:T(8,128)(2,1)} %bitcast.22), calls=%async_computation | async-start | bytes 2097152 | tf_op jit(solution)/shard_map/all_to_all | solution.py:209
  30.6 21.0 %collective-permute-done.2.r3 = bf16[512,1792]{1,0:T(8,128)(2,1)S(1)} collective-permute-done((bf16[512,1792]{1,0:T(8,128)(2,1)}, bf16[512,1792]{1,0:T(8,128)(2,1)S(1)}, u32[]{:S(2)}, u32[]{:S(2)}) %collective-permute-start.2) | collective-permute-done | bytes 1835040 | tf_op jit(solution)/shard_map/ppermute | solution.py:24
  51.6 3.1 %collective-permute-done.1.r1 = bf16[512,1792]{1,0:T(8,128)(2,1)} collective-permute-done((bf16[512,1792]{1,0:T(8,128)(2,1)}, bf16[512,1792]{1,0:T(8,128)(2,1)}, u32[]{:S(2)}, u32[]{:S(2)}) %collective-permute-start.1) | collective-permute-done | bytes 1835040 | tf_op jit(solution)/shard_map/ppermute | solution.py:24
  55.8 7.7 %all-to-all-start.1 = ((bf16[8,256,256]{2,1,0:T(8,128)(2,1)}), bf16[8,256,256]{2,1,0:T(8,128)(2,1)S(1)}, u32[]{:S(2)}, u32[]{:S(2)}) async-start(bf16[8,256,256]{2,1,0:T(8,128)(2,1)} %copy-done.3), calls=%async_computation.1 | async-start | bytes 2097152 | tf_op jit(solution)/shard_map/all_to_all | solution.py:213
  64.6 14.0 %all-to-all-done.1 = bf16[8,256,256]{2,1,0:T(8,128)(2,1)S(1)} async-done(((bf16[8,256,256]{2,1,0:T(8,128)(2,1)}), bf16[8,256,256]{2,1,0:T(8,128)(2,1)S(1)}, u32[]{:S(2)}, u32[]{:S(2)}) %all-to-all-start.1) | async-done | bytes 1048608 | tf_op jit(solution)/shard_map/all_to_all | solution.py:213
  78.6 6.2 %shard_map.62 = (bf16[256,512]{1,0:T(8,128)(2,1)S(1)}, bf16[2560,256]{1,0:T(8,128)(2,1)}, bf16[8,32,2048]{2,1,0:T(8,128)(2,1)S(1)}) custom-call(bf16[2048,256]{1,0:T(8,128)(2,1)S(1)} %bitcast.17, bf16[512,256]{1,0:T(8,128)(2,1)S(1)} %bitcast.21, bf16[512,256]{1,0:T(8,128)(2,1)S(1)} %collective-permute-done.4.far, bf16[512,2048]{1,0:T(8,128)(2,1)} %a0.1, ...), custom_call_target="tpu_custom_call" | custom-call | flops 2147483648 | bytes 8388608 | tf_op jit(solution)/shard_map/pallas_call | solution.py:33
  86.4 3.1 %collective-permute-start.6 = (bf16[2560,256]{1,0:T(8,128)(2,1)}, bf16[2560,256]{1,0:T(8,128)(2,1)}, u32[]{:S(2)}, u32[]{:S(2)}) collective-permute-start(bf16[2560,256]{1,0:T(8,128)(2,1)} %get-tuple-element.38), channel_id=1, source_target_pairs={{0,1},{1,0},{2,3},{3,2},{4,5},{5,4},{6,7},{7,6},{8,9},{9,8},{10,11... | collective-permute-start | bytes 3932168 | tf_op jit(solution)/shard_map/ppermute | solution.py:24
  89.5 3.6 %all-to-all-start.2 = ((bf16[8,32,2048]{2,1,0:T(8,128)(2,1)}), bf16[8,32,2048]{2,1,0:T(8,128)(2,1)S(1)}, u32[]{:S(2)}, u32[]{:S(2)}) async-start(bf16[8,32,2048]{2,1,0:T(8,128)(2,1)} %copy-done.8), calls=%async_computation.2 | async-start | bytes 2097152 | tf_op jit(solution)/shard_map/all_to_all | solution.py:222
  94.3 3.4 %shard_map.64 = (f32[2,256,512]{2,1,0:T(8,128)S(1)}, bf16[2,256,512]{2,1,0:T(8,128)(2,1)}, bf16[2,256,512]{2,1,0:T(8,128)(2,1)}, bf16[2,256,512]{2,1,0:T(8,128)(2,1)}) custom-call(bf16[2048,256]{1,0:T(8,128)(2,1)S(1)} %bitcast.18, bf16[256,512]{1,0:T(8,128)(2,1)S(1)} %copy-done.16, bf16[2560,256]{1,0:T(8,128)(2,1)} %collective-permute-done.6.message), custom_call_target="tpu_custom_call" | custom-call | flops 1073741824 | bytes 5242880 | tf_op jit(solution)/shard_map/pallas_call | solution.py:33
  101.3 3.7 %collective-permute-done.5.r2 = bf16[512,1792]{1,0:T(8,128)(2,1)} collective-permute-done((bf16[512,1792]{1,0:T(8,128)(2,1)}, bf16[512,1792]{1,0:T(8,128)(2,1)}, u32[]{:S(2)}, u32[]{:S(2)}) %collective-permute-start.5) | collective-permute-done | bytes 1835040 | tf_op jit(solution)/shard_map/ppermute | solution.py:24
  105.0 5.2 %all-to-all-done.2.blocks = bf16[8,32,2048]{2,1,0:T(8,128)(2,1)S(1)} async-done(((bf16[8,32,2048]{2,1,0:T(8,128)(2,1)}), bf16[8,32,2048]{2,1,0:T(8,128)(2,1)S(1)}, u32[]{:S(2)}, u32[]{:S(2)}) %all-to-all-start.2) | async-done | bytes 1048608 | tf_op jit(solution)/shard_map/all_to_all | solution.py:222
  112.1 3.9 %all-to-all-start.3 = ((bf16[32,32,256]{2,1,0:T(8,128)(2,1)}), bf16[32,32,256]{2,1,0:T(8,128)(2,1)S(1)}, u32[]{:S(2)}, u32[]{:S(2)}) async-start(bf16[32,32,256]{2,1,0:T(8,128)(2,1)} %bitcast.20), calls=%async_computation.3 | async-start | bytes 1048576 | tf_op jit(solution)/shard_map/all_to_all | solution.py:239
  116.0 4.7 %collective-permute-done.7.r1 = bf16[2,256,512]{2,1,0:T(8,128)(2,1)S(1)} collective-permute-done((bf16[2,256,512]{2,1,0:T(8,128)(2,1)}, bf16[2,256,512]{2,1,0:T(8,128)(2,1)S(1)}, u32[]{:S(2)}, u32[]{:S(2)}) %collective-permute-start.7) | collective-permute-done | bytes 524320 | tf_op jit(solution)/shard_map/ppermute | solution.py:24
  120.7 6.8 %collective-permute-done.8.r2 = bf16[2,256,512]{2,1,0:T(8,128)(2,1)} collective-permute-done((bf16[2,256,512]{2,1,0:T(8,128)(2,1)}, bf16[2,256,512]{2,1,0:T(8,128)(2,1)}, u32[]{:S(2)}, u32[]{:S(2)}) %collective-permute-start.8) | collective-permute-done | bytes 524320 | tf_op jit(solution)/shard_map/ppermute | solution.py:24
  131.7 8.0 %all-to-all-done.3 = bf16[32,32,256]{2,1,0:T(8,128)(2,1)S(1)} async-done(((bf16[32,32,256]{2,1,0:T(8,128)(2,1)}), bf16[32,32,256]{2,1,0:T(8,128)(2,1)S(1)}, u32[]{:S(2)}, u32[]{:S(2)}) %all-to-all-start.3) | async-done | bytes 524320 | tf_op jit(solution)/shard_map/all_to_all | solution.py:239
  143.1 4.7 %shard_map.66 = bf16[256,2304]{1,0:T(8,128)(2,1)S(1)} custom-call(bf16[4,256,256]{2,1,0:T(8,128)(2,1)S(1)} %bitcast.14, bf16[4,256,256]{2,1,0:T(8,128)(2,1)S(1)} %collective-permute-done.10.grad_o, bf16[512,1792]{1,0:T(8,128)(2,1)} %r0.3, bf16[512,1792]{1,0:T(8,128)(2,1)} %collective-permute-done.1.r1, bf16[512,1792]{1,0:T(8,128)(2,1)} %collective-permute-done.5.r2, ...), custom_call_target="tpu_custom_call" | custom-call | flops 1879048192 | bytes 9830400 | tf_op jit(solution)/shard_map/pallas_call | solution.py:33
  147.8 4.1 %all-to-all-start.4 = ((bf16[32,32,256]{2,1,0:T(8,128)(2,1)}), bf16[32,32,256]{2,1,0:T(8,128)(2,1)S(1)}, u32[]{:S(2)}, u32[]{:S(2)}) async-start(bf16[32,32,256]{2,1,0:T(8,128)(2,1)} %bitcast.19), calls=%async_computation.4 | async-start | bytes 1048576 | tf_op jit(solution)/shard_map/all_to_all | solution.py:239
  152.4 12.4 %all-to-all-done.4 = bf16[32,32,256]{2,1,0:T(8,128)(2,1)S(1)} async-done(((bf16[32,32,256]{2,1,0:T(8,128)(2,1)}), bf16[32,32,256]{2,1,0:T(8,128)(2,1)S(1)}, u32[]{:S(2)}, u32[]{:S(2)}) %all-to-all-start.4) | async-done | bytes 524320 | tf_op jit(solution)/shard_map/all_to_all | solution.py:239
  168.0 4.7 %shard_map.67 = f32[256,1792]{1,0:T(8,128)S(1)} custom-call(bf16[4,256,256]{2,1,0:T(8,128)(2,1)S(1)} %bitcast.16, bf16[4,256,256]{2,1,0:T(8,128)(2,1)S(1)} %collective-permute-done.11.grad_o, bf16[512,1792]{1,0:T(8,128)(2,1)} %r0.3, bf16[512,1792]{1,0:T(8,128)(2,1)} %collective-permute-done.1.r1, bf16[512,1792]{1,0:T(8,128)(2,1)} %collective-permute-done.5.r2, ...), custom_call_target="tpu_custom_call" | custom-call | flops 1879048192 | bytes 10223616 | tf_op jit(solution)/shard_map/pallas_call | solution.py:33
  173.9 10.2 %collective-permute-done.12 = bf16[256,2304]{1,0:T(8,128)(2,1)} collective-permute-done((bf16[256,2304]{1,0:T(8,128)(2,1)S(1)}, bf16[256,2304]{1,0:T(8,128)(2,1)}, u32[]{:S(2)}, u32[]{:S(2)}) %collective-permute-start.12) | collective-permute-done | bytes 1179680 | tf_op jit(solution)/shard_map/ppermute | solution.py:24
  (65 shorter events, 36.5 us)
Async XLA Ops:
  0.6 3.1 %copy-start = (bf16[2048,1792]{1,0:T(8,128)(2,1)S(1)}, bf16[2048,1792]{1,0:T(8,128)(2,1)}, u32[]{:S(2)}) copy-start(bf16[2048,1792]{1,0:T(8,128)(2,1)} %b.3) | copy-start | bytes 22020100
  8.1 8.7 %collective-permute-start = (f32[2048,256]{1,0:T(8,128)S(1)}, f32[2048,256]{1,0:T(8,128)S(1)}, u32[]{:S(2)}, u32[]{:S(2)}) collective-permute-start(f32[2048,256]{1,0:T(8,128)S(1)} %shard_map.60), channel_id=1, source_target_pairs={{0,1},{1,0},{2,3},{3,2},{4,5},{5,4},{6,7},{7,6},{8,9},{9,8},{10,11... | collective-permute-start | bytes 6291464 | tf_op jit(solution)/shard_map/ppermute | solution.py:24
  9.6 45.0 %collective-permute-start.3 = (bf16[512,2048]{1,0:T(8,128)(2,1)}, bf16[512,2048]{1,0:T(8,128)(2,1)}, u32[]{:S(2)}, u32[]{:S(2)}) collective-permute-start(bf16[512,2048]{1,0:T(8,128)(2,1)} %a0.1), channel_id=1, source_target_pairs={{0,1},{1,0},{2,3},{3,2},{4,5},{5,4},{6,7},{7,6},{8,9},{9,8},{10,11... | collective-permute-start | bytes 6291464 | tf_op jit(solution)/shard_map/ppermute | solution.py:24
  9.7 41.9 %collective-permute-start.2 = (bf16[512,1792]{1,0:T(8,128)(2,1)}, bf16[512,1792]{1,0:T(8,128)(2,1)S(1)}, u32[]{:S(2)}, u32[]{:S(2)}) collective-permute-start(bf16[512,1792]{1,0:T(8,128)(2,1)} %r0.3), channel_id=1, source_target_pairs={{0,48},{16,0},{32,16},{48,32},{1,49},{17,1},{33,17},{49,33},{2,50}... | collective-permute-start | bytes 5505032 | tf_op jit(solution)/shard_map/ppermute | solution.py:24
  12.3 42.4 %collective-permute-start.1 = (bf16[512,1792]{1,0:T(8,128)(2,1)}, bf16[512,1792]{1,0:T(8,128)(2,1)}, u32[]{:S(2)}, u32[]{:S(2)}) collective-permute-start(bf16[512,1792]{1,0:T(8,128)(2,1)} %r0.3), channel_id=1, source_target_pairs={{0,16},{16,32},{32,48},{48,0},{1,17},{17,33},{33,49},{49,1},{2,18}... | collective-permute-start | bytes 5505032 | tf_op jit(solution)/shard_map/ppermute | solution.py:24
  18.0 36.7 %all-to-all-start = ((bf16[8,256,256]{2,1,0:T(8,128)(2,1)}), bf16[8,256,256]{2,1,0:T(8,128)(2,1)S(1)}, u32[]{:S(2)}, u32[]{:S(2)}) async-start(bf16[8,256,256]{2,1,0:T(8,128)(2,1)} %bitcast.22), calls=%async_computation | async-start | bytes 2097152 | tf_op jit(solution)/shard_map/all_to_all | solution.py:209
  28.3 2.4 %collective-permute-start.4 = (bf16[512,256]{1,0:T(8,128)(2,1)}, bf16[512,256]{1,0:T(8,128)(2,1)S(1)}, u32[]{:S(2)}, u32[]{:S(2)}) collective-permute-start(bf16[512,256]{1,0:T(8,128)(2,1)} %bitcast.24), channel_id=1, source_target_pairs={{0,1},{1,0},{2,3},{3,2},{4,5},{5,4},{6,7},{7,6},{8,9},{9,8},{10,11... | collective-permute-start | bytes 786440 | tf_op jit(solution)/shard_map/ppermute | solution.py:24
  55.8 22.8 %all-to-all-start.1 = ((bf16[8,256,256]{2,1,0:T(8,128)(2,1)}), bf16[8,256,256]{2,1,0:T(8,128)(2,1)S(1)}, u32[]{:S(2)}, u32[]{:S(2)}) async-start(bf16[8,256,256]{2,1,0:T(8,128)(2,1)} %copy-done.3), calls=%async_computation.1 | async-start | bytes 2097152 | tf_op jit(solution)/shard_map/all_to_all | solution.py:213
  63.5 41.5 %collective-permute-start.5 = (bf16[512,1792]{1,0:T(8,128)(2,1)}, bf16[512,1792]{1,0:T(8,128)(2,1)}, u32[]{:S(2)}, u32[]{:S(2)}) collective-permute-start(bf16[512,1792]{1,0:T(8,128)(2,1)} %r0.3), channel_id=1, source_target_pairs={{0,32},{16,48},{32,0},{48,16},{1,33},{17,49},{33,1},{49,17},{2,34}... | collective-permute-start | bytes 5505032 | tf_op jit(solution)/shard_map/ppermute | solution.py:24
  78.5 6.2 %copy-start.6 = (bf16[8,256,256]{2,1,0:T(8,128)(2,1)}, bf16[8,256,256]{2,1,0:T(8,128)(2,1)S(1)}, u32[]{:S(2)}) copy-start(bf16[8,256,256]{2,1,0:T(8,128)(2,1)S(1)} %all-to-all-done.1) | copy-start | bytes 3145732
  86.4 6.6 %copy-start.16 = (bf16[256,512]{1,0:T(8,128)(2,1)S(1)}, bf16[256,512]{1,0:T(8,128)(2,1)}, u32[]{:S(2)}) copy-start(bf16[256,512]{1,0:T(8,128)(2,1)} %copy-done.15) | copy-start | bytes 786436
  86.4 6.6 %collective-permute-start.6 = (bf16[2560,256]{1,0:T(8,128)(2,1)}, bf16[2560,256]{1,0:T(8,128)(2,1)}, u32[]{:S(2)}, u32[]{:S(2)}) collective-permute-start(bf16[2560,256]{1,0:T(8,128)(2,1)} %get-tuple-element.38), channel_id=1, source_target_pairs={{0,1},{1,0},{2,3},{3,2},{4,5},{5,4},{6,7},{7,6},{8,9},{9,8},{10,11... | collective-permute-start | bytes 3932168 | tf_op jit(solution)/shard_map/ppermute | solution.py:24
  89.5 20.7 %all-to-all-start.2 = ((bf16[8,32,2048]{2,1,0:T(8,128)(2,1)}), bf16[8,32,2048]{2,1,0:T(8,128)(2,1)S(1)}, u32[]{:S(2)}, u32[]{:S(2)}) async-start(bf16[8,32,2048]{2,1,0:T(8,128)(2,1)} %copy-done.8), calls=%async_computation.2 | async-start | bytes 2097152 | tf_op jit(solution)/shard_map/all_to_all | solution.py:222
  98.6 22.0 %collective-permute-start.7 = (bf16[2,256,512]{2,1,0:T(8,128)(2,1)}, bf16[2,256,512]{2,1,0:T(8,128)(2,1)S(1)}, u32[]{:S(2)}, u32[]{:S(2)}) collective-permute-start(bf16[2,256,512]{2,1,0:T(8,128)(2,1)} %get-tuple-element.40), channel_id=1, source_target_pairs={{0,16},{16,32},{32,48},{48,0},{1,17},{17,33},{33,49},{49,1},{2,18}... | collective-permute-start | bytes 1572872 | tf_op jit(solution)/shard_map/ppermute | solution.py:24
  98.6 28.9 %collective-permute-start.8 = (bf16[2,256,512]{2,1,0:T(8,128)(2,1)}, bf16[2,256,512]{2,1,0:T(8,128)(2,1)}, u32[]{:S(2)}, u32[]{:S(2)}) collective-permute-start(bf16[2,256,512]{2,1,0:T(8,128)(2,1)} %get-tuple-element.41), channel_id=1, source_target_pairs={{0,32},{16,48},{32,0},{48,16},{1,33},{17,49},{33,1},{49,17},{2,34}... | collective-permute-start | bytes 1572872 | tf_op jit(solution)/shard_map/ppermute | solution.py:24
  100.0 27.5 %collective-permute-start.9 = (bf16[2,256,512]{2,1,0:T(8,128)(2,1)}, bf16[2,256,512]{2,1,0:T(8,128)(2,1)}, u32[]{:S(2)}, u32[]{:S(2)}) collective-permute-start(bf16[2,256,512]{2,1,0:T(8,128)(2,1)} %get-tuple-element.42), channel_id=1, source_target_pairs={{0,48},{16,0},{32,16},{48,32},{1,49},{17,1},{33,17},{49,33},{2,50}... | collective-permute-start | bytes 1572872 | tf_op jit(solution)/shard_map/ppermute | solution.py:24
  112.1 27.6 %all-to-all-start.3 = ((bf16[32,32,256]{2,1,0:T(8,128)(2,1)}), bf16[32,32,256]{2,1,0:T(8,128)(2,1)S(1)}, u32[]{:S(2)}, u32[]{:S(2)}) async-start(bf16[32,32,256]{2,1,0:T(8,128)(2,1)} %bitcast.20), calls=%async_computation.3 | async-start | bytes 1048576 | tf_op jit(solution)/shard_map/all_to_all | solution.py:239
  139.7 2.4 %collective-permute-start.10 = (bf16[4,256,256]{2,1,0:T(8,128)(2,1)S(1)}, bf16[4,256,256]{2,1,0:T(8,128)(2,1)S(1)}, u32[]{:S(2)}, u32[]{:S(2)}) collective-permute-start(bf16[4,256,256]{2,1,0:T(8,128)(2,1)S(1)} %bitcast.13), channel_id=1, source_target_pairs={{0,1},{1,0},{2,3},{3,2},{4,5},{5,4},{6,7},{7,6},{8,9},{9,8},{10,11... | collective-permute-start | bytes 1572872 | tf_op jit(solution)/shard_map/ppermute | solution.py:24
  147.8 17.0 %all-to-all-start.4 = ((bf16[32,32,256]{2,1,0:T(8,128)(2,1)}), bf16[32,32,256]{2,1,0:T(8,128)(2,1)S(1)}, u32[]{:S(2)}, u32[]{:S(2)}) async-start(bf16[32,32,256]{2,1,0:T(8,128)(2,1)} %bitcast.19), calls=%async_computation.4 | async-start | bytes 1048576 | tf_op jit(solution)/shard_map/all_to_all | solution.py:239
  151.9 32.3 %collective-permute-start.12 = (bf16[256,2304]{1,0:T(8,128)(2,1)S(1)}, bf16[256,2304]{1,0:T(8,128)(2,1)}, u32[]{:S(2)}, u32[]{:S(2)}) collective-permute-start(bf16[256,2304]{1,0:T(8,128)(2,1)S(1)} %shard_map.66), channel_id=1, source_target_pairs={{0,64},{64,0},{1,65},{65,1},{2,66},{66,2},{3,67},{67,3},{4,68},{68... | collective-permute-start | bytes 3538952 | tf_op jit(solution)/shard_map/ppermute | solution.py:24
  164.8 3.2 %collective-permute-start.11 = (bf16[4,256,256]{2,1,0:T(8,128)(2,1)S(1)}, bf16[4,256,256]{2,1,0:T(8,128)(2,1)S(1)}, u32[]{:S(2)}, u32[]{:S(2)}) collective-permute-start(bf16[4,256,256]{2,1,0:T(8,128)(2,1)S(1)} %bitcast.15), channel_id=1, source_target_pairs={{0,1},{1,0},{2,3},{3,2},{4,5},{5,4},{6,7},{7,6},{8,9},{9,8},{10,11... | collective-permute-start | bytes 1572872 | tf_op jit(solution)/shard_map/ppermute | solution.py:24
  172.7 1.2 copy-start.1
  173.9 11.6 %copy-start.10 = (f32[512,256]{1,0:T(8,128)S(1)}, f32[512,256]{1,0:T(8,128)}, u32[]{:S(2)}) copy-start(f32[512,256]{1,0:T(8,128)} %copy-done.9) | copy-start | bytes 1572868
  186.4 1.9 copy-start.2
  (11 other events, 10.1 us)

commit v17 on v15

--- a/solution.py
+++ b/solution.py
@@ -98,12 +98,7 @@
             left = target[rows].astype(F32) - dot(a[rows], codes[...])
             left = left.astype(BF).T
             held[:, j * outs + at : j * outs + at + step] = left
-            if j == 0:
-                own[:, rows] = left
-            else:
-                for c in range(0, step, 256):
-                    message[rank + at + c : rank + at + c + 256] = left[:, c : c + 256]
-    message[:rank] = codes[...]
+            (own if j == 0 else message)[:, rows] = left
     sub = partial.shape[1]
     for at in range(0, rank, 512):
         cols = slice(at, at + 512)
@@ -172,7 +167,7 @@
     )(grad_m, grad_o, row, *joined)
 
 
-def term_kernel(codes, own, message, keep, s1, s2, s3):
+def term_kernel(codes, own, codes_o, message, keep, s1, s2, s3):
     x = lax.axis_index("x")
     rank, outs = codes.shape[0], own.shape[1]
     width = rank // 8
@@ -180,10 +175,10 @@
         for side in range(2):
             start = side * (rank // 2) + lax.rem(x + k, 4) * width
             rows = pl.ds(pl.multiple_of(start, width), width)
-            left, right = codes[rows, :], message[rows, :]
+            left, right = codes[rows, :], codes_o[rows, :]
             for c in range(0, outs, 256):
                 acc = dot(left, own[:, c : c + 256])
-                acc = acc + dot(right, message[rank + c : rank + c + 256])
+                acc = acc + dot(right, message[:, c : c + 256])
                 out[side, :, c : c + 256] = acc.astype(out.dtype)
 
 
@@ -218,9 +213,11 @@
     codes = call(sum_and_copy, [like((8, width, half))], blocks)
     codes = lax.all_to_all(codes, ZY, 0, 0).reshape(rank, half)
 
+    codes_o = swap(codes, "core")
+
     own, message, partial = call(
         residual_kernel,
-        [like((half, outs)), like((rank + outs, half)), like((8, sub, rank))],
+        [like((half, outs)), like((half, outs)), like((8, sub, rank))],
         codes, near_t, pair_t, proj_a, pair_a,
         scratch=[pltpu.VMEM((half, 2 * outs), BF)],
         flops=8 * half * rank * outs,
@@ -231,24 +228,25 @@
     terms = call(
         term_kernel,
         [like(piece.shape, F32), piece, piece, piece],
-        codes, own, swap(message, "core"),
+        codes, own, codes_o, swap(message, "core"),
         flops=2 * tokens * rank * outs,
     )
-    near = [shift(terms[k], "x", 4, k) for k in (1, 3)]
+    terms = [terms[0]] + [shift(terms[k], "x", 4, k) for k in (1, 2, 3)]
 
     barrier = lax.optimization_barrier
-    blocks, row, near, later = barrier((blocks, row, near, terms[2]))
-    terms = [terms[0], shift(later, "x", 4, 2)] + near
+    blocks, row = barrier((blocks, row))
     split = call(spread_kernel, [like((4, 8, sub, 2 * width))], blocks, scratch=[pltpu.VMEM((sub, rank), BF)])
     grad = lax.all_to_all(split.reshape(32, sub, 2 * width), ("x", "z", "y_hi"), 0, 0)
     grad = grad.reshape(4, half, 2 * width)
-    grad, *terms = barrier((grad, *terms))
     grad_o = swap(grad, "core")
+    away = last_call(grad, grad_o, row, 0, BF)
+    away = swap(away, "y_lo").astype(F32)
+    later, *terms = barrier((grad, *terms))
+    here = last_call(later, grad_o, row, 1, F32)
     term_o, term_a = call(term_sum_kernel, [like((width, outs), F32), like((width, outs))], *terms)
-    away = swap(last_call(grad, grad_o, row, 0, BF, term_a), "y_lo").astype(F32)
-    here = last_call(grad, grad_o, row, 1, F32)
+    term_a = swap(term_a, "y_lo").astype(F32)
     here, term_o = barrier((here, term_o))
-    return (((term_o + away[:, wide:]) * scale).T, (here + away[:, :wide]) * scale)
+    return (((term_o + term_a) * scale).T, (here + away) * scale)
 
 
 def solution(mesh):

time: 184 us -> 170 us (0.924)
  blocking collectives: 23.9 us -> 43.5 us
  waiting for transfers between devices: 71.8 us -> 52.6 us
  starting transfers between devices: 32.4 us -> 22.1 us
  local copies, waits for them, and re-layouts: 11 us -> 6.79 us
    ppermute x9 -> x11, waiting for transfers between devices: 50.6 us -> 26.1 us  [shift(): lax.ppermute(array, axis, [(i, (i + step) % size) for i in range(size)])]
    all_to_all x0 -> x1, blocking collectives: none -> 19.6 us  [local(): blocks = lax.all_to_all(partial, ZY, 0, 0)]
    all_to_all x1, waiting for transfers between devices: 0.01 us -> 14.1 us  [local(): lax.all_to_all(split.reshape(32, sub, 2 * width), ('x', 'z', 'y_hi'), 0, 0)]
    all_to_all x1 -> x0, waiting for transfers between devices: 8.69 us -> none  [local(): blocks = lax.all_to_all(partial, ZY, 0, 0)]
    all_to_all x1, starting transfers between devices: 9.57 us -> 5.25 us  [local(): lax.all_to_all(split.reshape(32, sub, 2 * width), ('x', 'z', 'y_hi'), 0, 0)]
    unnamed x23 -> x13, local copies, waits for them, and re-layouts: 11 us -> 6.75 us
    all_to_all x1 -> x0, starting transfers between devices: 3.56 us -> none  [local(): blocks = lax.all_to_all(partial, ZY, 0, 0)]
    ppermute x9 -> x11, starting transfers between devices: 15.7 us -> 13.3 us  [shift(): lax.ppermute(array, axis, [(i, (i + step) % size) for i in range(size)])]
  transfers between devices with their start and end apart: 13 -> 14, of which waited for: 8 -> 9; matrix products, arithmetic and copies ran while one was open for 0% -> 1% of each run, Pallas kernels for 12% -> 15%
where the time goes in v17:
time: 170 us; the launch traced here: 169 us
  waiting for transfers between devices  52.6 us (31%)
  blocking collectives  43.5 us (26%)
  Pallas kernels  27.1 us (16%)
  starting transfers between devices  22.1 us (13%)
  between operations  14.2 us (8%)
  local copies, waits for them, and re-layouts  6.79 us (4%)
  other arithmetic  2.99 us (2%)
    ppermute x11, waiting for transfers between devices, shift(): lax.ppermute(array, axis, [(i, (i + step) % size) for i in range(size)])  26.1 us
    all_to_all x1, blocking collectives, local(): blocks = lax.all_to_all(mine, ZY, 0, 0)  23.9 us
    all_to_all x1, blocking collectives, local(): blocks = lax.all_to_all(partial, ZY, 0, 0)  19.6 us
    all_to_all x1, waiting for transfers between devices, local(): lax.all_to_all(split.reshape(32, sub, 2 * width), ('x', 'z', 'y_hi'), 0, 0)  14.1 us
    ppermute x11, starting transfers between devices, shift(): lax.ppermute(array, axis, [(i, (i + step) % size) for i in range(size)])  13.3 us
    pallas_call x2, Pallas kernels, last_call(): pl.pallas_call(functools.partial(last_kernel, side), out_shape=like((widt...  12.7 us
    all_to_all x1, waiting for transfers between devices, local(): codes = lax.all_to_all(codes, ZY, 0, 0).reshape(rank, half)  11.8 us
    pallas_call x5, Pallas kernels, call(): pl.pallas_call(body, out_shape=outs if len(outs) > 1 else outs[0], in_spe...  8.56 us
  transfers between devices with their start and end apart: 14, of which 9 were waited for; matrix products, arithmetic and copies ran while one was open for 1% of the time, Pallas kernels for 15%

profile of v17, /device:TPU:1, one launch (start us, length us, event | category | flops | bytes accessed | tf_op | source)
XLA Modules:
  0.0 169.3 jit_solution(4012342702017325492)
XLA Ops:
  8.7 3.1 %copy-done = bf16[2048,1792]{1,0:T(8,128)(2,1)S(1)} copy-done((bf16[2048,1792]{1,0:T(8,128)(2,1)S(1)}, bf16[2048,1792]{1,0:T(8,128)(2,1)}, u32[]{:S(2)}) %copy-start) | copy-done | bytes 7340056
  11.7 2.9 %shard_map.60 = f32[2048,256]{1,0:T(8,128)S(1)} custom-call(bf16[512,1792]{1,0:T(8,128)(2,1)S(1)} %copy-done.1, bf16[2048,1792]{1,0:T(8,128)(2,1)S(1)} %copy-done), custom_call_target="tpu_custom_call" | custom-call | flops 1879048192 | bytes 7340032 | tf_op jit(solution)/shard_map/pallas_call | solution.py:69
  14.7 1.5 collective-permute-start
  16.3 2.9 %shard_map.59 = f32[2048,256]{1,0:T(8,128)S(1)} custom-call(bf16[512,1792]{1,0:T(8,128)(2,1)S(1)} %copy-done.1, bf16[2048,1792]{1,0:T(8,128)(2,1)S(1)} %copy-done), custom_call_target="tpu_custom_call" | custom-call | flops 1879048192 | bytes 7340032 | tf_op jit(solution)/shard_map/pallas_call | solution.py:69
  19.2 2.8 %collective-permute-done = f32[2048,256]{1,0:T(8,128)S(1)} collective-permute-done((f32[2048,256]{1,0:T(8,128)S(1)}, f32[2048,256]{1,0:T(8,128)S(1)}, u32[]{:S(2)}, u32[]{:S(2)}) %collective-permute-start) | collective-permute-done | bytes 2097184 | tf_op jit(solution)/shard_map/ppermute | solution.py:24
  22.4 23.9 %all_to_all.20.blocks = bf16[8,256,256]{2,1,0:T(8,128)(2,1)S(1)} all-to-all(bf16[8,256,256]{2,1,0:T(8,128)(2,1)S(1)} %bitcast.18), channel_id=1, replica_groups=mesh['y_lo'=2,'x'=4,'z'=4,'y_hi'=2,'core'=2] {'z','y_hi'}, dimensions={0} | all-to-all | bytes 2097152 | tf_op jit(solution)/shard_map/all_to_all | solution.py:212
  47.3 3.6 %all-to-all-start.1 = ((bf16[8,256,256]{2,1,0:T(8,128)(2,1)}), bf16[8,256,256]{2,1,0:T(8,128)(2,1)S(1)}, u32[]{:S(2)}, u32[]{:S(2)}) async-start(bf16[8,256,256]{2,1,0:T(8,128)(2,1)} %shard_map.61), calls=%async_computation.1 | async-start | bytes 2097152 | tf_op jit(solution)/shard_map/all_to_all | solution.py:214
  51.1 1.9 %collective-permute-start.1 = (bf16[512,256]{1,0:T(8,128)(2,1)S(1)}, bf16[512,256]{1,0:T(8,128)(2,1)S(1)}, u32[]{:S(2)}, u32[]{:S(2)}) collective-permute-start(bf16[512,256]{1,0:T(8,128)(2,1)S(1)} %bitcast.19), channel_id=1, source_target_pairs={{0,1},{1,0},{2,3},{3,2},{4,5},{5,4},{6,7},{7,6},{8,9},{9,8},{10,11... | collective-permute-start | bytes 786440 | tf_op jit(solution)/shard_map/ppermute | solution.py:24
  54.2 11.8 %all-to-all-done.1 = bf16[8,256,256]{2,1,0:T(8,128)(2,1)S(1)} async-done(((bf16[8,256,256]{2,1,0:T(8,128)(2,1)}), bf16[8,256,256]{2,1,0:T(8,128)(2,1)S(1)}, u32[]{:S(2)}, u32[]{:S(2)}) %all-to-all-start.1) | async-done | bytes 1048608 | tf_op jit(solution)/shard_map/all_to_all | solution.py:214
  66.0 4.7 %shard_map.62 = (bf16[256,512]{1,0:T(8,128)(2,1)S(1)}, bf16[256,512]{1,0:T(8,128)(2,1)S(1)}, bf16[8,32,2048]{2,1,0:T(8,128)(2,1)S(1)}) custom-call(bf16[2048,256]{1,0:T(8,128)(2,1)S(1)} %bitcast.12, bf16[512,256]{1,0:T(8,128)(2,1)S(1)} %bitcast.15, bf16[512,256]{1,0:T(8,128)(2,1)S(1)} %collective-permute-done.1.far, bf16[512,2048]{1,0:T(8,128)(2,1)} %a0.1, ...), custom_call_target="tpu_custom_call" | custom-call | flops 2147483648 | bytes 7340032 | tf_op jit(solution)/shard_map/pallas_call | solution.py:33
  71.4 19.6 %all_to_all.21.blocks = bf16[8,32,2048]{2,1,0:T(8,128)(2,1)S(1)} all-to-all(bf16[8,32,2048]{2,1,0:T(8,128)(2,1)S(1)} %get-tuple-element.20), channel_id=1, replica_groups=mesh['y_lo'=2,'x'=4,'z'=4,'y_hi'=2,'core'=2] {'z','y_hi'}, dimensions={0} | all-to-all | bytes 2097152 | tf_op jit(solution)/shard_map/all_to_all | solution.py:225
  91.0 1.3 shard_map.63
  92.3 5.2 %all-to-all-start.3 = ((bf16[32,32,512]{2,1,0:T(8,128)(2,1)}), bf16[32,32,512]{2,1,0:T(8,128)(2,1)S(1)}, u32[]{:S(2)}, u32[]{:S(2)}) async-start(bf16[32,32,512]{2,1,0:T(8,128)(2,1)} %bitcast.5), calls=%async_computation.3 | async-start | bytes 2097152 | tf_op jit(solution)/shard_map/all_to_all | solution.py:239
  97.6 2.9 %collective-permute-start.3 = (bf16[2048,256]{1,0:T(8,128)(2,1)S(1)}, bf16[2048,256]{1,0:T(8,128)(2,1)S(1)}, u32[]{:S(2)}, u32[]{:S(2)}) collective-permute-start(bf16[2048,256]{1,0:T(8,128)(2,1)S(1)} %bitcast.13), channel_id=1, source_target_pairs={{0,1},{1,0},{2,3},{3,2},{4,5},{5,4},{6,7},{7,6},{8,9},{9,8},{10,11... | collective-permute-start | bytes 3145736 | tf_op jit(solution)/shard_map/ppermute | solution.py:24
  100.4 14.1 %all-to-all-done.3 = bf16[32,32,512]{2,1,0:T(8,128)(2,1)S(1)} async-done(((bf16[32,32,512]{2,1,0:T(8,128)(2,1)}), bf16[32,32,512]{2,1,0:T(8,128)(2,1)S(1)}, u32[]{:S(2)}, u32[]{:S(2)}) %all-to-all-start.3) | async-done | bytes 1048608 | tf_op jit(solution)/shard_map/all_to_all | solution.py:239
  114.5 3.0 %collective-permute-start.8 = (bf16[4,256,512]{2,1,0:T(8,128)(2,1)S(1)}, bf16[4,256,512]{2,1,0:T(8,128)(2,1)S(1)}, u32[]{:S(2)}, u32[]{:S(2)}) collective-permute-start(bf16[4,256,512]{2,1,0:T(8,128)(2,1)S(1)} %bitcast.9), channel_id=1, source_target_pairs={{0,1},{1,0},{2,3},{3,2},{4,5},{5,4},{6,7},{7,6},{8,9},{9,8},{10,11... | collective-permute-start | bytes 3145736 | tf_op jit(solution)/shard_map/ppermute | solution.py:24
  117.5 2.7 %collective-permute-done.4.message = bf16[256,512]{1,0:T(8,128)(2,1)S(1)} collective-permute-done((bf16[256,512]{1,0:T(8,128)(2,1)S(1)}, bf16[256,512]{1,0:T(8,128)(2,1)S(1)}, u32[]{:S(2)}, u32[]{:S(2)}) %collective-permute-start.4) | collective-permute-done | bytes 262176 | tf_op jit(solution)/shard_map/ppermute | solution.py:24
  122.5 1.9 %collective-permute-start.6 = (bf16[2,256,512]{2,1,0:T(8,128)(2,1)S(1)}, bf16[2,256,512]{2,1,0:T(8,128)(2,1)S(1)}, u32[]{:S(2)}, u32[]{:S(2)}) collective-permute-start(bf16[2,256,512]{2,1,0:T(8,128)(2,1)S(1)} %get-tuple-element.26), channel_id=1, source_target_pairs={{0,32},{16,48},{32,0},{48,16},{1,33},{17,49},{33,1},{49,17},{2,34}... | collective-permute-start | bytes 1572872 | tf_op jit(solution)/shard_map/ppermute | solution.py:24
  125.1 6.9 %shard_map.67 = bf16[256,1792]{1,0:T(8,128)(2,1)} custom-call(bf16[4,256,512]{2,1,0:T(8,128)(2,1)S(1)} %bitcast.10, bf16[4,256,512]{2,1,0:T(8,128)(2,1)S(1)} %collective-permute-done.8.grad_o, bf16[4,512,1792]{2,1,0:T(8,128)(2,1)} %bitcast.16), custom_call_target="tpu_custom_call" | custom-call | flops 1879048192 | bytes 7340032 | tf_op jit(solution)/shard_map/pallas_call | solution.py:153
  132.7 4.8 %collective-permute-done.5.r1 = bf16[2,256,512]{2,1,0:T(8,128)(2,1)S(1)} collective-permute-done((bf16[2,256,512]{2,1,0:T(8,128)(2,1)S(1)}, bf16[2,256,512]{2,1,0:T(8,128)(2,1)S(1)}, u32[]{:S(2)}, u32[]{:S(2)}) %collective-permute-start.5) | collective-permute-done | bytes 524320 | tf_op jit(solution)/shard_map/ppermute | solution.py:24
  137.5 9.8 %collective-permute-done.6.r2 = bf16[2,256,512]{2,1,0:T(8,128)(2,1)S(1)} collective-permute-done((bf16[2,256,512]{2,1,0:T(8,128)(2,1)S(1)}, bf16[2,256,512]{2,1,0:T(8,128)(2,1)S(1)}, u32[]{:S(2)}, u32[]{:S(2)}) %collective-permute-start.6) | collective-permute-done | bytes 524320 | tf_op jit(solution)/shard_map/ppermute | solution.py:24
  149.2 5.9 %shard_map.65 = f32[256,1792]{1,0:T(8,128)S(1)} custom-call(bf16[4,256,512]{2,1,0:T(8,128)(2,1)S(1)} %bitcast.11, bf16[4,256,512]{2,1,0:T(8,128)(2,1)S(1)} %collective-permute-done.8.grad_o, bf16[4,512,1792]{2,1,0:T(8,128)(2,1)} %bitcast.17), custom_call_target="tpu_custom_call" | custom-call | flops 1879048192 | bytes 7340032 | tf_op jit(solution)/shard_map/pallas_call | solution.py:153
  155.0 3.8 %collective-permute-done.9 = bf16[256,512]{1,0:T(8,128)(2,1)S(1)} collective-permute-done((bf16[256,512]{1,0:T(8,128)(2,1)S(1)}, bf16[256,512]{1,0:T(8,128)(2,1)S(1)}, u32[]{:S(2)}, u32[]{:S(2)}) %collective-permute-start.9) | collective-permute-done | bytes 262176 | tf_op jit(solution)/shard_map/ppermute | solution.py:24
  159.9 2.6 %add_multiply_fusion = f32[256,1792]{1,0:T(8,128)} fusion(f32[256,1792]{1,0:T(8,128)S(1)} %shard_map.65, bf16[256,1792]{1,0:T(8,128)(2,1)} %collective-permute-done.10), kind=kLoop, calls=%fused_computation.1 | loop fusion | flops 1376256 | bytes 4587520 | tf_op jit(solution)/shard_map/mul | solution.py:249
  (33 shorter events, 11.6 us)
Async XLA Ops:
  7.2 1.5 copy-start.1
  7.2 83.9 %all-gather.3.cloned.1.call-start = ((), (), s32[]{:S(2)}) async-start(), calls=%async_computation.4 | async-start | bytes 9175040 | tf_op jit(solution)/shard_map/all_gather | solution.py:204
  8.7 3.1 %copy-start = (bf16[2048,1792]{1,0:T(8,128)(2,1)S(1)}, bf16[2048,1792]{1,0:T(8,128)(2,1)}, u32[]{:S(2)}) copy-start(bf16[2048,1792]{1,0:T(8,128)(2,1)} %b.3) | copy-start | bytes 22020100
  14.7 7.4 %collective-permute-start = (f32[2048,256]{1,0:T(8,128)S(1)}, f32[2048,256]{1,0:T(8,128)S(1)}, u32[]{:S(2)}, u32[]{:S(2)}) collective-permute-start(f32[2048,256]{1,0:T(8,128)S(1)} %shard_map.60), channel_id=1, source_target_pairs={{0,1},{1,0},{2,3},{3,2},{4,5},{5,4},{6,7},{7,6},{8,9},{9,8},{10,11... | collective-permute-start | bytes 6291464 | tf_op jit(solution)/shard_map/ppermute | solution.py:24
  16.2 38.0 %collective-permute-start.2 = (bf16[512,2048]{1,0:T(8,128)(2,1)}, bf16[512,2048]{1,0:T(8,128)(2,1)}, u32[]{:S(2)}, u32[]{:S(2)}) collective-permute-start(bf16[512,2048]{1,0:T(8,128)(2,1)} %a0.1), channel_id=1, source_target_pairs={{0,1},{1,0},{2,3},{3,2},{4,5},{5,4},{6,7},{7,6},{8,9},{9,8},{10,11... | collective-permute-start | bytes 6291464 | tf_op jit(solution)/shard_map/ppermute | solution.py:24
  46.2 4.7 %copy-start.4 = (bf16[512,512]{1,0:T(8,128)(2,1)S(1)}, bf16[512,512]{1,0:T(8,128)(2,1)}, u32[]{:S(2)}) copy-start(bf16[512,512]{1,0:T(8,128)(2,1)} %param.5) | copy-start | bytes 1572868
  47.3 18.6 %all-to-all-start.1 = ((bf16[8,256,256]{2,1,0:T(8,128)(2,1)}), bf16[8,256,256]{2,1,0:T(8,128)(2,1)S(1)}, u32[]{:S(2)}, u32[]{:S(2)}) async-start(bf16[8,256,256]{2,1,0:T(8,128)(2,1)} %shard_map.61), calls=%async_computation.1 | async-start | bytes 2097152 | tf_op jit(solution)/shard_map/all_to_all | solution.py:214
  51.1 3.1 %collective-permute-start.1 = (bf16[512,256]{1,0:T(8,128)(2,1)S(1)}, bf16[512,256]{1,0:T(8,128)(2,1)S(1)}, u32[]{:S(2)}, u32[]{:S(2)}) collective-permute-start(bf16[512,256]{1,0:T(8,128)(2,1)S(1)} %bitcast.19), channel_id=1, source_target_pairs={{0,1},{1,0},{2,3},{3,2},{4,5},{5,4},{6,7},{7,6},{8,9},{9,8},{10,11... | collective-permute-start | bytes 786440 | tf_op jit(solution)/shard_map/ppermute | solution.py:24
  70.7 0.7 copy-start.2
  92.3 22.2 %all-to-all-start.3 = ((bf16[32,32,512]{2,1,0:T(8,128)(2,1)}), bf16[32,32,512]{2,1,0:T(8,128)(2,1)S(1)}, u32[]{:S(2)}, u32[]{:S(2)}) async-start(bf16[32,32,512]{2,1,0:T(8,128)(2,1)} %bitcast.5), calls=%async_computation.3 | async-start | bytes 2097152 | tf_op jit(solution)/shard_map/all_to_all | solution.py:239
  97.6 22.6 %collective-permute-start.3 = (bf16[2048,256]{1,0:T(8,128)(2,1)S(1)}, bf16[2048,256]{1,0:T(8,128)(2,1)S(1)}, u32[]{:S(2)}, u32[]{:S(2)}) collective-permute-start(bf16[2048,256]{1,0:T(8,128)(2,1)S(1)} %bitcast.13), channel_id=1, source_target_pairs={{0,1},{1,0},{2,3},{3,2},{4,5},{5,4},{6,7},{7,6},{8,9},{9,8},{10,11... | collective-permute-start | bytes 3145736 | tf_op jit(solution)/shard_map/ppermute | solution.py:24
  114.5 10.6 %collective-permute-start.8 = (bf16[4,256,512]{2,1,0:T(8,128)(2,1)S(1)}, bf16[4,256,512]{2,1,0:T(8,128)(2,1)S(1)}, u32[]{:S(2)}, u32[]{:S(2)}) collective-permute-start(bf16[4,256,512]{2,1,0:T(8,128)(2,1)S(1)} %bitcast.9), channel_id=1, source_target_pairs={{0,1},{1,0},{2,3},{3,2},{4,5},{5,4},{6,7},{7,6},{8,9},{9,8},{10,11... | collective-permute-start | bytes 3145736 | tf_op jit(solution)/shard_map/ppermute | solution.py:24
  117.5 2.7 %collective-permute-start.4 = (bf16[256,512]{1,0:T(8,128)(2,1)S(1)}, bf16[256,512]{1,0:T(8,128)(2,1)S(1)}, u32[]{:S(2)}, u32[]{:S(2)}) collective-permute-start(bf16[256,512]{1,0:T(8,128)(2,1)S(1)} %get-tuple-element.23), channel_id=1, source_target_pairs={{0,1},{1,0},{2,3},{3,2},{4,5},{5,4},{6,7},{7,6},{8,9},{9,8},{10,11... | collective-permute-start | bytes 786440 | tf_op jit(solution)/shard_map/ppermute | solution.py:24
  120.2 1.0 copy-start.3
  122.4 15.1 %collective-permute-start.5 = (bf16[2,256,512]{2,1,0:T(8,128)(2,1)S(1)}, bf16[2,256,512]{2,1,0:T(8,128)(2,1)S(1)}, u32[]{:S(2)}, u32[]{:S(2)}) collective-permute-start(bf16[2,256,512]{2,1,0:T(8,128)(2,1)S(1)} %get-tuple-element.25), channel_id=1, source_target_pairs={{0,16},{16,32},{32,48},{48,0},{1,17},{17,33},{33,49},{49,1},{2,18}... | collective-permute-start | bytes 1572872 | tf_op jit(solution)/shard_map/ppermute | solution.py:24
  122.5 24.9 %collective-permute-start.6 = (bf16[2,256,512]{2,1,0:T(8,128)(2,1)S(1)}, bf16[2,256,512]{2,1,0:T(8,128)(2,1)S(1)}, u32[]{:S(2)}, u32[]{:S(2)}) collective-permute-start(bf16[2,256,512]{2,1,0:T(8,128)(2,1)S(1)} %get-tuple-element.26), channel_id=1, source_target_pairs={{0,32},{16,48},{32,0},{48,16},{1,33},{17,49},{33,1},{49,17},{2,34}... | collective-permute-start | bytes 1572872 | tf_op jit(solution)/shard_map/ppermute | solution.py:24
  124.4 24.1 %collective-permute-start.7 = (bf16[2,256,512]{2,1,0:T(8,128)(2,1)S(1)}, bf16[2,256,512]{2,1,0:T(8,128)(2,1)S(1)}, u32[]{:S(2)}, u32[]{:S(2)}) collective-permute-start(bf16[2,256,512]{2,1,0:T(8,128)(2,1)S(1)} %get-tuple-element.27), channel_id=1, source_target_pairs={{0,48},{16,0},{32,16},{48,32},{1,49},{17,1},{33,17},{49,33},{2,50}... | collective-permute-start | bytes 1572872 | tf_op jit(solution)/shard_map/ppermute | solution.py:24
  132.0 27.9 %collective-permute-start.10 = (bf16[256,1792]{1,0:T(8,128)(2,1)}, bf16[256,1792]{1,0:T(8,128)(2,1)}, u32[]{:S(2)}, u32[]{:S(2)}) collective-permute-start(bf16[256,1792]{1,0:T(8,128)(2,1)} %shard_map.67), channel_id=1, source_target_pairs={{0,64},{64,0},{1,65},{65,1},{2,66},{66,2},{3,67},{67,3},{4,68},{68... | collective-permute-start | bytes 2752520 | tf_op jit(solution)/shard_map/ppermute | solution.py:24
  148.7 10.1 %collective-permute-start.9 = (bf16[256,512]{1,0:T(8,128)(2,1)S(1)}, bf16[256,512]{1,0:T(8,128)(2,1)S(1)}, u32[]{:S(2)}, u32[]{:S(2)}) collective-permute-start(bf16[256,512]{1,0:T(8,128)(2,1)S(1)} %get-tuple-element.36), channel_id=1, source_target_pairs={{0,64},{64,0},{1,65},{65,1},{2,66},{66,2},{3,67},{67,3},{4,68},{68... | collective-permute-start | bytes 786440 | tf_op jit(solution)/shard_map/ppermute | solution.py:24
Sparse Core Ops, SparseCore 0:
  9.7 77.5 all-gather.2

commit v18 on v17

--- a/solution.py
+++ b/solution.py
@@ -231,10 +231,11 @@
         codes, own, codes_o, swap(message, "core"),
         flops=2 * tokens * rank * outs,
     )
-    terms = [terms[0]] + [shift(terms[k], "x", 4, k) for k in (1, 2, 3)]
+    near = [shift(terms[k], "x", 4, k) for k in (1, 3)]
 
     barrier = lax.optimization_barrier
-    blocks, row = barrier((blocks, row))
+    blocks, row, near, later = barrier((blocks, row, near, terms[2]))
+    terms = [terms[0], shift(later, "x", 4, 2)] + near
     split = call(spread_kernel, [like((4, 8, sub, 2 * width))], blocks, scratch=[pltpu.VMEM((sub, rank), BF)])
     grad = lax.all_to_all(split.reshape(32, sub, 2 * width), ("x", "z", "y_hi"), 0, 0)
     grad = grad.reshape(4, half, 2 * width)

time: 170 us -> 179 us (1.053)
  local copies, waits for them, and re-layouts: 6.79 us -> 9.95 us
  waiting for transfers between devices: 52.6 us -> 54.5 us
  blocking collectives: 43.5 us -> 45.3 us
    ppermute x11, waiting for transfers between devices: 26.1 us -> 31.6 us  [shift(): lax.ppermute(array, axis, [(i, (i + step) % size) for i in range(size)])]
    all_to_all x2, waiting for transfers between devices: 25.8 us -> 22.2 us  [the longest x1 15.9 us: local(): blocks = lax.all_to_all(mine, ZY, 0, 0)]
    unnamed x13 -> x21, local copies, waits for them, and re-layouts: 6.75 us -> 9.92 us
    all_to_all x2, starting transfers between devices: 8.81 us -> 11.3 us  [the longest x1 7.75 us: local(): blocks = lax.all_to_all(mine, ZY, 0, 0)]
    all_to_all x2, blocking collectives: 43.5 us -> 45.3 us  [the longest x1 25.8 us: local(): lax.all_to_all(split.reshape(32, sub, 2 * width), ('x', 'z', 'y_hi'), 0, 0)]
where the time goes in v18:
time: 179 us
  waiting for transfers between devices  54.5 us (30%)
  blocking collectives  45.3 us (25%)
  Pallas kernels  27 us (15%)
  starting transfers between devices  23.8 us (13%)
  between operations  14.1 us (8%)
  local copies, waits for them, and re-layouts  9.95 us (6%)
  other arithmetic  3.84 us (2%)
    ppermute x11, waiting for transfers between devices, shift(): lax.ppermute(array, axis, [(i, (i + step) % size) for i in range(size)])  31.6 us
    all_to_all x1, blocking collectives, local(): lax.all_to_all(split.reshape(32, sub, 2 * width), ('x', 'z', 'y_hi'), 0, 0)  25.8 us
    all_to_all x1, blocking collectives, local(): codes = lax.all_to_all(codes, ZY, 0, 0).reshape(rank, half)  19.5 us
    all_to_all x1, waiting for transfers between devices, local(): blocks = lax.all_to_all(mine, ZY, 0, 0)  15.9 us
    pallas_call x2, Pallas kernels, last_call(): pl.pallas_call(functools.partial(last_kernel, side), out_shape=like((widt...  12.7 us
    ppermute x11, starting transfers between devices, shift(): lax.ppermute(array, axis, [(i, (i + step) % size) for i in range(size)])  12.5 us
    unnamed x21, local copies, waits for them, and re-layouts  9.92 us
    pallas_call x5, Pallas kernels, call(): pl.pallas_call(body, out_shape=outs if len(outs) > 1 else outs[0], in_spe...  8.44 us
  transfers between devices with their start and end apart: 14, of which 9 were waited for; matrix products, arithmetic and copies ran while one was open for 1% of the time, Pallas kernels for 15%

profile of v18, /device:TPU:1, one launch (start us, length us, event | category | flops | bytes accessed | tf_op | source)
XLA Modules:
  0.0 178.6 jit_solution(6217321381976468484)
XLA Ops:
  8.7 3.1 %copy-done = bf16[2048,1792]{1,0:T(8,128)(2,1)S(1)} copy-done((bf16[2048,1792]{1,0:T(8,128)(2,1)S(1)}, bf16[2048,1792]{1,0:T(8,128)(2,1)}, u32[]{:S(2)}) %copy-start) | copy-done | bytes 7340056
  11.7 2.9 %shard_map.60 = f32[2048,256]{1,0:T(8,128)S(1)} custom-call(bf16[512,1792]{1,0:T(8,128)(2,1)S(1)} %copy-done.1, bf16[2048,1792]{1,0:T(8,128)(2,1)S(1)} %copy-done), custom_call_target="tpu_custom_call" | custom-call | flops 1879048192 | bytes 7340032 | tf_op jit(solution)/shard_map/pallas_call | solution.py:69
  14.7 1.5 collective-permute-start
  16.2 2.9 %shard_map.59 = f32[2048,256]{1,0:T(8,128)S(1)} custom-call(bf16[512,1792]{1,0:T(8,128)(2,1)S(1)} %copy-done.1, bf16[2048,1792]{1,0:T(8,128)(2,1)S(1)} %copy-done), custom_call_target="tpu_custom_call" | custom-call | flops 1879048192 | bytes 7340032 | tf_op jit(solution)/shard_map/pallas_call | solution.py:69
  21.1 7.7 %all-to-all-start = ((bf16[8,256,256]{2,1,0:T(8,128)(2,1)}), bf16[8,256,256]{2,1,0:T(8,128)(2,1)S(1)}, u32[]{:S(2)}, u32[]{:S(2)}) async-start(bf16[8,256,256]{2,1,0:T(8,128)(2,1)} %bitcast), calls=%async_computation | async-start | bytes 2097152 | tf_op jit(solution)/shard_map/all_to_all | solution.py:212
  29.6 15.9 %all-to-all-done.blocks = bf16[8,256,256]{2,1,0:T(8,128)(2,1)S(1)} async-done(((bf16[8,256,256]{2,1,0:T(8,128)(2,1)}), bf16[8,256,256]{2,1,0:T(8,128)(2,1)S(1)}, u32[]{:S(2)}, u32[]{:S(2)}) %all-to-all-start) | async-done | bytes 1048608 | tf_op jit(solution)/shard_map/all_to_all | solution.py:212
  45.7 19.5 %all_to_all.20 = bf16[8,256,256]{2,1,0:T(8,128)(2,1)S(1)} all-to-all(bf16[8,256,256]{2,1,0:T(8,128)(2,1)S(1)} %shard_map.61), channel_id=1, replica_groups=mesh['y_lo'=2,'x'=4,'z'=4,'y_hi'=2,'core'=2] {'z','y_hi'}, dimensions={0} | all-to-all | bytes 2097152 | tf_op jit(solution)/shard_map/all_to_all | solution.py:214
  65.2 1.9 %collective-permute-start.3 = (bf16[2048,256]{1,0:T(8,128)(2,1)S(1)}, bf16[2048,256]{1,0:T(8,128)(2,1)S(1)}, u32[]{:S(2)}, u32[]{:S(2)}) collective-permute-start(bf16[2048,256]{1,0:T(8,128)(2,1)S(1)} %bitcast.13), channel_id=1, source_target_pairs={{0,1},{1,0},{2,3},{3,2},{4,5},{5,4},{6,7},{7,6},{8,9},{9,8},{10,11... | collective-permute-start | bytes 3145736 | tf_op jit(solution)/shard_map/ppermute | solution.py:24
  67.5 2.2 %collective-permute-done.1.far = bf16[512,256]{1,0:T(8,128)(2,1)S(1)} collective-permute-done((bf16[512,256]{1,0:T(8,128)(2,1)S(1)}, bf16[512,256]{1,0:T(8,128)(2,1)S(1)}, u32[]{:S(2)}, u32[]{:S(2)}) %collective-permute-start.1) | collective-permute-done | bytes 262176 | tf_op jit(solution)/shard_map/ppermute | solution.py:24
  69.8 5.7 %shard_map.62 = (bf16[256,512]{1,0:T(8,128)(2,1)S(1)}, bf16[256,512]{1,0:T(8,128)(2,1)S(1)}, bf16[8,32,2048]{2,1,0:T(8,128)(2,1)}) custom-call(bf16[2048,256]{1,0:T(8,128)(2,1)S(1)} %bitcast.14, bf16[512,256]{1,0:T(8,128)(2,1)S(1)} %bitcast.16, bf16[512,256]{1,0:T(8,128)(2,1)S(1)} %collective-permute-done.1.far, bf16[512,2048]{1,0:T(8,128)(2,1)} %a0.1, ...), custom_call_target="tpu_custom_call" | custom-call | flops 2147483648 | bytes 7340032 | tf_op jit(solution)/shard_map/pallas_call | solution.py:33
  76.2 3.6 %all-to-all-start.2 = ((bf16[8,32,2048]{2,1,0:T(8,128)(2,1)}), bf16[8,32,2048]{2,1,0:T(8,128)(2,1)S(1)}, u32[]{:S(2)}, u32[]{:S(2)}) async-start(bf16[8,32,2048]{2,1,0:T(8,128)(2,1)} %get-tuple-element.23), calls=%async_computation.2 | async-start | bytes 2097152 | tf_op jit(solution)/shard_map/all_to_all | solution.py:225
  82.5 1.2 copy-done.3
  84.7 2.1 %shard_map.63 = (f32[2,256,512]{2,1,0:T(8,128)S(1)}, bf16[2,256,512]{2,1,0:T(8,128)(2,1)}, bf16[2,256,512]{2,1,0:T(8,128)(2,1)S(1)}, bf16[2,256,512]{2,1,0:T(8,128)(2,1)}) custom-call(bf16[2048,256]{1,0:T(8,128)(2,1)S(1)} %bitcast.15, bf16[256,512]{1,0:T(8,128)(2,1)S(1)} %copy-done.7, bf16[2048,256]{1,0:T(8,128)(2,1)S(1)} %copy-done.3, ...), custom_call_target="tpu_custom_call" | custom-call | flops 1073741824 | bytes 5242880 | tf_op jit(solution)/shard_map/pallas_call | solution.py:33
  88.8 1.5 collective-permute-start.6
  90.3 6.3 %all-to-all-done.2.blocks = bf16[8,32,2048]{2,1,0:T(8,128)(2,1)S(1)} async-done(((bf16[8,32,2048]{2,1,0:T(8,128)(2,1)}), bf16[8,32,2048]{2,1,0:T(8,128)(2,1)S(1)}, u32[]{:S(2)}, u32[]{:S(2)}) %all-to-all-start.2) | async-done | bytes 1048608 | tf_op jit(solution)/shard_map/all_to_all | solution.py:225
  96.6 5.5 %collective-permute-done.5.r2 = bf16[2,256,512]{2,1,0:T(8,128)(2,1)S(1)} collective-permute-done((bf16[2,256,512]{2,1,0:T(8,128)(2,1)}, bf16[2,256,512]{2,1,0:T(8,128)(2,1)S(1)}, u32[]{:S(2)}, u32[]{:S(2)}) %collective-permute-start.5) | collective-permute-done | bytes 524320 | tf_op jit(solution)/shard_map/ppermute | solution.py:24
  102.5 25.8 %all_to_all.21 = bf16[32,32,512]{2,1,0:T(8,128)(2,1)S(1)} all-to-all(bf16[32,32,512]{2,1,0:T(8,128)(2,1)S(1)} %bitcast.12), channel_id=1, replica_groups=mesh['y_lo'=2,'x'=4,'z'=4,'y_hi'=2,'core'=2] {'x','z','y_hi'}, dimensions={0} | all-to-all | bytes 2097152 | tf_op jit(solution)/shard_map/all_to_all | solution.py:240
  128.3 3.2 %collective-permute-start.8 = (bf16[4,256,512]{2,1,0:T(8,128)(2,1)S(1)}, bf16[4,256,512]{2,1,0:T(8,128)(2,1)S(1)}, u32[]{:S(2)}, u32[]{:S(2)}) collective-permute-start(bf16[4,256,512]{2,1,0:T(8,128)(2,1)S(1)} %bitcast.9), channel_id=1, source_target_pairs={{0,1},{1,0},{2,3},{3,2},{4,5},{5,4},{6,7},{7,6},{8,9},{9,8},{10,11... | collective-permute-start | bytes 3145736 | tf_op jit(solution)/shard_map/ppermute | solution.py:24
  131.9 1.8 collective-permute-done.8.grad_o
  133.7 6.9 %shard_map.67 = bf16[256,1792]{1,0:T(8,128)(2,1)} custom-call(bf16[4,256,512]{2,1,0:T(8,128)(2,1)S(1)} %bitcast.10, bf16[4,256,512]{2,1,0:T(8,128)(2,1)S(1)} %collective-permute-done.8.grad_o, bf16[4,512,1792]{2,1,0:T(8,128)(2,1)} %bitcast.17), custom_call_target="tpu_custom_call" | custom-call | flops 1879048192 | bytes 7340032 | tf_op jit(solution)/shard_map/pallas_call | solution.py:153
  141.2 5.3 %collective-permute-done.7.r1 = bf16[2,256,512]{2,1,0:T(8,128)(2,1)S(1)} collective-permute-done((bf16[2,256,512]{2,1,0:T(8,128)(2,1)S(1)}, bf16[2,256,512]{2,1,0:T(8,128)(2,1)S(1)}, u32[]{:S(2)}, u32[]{:S(2)}) %collective-permute-start.7) | collective-permute-done | bytes 524320 | tf_op jit(solution)/shard_map/ppermute | solution.py:24
  147.5 5.9 %shard_map.65 = f32[256,1792]{1,0:T(8,128)S(1)} custom-call(bf16[4,256,512]{2,1,0:T(8,128)(2,1)S(1)} %bitcast.11, bf16[4,256,512]{2,1,0:T(8,128)(2,1)S(1)} %collective-permute-done.8.grad_o, bf16[4,512,1792]{2,1,0:T(8,128)(2,1)} %bitcast.18), custom_call_target="tpu_custom_call" | custom-call | flops 1879048192 | bytes 7340032 | tf_op jit(solution)/shard_map/pallas_call | solution.py:153
  153.4 14.7 %collective-permute-done.9 = bf16[256,512]{1,0:T(8,128)(2,1)S(1)} collective-permute-done((bf16[256,512]{1,0:T(8,128)(2,1)S(1)}, bf16[256,512]{1,0:T(8,128)(2,1)S(1)}, u32[]{:S(2)}, u32[]{:S(2)}) %collective-permute-start.9) | collective-permute-done | bytes 262176 | tf_op jit(solution)/shard_map/ppermute | solution.py:24
  169.1 2.6 %add_multiply_fusion = f32[256,1792]{1,0:T(8,128)} fusion(f32[256,1792]{1,0:T(8,128)S(1)} %shard_map.65, bf16[256,1792]{1,0:T(8,128)(2,1)} %collective-permute-done.10), kind=kLoop, calls=%fused_computation.1 | loop fusion | flops 1376256 | bytes 4587520 | tf_op jit(solution)/shard_map/mul | solution.py:250
  (41 shorter events, 14.7 us)
Async XLA Ops:
  7.2 1.5 copy-start.1
  7.2 95.0 %all-gather.3.cloned.1.call-start = ((), (), s32[]{:S(2)}) async-start(), calls=%async_computation.4 | async-start | bytes 9175040 | tf_op jit(solution)/shard_map/all_gather | solution.py:204
  8.7 3.1 %copy-start = (bf16[2048,1792]{1,0:T(8,128)(2,1)S(1)}, bf16[2048,1792]{1,0:T(8,128)(2,1)}, u32[]{:S(2)}) copy-start(bf16[2048,1792]{1,0:T(8,128)(2,1)} %b.3) | copy-start | bytes 22020100
  14.7 5.3 %collective-permute-start = (f32[2048,256]{1,0:T(8,128)S(1)}, f32[2048,256]{1,0:T(8,128)S(1)}, u32[]{:S(2)}, u32[]{:S(2)}) collective-permute-start(f32[2048,256]{1,0:T(8,128)S(1)} %shard_map.60), channel_id=1, source_target_pairs={{0,1},{1,0},{2,3},{3,2},{4,5},{5,4},{6,7},{7,6},{8,9},{9,8},{10,11... | collective-permute-start | bytes 6291464 | tf_op jit(solution)/shard_map/ppermute | solution.py:24
  21.1 24.4 %all-to-all-start = ((bf16[8,256,256]{2,1,0:T(8,128)(2,1)}), bf16[8,256,256]{2,1,0:T(8,128)(2,1)S(1)}, u32[]{:S(2)}, u32[]{:S(2)}) async-start(bf16[8,256,256]{2,1,0:T(8,128)(2,1)} %bitcast), calls=%async_computation | async-start | bytes 2097152 | tf_op jit(solution)/shard_map/all_to_all | solution.py:212
  28.9 38.2 %copy-start.8 = (bf16[512,512]{1,0:T(8,128)(2,1)S(1)}, bf16[512,512]{1,0:T(8,128)(2,1)}, u32[]{:S(2)}) copy-start(bf16[512,512]{1,0:T(8,128)(2,1)} %param.5) | copy-start | bytes 1572868
  28.9 40.9 %collective-permute-start.2 = (bf16[512,2048]{1,0:T(8,128)(2,1)}, bf16[512,2048]{1,0:T(8,128)(2,1)}, u32[]{:S(2)}, u32[]{:S(2)}) collective-permute-start(bf16[512,2048]{1,0:T(8,128)(2,1)} %a0.1), channel_id=1, source_target_pairs={{0,1},{1,0},{2,3},{3,2},{4,5},{5,4},{6,7},{7,6},{8,9},{9,8},{10,11... | collective-permute-start | bytes 6291464 | tf_op jit(solution)/shard_map/ppermute | solution.py:24
  65.2 16.3 %collective-permute-start.3 = (bf16[2048,256]{1,0:T(8,128)(2,1)S(1)}, bf16[2048,256]{1,0:T(8,128)(2,1)S(1)}, u32[]{:S(2)}, u32[]{:S(2)}) collective-permute-start(bf16[2048,256]{1,0:T(8,128)(2,1)S(1)} %bitcast.13), channel_id=1, source_target_pairs={{0,1},{1,0},{2,3},{3,2},{4,5},{5,4},{6,7},{7,6},{8,9},{9,8},{10,11... | collective-permute-start | bytes 3145736 | tf_op jit(solution)/shard_map/ppermute | solution.py:24
  67.3 2.5 %collective-permute-start.1 = (bf16[512,256]{1,0:T(8,128)(2,1)S(1)}, bf16[512,256]{1,0:T(8,128)(2,1)S(1)}, u32[]{:S(2)}, u32[]{:S(2)}) collective-permute-start(bf16[512,256]{1,0:T(8,128)(2,1)S(1)} %bitcast.19), channel_id=1, source_target_pairs={{0,1},{1,0},{2,3},{3,2},{4,5},{5,4},{6,7},{7,6},{8,9},{9,8},{10,11... | collective-permute-start | bytes 786440 | tf_op jit(solution)/shard_map/ppermute | solution.py:24
  75.5 0.7 copy-start.6
  76.2 20.4 %all-to-all-start.2 = ((bf16[8,32,2048]{2,1,0:T(8,128)(2,1)}), bf16[8,32,2048]{2,1,0:T(8,128)(2,1)S(1)}, u32[]{:S(2)}, u32[]{:S(2)}) async-start(bf16[8,32,2048]{2,1,0:T(8,128)(2,1)} %get-tuple-element.23), calls=%async_computation.2 | async-start | bytes 2097152 | tf_op jit(solution)/shard_map/all_to_all | solution.py:225
  79.8 1.6 collective-permute-start.4
  81.4 1.1 copy-start.2
  82.5 1.2 copy-start.3
  83.7 0.9 copy-start.7
  86.8 0.9 copy-start.4
  87.6 14.6 %collective-permute-start.5 = (bf16[2,256,512]{2,1,0:T(8,128)(2,1)}, bf16[2,256,512]{2,1,0:T(8,128)(2,1)S(1)}, u32[]{:S(2)}, u32[]{:S(2)}) collective-permute-start(bf16[2,256,512]{2,1,0:T(8,128)(2,1)} %get-tuple-element.26), channel_id=1, source_target_pairs={{0,16},{16,32},{32,48},{48,0},{1,17},{17,33},{33,49},{49,1},{2,18}... | collective-permute-start | bytes 1572872 | tf_op jit(solution)/shard_map/ppermute | solution.py:24
  88.8 13.4 %collective-permute-start.6 = (bf16[2,256,512]{2,1,0:T(8,128)(2,1)}, bf16[2,256,512]{2,1,0:T(8,128)(2,1)S(1)}, u32[]{:S(2)}, u32[]{:S(2)}) collective-permute-start(bf16[2,256,512]{2,1,0:T(8,128)(2,1)} %get-tuple-element.27), channel_id=1, source_target_pairs={{0,48},{16,0},{32,16},{48,32},{1,49},{17,1},{33,17},{49,33},{2,50}... | collective-permute-start | bytes 1572872 | tf_op jit(solution)/shard_map/ppermute | solution.py:24
  102.2 29.3 %copy-start.5 = (bf16[2,256,512]{2,1,0:T(8,128)(2,1)S(1)}, bf16[2,256,512]{2,1,0:T(8,128)(2,1)}, u32[]{:S(2)}) copy-start(bf16[2,256,512]{2,1,0:T(8,128)(2,1)} %copy-done.4) | copy-start | bytes 1572868
  128.3 5.5 %collective-permute-start.8 = (bf16[4,256,512]{2,1,0:T(8,128)(2,1)S(1)}, bf16[4,256,512]{2,1,0:T(8,128)(2,1)S(1)}, u32[]{:S(2)}, u32[]{:S(2)}) collective-permute-start(bf16[4,256,512]{2,1,0:T(8,128)(2,1)S(1)} %bitcast.9), channel_id=1, source_target_pairs={{0,1},{1,0},{2,3},{3,2},{4,5},{5,4},{6,7},{7,6},{8,9},{9,8},{10,11... | collective-permute-start | bytes 3145736 | tf_op jit(solution)/shard_map/ppermute | solution.py:24
  131.4 15.1 %collective-permute-start.7 = (bf16[2,256,512]{2,1,0:T(8,128)(2,1)S(1)}, bf16[2,256,512]{2,1,0:T(8,128)(2,1)S(1)}, u32[]{:S(2)}, u32[]{:S(2)}) collective-permute-start(bf16[2,256,512]{2,1,0:T(8,128)(2,1)S(1)} %copy-done.5), channel_id=1, source_target_pairs={{0,32},{16,48},{32,0},{48,16},{1,33},{17,49},{33,1},{49,17},{2,34}... | collective-permute-start | bytes 1572872 | tf_op jit(solution)/shard_map/ppermute | solution.py:24
  140.6 28.5 %collective-permute-start.10 = (bf16[256,1792]{1,0:T(8,128)(2,1)}, bf16[256,1792]{1,0:T(8,128)(2,1)}, u32[]{:S(2)}, u32[]{:S(2)}) collective-permute-start(bf16[256,1792]{1,0:T(8,128)(2,1)} %shard_map.67), channel_id=1, source_target_pairs={{0,64},{64,0},{1,65},{65,1},{2,66},{66,2},{3,67},{67,3},{4,68},{68... | collective-permute-start | bytes 2752520 | tf_op jit(solution)/shard_map/ppermute | solution.py:24
  146.7 21.4 %collective-permute-start.9 = (bf16[256,512]{1,0:T(8,128)(2,1)S(1)}, bf16[256,512]{1,0:T(8,128)(2,1)S(1)}, u32[]{:S(2)}, u32[]{:S(2)}) collective-permute-start(bf16[256,512]{1,0:T(8,128)(2,1)S(1)} %get-tuple-element.42), channel_id=1, source_target_pairs={{0,64},{64,0},{1,65},{65,1},{2,66},{66,2},{3,67},{67,3},{4,68},{68... | collective-permute-start | bytes 786440 | tf_op jit(solution)/shard_map/ppermute | solution.py:24
Sparse Core Ops, SparseCore 0:
  9.7 77.5 all-gather.2

commit v19 on v17

--- a/solution.py
+++ b/solution.py
@@ -234,7 +234,7 @@
     terms = [terms[0]] + [shift(terms[k], "x", 4, k) for k in (1, 2, 3)]
 
     barrier = lax.optimization_barrier
-    blocks, row = barrier((blocks, row))
+    blocks, row, terms[0] = barrier((blocks, row, terms[0]))
     split = call(spread_kernel, [like((4, 8, sub, 2 * width))], blocks, scratch=[pltpu.VMEM((sub, rank), BF)])
     grad = lax.all_to_all(split.reshape(32, sub, 2 * width), ("x", "z", "y_hi"), 0, 0)
     grad = grad.reshape(4, half, 2 * width)

time: 170 us -> 170 us (level)
  waiting for transfers between devices: 52.6 us -> 46.7 us
  local copies, waits for them, and re-layouts: 6.79 us -> 11.6 us
  blocking collectives: 43.5 us -> 47.1 us
  starting transfers between devices: 22.1 us -> 20.1 us
    all_to_all x1, waiting for transfers between devices: 14.1 us -> 8.67 us  [local(): blocks = lax.all_to_all(partial, ZY, 0, 0)]
    unnamed x13 -> x29, local copies, waits for them, and re-layouts: 6.75 us -> 11.5 us
    all_to_all x1, blocking collectives: 19.6 us -> 23.2 us  [local(): lax.all_to_all(split.reshape(32, sub, 2 * width), ('x', 'z', 'y_hi'), 0, 0)]
    ppermute x11, waiting for transfers between devices: 26.1 us -> 24.3 us  [shift(): lax.ppermute(array, axis, [(i, (i + step) % size) for i in range(size)])]
  transfers between devices with their start and end apart: 14 -> 14, of which waited for: 9 -> 7; matrix products, arithmetic and copies ran while one was open for 1% -> 1% of each run, Pallas kernels for 15% -> 16%
where the time goes in v19:
time: 170 us
  blocking collectives  47.1 us (28%)
  waiting for transfers between devices  46.7 us (27%)
  Pallas kernels  27.2 us (16%)
  starting transfers between devices  20.1 us (12%)
  between operations  14.2 us (8%)
  local copies, waits for them, and re-layouts  11.6 us (7%)
  other arithmetic  2.99 us (2%)
    ppermute x11, waiting for transfers between devices, shift(): lax.ppermute(array, axis, [(i, (i + step) % size) for i in range(size)])  24.3 us
    all_to_all x1, blocking collectives, local(): blocks = lax.all_to_all(mine, ZY, 0, 0)  23.9 us
    all_to_all x1, blocking collectives, local(): lax.all_to_all(split.reshape(32, sub, 2 * width), ('x', 'z', 'y_hi'), 0, 0)  23.2 us
    all_to_all x1, waiting for transfers between devices, local(): codes = lax.all_to_all(codes, ZY, 0, 0).reshape(rank, half)  13 us
    ppermute x11, starting transfers between devices, shift(): lax.ppermute(array, axis, [(i, (i + step) % size) for i in range(size)])  12.9 us
    pallas_call x2, Pallas kernels, last_call(): pl.pallas_call(functools.partial(last_kernel, side), out_shape=like((widt...  12.7 us
    unnamed x29, local copies, waits for them, and re-layouts  11.5 us
    all_to_all x1, waiting for transfers between devices, local(): blocks = lax.all_to_all(partial, ZY, 0, 0)  8.67 us
  transfers between devices with their start and end apart: 14, of which 7 were waited for; matrix products, arithmetic and copies ran while one was open for 1% of the time, Pallas kernels for 16%

profile of v19, /device:TPU:1, one launch (start us, length us, event | category | flops | bytes accessed | tf_op | source)
XLA Modules:
  0.0 169.7 jit_solution(8613040686765485329)
XLA Ops:
  8.7 3.1 %copy-done = bf16[2048,1792]{1,0:T(8,128)(2,1)S(1)} copy-done((bf16[2048,1792]{1,0:T(8,128)(2,1)S(1)}, bf16[2048,1792]{1,0:T(8,128)(2,1)}, u32[]{:S(2)}) %copy-start) | copy-done | bytes 7340056
  11.7 2.9 %shard_map.60 = f32[2048,256]{1,0:T(8,128)S(1)} custom-call(bf16[512,1792]{1,0:T(8,128)(2,1)S(1)} %copy-done.1, bf16[2048,1792]{1,0:T(8,128)(2,1)S(1)} %copy-done), custom_call_target="tpu_custom_call" | custom-call | flops 1879048192 | bytes 7340032 | tf_op jit(solution)/shard_map/pallas_call | solution.py:69
  14.7 1.5 collective-permute-start
  16.3 2.9 %shard_map.59 = f32[2048,256]{1,0:T(8,128)S(1)} custom-call(bf16[512,1792]{1,0:T(8,128)(2,1)S(1)} %copy-done.1, bf16[2048,1792]{1,0:T(8,128)(2,1)S(1)} %copy-done), custom_call_target="tpu_custom_call" | custom-call | flops 1879048192 | bytes 7340032 | tf_op jit(solution)/shard_map/pallas_call | solution.py:69
  19.2 2.8 %collective-permute-done = f32[2048,256]{1,0:T(8,128)S(1)} collective-permute-done((f32[2048,256]{1,0:T(8,128)S(1)}, f32[2048,256]{1,0:T(8,128)S(1)}, u32[]{:S(2)}, u32[]{:S(2)}) %collective-permute-start) | collective-permute-done | bytes 2097184 | tf_op jit(solution)/shard_map/ppermute | solution.py:24
  22.4 23.9 %all_to_all.20.blocks = bf16[8,256,256]{2,1,0:T(8,128)(2,1)S(1)} all-to-all(bf16[8,256,256]{2,1,0:T(8,128)(2,1)S(1)} %bitcast.19), channel_id=1, replica_groups=mesh['y_lo'=2,'x'=4,'z'=4,'y_hi'=2,'core'=2] {'z','y_hi'}, dimensions={0} | all-to-all | bytes 2097152 | tf_op jit(solution)/shard_map/all_to_all | solution.py:212
  47.3 3.6 %all-to-all-start.1 = ((bf16[8,256,256]{2,1,0:T(8,128)(2,1)}), bf16[8,256,256]{2,1,0:T(8,128)(2,1)S(1)}, u32[]{:S(2)}, u32[]{:S(2)}) async-start(bf16[8,256,256]{2,1,0:T(8,128)(2,1)} %shard_map.61), calls=%async_computation.1 | async-start | bytes 2097152 | tf_op jit(solution)/shard_map/all_to_all | solution.py:214
  51.1 1.9 %collective-permute-start.1 = (bf16[512,256]{1,0:T(8,128)(2,1)S(1)}, bf16[512,256]{1,0:T(8,128)(2,1)S(1)}, u32[]{:S(2)}, u32[]{:S(2)}) collective-permute-start(bf16[512,256]{1,0:T(8,128)(2,1)S(1)} %bitcast.20), channel_id=1, source_target_pairs={{0,1},{1,0},{2,3},{3,2},{4,5},{5,4},{6,7},{7,6},{8,9},{9,8},{10,11... | collective-permute-start | bytes 786440 | tf_op jit(solution)/shard_map/ppermute | solution.py:24
  53.0 13.0 %all-to-all-done.1 = bf16[8,256,256]{2,1,0:T(8,128)(2,1)S(1)} async-done(((bf16[8,256,256]{2,1,0:T(8,128)(2,1)}), bf16[8,256,256]{2,1,0:T(8,128)(2,1)S(1)}, u32[]{:S(2)}, u32[]{:S(2)}) %all-to-all-start.1) | async-done | bytes 1048608 | tf_op jit(solution)/shard_map/all_to_all | solution.py:214
  66.0 3.0 %collective-permute-start.3 = (bf16[2048,256]{1,0:T(8,128)(2,1)S(1)}, bf16[2048,256]{1,0:T(8,128)(2,1)S(1)}, u32[]{:S(2)}, u32[]{:S(2)}) collective-permute-start(bf16[2048,256]{1,0:T(8,128)(2,1)S(1)} %bitcast.13), channel_id=1, source_target_pairs={{0,1},{1,0},{2,3},{3,2},{4,5},{5,4},{6,7},{7,6},{8,9},{9,8},{10,11... | collective-permute-start | bytes 3145736 | tf_op jit(solution)/shard_map/ppermute | solution.py:24
  69.2 5.8 %shard_map.62 = (bf16[256,512]{1,0:T(8,128)(2,1)S(1)}, bf16[256,512]{1,0:T(8,128)(2,1)S(1)}, bf16[8,32,2048]{2,1,0:T(8,128)(2,1)}) custom-call(bf16[2048,256]{1,0:T(8,128)(2,1)S(1)} %bitcast.14, bf16[512,256]{1,0:T(8,128)(2,1)S(1)} %bitcast.16, bf16[512,256]{1,0:T(8,128)(2,1)S(1)} %collective-permute-done.1.far, bf16[512,2048]{1,0:T(8,128)(2,1)} %a0.1, ...), custom_call_target="tpu_custom_call" | custom-call | flops 2147483648 | bytes 7340032 | tf_op jit(solution)/shard_map/pallas_call | solution.py:33
  75.7 3.6 %all-to-all-start.2 = ((bf16[8,32,2048]{2,1,0:T(8,128)(2,1)}), bf16[8,32,2048]{2,1,0:T(8,128)(2,1)S(1)}, u32[]{:S(2)}, u32[]{:S(2)}) async-start(bf16[8,32,2048]{2,1,0:T(8,128)(2,1)} %get-tuple-element.21), calls=%async_computation.2 | async-start | bytes 2097152 | tf_op jit(solution)/shard_map/all_to_all | solution.py:225
  79.3 1.5 collective-permute-done.4.message
  81.9 1.2 copy-done.3
  84.1 1.2 shard_map.63
  87.8 8.7 %all-to-all-done.2.blocks = bf16[8,32,2048]{2,1,0:T(8,128)(2,1)S(1)} async-done(((bf16[8,32,2048]{2,1,0:T(8,128)(2,1)}), bf16[8,32,2048]{2,1,0:T(8,128)(2,1)S(1)}, u32[]{:S(2)}, u32[]{:S(2)}) %all-to-all-start.2) | async-done | bytes 1048608 | tf_op jit(solution)/shard_map/all_to_all | solution.py:225
  96.8 23.2 %all_to_all.21 = bf16[32,32,512]{2,1,0:T(8,128)(2,1)S(1)} all-to-all(bf16[32,32,512]{2,1,0:T(8,128)(2,1)S(1)} %bitcast.12), channel_id=1, replica_groups=mesh['y_lo'=2,'x'=4,'z'=4,'y_hi'=2,'core'=2] {'x','z','y_hi'}, dimensions={0} | all-to-all | bytes 2097152 | tf_op jit(solution)/shard_map/all_to_all | solution.py:239
  120.0 2.3 %collective-permute-start.8 = (bf16[4,256,512]{2,1,0:T(8,128)(2,1)S(1)}, bf16[4,256,512]{2,1,0:T(8,128)(2,1)S(1)}, u32[]{:S(2)}, u32[]{:S(2)}) collective-permute-start(bf16[4,256,512]{2,1,0:T(8,128)(2,1)S(1)} %bitcast.9), channel_id=1, source_target_pairs={{0,1},{1,0},{2,3},{3,2},{4,5},{5,4},{6,7},{7,6},{8,9},{9,8},{10,11... | collective-permute-start | bytes 3145736 | tf_op jit(solution)/shard_map/ppermute | solution.py:24
  122.3 1.9 %collective-permute-start.6 = (bf16[2,256,512]{2,1,0:T(8,128)(2,1)S(1)}, bf16[2,256,512]{2,1,0:T(8,128)(2,1)S(1)}, u32[]{:S(2)}, u32[]{:S(2)}) collective-permute-start(bf16[2,256,512]{2,1,0:T(8,128)(2,1)S(1)} %copy-done.7), channel_id=1, source_target_pairs={{0,32},{16,48},{32,0},{48,16},{1,33},{17,49},{33,1},{49,17},{2,34}... | collective-permute-start | bytes 1572872 | tf_op jit(solution)/shard_map/ppermute | solution.py:24
  125.0 6.9 %shard_map.67 = bf16[256,1792]{1,0:T(8,128)(2,1)} custom-call(bf16[4,256,512]{2,1,0:T(8,128)(2,1)S(1)} %bitcast.10, bf16[4,256,512]{2,1,0:T(8,128)(2,1)S(1)} %collective-permute-done.8.grad_o, bf16[4,512,1792]{2,1,0:T(8,128)(2,1)} %bitcast.17), custom_call_target="tpu_custom_call" | custom-call | flops 1879048192 | bytes 7340032 | tf_op jit(solution)/shard_map/pallas_call | solution.py:153
  132.6 15.7 %collective-permute-done.5.r1 = bf16[2,256,512]{2,1,0:T(8,128)(2,1)S(1)} collective-permute-done((bf16[2,256,512]{2,1,0:T(8,128)(2,1)S(1)}, bf16[2,256,512]{2,1,0:T(8,128)(2,1)S(1)}, u32[]{:S(2)}, u32[]{:S(2)}) %collective-permute-start.5) | collective-permute-done | bytes 524320 | tf_op jit(solution)/shard_map/ppermute | solution.py:24
  149.4 5.9 %shard_map.65 = f32[256,1792]{1,0:T(8,128)S(1)} custom-call(bf16[4,256,512]{2,1,0:T(8,128)(2,1)S(1)} %bitcast.11, bf16[4,256,512]{2,1,0:T(8,128)(2,1)S(1)} %collective-permute-done.8.grad_o, bf16[4,512,1792]{2,1,0:T(8,128)(2,1)} %bitcast.18), custom_call_target="tpu_custom_call" | custom-call | flops 1879048192 | bytes 7340032 | tf_op jit(solution)/shard_map/pallas_call | solution.py:153
  155.3 3.9 %collective-permute-done.9 = bf16[256,512]{1,0:T(8,128)(2,1)S(1)} collective-permute-done((bf16[256,512]{1,0:T(8,128)(2,1)S(1)}, bf16[256,512]{1,0:T(8,128)(2,1)S(1)}, u32[]{:S(2)}, u32[]{:S(2)}) %collective-permute-start.9) | collective-permute-done | bytes 262176 | tf_op jit(solution)/shard_map/ppermute | solution.py:24
  160.3 2.6 %add_multiply_fusion = f32[256,1792]{1,0:T(8,128)} fusion(f32[256,1792]{1,0:T(8,128)S(1)} %shard_map.65, bf16[256,1792]{1,0:T(8,128)(2,1)} %collective-permute-done.10), kind=kLoop, calls=%fused_computation.1 | loop fusion | flops 1376256 | bytes 4587520 | tf_op jit(solution)/shard_map/mul | solution.py:249
  (49 shorter events, 12.7 us)
Async XLA Ops:
  7.2 1.5 copy-start.1
  7.2 89.3 %all-gather.3.cloned.1.call-start = ((), (), s32[]{:S(2)}) async-start(), calls=%async_computation.4 | async-start | bytes 9175040 | tf_op jit(solution)/shard_map/all_gather | solution.py:204
  8.7 3.1 %copy-start = (bf16[2048,1792]{1,0:T(8,128)(2,1)S(1)}, bf16[2048,1792]{1,0:T(8,128)(2,1)}, u32[]{:S(2)}) copy-start(bf16[2048,1792]{1,0:T(8,128)(2,1)} %b.3) | copy-start | bytes 22020100
  14.7 7.4 %collective-permute-start = (f32[2048,256]{1,0:T(8,128)S(1)}, f32[2048,256]{1,0:T(8,128)S(1)}, u32[]{:S(2)}, u32[]{:S(2)}) collective-permute-start(f32[2048,256]{1,0:T(8,128)S(1)} %shard_map.60), channel_id=1, source_target_pairs={{0,1},{1,0},{2,3},{3,2},{4,5},{5,4},{6,7},{7,6},{8,9},{9,8},{10,11... | collective-permute-start | bytes 6291464 | tf_op jit(solution)/shard_map/ppermute | solution.py:24
  16.2 53.0 %collective-permute-start.2 = (bf16[512,2048]{1,0:T(8,128)(2,1)}, bf16[512,2048]{1,0:T(8,128)(2,1)}, u32[]{:S(2)}, u32[]{:S(2)}) collective-permute-start(bf16[512,2048]{1,0:T(8,128)(2,1)} %a0.1), channel_id=1, source_target_pairs={{0,1},{1,0},{2,3},{3,2},{4,5},{5,4},{6,7},{7,6},{8,9},{9,8},{10,11... | collective-permute-start | bytes 6291464 | tf_op jit(solution)/shard_map/ppermute | solution.py:24
  46.2 4.7 %copy-start.12 = (bf16[512,512]{1,0:T(8,128)(2,1)S(1)}, bf16[512,512]{1,0:T(8,128)(2,1)}, u32[]{:S(2)}) copy-start(bf16[512,512]{1,0:T(8,128)(2,1)} %param.5) | copy-start | bytes 1572868
  47.3 18.6 %all-to-all-start.1 = ((bf16[8,256,256]{2,1,0:T(8,128)(2,1)}), bf16[8,256,256]{2,1,0:T(8,128)(2,1)S(1)}, u32[]{:S(2)}, u32[]{:S(2)}) async-start(bf16[8,256,256]{2,1,0:T(8,128)(2,1)} %shard_map.61), calls=%async_computation.1 | async-start | bytes 2097152 | tf_op jit(solution)/shard_map/all_to_all | solution.py:214
  51.1 18.0 %collective-permute-start.1 = (bf16[512,256]{1,0:T(8,128)(2,1)S(1)}, bf16[512,256]{1,0:T(8,128)(2,1)S(1)}, u32[]{:S(2)}, u32[]{:S(2)}) collective-permute-start(bf16[512,256]{1,0:T(8,128)(2,1)S(1)} %bitcast.20), channel_id=1, source_target_pairs={{0,1},{1,0},{2,3},{3,2},{4,5},{5,4},{6,7},{7,6},{8,9},{9,8},{10,11... | collective-permute-start | bytes 786440 | tf_op jit(solution)/shard_map/ppermute | solution.py:24
  66.0 14.9 %collective-permute-start.3 = (bf16[2048,256]{1,0:T(8,128)(2,1)S(1)}, bf16[2048,256]{1,0:T(8,128)(2,1)S(1)}, u32[]{:S(2)}, u32[]{:S(2)}) collective-permute-start(bf16[2048,256]{1,0:T(8,128)(2,1)S(1)} %bitcast.13), channel_id=1, source_target_pairs={{0,1},{1,0},{2,3},{3,2},{4,5},{5,4},{6,7},{7,6},{8,9},{9,8},{10,11... | collective-permute-start | bytes 3145736 | tf_op jit(solution)/shard_map/ppermute | solution.py:24
  75.7 20.8 %all-to-all-start.2 = ((bf16[8,32,2048]{2,1,0:T(8,128)(2,1)}), bf16[8,32,2048]{2,1,0:T(8,128)(2,1)S(1)}, u32[]{:S(2)}, u32[]{:S(2)}) async-start(bf16[8,32,2048]{2,1,0:T(8,128)(2,1)} %get-tuple-element.21), calls=%async_computation.2 | async-start | bytes 2097152 | tf_op jit(solution)/shard_map/all_to_all | solution.py:225
  79.2 1.6 collective-permute-start.4
  80.8 1.1 copy-start.2
  81.9 1.2 copy-start.3
  83.1 0.9 copy-start.11
  86.2 0.8 copy-start.6
  96.5 25.8 %copy-start.9 = (bf16[2,256,512]{2,1,0:T(8,128)(2,1)S(1)}, bf16[2,256,512]{2,1,0:T(8,128)(2,1)}, u32[]{:S(2)}) copy-start(bf16[2,256,512]{2,1,0:T(8,128)(2,1)} %copy-done.8) | copy-start | bytes 1572868
  96.5 25.8 %copy-start.7 = (bf16[2,256,512]{2,1,0:T(8,128)(2,1)S(1)}, bf16[2,256,512]{2,1,0:T(8,128)(2,1)}, u32[]{:S(2)}) copy-start(bf16[2,256,512]{2,1,0:T(8,128)(2,1)} %copy-done.6) | copy-start | bytes 1572868
  96.5 27.7 %copy-start.5 = (bf16[2,256,512]{2,1,0:T(8,128)(2,1)S(1)}, bf16[2,256,512]{2,1,0:T(8,128)(2,1)}, u32[]{:S(2)}) copy-start(bf16[2,256,512]{2,1,0:T(8,128)(2,1)} %copy-done.4) | copy-start | bytes 1572868
  120.0 5.1 %collective-permute-start.8 = (bf16[4,256,512]{2,1,0:T(8,128)(2,1)S(1)}, bf16[4,256,512]{2,1,0:T(8,128)(2,1)S(1)}, u32[]{:S(2)}, u32[]{:S(2)}) collective-permute-start(bf16[4,256,512]{2,1,0:T(8,128)(2,1)S(1)} %bitcast.9), channel_id=1, source_target_pairs={{0,1},{1,0},{2,3},{3,2},{4,5},{5,4},{6,7},{7,6},{8,9},{9,8},{10,11... | collective-permute-start | bytes 3145736 | tf_op jit(solution)/shard_map/ppermute | solution.py:24
  122.3 26.0 %collective-permute-start.5 = (bf16[2,256,512]{2,1,0:T(8,128)(2,1)S(1)}, bf16[2,256,512]{2,1,0:T(8,128)(2,1)S(1)}, u32[]{:S(2)}, u32[]{:S(2)}) collective-permute-start(bf16[2,256,512]{2,1,0:T(8,128)(2,1)S(1)} %copy-done.9), channel_id=1, source_target_pairs={{0,16},{16,32},{32,48},{48,0},{1,17},{17,33},{33,49},{49,1},{2,18}... | collective-permute-start | bytes 1572872 | tf_op jit(solution)/shard_map/ppermute | solution.py:24
  122.3 26.0 %collective-permute-start.6 = (bf16[2,256,512]{2,1,0:T(8,128)(2,1)S(1)}, bf16[2,256,512]{2,1,0:T(8,128)(2,1)S(1)}, u32[]{:S(2)}, u32[]{:S(2)}) collective-permute-start(bf16[2,256,512]{2,1,0:T(8,128)(2,1)S(1)} %copy-done.7), channel_id=1, source_target_pairs={{0,32},{16,48},{32,0},{48,16},{1,33},{17,49},{33,1},{49,17},{2,34}... | collective-permute-start | bytes 1572872 | tf_op jit(solution)/shard_map/ppermute | solution.py:24
  124.2 24.5 %collective-permute-start.7 = (bf16[2,256,512]{2,1,0:T(8,128)(2,1)S(1)}, bf16[2,256,512]{2,1,0:T(8,128)(2,1)S(1)}, u32[]{:S(2)}, u32[]{:S(2)}) collective-permute-start(bf16[2,256,512]{2,1,0:T(8,128)(2,1)S(1)} %copy-done.5), channel_id=1, source_target_pairs={{0,48},{16,0},{32,16},{48,32},{1,49},{17,1},{33,17},{49,33},{2,50}... | collective-permute-start | bytes 1572872 | tf_op jit(solution)/shard_map/ppermute | solution.py:24
  131.9 28.4 %collective-permute-start.10 = (bf16[256,1792]{1,0:T(8,128)(2,1)}, bf16[256,1792]{1,0:T(8,128)(2,1)}, u32[]{:S(2)}, u32[]{:S(2)}) collective-permute-start(bf16[256,1792]{1,0:T(8,128)(2,1)} %shard_map.67), channel_id=1, source_target_pairs={{0,64},{64,0},{1,65},{65,1},{2,66},{66,2},{3,67},{67,3},{4,68},{68... | collective-permute-start | bytes 2752520 | tf_op jit(solution)/shard_map/ppermute | solution.py:24
  148.9 10.3 %collective-permute-start.9 = (bf16[256,512]{1,0:T(8,128)(2,1)S(1)}, bf16[256,512]{1,0:T(8,128)(2,1)S(1)}, u32[]{:S(2)}, u32[]{:S(2)}) collective-permute-start(bf16[256,512]{1,0:T(8,128)(2,1)S(1)} %get-tuple-element.38), channel_id=1, source_target_pairs={{0,64},{64,0},{1,65},{65,1},{2,66},{66,2},{3,67},{67,3},{4,68},{68... | collective-permute-start | bytes 786440 | tf_op jit(solution)/shard_map/ppermute | solution.py:24
  (3 other events, 2.3 us)
Sparse Core Ops, SparseCore 0:
  9.7 77.5 all-gather.2

commit v20 on v13

--- a/solution.py
+++ b/solution.py
@@ -98,12 +98,7 @@
             left = target[rows].astype(F32) - dot(a[rows], codes[...])
             left = left.astype(BF).T
             held[:, j * outs + at : j * outs + at + step] = left
-            if j == 0:
-                own[:, rows] = left
-            else:
-                for c in range(0, step, 256):
-                    message[rank + at + c : rank + at + c + 256] = left[:, c : c + 256]
-    message[:rank] = codes[...]
+            (own if j == 0 else message)[:, rows] = left
     sub = partial.shape[1]
     for at in range(0, rank, 512):
         cols = slice(at, at + 512)
@@ -123,27 +118,6 @@
             piece = held[:, pl.ds(start, width)]
             for i in range(out.shape[1]):
                 out[x, i, :, at : at + width] = piece
-
-
-def hold_kernel(row, out, sems):
-    parts = sems.shape[0]
-    copies = [pltpu.make_async_copy(row.at[i], out.at[i], sems.at[i]) for i in range(parts)]
-    for copy in copies:
-        copy.start()
-    for copy in copies:
-        copy.wait()
-
-
-def hold(row):
-    return pl.pallas_call(
-        hold_kernel,
-        out_shape=like(row.shape),
-        in_specs=[ANY],
-        out_specs=VMEM,
-        scratch_shapes=[pltpu.SemaphoreType.DMA((row.shape[0],))],
-        compiler_params=pltpu.CompilerParams(vmem_limit_bytes=16 * 1024 * 1024),
-        cost_estimate=pl.CostEstimate(flops=0, bytes_accessed=4 * row.size, transcendentals=0),
-    )(row)
 
 
 def last_kernel(side, other, grad, acts, *refs):
@@ -182,7 +156,7 @@
     )
 
 
-def term_kernel(codes, own, message, keep, s1, s2, s3):
+def term_kernel(codes, own, codes_o, message, keep, s1, s2, s3):
     x = lax.axis_index("x")
     rank, outs = codes.shape[0], own.shape[1]
     width = rank // 8
@@ -190,10 +164,10 @@
         for side in range(2):
             start = side * (rank // 2) + lax.rem(x + k, 4) * width
             rows = pl.ds(pl.multiple_of(start, width), width)
-            left, right = codes[rows, :], message[rows, :]
+            left, right = codes[rows, :], codes_o[rows, :]
             for c in range(0, outs, 256):
                 acc = dot(left, own[:, c : c + 256])
-                acc = acc + dot(right, message[rank + c : rank + c + 256])
+                acc = acc + dot(right, message[:, c : c + 256])
                 out[side, :, c : c + 256] = acc.astype(out.dtype)
 
 
@@ -230,36 +204,37 @@
 
     own, message, partial = call(
         residual_kernel,
-        [like((half, outs)), like((rank + outs, half)), like((8, sub, rank))],
+        [like((half, outs)), like((half, outs)), like((8, sub, rank))],
         codes, near_t, pair_t, proj_a, pair_a,
         scratch=[pltpu.VMEM((half, 2 * outs), BF)],
         flops=8 * half * rank * outs,
     )
+    partial, codes = lax.optimization_barrier((partial, codes))
+    codes_o = swap(codes, "core")
     blocks = lax.all_to_all(partial, ZY, 0, 0)
 
     piece = like((2, width, outs))
     terms = call(
         term_kernel,
         [like(piece.shape, F32), piece, piece, piece],
-        codes, own, swap(message, "core"),
+        codes, own, codes_o, swap(message, "core"),
         flops=2 * tokens * rank * outs,
     )
     terms = [terms[0]] + [shift(terms[k], "x", 4, k) for k in (1, 2, 3)]
 
     barrier = lax.optimization_barrier
-    blocks, row = barrier((blocks, row))
-    split = call(spread_kernel, [like((4, 8, sub, 2 * width))], blocks, scratch=[pltpu.VMEM((sub, rank), BF)])
-    split, row = barrier((split, row))
-    held = hold(row)
+    blocks, row, terms[0] = barrier((blocks, row, terms[0]))
+    split = call(spread_kernel, [like((4, 8, sub, 2 * width))], blocks, scratch=[pltpu.VMEM((sub, rank), BF)], flops=15 * 10**9)
     grad = lax.all_to_all(split.reshape(32, sub, 2 * width), ("x", "z", "y_hi"), 0, 0)
     grad = grad.reshape(4, half, 2 * width)
-    grad, held, *terms = barrier((grad, held, *terms))
     grad_o = swap(grad, "core")
+    away = last_call(grad, grad_o, row, 0, BF)
+    away = swap(away, "y_lo").astype(F32)
+    here = last_call(grad, grad_o, row, 1, F32)
     term_o, term_a = call(term_sum_kernel, [like((width, outs), F32), like((width, outs))], *terms)
-    away = swap(last_call(grad, grad_o, held, 0, BF, term_a), "y_lo").astype(F32)
-    here = last_call(grad, grad_o, held, 1, F32)
+    term_a = swap(term_a, "y_lo").astype(F32)
     here, term_o = barrier((here, term_o))
-    return (((term_o + away[:, wide:]) * scale).T, (here + away[:, :wide]) * scale)
+    return (((term_o + term_a) * scale).T, (here + away) * scale)
 
 
 def solution(mesh):

time: 188 us -> 167 us (0.89)
  local copies, waits for them, and re-layouts: 22 us -> 11.6 us
  waiting for transfers between devices: 61.6 us -> 51.4 us
  blocking collectives: 43.4 us -> 47.2 us
  starting transfers between devices: 23.3 us -> 20 us
    ppermute x9 -> x11, waiting for transfers between devices: 49.1 us -> 30.2 us  [shift(): lax.ppermute(array, axis, [(i, (i + step) % size) for i in range(size)])]
    unnamed x29 -> x33, local copies, waits for them, and re-layouts: 21.9 us -> 11.5 us
    all_to_all x1, waiting for transfers between devices: 0.01 us -> 8.72 us  [local(): blocks = lax.all_to_all(partial, ZY, 0, 0)]
    all_to_all x1, blocking collectives: 19.5 us -> 23.3 us  [local(): lax.all_to_all(split.reshape(32, sub, 2 * width), ('x', 'z', 'y_hi'), 0, 0)]
    all_to_all x1, starting transfers between devices: 5.72 us -> 3.56 us  [local(): blocks = lax.all_to_all(partial, ZY, 0, 0)]
    ppermute x9 -> x11, starting transfers between devices: 14 us -> 12.8 us  [shift(): lax.ppermute(array, axis, [(i, (i + step) % size) for i in range(size)])]
  transfers between devices with their start and end apart: 12 -> 14, of which waited for: 6 -> 8; matrix products, arithmetic and copies ran while one was open for 0% -> 1% of each run, Pallas kernels for 10% -> 11%
where the time goes in v20:
time: 167 us; the launch traced here: 166 us
  waiting for transfers between devices  51.4 us (31%)
  blocking collectives  47.2 us (28%)
  starting transfers between devices  20 us (12%)
  Pallas kernels  19 us (11%)
  between operations  14.2 us (9%)
  local copies, waits for them, and re-layouts  11.6 us (7%)
  other arithmetic  2.99 us (2%)
    ppermute x11, waiting for transfers between devices, shift(): lax.ppermute(array, axis, [(i, (i + step) % size) for i in range(size)])  30.2 us
    all_to_all x1, blocking collectives, local(): blocks = lax.all_to_all(mine, ZY, 0, 0)  23.9 us
    all_to_all x1, blocking collectives, local(): lax.all_to_all(split.reshape(32, sub, 2 * width), ('x', 'z', 'y_hi'), 0, 0)  23.3 us
    pallas_call x9, Pallas kernels, call(): pl.pallas_call(body, out_shape=outs if len(outs) > 1 else outs[0], in_spe...  13.2 us
    ppermute x11, starting transfers between devices, shift(): lax.ppermute(array, axis, [(i, (i + step) % size) for i in range(size)])  12.8 us
    all_to_all x1, waiting for transfers between devices, local(): codes = lax.all_to_all(codes, ZY, 0, 0).reshape(rank, half)  11.8 us
    unnamed x33, local copies, waits for them, and re-layouts  11.5 us
    all_to_all x1, waiting for transfers between devices, local(): blocks = lax.all_to_all(partial, ZY, 0, 0)  8.72 us
  transfers between devices with their start and end apart: 14, of which 8 were waited for; matrix products, arithmetic and copies ran while one was open for 1% of the time, Pallas kernels for 11%

profile of v20, /device:TPU:1, one launch (start us, length us, event | category | flops | bytes accessed | tf_op | source)
XLA Modules:
  0.0 166.3 jit_solution(4835226285871988704)
XLA Ops:
  8.7 3.1 %copy-done = bf16[2048,1792]{1,0:T(8,128)(2,1)S(1)} copy-done((bf16[2048,1792]{1,0:T(8,128)(2,1)S(1)}, bf16[2048,1792]{1,0:T(8,128)(2,1)}, u32[]{:S(2)}) %copy-start) | copy-done | bytes 7340056
  11.7 2.9 %shard_map.60 = f32[2048,256]{1,0:T(8,128)S(1)} custom-call(bf16[512,1792]{1,0:T(8,128)(2,1)S(1)} %copy-done.1, bf16[2048,1792]{1,0:T(8,128)(2,1)S(1)} %copy-done), custom_call_target="tpu_custom_call" | custom-call | flops 1879048192 | bytes 7340032 | tf_op jit(solution)/shard_map/pallas_call | solution.py:69
  14.7 1.5 collective-permute-start
  16.3 2.9 %shard_map.59 = f32[2048,256]{1,0:T(8,128)S(1)} custom-call(bf16[512,1792]{1,0:T(8,128)(2,1)S(1)} %copy-done.1, bf16[2048,1792]{1,0:T(8,128)(2,1)S(1)} %copy-done), custom_call_target="tpu_custom_call" | custom-call | flops 1879048192 | bytes 7340032 | tf_op jit(solution)/shard_map/pallas_call | solution.py:69
  19.2 2.8 %collective-permute-done = f32[2048,256]{1,0:T(8,128)S(1)} collective-permute-done((f32[2048,256]{1,0:T(8,128)S(1)}, f32[2048,256]{1,0:T(8,128)S(1)}, u32[]{:S(2)}, u32[]{:S(2)}) %collective-permute-start) | collective-permute-done | bytes 2097184 | tf_op jit(solution)/shard_map/ppermute | solution.py:24
  22.4 23.9 %all_to_all.20.blocks = bf16[8,256,256]{2,1,0:T(8,128)(2,1)S(1)} all-to-all(bf16[8,256,256]{2,1,0:T(8,128)(2,1)S(1)} %bitcast.23), channel_id=1, replica_groups=mesh['y_lo'=2,'x'=4,'z'=4,'y_hi'=2,'core'=2] {'z','y_hi'}, dimensions={0} | all-to-all | bytes 2097152 | tf_op jit(solution)/shard_map/all_to_all | solution.py:201
  47.3 3.6 %all-to-all-start.1 = ((bf16[8,256,256]{2,1,0:T(8,128)(2,1)}), bf16[8,256,256]{2,1,0:T(8,128)(2,1)S(1)}, u32[]{:S(2)}, u32[]{:S(2)}) async-start(bf16[8,256,256]{2,1,0:T(8,128)(2,1)} %shard_map.61), calls=%async_computation.1 | async-start | bytes 2097152 | tf_op jit(solution)/shard_map/all_to_all | solution.py:203
  51.1 1.9 %collective-permute-start.1 = (bf16[512,256]{1,0:T(8,128)(2,1)S(1)}, bf16[512,256]{1,0:T(8,128)(2,1)S(1)}, u32[]{:S(2)}, u32[]{:S(2)}) collective-permute-start(bf16[512,256]{1,0:T(8,128)(2,1)S(1)} %bitcast.24), channel_id=1, source_target_pairs={{0,1},{1,0},{2,3},{3,2},{4,5},{5,4},{6,7},{7,6},{8,9},{9,8},{10,11... | collective-permute-start | bytes 786440 | tf_op jit(solution)/shard_map/ppermute | solution.py:24
  54.2 11.8 %all-to-all-done.1 = bf16[8,256,256]{2,1,0:T(8,128)(2,1)S(1)} async-done(((bf16[8,256,256]{2,1,0:T(8,128)(2,1)}), bf16[8,256,256]{2,1,0:T(8,128)(2,1)S(1)}, u32[]{:S(2)}, u32[]{:S(2)}) %all-to-all-start.1) | async-done | bytes 1048608 | tf_op jit(solution)/shard_map/all_to_all | solution.py:203
  66.0 5.7 %shard_map.62 = (bf16[256,512]{1,0:T(8,128)(2,1)S(1)}, bf16[256,512]{1,0:T(8,128)(2,1)S(1)}, bf16[8,32,2048]{2,1,0:T(8,128)(2,1)}) custom-call(bf16[2048,256]{1,0:T(8,128)(2,1)S(1)} %bitcast.18, bf16[512,256]{1,0:T(8,128)(2,1)S(1)} %bitcast.22, bf16[512,256]{1,0:T(8,128)(2,1)S(1)} %collective-permute-done.1.far, bf16[512,2048]{1,0:T(8,128)(2,1)} %a0.1, ...), custom_call_target="tpu_custom_call" | custom-call | flops 2147483648 | bytes 7340032 | tf_op jit(solution)/shard_map/pallas_call | solution.py:33
  72.4 3.1 %collective-permute-start.3 = (bf16[2048,256]{1,0:T(8,128)(2,1)S(1)}, bf16[2048,256]{1,0:T(8,128)(2,1)S(1)}, u32[]{:S(2)}, u32[]{:S(2)}) collective-permute-start(bf16[2048,256]{1,0:T(8,128)(2,1)S(1)} %bitcast.19), channel_id=1, source_target_pairs={{0,1},{1,0},{2,3},{3,2},{4,5},{5,4},{6,7},{7,6},{8,9},{9,8},{10,11... | collective-permute-start | bytes 3145736 | tf_op jit(solution)/shard_map/ppermute | solution.py:24
  75.5 3.6 %all-to-all-start.2 = ((bf16[8,32,2048]{2,1,0:T(8,128)(2,1)}), bf16[8,32,2048]{2,1,0:T(8,128)(2,1)S(1)}, u32[]{:S(2)}, u32[]{:S(2)}) async-start(bf16[8,32,2048]{2,1,0:T(8,128)(2,1)} %get-tuple-element.19), calls=%async_computation.2 | async-start | bytes 2097152 | tf_op jit(solution)/shard_map/all_to_all | solution.py:214
  79.2 1.5 collective-permute-done.4.message
  81.8 1.2 copy-done.3
  84.0 1.2 shard_map.63
  87.7 8.7 %all-to-all-done.2.blocks = bf16[8,32,2048]{2,1,0:T(8,128)(2,1)S(1)} async-done(((bf16[8,32,2048]{2,1,0:T(8,128)(2,1)}), bf16[8,32,2048]{2,1,0:T(8,128)(2,1)S(1)}, u32[]{:S(2)}, u32[]{:S(2)}) %all-to-all-start.2) | async-done | bytes 1048608 | tf_op jit(solution)/shard_map/all_to_all | solution.py:214
  96.7 23.3 %all_to_all.21 = bf16[32,32,512]{2,1,0:T(8,128)(2,1)S(1)} all-to-all(bf16[32,32,512]{2,1,0:T(8,128)(2,1)S(1)} %bitcast.21), channel_id=1, replica_groups=mesh['y_lo'=2,'x'=4,'z'=4,'y_hi'=2,'core'=2] {'x','z','y_hi'}, dimensions={0} | all-to-all | bytes 2097152 | tf_op jit(solution)/shard_map/all_to_all | solution.py:228
  120.0 2.3 %collective-permute-start.5 = (bf16[4,256,512]{2,1,0:T(8,128)(2,1)S(1)}, bf16[4,256,512]{2,1,0:T(8,128)(2,1)S(1)}, u32[]{:S(2)}, u32[]{:S(2)}) collective-permute-start(bf16[4,256,512]{2,1,0:T(8,128)(2,1)S(1)} %bitcast.15), channel_id=1, source_target_pairs={{0,1},{1,0},{2,3},{3,2},{4,5},{5,4},{6,7},{7,6},{8,9},{9,8},{10,11... | collective-permute-start | bytes 3145736 | tf_op jit(solution)/shard_map/ppermute | solution.py:24
  122.3 1.9 %collective-permute-start.7 = (bf16[2,256,512]{2,1,0:T(8,128)(2,1)S(1)}, bf16[2,256,512]{2,1,0:T(8,128)(2,1)S(1)}, u32[]{:S(2)}, u32[]{:S(2)}) collective-permute-start(bf16[2,256,512]{2,1,0:T(8,128)(2,1)S(1)} %copy-done.7), channel_id=1, source_target_pairs={{0,32},{16,48},{32,0},{48,16},{1,33},{17,49},{33,1},{49,17},{2,34}... | collective-permute-start | bytes 1572872 | tf_op jit(solution)/shard_map/ppermute | solution.py:24
  126.2 1.2 shard_map.69
  127.9 20.4 %collective-permute-done.6.r1 = bf16[2,256,512]{2,1,0:T(8,128)(2,1)S(1)} collective-permute-done((bf16[2,256,512]{2,1,0:T(8,128)(2,1)S(1)}, bf16[2,256,512]{2,1,0:T(8,128)(2,1)S(1)}, u32[]{:S(2)}, u32[]{:S(2)}) %collective-permute-start.6) | collective-permute-done | bytes 524320 | tf_op jit(solution)/shard_map/ppermute | solution.py:24
  150.6 1.2 shard_map.66
  151.8 4.0 %collective-permute-done.9 = bf16[256,512]{1,0:T(8,128)(2,1)S(1)} collective-permute-done((bf16[256,512]{1,0:T(8,128)(2,1)S(1)}, bf16[256,512]{1,0:T(8,128)(2,1)S(1)}, u32[]{:S(2)}, u32[]{:S(2)}) %collective-permute-start.9) | collective-permute-done | bytes 262176 | tf_op jit(solution)/shard_map/ppermute | solution.py:24
  156.9 2.6 %add_multiply_fusion = f32[256,1792]{1,0:T(8,128)} fusion(f32[256,1792]{1,0:T(8,128)S(1)} %shard_map.66, bf16[256,1792]{1,0:T(8,128)(2,1)} %collective-permute-done.10), kind=kLoop, calls=%fused_computation.1 | loop fusion | flops 1376256 | bytes 4587520 | tf_op jit(solution)/shard_map/mul | solution.py:237
  (56 shorter events, 15.8 us)
Async XLA Ops:
  7.2 1.5 copy-start.1
  7.2 89.2 %all-gather.3.cloned.1.call-start = ((), (), s32[]{:S(2)}) async-start(), calls=%async_computation.4 | async-start | bytes 9175040 | tf_op jit(solution)/shard_map/all_gather | solution.py:193
  8.7 3.1 %copy-start = (bf16[2048,1792]{1,0:T(8,128)(2,1)S(1)}, bf16[2048,1792]{1,0:T(8,128)(2,1)}, u32[]{:S(2)}) copy-start(bf16[2048,1792]{1,0:T(8,128)(2,1)} %b.3) | copy-start | bytes 22020100
  14.7 7.4 %collective-permute-start = (f32[2048,256]{1,0:T(8,128)S(1)}, f32[2048,256]{1,0:T(8,128)S(1)}, u32[]{:S(2)}, u32[]{:S(2)}) collective-permute-start(f32[2048,256]{1,0:T(8,128)S(1)} %shard_map.60), channel_id=1, source_target_pairs={{0,1},{1,0},{2,3},{3,2},{4,5},{5,4},{6,7},{7,6},{8,9},{9,8},{10,11... | collective-permute-start | bytes 6291464 | tf_op jit(solution)/shard_map/ppermute | solution.py:24
  16.2 38.0 %collective-permute-start.2 = (bf16[512,2048]{1,0:T(8,128)(2,1)}, bf16[512,2048]{1,0:T(8,128)(2,1)}, u32[]{:S(2)}, u32[]{:S(2)}) collective-permute-start(bf16[512,2048]{1,0:T(8,128)(2,1)} %a0.1), channel_id=1, source_target_pairs={{0,1},{1,0},{2,3},{3,2},{4,5},{5,4},{6,7},{7,6},{8,9},{9,8},{10,11... | collective-permute-start | bytes 6291464 | tf_op jit(solution)/shard_map/ppermute | solution.py:24
  46.2 4.7 %copy-start.12 = (bf16[512,512]{1,0:T(8,128)(2,1)S(1)}, bf16[512,512]{1,0:T(8,128)(2,1)}, u32[]{:S(2)}) copy-start(bf16[512,512]{1,0:T(8,128)(2,1)} %param.5) | copy-start | bytes 1572868
  47.3 18.6 %all-to-all-start.1 = ((bf16[8,256,256]{2,1,0:T(8,128)(2,1)}), bf16[8,256,256]{2,1,0:T(8,128)(2,1)S(1)}, u32[]{:S(2)}, u32[]{:S(2)}) async-start(bf16[8,256,256]{2,1,0:T(8,128)(2,1)} %shard_map.61), calls=%async_computation.1 | async-start | bytes 2097152 | tf_op jit(solution)/shard_map/all_to_all | solution.py:203
  51.1 3.1 %collective-permute-start.1 = (bf16[512,256]{1,0:T(8,128)(2,1)S(1)}, bf16[512,256]{1,0:T(8,128)(2,1)S(1)}, u32[]{:S(2)}, u32[]{:S(2)}) collective-permute-start(bf16[512,256]{1,0:T(8,128)(2,1)S(1)} %bitcast.24), channel_id=1, source_target_pairs={{0,1},{1,0},{2,3},{3,2},{4,5},{5,4},{6,7},{7,6},{8,9},{9,8},{10,11... | collective-permute-start | bytes 786440 | tf_op jit(solution)/shard_map/ppermute | solution.py:24
  72.4 8.3 %collective-permute-start.3 = (bf16[2048,256]{1,0:T(8,128)(2,1)S(1)}, bf16[2048,256]{1,0:T(8,128)(2,1)S(1)}, u32[]{:S(2)}, u32[]{:S(2)}) collective-permute-start(bf16[2048,256]{1,0:T(8,128)(2,1)S(1)} %bitcast.19), channel_id=1, source_target_pairs={{0,1},{1,0},{2,3},{3,2},{4,5},{5,4},{6,7},{7,6},{8,9},{9,8},{10,11... | collective-permute-start | bytes 3145736 | tf_op jit(solution)/shard_map/ppermute | solution.py:24
  75.5 20.9 %all-to-all-start.2 = ((bf16[8,32,2048]{2,1,0:T(8,128)(2,1)}), bf16[8,32,2048]{2,1,0:T(8,128)(2,1)S(1)}, u32[]{:S(2)}, u32[]{:S(2)}) async-start(bf16[8,32,2048]{2,1,0:T(8,128)(2,1)} %get-tuple-element.19), calls=%async_computation.2 | async-start | bytes 2097152 | tf_op jit(solution)/shard_map/all_to_all | solution.py:214
  79.1 1.6 collective-permute-start.4
  80.7 1.1 copy-start.2
  81.8 1.2 copy-start.3
  96.4 28.7 %slice-start = ((s8[7340032]{0:T(1024)(128)(4,1)}), s8[4194304]{0:T(1024)(128)(4,1)S(1)}, s32[]{:S(2)}) async-start(s8[7340032]{0:T(1024)(128)(4,1)} %bitcast.9), calls=%async_computation.5 | async-start | bytes 8388608
  96.4 28.7 %slice-start.1 = ((s8[7340032]{0:T(1024)(128)(4,1)}), s8[3145728]{0:T(1024)(128)(4,1)S(1)}, s32[]{:S(2)}) async-start(s8[7340032]{0:T(1024)(128)(4,1)} %bitcast.9), calls=%async_computation.6 | async-start | bytes 6291456
  96.7 25.6 %copy-start.9 = (bf16[2,256,512]{2,1,0:T(8,128)(2,1)S(1)}, bf16[2,256,512]{2,1,0:T(8,128)(2,1)}, u32[]{:S(2)}) copy-start(bf16[2,256,512]{2,1,0:T(8,128)(2,1)} %copy-done.8) | copy-start | bytes 1572868
  96.7 25.6 %copy-start.7 = (bf16[2,256,512]{2,1,0:T(8,128)(2,1)S(1)}, bf16[2,256,512]{2,1,0:T(8,128)(2,1)}, u32[]{:S(2)}) copy-start(bf16[2,256,512]{2,1,0:T(8,128)(2,1)} %copy-done.6) | copy-start | bytes 1572868
  96.7 27.5 %copy-start.5 = (bf16[2,256,512]{2,1,0:T(8,128)(2,1)S(1)}, bf16[2,256,512]{2,1,0:T(8,128)(2,1)}, u32[]{:S(2)}) copy-start(bf16[2,256,512]{2,1,0:T(8,128)(2,1)} %copy-done.4) | copy-start | bytes 1572868
  120.0 6.2 %collective-permute-start.5 = (bf16[4,256,512]{2,1,0:T(8,128)(2,1)S(1)}, bf16[4,256,512]{2,1,0:T(8,128)(2,1)S(1)}, u32[]{:S(2)}, u32[]{:S(2)}) collective-permute-start(bf16[4,256,512]{2,1,0:T(8,128)(2,1)S(1)} %bitcast.15), channel_id=1, source_target_pairs={{0,1},{1,0},{2,3},{3,2},{4,5},{5,4},{6,7},{7,6},{8,9},{9,8},{10,11... | collective-permute-start | bytes 3145736 | tf_op jit(solution)/shard_map/ppermute | solution.py:24
  122.3 26.0 %collective-permute-start.6 = (bf16[2,256,512]{2,1,0:T(8,128)(2,1)S(1)}, bf16[2,256,512]{2,1,0:T(8,128)(2,1)S(1)}, u32[]{:S(2)}, u32[]{:S(2)}) collective-permute-start(bf16[2,256,512]{2,1,0:T(8,128)(2,1)S(1)} %copy-done.9), channel_id=1, source_target_pairs={{0,16},{16,32},{32,48},{48,0},{1,17},{17,33},{33,49},{49,1},{2,18}... | collective-permute-start | bytes 1572872 | tf_op jit(solution)/shard_map/ppermute | solution.py:24
  122.3 26.0 %collective-permute-start.7 = (bf16[2,256,512]{2,1,0:T(8,128)(2,1)S(1)}, bf16[2,256,512]{2,1,0:T(8,128)(2,1)S(1)}, u32[]{:S(2)}, u32[]{:S(2)}) collective-permute-start(bf16[2,256,512]{2,1,0:T(8,128)(2,1)S(1)} %copy-done.7), channel_id=1, source_target_pairs={{0,32},{16,48},{32,0},{48,16},{1,33},{17,49},{33,1},{49,17},{2,34}... | collective-permute-start | bytes 1572872 | tf_op jit(solution)/shard_map/ppermute | solution.py:24
  124.2 24.5 %collective-permute-start.8 = (bf16[2,256,512]{2,1,0:T(8,128)(2,1)S(1)}, bf16[2,256,512]{2,1,0:T(8,128)(2,1)S(1)}, u32[]{:S(2)}, u32[]{:S(2)}) collective-permute-start(bf16[2,256,512]{2,1,0:T(8,128)(2,1)S(1)} %copy-done.5), channel_id=1, source_target_pairs={{0,48},{16,0},{32,16},{48,32},{1,49},{17,1},{33,17},{49,33},{2,50}... | collective-permute-start | bytes 1572872 | tf_op jit(solution)/shard_map/ppermute | solution.py:24
  127.4 29.5 %collective-permute-start.10 = (bf16[256,1792]{1,0:T(8,128)(2,1)S(1)}, bf16[256,1792]{1,0:T(8,128)(2,1)}, u32[]{:S(2)}, u32[]{:S(2)}) collective-permute-start(bf16[256,1792]{1,0:T(8,128)(2,1)S(1)} %shard_map.69), channel_id=1, source_target_pairs={{0,64},{64,0},{1,65},{65,1},{2,66},{66,2},{3,67},{67,3},{4,68},{68... | collective-permute-start | bytes 2752520 | tf_op jit(solution)/shard_map/ppermute | solution.py:24
  148.9 6.9 %collective-permute-start.9 = (bf16[256,512]{1,0:T(8,128)(2,1)S(1)}, bf16[256,512]{1,0:T(8,128)(2,1)S(1)}, u32[]{:S(2)}, u32[]{:S(2)}) collective-permute-start(bf16[256,512]{1,0:T(8,128)(2,1)S(1)} %get-tuple-element.32), channel_id=1, source_target_pairs={{0,64},{64,0},{1,65},{65,1},{2,66},{66,2},{3,67},{67,3},{4,68},{68... | collective-permute-start | bytes 786440 | tf_op jit(solution)/shard_map/ppermute | solution.py:24
  (5 other events, 4.1 us)
Sparse Core Ops, SparseCore 0:
  9.7 77.5 all-gather.2

commit v21 on v20

--- a/solution.py
+++ b/solution.py
@@ -224,14 +224,17 @@
 
     barrier = lax.optimization_barrier
     blocks, row, terms[0] = barrier((blocks, row, terms[0]))
-    split = call(spread_kernel, [like((4, 8, sub, 2 * width))], blocks, scratch=[pltpu.VMEM((sub, rank), BF)], flops=15 * 10**9)
+    split = call(spread_kernel, [like((4, 8, sub, 2 * width))], blocks, scratch=[pltpu.VMEM((sub, rank), BF)])
     grad = lax.all_to_all(split.reshape(32, sub, 2 * width), ("x", "z", "y_hi"), 0, 0)
     grad = grad.reshape(4, half, 2 * width)
+    term_o, term_a = call(
+        term_sum_kernel, [like((width, outs), F32), like((width, outs))], *terms, flops=30 * 10**9
+    )
+    grad, term_o, term_a = barrier((grad, term_o, term_a))
     grad_o = swap(grad, "core")
     away = last_call(grad, grad_o, row, 0, BF)
     away = swap(away, "y_lo").astype(F32)
     here = last_call(grad, grad_o, row, 1, F32)
-    term_o, term_a = call(term_sum_kernel, [like((width, outs), F32), like((width, outs))], *terms)
     term_a = swap(term_a, "y_lo").astype(F32)
     here, term_o = barrier((here, term_o))
     return (((term_o + term_a) * scale).T, (here + away) * scale)

time: 167 us -> 178 us (1.066)
  blocking collectives: 47.2 us -> 23.9 us
  waiting for transfers between devices: 51.4 us -> 65.7 us
  local copies, waits for them, and re-layouts: 11.6 us -> 22.5 us
  starting transfers between devices: 20 us -> 26.4 us
  Pallas kernels: 19 us -> 20.8 us
    all_to_all x1 -> x0, blocking collectives: 23.3 us -> none  [local(): lax.all_to_all(split.reshape(32, sub, 2 * width), ('x', 'z', 'y_hi'), 0, 0)]
    all_to_all x0 -> x1, waiting for transfers between devices: none -> 14.8 us  [local(): lax.all_to_all(split.reshape(32, sub, 2 * width), ('x', 'z', 'y_hi'), 0, 0)]
    unnamed x33 -> x25, local copies, waits for them, and re-layouts: 11.5 us -> 22.4 us
    all_to_all x0 -> x1, starting transfers between devices: none -> 5.57 us  [local(): lax.all_to_all(split.reshape(32, sub, 2 * width), ('x', 'z', 'y_hi'), 0, 0)]
    all_to_all x1, waiting for transfers between devices: 8.72 us -> 6.83 us  [local(): blocks = lax.all_to_all(partial, ZY, 0, 0)]
    pallas_call x9, Pallas kernels: 13.2 us -> 15 us  [call(): pl.pallas_call(body, out_shape=outs if len(outs) > 1 else outs[0], in_spe...]
  transfers between devices with their start and end apart: 14 -> 15, of which waited for: 8 -> 8; matrix products, arithmetic and copies ran while one was open for 1% -> 2% of each run, Pallas kernels for 11% -> 11%
where the time goes in v21:
time: 178 us; the launch traced here: 177 us
  waiting for transfers between devices  65.7 us (37%)
  starting transfers between devices  26.4 us (15%)
  blocking collectives  23.9 us (13%)
  local copies, waits for them, and re-layouts  22.5 us (13%)
  Pallas kernels  20.8 us (12%)
  between operations  14.2 us (8%)
  other arithmetic  3.79 us (2%)
    ppermute x11, waiting for transfers between devices, shift(): lax.ppermute(array, axis, [(i, (i + step) % size) for i in range(size)])  31.6 us
    all_to_all x1, blocking collectives, local(): blocks = lax.all_to_all(mine, ZY, 0, 0)  23.9 us
    unnamed x25, local copies, waits for them, and re-layouts  22.4 us
    pallas_call x9, Pallas kernels, call(): pl.pallas_call(body, out_shape=outs if len(outs) > 1 else outs[0], in_spe...  15 us
    all_to_all x1, waiting for transfers between devices, local(): lax.all_to_all(split.reshape(32, sub, 2 * width), ('x', 'z', 'y_hi'), 0, 0)  14.8 us
    ppermute x11, starting transfers between devices, shift(): lax.ppermute(array, axis, [(i, (i + step) % size) for i in range(size)])  13.7 us
    all_to_all x1, waiting for transfers between devices, local(): codes = lax.all_to_all(codes, ZY, 0, 0).reshape(rank, half)  11.8 us
    all_to_all x1, waiting for transfers between devices, local(): blocks = lax.all_to_all(partial, ZY, 0, 0)  6.83 us
  transfers between devices with their start and end apart: 15, of which 8 were waited for; matrix products, arithmetic and copies ran while one was open for 2% of the time, Pallas kernels for 11%

profile of v21, /device:TPU:1, one launch (start us, length us, event | category | flops | bytes accessed | tf_op | source)
XLA Modules:
  0.0 177.2 jit_solution(7622813062449970983)
XLA Ops:
  8.7 3.1 %copy-done.4 = bf16[2048,1792]{1,0:T(8,128)(2,1)S(1)} copy-done((bf16[2048,1792]{1,0:T(8,128)(2,1)S(1)}, bf16[2048,1792]{1,0:T(8,128)(2,1)}, u32[]{:S(2)}) %copy-start.4) | copy-done | bytes 7340056
  11.7 2.9 %shard_map.60 = f32[2048,256]{1,0:T(8,128)S(1)} custom-call(bf16[512,1792]{1,0:T(8,128)(2,1)S(1)} %copy-done.5, bf16[2048,1792]{1,0:T(8,128)(2,1)S(1)} %copy-done.4), custom_call_target="tpu_custom_call" | custom-call | flops 1879048192 | bytes 7340032 | tf_op jit(solution)/shard_map/pallas_call | solution.py:69
  16.3 2.9 %shard_map.59 = f32[2048,256]{1,0:T(8,128)S(1)} custom-call(bf16[512,1792]{1,0:T(8,128)(2,1)S(1)} %copy-done.5, bf16[2048,1792]{1,0:T(8,128)(2,1)S(1)} %copy-done.4), custom_call_target="tpu_custom_call" | custom-call | flops 1879048192 | bytes 7340032 | tf_op jit(solution)/shard_map/pallas_call | solution.py:69
  19.2 2.8 %collective-permute-done = f32[2048,256]{1,0:T(8,128)S(1)} collective-permute-done((f32[2048,256]{1,0:T(8,128)S(1)}, f32[2048,256]{1,0:T(8,128)S(1)}, u32[]{:S(2)}, u32[]{:S(2)}) %collective-permute-start) | collective-permute-done | bytes 2097184 | tf_op jit(solution)/shard_map/ppermute | solution.py:24
  22.4 23.9 %all_to_all.20.blocks = bf16[8,256,256]{2,1,0:T(8,128)(2,1)S(1)} all-to-all(bf16[8,256,256]{2,1,0:T(8,128)(2,1)S(1)} %bitcast.20), channel_id=1, replica_groups=mesh['y_lo'=2,'x'=4,'z'=4,'y_hi'=2,'core'=2] {'z','y_hi'}, dimensions={0} | all-to-all | bytes 2097152 | tf_op jit(solution)/shard_map/all_to_all | solution.py:201
  47.3 3.6 %all-to-all-start.1 = ((bf16[8,256,256]{2,1,0:T(8,128)(2,1)}), bf16[8,256,256]{2,1,0:T(8,128)(2,1)S(1)}, u32[]{:S(2)}, u32[]{:S(2)}) async-start(bf16[8,256,256]{2,1,0:T(8,128)(2,1)} %shard_map.61), calls=%async_computation.1 | async-start | bytes 2097152 | tf_op jit(solution)/shard_map/all_to_all | solution.py:203
  51.1 1.9 %collective-permute-start.1 = (bf16[512,256]{1,0:T(8,128)(2,1)S(1)}, bf16[512,256]{1,0:T(8,128)(2,1)S(1)}, u32[]{:S(2)}, u32[]{:S(2)}) collective-permute-start(bf16[512,256]{1,0:T(8,128)(2,1)S(1)} %bitcast.21), channel_id=1, source_target_pairs={{0,1},{1,0},{2,3},{3,2},{4,5},{5,4},{6,7},{7,6},{8,9},{9,8},{10,11... | collective-permute-start | bytes 786440 | tf_op jit(solution)/shard_map/ppermute | solution.py:24
  54.2 11.8 %all-to-all-done.1 = bf16[8,256,256]{2,1,0:T(8,128)(2,1)S(1)} async-done(((bf16[8,256,256]{2,1,0:T(8,128)(2,1)}), bf16[8,256,256]{2,1,0:T(8,128)(2,1)S(1)}, u32[]{:S(2)}, u32[]{:S(2)}) %all-to-all-start.1) | async-done | bytes 1048608 | tf_op jit(solution)/shard_map/all_to_all | solution.py:203
  66.0 5.7 %shard_map.62 = (bf16[256,512]{1,0:T(8,128)(2,1)S(1)}, bf16[256,512]{1,0:T(8,128)(2,1)S(1)}, bf16[8,32,2048]{2,1,0:T(8,128)(2,1)}) custom-call(bf16[2048,256]{1,0:T(8,128)(2,1)S(1)} %bitcast.16, bf16[512,256]{1,0:T(8,128)(2,1)S(1)} %bitcast.19, bf16[512,256]{1,0:T(8,128)(2,1)S(1)} %collective-permute-done.1.far, bf16[512,2048]{1,0:T(8,128)(2,1)} %a0.1, ...), custom_call_target="tpu_custom_call" | custom-call | flops 2147483648 | bytes 7340032 | tf_op jit(solution)/shard_map/pallas_call | solution.py:33
  72.4 3.1 %collective-permute-start.3 = (bf16[2048,256]{1,0:T(8,128)(2,1)S(1)}, bf16[2048,256]{1,0:T(8,128)(2,1)S(1)}, u32[]{:S(2)}, u32[]{:S(2)}) collective-permute-start(bf16[2048,256]{1,0:T(8,128)(2,1)S(1)} %bitcast.17), channel_id=1, source_target_pairs={{0,1},{1,0},{2,3},{3,2},{4,5},{5,4},{6,7},{7,6},{8,9},{9,8},{10,11... | collective-permute-start | bytes 3145736 | tf_op jit(solution)/shard_map/ppermute | solution.py:24
  75.5 3.6 %all-to-all-start.2 = ((bf16[8,32,2048]{2,1,0:T(8,128)(2,1)}), bf16[8,32,2048]{2,1,0:T(8,128)(2,1)S(1)}, u32[]{:S(2)}, u32[]{:S(2)}) async-start(bf16[8,32,2048]{2,1,0:T(8,128)(2,1)} %get-tuple-element.22), calls=%async_computation.2 | async-start | bytes 2097152 | tf_op jit(solution)/shard_map/all_to_all | solution.py:214
  81.7 2.1 %shard_map.63 = (f32[2,256,512]{2,1,0:T(8,128)S(1)}, bf16[2,256,512]{2,1,0:T(8,128)(2,1)}, bf16[2,256,512]{2,1,0:T(8,128)(2,1)}, bf16[2,256,512]{2,1,0:T(8,128)(2,1)}) custom-call(bf16[2048,256]{1,0:T(8,128)(2,1)S(1)} %bitcast.18, bf16[256,512]{1,0:T(8,128)(2,1)S(1)} %copy-done.9, bf16[2048,256]{1,0:T(8,128)(2,1)S(1)} %collective-permute-done.3.codes_o, ...), custom_call_target="tpu_custom_call" | custom-call | flops 1073741824 | bytes 5242880 | tf_op jit(solution)/shard_map/pallas_call | solution.py:33
  86.0 2.4 %collective-permute-start.6 = (bf16[2,256,512]{2,1,0:T(8,128)(2,1)}, bf16[2,256,512]{2,1,0:T(8,128)(2,1)S(1)}, u32[]{:S(2)}, u32[]{:S(2)}) collective-permute-start(bf16[2,256,512]{2,1,0:T(8,128)(2,1)} %get-tuple-element.30), channel_id=1, source_target_pairs={{0,32},{16,48},{32,0},{48,16},{1,33},{17,49},{33,1},{49,17},{2,34}... | collective-permute-start | bytes 1572872 | tf_op jit(solution)/shard_map/ppermute | solution.py:24
  89.6 6.8 %all-to-all-done.2.blocks = bf16[8,32,2048]{2,1,0:T(8,128)(2,1)S(1)} async-done(((bf16[8,32,2048]{2,1,0:T(8,128)(2,1)}), bf16[8,32,2048]{2,1,0:T(8,128)(2,1)S(1)}, u32[]{:S(2)}, u32[]{:S(2)}) %all-to-all-start.2) | async-done | bytes 1048608 | tf_op jit(solution)/shard_map/all_to_all | solution.py:214
  97.7 5.6 %all-to-all-start.3 = ((bf16[32,32,512]{2,1,0:T(8,128)(2,1)}), bf16[32,32,512]{2,1,0:T(8,128)(2,1)S(1)}, u32[]{:S(2)}, u32[]{:S(2)}) async-start(bf16[32,32,512]{2,1,0:T(8,128)(2,1)} %bitcast.5), calls=%async_computation.3 | async-start | bytes 2097152 | tf_op jit(solution)/shard_map/all_to_all | solution.py:228
  103.2 8.6 %collective-permute-done.6.r2 = bf16[2,256,512]{2,1,0:T(8,128)(2,1)S(1)} collective-permute-done((bf16[2,256,512]{2,1,0:T(8,128)(2,1)}, bf16[2,256,512]{2,1,0:T(8,128)(2,1)S(1)}, u32[]{:S(2)}, u32[]{:S(2)}) %collective-permute-start.6) | collective-permute-done | bytes 524320 | tf_op jit(solution)/shard_map/ppermute | solution.py:24
  113.2 14.8 %all-to-all-done.3 = bf16[32,32,512]{2,1,0:T(8,128)(2,1)S(1)} async-done(((bf16[32,32,512]{2,1,0:T(8,128)(2,1)}), bf16[32,32,512]{2,1,0:T(8,128)(2,1)S(1)}, u32[]{:S(2)}, u32[]{:S(2)}) %all-to-all-start.3) | async-done | bytes 1048608 | tf_op jit(solution)/shard_map/all_to_all | solution.py:228
  128.7 3.1 %copy-done = bf16[2048,1792]{1,0:T(8,128)(2,1)S(1)} copy-done((bf16[2048,1792]{1,0:T(8,128)(2,1)S(1)}, bf16[2048,1792]{1,0:T(8,128)(2,1)}, u32[]{:S(2)}) %copy-start) | copy-done | bytes 7340056
  133.0 3.1 %copy-done.1 = bf16[2048,1792]{1,0:T(8,128)(2,1)S(1)} copy-done((bf16[2048,1792]{1,0:T(8,128)(2,1)S(1)}, bf16[2048,1792]{1,0:T(8,128)(2,1)}, u32[]{:S(2)}) %copy-start.1) | copy-done | bytes 7340056
  138.8 3.1 %copy-done.2 = bf16[2048,1792]{1,0:T(8,128)(2,1)S(1)} copy-done((bf16[2048,1792]{1,0:T(8,128)(2,1)S(1)}, bf16[2048,1792]{1,0:T(8,128)(2,1)}, u32[]{:S(2)}) %copy-start.2) | copy-done | bytes 7340056
  143.0 3.1 %copy-done.3 = bf16[2048,1792]{1,0:T(8,128)(2,1)S(1)} copy-done((bf16[2048,1792]{1,0:T(8,128)(2,1)S(1)}, bf16[2048,1792]{1,0:T(8,128)(2,1)}, u32[]{:S(2)}) %copy-start.3) | copy-done | bytes 7340056
  147.3 17.6 %collective-permute-done.9 = bf16[256,512]{1,0:T(8,128)(2,1)S(1)} collective-permute-done((bf16[256,512]{1,0:T(8,128)(2,1)S(1)}, bf16[256,512]{1,0:T(8,128)(2,1)S(1)}, u32[]{:S(2)}, u32[]{:S(2)}) %collective-permute-start.9) | collective-permute-done | bytes 262176 | tf_op jit(solution)/shard_map/ppermute | solution.py:24
  165.8 2.0 %copy.8 = f32[512,256]{1,0:T(8,128)} copy(f32[512,256]{0,1:T(8,128)} %multiply_bitcast_fusion) | data formatting | bytes 1048576
  167.8 2.6 %add_multiply_fusion = f32[256,1792]{1,0:T(8,128)} fusion(f32[256,1792]{1,0:T(8,128)S(1)} %shard_map.67, bf16[256,1792]{1,0:T(8,128)(2,1)} %collective-permute-done.10), kind=kLoop, calls=%fused_computation.1 | loop fusion | flops 1376256 | bytes 4587520 | tf_op jit(solution)/shard_map/mul | solution.py:240
  (48 shorter events, 22.9 us)
Async XLA Ops:
  7.2 1.5 copy-start.5
  7.2 89.2 %all-gather.3.cloned.1.call-start = ((), (), s32[]{:S(2)}) async-start(), calls=%async_computation.4 | async-start | bytes 9175040 | tf_op jit(solution)/shard_map/all_gather | solution.py:193
  8.7 3.1 %copy-start.4 = (bf16[2048,1792]{1,0:T(8,128)(2,1)S(1)}, bf16[2048,1792]{1,0:T(8,128)(2,1)}, u32[]{:S(2)}) copy-start(bf16[2048,1792]{1,0:T(8,128)(2,1)} %b.3) | copy-start | bytes 22020100
  14.7 7.4 %collective-permute-start = (f32[2048,256]{1,0:T(8,128)S(1)}, f32[2048,256]{1,0:T(8,128)S(1)}, u32[]{:S(2)}, u32[]{:S(2)}) collective-permute-start(f32[2048,256]{1,0:T(8,128)S(1)} %shard_map.60), channel_id=1, source_target_pairs={{0,1},{1,0},{2,3},{3,2},{4,5},{5,4},{6,7},{7,6},{8,9},{9,8},{10,11... | collective-permute-start | bytes 6291464 | tf_op jit(solution)/shard_map/ppermute | solution.py:24
  16.2 38.0 %collective-permute-start.2 = (bf16[512,2048]{1,0:T(8,128)(2,1)}, bf16[512,2048]{1,0:T(8,128)(2,1)}, u32[]{:S(2)}, u32[]{:S(2)}) collective-permute-start(bf16[512,2048]{1,0:T(8,128)(2,1)} %a0.1), channel_id=1, source_target_pairs={{0,1},{1,0},{2,3},{3,2},{4,5},{5,4},{6,7},{7,6},{8,9},{9,8},{10,11... | collective-permute-start | bytes 6291464 | tf_op jit(solution)/shard_map/ppermute | solution.py:24
  46.2 4.7 %copy-start.10 = (bf16[512,512]{1,0:T(8,128)(2,1)S(1)}, bf16[512,512]{1,0:T(8,128)(2,1)}, u32[]{:S(2)}) copy-start(bf16[512,512]{1,0:T(8,128)(2,1)} %param.5) | copy-start | bytes 1572868
  47.3 18.6 %all-to-all-start.1 = ((bf16[8,256,256]{2,1,0:T(8,128)(2,1)}), bf16[8,256,256]{2,1,0:T(8,128)(2,1)S(1)}, u32[]{:S(2)}, u32[]{:S(2)}) async-start(bf16[8,256,256]{2,1,0:T(8,128)(2,1)} %shard_map.61), calls=%async_computation.1 | async-start | bytes 2097152 | tf_op jit(solution)/shard_map/all_to_all | solution.py:203
  51.1 3.1 %collective-permute-start.1 = (bf16[512,256]{1,0:T(8,128)(2,1)S(1)}, bf16[512,256]{1,0:T(8,128)(2,1)S(1)}, u32[]{:S(2)}, u32[]{:S(2)}) collective-permute-start(bf16[512,256]{1,0:T(8,128)(2,1)S(1)} %bitcast.21), channel_id=1, source_target_pairs={{0,1},{1,0},{2,3},{3,2},{4,5},{5,4},{6,7},{7,6},{8,9},{9,8},{10,11... | collective-permute-start | bytes 786440 | tf_op jit(solution)/shard_map/ppermute | solution.py:24
  72.4 8.3 %collective-permute-start.3 = (bf16[2048,256]{1,0:T(8,128)(2,1)S(1)}, bf16[2048,256]{1,0:T(8,128)(2,1)S(1)}, u32[]{:S(2)}, u32[]{:S(2)}) collective-permute-start(bf16[2048,256]{1,0:T(8,128)(2,1)S(1)} %bitcast.17), channel_id=1, source_target_pairs={{0,1},{1,0},{2,3},{3,2},{4,5},{5,4},{6,7},{7,6},{8,9},{9,8},{10,11... | collective-permute-start | bytes 3145736 | tf_op jit(solution)/shard_map/ppermute | solution.py:24
  75.5 20.9 %all-to-all-start.2 = ((bf16[8,32,2048]{2,1,0:T(8,128)(2,1)}), bf16[8,32,2048]{2,1,0:T(8,128)(2,1)S(1)}, u32[]{:S(2)}, u32[]{:S(2)}) async-start(bf16[8,32,2048]{2,1,0:T(8,128)(2,1)} %get-tuple-element.22), calls=%async_computation.2 | async-start | bytes 2097152 | tf_op jit(solution)/shard_map/all_to_all | solution.py:214
  79.1 1.6 collective-permute-start.4
  83.7 1.1 copy-start.6
  84.8 18.4 %collective-permute-start.5 = (bf16[2,256,512]{2,1,0:T(8,128)(2,1)}, bf16[2,256,512]{2,1,0:T(8,128)(2,1)S(1)}, u32[]{:S(2)}, u32[]{:S(2)}) collective-permute-start(bf16[2,256,512]{2,1,0:T(8,128)(2,1)} %get-tuple-element.29), channel_id=1, source_target_pairs={{0,16},{16,32},{32,48},{48,0},{1,17},{17,33},{33,49},{49,1},{2,18}... | collective-permute-start | bytes 1572872 | tf_op jit(solution)/shard_map/ppermute | solution.py:24
  86.0 25.8 %collective-permute-start.6 = (bf16[2,256,512]{2,1,0:T(8,128)(2,1)}, bf16[2,256,512]{2,1,0:T(8,128)(2,1)S(1)}, u32[]{:S(2)}, u32[]{:S(2)}) collective-permute-start(bf16[2,256,512]{2,1,0:T(8,128)(2,1)} %get-tuple-element.30), channel_id=1, source_target_pairs={{0,32},{16,48},{32,0},{48,16},{1,33},{17,49},{33,1},{49,17},{2,34}... | collective-permute-start | bytes 1572872 | tf_op jit(solution)/shard_map/ppermute | solution.py:24
  88.4 23.4 %collective-permute-start.7 = (bf16[2,256,512]{2,1,0:T(8,128)(2,1)}, bf16[2,256,512]{2,1,0:T(8,128)(2,1)S(1)}, u32[]{:S(2)}, u32[]{:S(2)}) collective-permute-start(bf16[2,256,512]{2,1,0:T(8,128)(2,1)} %get-tuple-element.31), channel_id=1, source_target_pairs={{0,48},{16,0},{32,16},{48,32},{1,49},{17,1},{33,17},{49,33},{2,50}... | collective-permute-start | bytes 1572872 | tf_op jit(solution)/shard_map/ppermute | solution.py:24
  97.7 30.4 %all-to-all-start.3 = ((bf16[32,32,512]{2,1,0:T(8,128)(2,1)}), bf16[32,32,512]{2,1,0:T(8,128)(2,1)S(1)}, u32[]{:S(2)}, u32[]{:S(2)}) async-start(bf16[32,32,512]{2,1,0:T(8,128)(2,1)} %bitcast.5), calls=%async_computation.3 | async-start | bytes 2097152 | tf_op jit(solution)/shard_map/all_to_all | solution.py:228
  111.8 1.2 copy-start.7
  128.0 4.9 %collective-permute-start.8 = (bf16[4,256,512]{2,1,0:T(8,128)(2,1)S(1)}, bf16[4,256,512]{2,1,0:T(8,128)(2,1)S(1)}, u32[]{:S(2)}, u32[]{:S(2)}) collective-permute-start(bf16[4,256,512]{2,1,0:T(8,128)(2,1)S(1)} %bitcast.13), channel_id=1, source_target_pairs={{0,1},{1,0},{2,3},{3,2},{4,5},{5,4},{6,7},{7,6},{8,9},{9,8},{10,11... | collective-permute-start | bytes 3145736 | tf_op jit(solution)/shard_map/ppermute | solution.py:24
  128.7 3.1 %copy-start = (bf16[2048,1792]{1,0:T(8,128)(2,1)S(1)}, bf16[2048,1792]{1,0:T(8,128)(2,1)}, u32[]{:S(2)}) copy-start(bf16[2048,1792]{1,0:T(8,128)(2,1)} %all-gather.3.cloned.1.call-done) | copy-start | bytes 22020100
  133.0 3.1 %copy-start.1 = (bf16[2048,1792]{1,0:T(8,128)(2,1)S(1)}, bf16[2048,1792]{1,0:T(8,128)(2,1)}, u32[]{:S(2)}) copy-start(bf16[2048,1792]{1,0:T(8,128)(2,1)} %all-gather.3.cloned.1.call-done) | copy-start | bytes 22020100
  137.2 30.6 %collective-permute-start.10 = (bf16[256,1792]{1,0:T(8,128)(2,1)S(1)}, bf16[256,1792]{1,0:T(8,128)(2,1)}, u32[]{:S(2)}, u32[]{:S(2)}) collective-permute-start(bf16[256,1792]{1,0:T(8,128)(2,1)S(1)} %shard_map.69), channel_id=1, source_target_pairs={{0,64},{64,0},{1,65},{65,1},{2,66},{66,2},{3,67},{67,3},{4,68},{68... | collective-permute-start | bytes 2752520 | tf_op jit(solution)/shard_map/ppermute | solution.py:24
  137.7 27.2 %collective-permute-start.9 = (bf16[256,512]{1,0:T(8,128)(2,1)S(1)}, bf16[256,512]{1,0:T(8,128)(2,1)S(1)}, u32[]{:S(2)}, u32[]{:S(2)}) collective-permute-start(bf16[256,512]{1,0:T(8,128)(2,1)S(1)} %get-tuple-element.38), channel_id=1, source_target_pairs={{0,64},{64,0},{1,65},{65,1},{2,66},{66,2},{3,67},{67,3},{4,68},{68... | collective-permute-start | bytes 786440 | tf_op jit(solution)/shard_map/ppermute | solution.py:24
  138.8 3.1 %copy-start.2 = (bf16[2048,1792]{1,0:T(8,128)(2,1)S(1)}, bf16[2048,1792]{1,0:T(8,128)(2,1)}, u32[]{:S(2)}) copy-start(bf16[2048,1792]{1,0:T(8,128)(2,1)} %all-gather.3.cloned.1.call-done) | copy-start | bytes 22020100
  143.0 3.1 %copy-start.3 = (bf16[2048,1792]{1,0:T(8,128)(2,1)S(1)}, bf16[2048,1792]{1,0:T(8,128)(2,1)}, u32[]{:S(2)}) copy-start(bf16[2048,1792]{1,0:T(8,128)(2,1)} %all-gather.3.cloned.1.call-done) | copy-start | bytes 22020100
  (2 other events, 1.7 us)
Sparse Core Ops, SparseCore 0:
  9.7 77.5 all-gather.2

commit v22 on v20

--- a/solution.py
+++ b/solution.py
@@ -177,7 +177,7 @@
         value = keep[side]
         for r in (r1, r2, r3):
             value = value + r[side].astype(F32)
-        out[...] = value.astype(out.dtype)
+        out[...] = value.T.astype(out.dtype)
 
 
 def local(acts, target, proj_b, proj_a):
@@ -231,10 +231,11 @@
     away = last_call(grad, grad_o, row, 0, BF)
     away = swap(away, "y_lo").astype(F32)
     here = last_call(grad, grad_o, row, 1, F32)
-    term_o, term_a = call(term_sum_kernel, [like((width, outs), F32), like((width, outs))], *terms)
+    term_o, term_a = call(term_sum_kernel, [like((outs, width), F32), like((outs, width))], *terms)
     term_a = swap(term_a, "y_lo").astype(F32)
-    here, term_o = barrier((here, term_o))
-    return (((term_o + term_a) * scale).T, (here + away) * scale)
+    grad_b = (here + away) * scale
+    grad_b, term_o = barrier((grad_b, term_o))
+    return ((term_o + term_a) * scale, grad_b)
 
 
 def solution(mesh):

time: 167 us -> 168 us (level)
    unnamed x33 -> x32, local copies, waits for them, and re-layouts: 11.5 us -> 10.5 us
  transfers between devices with their start and end apart: 14 -> 14, of which waited for: 8 -> 10; matrix products, arithmetic and copies ran while one was open for 1% -> 1% of each run, Pallas kernels for 11% -> 11%
where the time goes in v22:
time: 168 us; the launch traced here: 166 us
  waiting for transfers between devices  51.7 us (31%)
  blocking collectives  47.2 us (28%)
  starting transfers between devices  20.5 us (12%)
  Pallas kernels  19.1 us (11%)
  between operations  14.2 us (8%)
  local copies, waits for them, and re-layouts  10.6 us (6%)
  other arithmetic  2.59 us (2%)
    ppermute x11, waiting for transfers between devices, shift(): lax.ppermute(array, axis, [(i, (i + step) % size) for i in range(size)])  30.6 us
    all_to_all x1, blocking collectives, local(): blocks = lax.all_to_all(mine, ZY, 0, 0)  23.9 us
    all_to_all x1, blocking collectives, local(): lax.all_to_all(split.reshape(32, sub, 2 * width), ('x', 'z', 'y_hi'), 0, 0)  23.3 us
    ppermute x11, starting transfers between devices, shift(): lax.ppermute(array, axis, [(i, (i + step) % size) for i in range(size)])  13.4 us
    pallas_call x9, Pallas kernels, call(): pl.pallas_call(body, out_shape=outs if len(outs) > 1 else outs[0], in_spe...  13.3 us
    all_to_all x1, waiting for transfers between devices, local(): codes = lax.all_to_all(codes, ZY, 0, 0).reshape(rank, half)  11.8 us
    unnamed x32, local copies, waits for them, and re-layouts  10.5 us
    all_to_all x1, waiting for transfers between devices, local(): blocks = lax.all_to_all(partial, ZY, 0, 0)  8.72 us
  transfers between devices with their start and end apart: 14, of which 10 were waited for; matrix products, arithmetic and copies ran while one was open for 1% of the time, Pallas kernels for 11%

profile of v22, /device:TPU:1, one launch (start us, length us, event | category | flops | bytes accessed | tf_op | source)
XLA Modules:
  0.0 165.9 jit_solution(5530029045480401366)
XLA Ops:
  8.7 3.1 %copy-done = bf16[2048,1792]{1,0:T(8,128)(2,1)S(1)} copy-done((bf16[2048,1792]{1,0:T(8,128)(2,1)S(1)}, bf16[2048,1792]{1,0:T(8,128)(2,1)}, u32[]{:S(2)}) %copy-start) | copy-done | bytes 7340056
  11.7 2.9 %shard_map.60 = f32[2048,256]{1,0:T(8,128)S(1)} custom-call(bf16[512,1792]{1,0:T(8,128)(2,1)S(1)} %copy-done.1, bf16[2048,1792]{1,0:T(8,128)(2,1)S(1)} %copy-done), custom_call_target="tpu_custom_call" | custom-call | flops 1879048192 | bytes 7340032 | tf_op jit(solution)/shard_map/pallas_call | solution.py:69
  14.7 1.5 collective-permute-start
  16.3 2.9 %shard_map.59 = f32[2048,256]{1,0:T(8,128)S(1)} custom-call(bf16[512,1792]{1,0:T(8,128)(2,1)S(1)} %copy-done.1, bf16[2048,1792]{1,0:T(8,128)(2,1)S(1)} %copy-done), custom_call_target="tpu_custom_call" | custom-call | flops 1879048192 | bytes 7340032 | tf_op jit(solution)/shard_map/pallas_call | solution.py:69
  19.2 2.8 %collective-permute-done = f32[2048,256]{1,0:T(8,128)S(1)} collective-permute-done((f32[2048,256]{1,0:T(8,128)S(1)}, f32[2048,256]{1,0:T(8,128)S(1)}, u32[]{:S(2)}, u32[]{:S(2)}) %collective-permute-start) | collective-permute-done | bytes 2097184 | tf_op jit(solution)/shard_map/ppermute | solution.py:24
  22.4 23.9 %all_to_all.20.blocks = bf16[8,256,256]{2,1,0:T(8,128)(2,1)S(1)} all-to-all(bf16[8,256,256]{2,1,0:T(8,128)(2,1)S(1)} %bitcast.21), channel_id=1, replica_groups=mesh['y_lo'=2,'x'=4,'z'=4,'y_hi'=2,'core'=2] {'z','y_hi'}, dimensions={0} | all-to-all | bytes 2097152 | tf_op jit(solution)/shard_map/all_to_all | solution.py:201
  47.3 3.6 %all-to-all-start.1 = ((bf16[8,256,256]{2,1,0:T(8,128)(2,1)}), bf16[8,256,256]{2,1,0:T(8,128)(2,1)S(1)}, u32[]{:S(2)}, u32[]{:S(2)}) async-start(bf16[8,256,256]{2,1,0:T(8,128)(2,1)} %shard_map.61), calls=%async_computation.1 | async-start | bytes 2097152 | tf_op jit(solution)/shard_map/all_to_all | solution.py:203
  51.1 1.9 %collective-permute-start.1 = (bf16[512,256]{1,0:T(8,128)(2,1)S(1)}, bf16[512,256]{1,0:T(8,128)(2,1)S(1)}, u32[]{:S(2)}, u32[]{:S(2)}) collective-permute-start(bf16[512,256]{1,0:T(8,128)(2,1)S(1)} %bitcast.22), channel_id=1, source_target_pairs={{0,1},{1,0},{2,3},{3,2},{4,5},{5,4},{6,7},{7,6},{8,9},{9,8},{10,11... | collective-permute-start | bytes 786440 | tf_op jit(solution)/shard_map/ppermute | solution.py:24
  54.2 11.8 %all-to-all-done.1 = bf16[8,256,256]{2,1,0:T(8,128)(2,1)S(1)} async-done(((bf16[8,256,256]{2,1,0:T(8,128)(2,1)}), bf16[8,256,256]{2,1,0:T(8,128)(2,1)S(1)}, u32[]{:S(2)}, u32[]{:S(2)}) %all-to-all-start.1) | async-done | bytes 1048608 | tf_op jit(solution)/shard_map/all_to_all | solution.py:203
  66.0 5.7 %shard_map.62 = (bf16[256,512]{1,0:T(8,128)(2,1)S(1)}, bf16[256,512]{1,0:T(8,128)(2,1)S(1)}, bf16[8,32,2048]{2,1,0:T(8,128)(2,1)}) custom-call(bf16[2048,256]{1,0:T(8,128)(2,1)S(1)} %bitcast.16, bf16[512,256]{1,0:T(8,128)(2,1)S(1)} %bitcast.20, bf16[512,256]{1,0:T(8,128)(2,1)S(1)} %collective-permute-done.1.far, bf16[512,2048]{1,0:T(8,128)(2,1)} %a0.1, ...), custom_call_target="tpu_custom_call" | custom-call | flops 2147483648 | bytes 7340032 | tf_op jit(solution)/shard_map/pallas_call | solution.py:33
  72.4 3.1 %collective-permute-start.3 = (bf16[2048,256]{1,0:T(8,128)(2,1)S(1)}, bf16[2048,256]{1,0:T(8,128)(2,1)S(1)}, u32[]{:S(2)}, u32[]{:S(2)}) collective-permute-start(bf16[2048,256]{1,0:T(8,128)(2,1)S(1)} %bitcast.17), channel_id=1, source_target_pairs={{0,1},{1,0},{2,3},{3,2},{4,5},{5,4},{6,7},{7,6},{8,9},{9,8},{10,11... | collective-permute-start | bytes 3145736 | tf_op jit(solution)/shard_map/ppermute | solution.py:24
  75.5 3.6 %all-to-all-start.2 = ((bf16[8,32,2048]{2,1,0:T(8,128)(2,1)}), bf16[8,32,2048]{2,1,0:T(8,128)(2,1)S(1)}, u32[]{:S(2)}, u32[]{:S(2)}) async-start(bf16[8,32,2048]{2,1,0:T(8,128)(2,1)} %get-tuple-element.19), calls=%async_computation.2 | async-start | bytes 2097152 | tf_op jit(solution)/shard_map/all_to_all | solution.py:214
  79.2 1.5 collective-permute-done.4.message
  81.8 1.2 copy-done.3
  84.0 1.2 shard_map.63
  87.7 8.7 %all-to-all-done.2.blocks = bf16[8,32,2048]{2,1,0:T(8,128)(2,1)S(1)} async-done(((bf16[8,32,2048]{2,1,0:T(8,128)(2,1)}), bf16[8,32,2048]{2,1,0:T(8,128)(2,1)S(1)}, u32[]{:S(2)}, u32[]{:S(2)}) %all-to-all-start.2) | async-done | bytes 1048608 | tf_op jit(solution)/shard_map/all_to_all | solution.py:214
  96.7 23.3 %all_to_all.21 = bf16[32,32,512]{2,1,0:T(8,128)(2,1)S(1)} all-to-all(bf16[32,32,512]{2,1,0:T(8,128)(2,1)S(1)} %bitcast.19), channel_id=1, replica_groups=mesh['y_lo'=2,'x'=4,'z'=4,'y_hi'=2,'core'=2] {'x','z','y_hi'}, dimensions={0} | all-to-all | bytes 2097152 | tf_op jit(solution)/shard_map/all_to_all | solution.py:228
  120.0 2.3 %collective-permute-start.5 = (bf16[4,256,512]{2,1,0:T(8,128)(2,1)S(1)}, bf16[4,256,512]{2,1,0:T(8,128)(2,1)S(1)}, u32[]{:S(2)}, u32[]{:S(2)}) collective-permute-start(bf16[4,256,512]{2,1,0:T(8,128)(2,1)S(1)} %bitcast.13), channel_id=1, source_target_pairs={{0,1},{1,0},{2,3},{3,2},{4,5},{5,4},{6,7},{7,6},{8,9},{9,8},{10,11... | collective-permute-start | bytes 3145736 | tf_op jit(solution)/shard_map/ppermute | solution.py:24
  124.6 1.2 shard_map.68
  126.3 2.0 %collective-permute-start.8 = (bf16[2,256,512]{2,1,0:T(8,128)(2,1)S(1)}, bf16[2,256,512]{2,1,0:T(8,128)(2,1)S(1)}, u32[]{:S(2)}, u32[]{:S(2)}) collective-permute-start(bf16[2,256,512]{2,1,0:T(8,128)(2,1)S(1)} %copy-done.7), channel_id=1, source_target_pairs={{0,32},{16,48},{32,0},{48,16},{1,33},{17,49},{33,1},{49,17},{2,34}... | collective-permute-start | bytes 1572872 | tf_op jit(solution)/shard_map/ppermute | solution.py:24
  129.0 12.0 %collective-permute-done.7.r1 = bf16[2,256,512]{2,1,0:T(8,128)(2,1)S(1)} collective-permute-done((bf16[2,256,512]{2,1,0:T(8,128)(2,1)S(1)}, bf16[2,256,512]{2,1,0:T(8,128)(2,1)S(1)}, u32[]{:S(2)}, u32[]{:S(2)}) %collective-permute-start.7) | collective-permute-done | bytes 524320 | tf_op jit(solution)/shard_map/ppermute | solution.py:24
  141.0 9.9 %collective-permute-done.8.r2 = bf16[2,256,512]{2,1,0:T(8,128)(2,1)S(1)} collective-permute-done((bf16[2,256,512]{2,1,0:T(8,128)(2,1)S(1)}, bf16[2,256,512]{2,1,0:T(8,128)(2,1)S(1)}, u32[]{:S(2)}, u32[]{:S(2)}) %collective-permute-start.8) | collective-permute-done | bytes 524320 | tf_op jit(solution)/shard_map/ppermute | solution.py:24
  155.6 1.4 add_multiply_fusion
  157.0 1.2 collective-permute-done.10
  (55 shorter events, 19.0 us)
Async XLA Ops:
  7.2 1.5 copy-start.1
  7.2 89.2 %all-gather.3.cloned.1.call-start = ((), (), s32[]{:S(2)}) async-start(), calls=%async_computation.4 | async-start | bytes 9175040 | tf_op jit(solution)/shard_map/all_gather | solution.py:193
  8.7 3.1 %copy-start = (bf16[2048,1792]{1,0:T(8,128)(2,1)S(1)}, bf16[2048,1792]{1,0:T(8,128)(2,1)}, u32[]{:S(2)}) copy-start(bf16[2048,1792]{1,0:T(8,128)(2,1)} %b.3) | copy-start | bytes 22020100
  14.7 7.4 %collective-permute-start = (f32[2048,256]{1,0:T(8,128)S(1)}, f32[2048,256]{1,0:T(8,128)S(1)}, u32[]{:S(2)}, u32[]{:S(2)}) collective-permute-start(f32[2048,256]{1,0:T(8,128)S(1)} %shard_map.60), channel_id=1, source_target_pairs={{0,1},{1,0},{2,3},{3,2},{4,5},{5,4},{6,7},{7,6},{8,9},{9,8},{10,11... | collective-permute-start | bytes 6291464 | tf_op jit(solution)/shard_map/ppermute | solution.py:24
  16.2 38.0 %collective-permute-start.2 = (bf16[512,2048]{1,0:T(8,128)(2,1)}, bf16[512,2048]{1,0:T(8,128)(2,1)}, u32[]{:S(2)}, u32[]{:S(2)}) collective-permute-start(bf16[512,2048]{1,0:T(8,128)(2,1)} %a0.1), channel_id=1, source_target_pairs={{0,1},{1,0},{2,3},{3,2},{4,5},{5,4},{6,7},{7,6},{8,9},{9,8},{10,11... | collective-permute-start | bytes 6291464 | tf_op jit(solution)/shard_map/ppermute | solution.py:24
  46.2 4.7 %copy-start.12 = (bf16[512,512]{1,0:T(8,128)(2,1)S(1)}, bf16[512,512]{1,0:T(8,128)(2,1)}, u32[]{:S(2)}) copy-start(bf16[512,512]{1,0:T(8,128)(2,1)} %param.5) | copy-start | bytes 1572868
  47.3 18.6 %all-to-all-start.1 = ((bf16[8,256,256]{2,1,0:T(8,128)(2,1)}), bf16[8,256,256]{2,1,0:T(8,128)(2,1)S(1)}, u32[]{:S(2)}, u32[]{:S(2)}) async-start(bf16[8,256,256]{2,1,0:T(8,128)(2,1)} %shard_map.61), calls=%async_computation.1 | async-start | bytes 2097152 | tf_op jit(solution)/shard_map/all_to_all | solution.py:203
  51.1 3.1 %collective-permute-start.1 = (bf16[512,256]{1,0:T(8,128)(2,1)S(1)}, bf16[512,256]{1,0:T(8,128)(2,1)S(1)}, u32[]{:S(2)}, u32[]{:S(2)}) collective-permute-start(bf16[512,256]{1,0:T(8,128)(2,1)S(1)} %bitcast.22), channel_id=1, source_target_pairs={{0,1},{1,0},{2,3},{3,2},{4,5},{5,4},{6,7},{7,6},{8,9},{9,8},{10,11... | collective-permute-start | bytes 786440 | tf_op jit(solution)/shard_map/ppermute | solution.py:24
  72.4 8.3 %collective-permute-start.3 = (bf16[2048,256]{1,0:T(8,128)(2,1)S(1)}, bf16[2048,256]{1,0:T(8,128)(2,1)S(1)}, u32[]{:S(2)}, u32[]{:S(2)}) collective-permute-start(bf16[2048,256]{1,0:T(8,128)(2,1)S(1)} %bitcast.17), channel_id=1, source_target_pairs={{0,1},{1,0},{2,3},{3,2},{4,5},{5,4},{6,7},{7,6},{8,9},{9,8},{10,11... | collective-permute-start | bytes 3145736 | tf_op jit(solution)/shard_map/ppermute | solution.py:24
  75.5 20.9 %all-to-all-start.2 = ((bf16[8,32,2048]{2,1,0:T(8,128)(2,1)}), bf16[8,32,2048]{2,1,0:T(8,128)(2,1)S(1)}, u32[]{:S(2)}, u32[]{:S(2)}) async-start(bf16[8,32,2048]{2,1,0:T(8,128)(2,1)} %get-tuple-element.19), calls=%async_computation.2 | async-start | bytes 2097152 | tf_op jit(solution)/shard_map/all_to_all | solution.py:214
  79.1 1.6 collective-permute-start.4
  80.7 1.1 copy-start.2
  81.8 1.2 copy-start.3
  96.4 25.9 %slice-start = ((s8[7340032]{0:T(1024)(128)(4,1)}), s8[4194304]{0:T(1024)(128)(4,1)S(1)}, s32[]{:S(2)}) async-start(s8[7340032]{0:T(1024)(128)(4,1)} %bitcast.7), calls=%async_computation.5 | async-start | bytes 8388608
  96.4 25.9 %slice-start.1 = ((s8[7340032]{0:T(1024)(128)(4,1)}), s8[3145728]{0:T(1024)(128)(4,1)S(1)}, s32[]{:S(2)}) async-start(s8[7340032]{0:T(1024)(128)(4,1)} %bitcast.7), calls=%async_computation.6 | async-start | bytes 6291456
  120.0 4.6 %collective-permute-start.5 = (bf16[4,256,512]{2,1,0:T(8,128)(2,1)S(1)}, bf16[4,256,512]{2,1,0:T(8,128)(2,1)S(1)}, u32[]{:S(2)}, u32[]{:S(2)}) collective-permute-start(bf16[4,256,512]{2,1,0:T(8,128)(2,1)S(1)} %bitcast.13), channel_id=1, source_target_pairs={{0,1},{1,0},{2,3},{3,2},{4,5},{5,4},{6,7},{7,6},{8,9},{9,8},{10,11... | collective-permute-start | bytes 3145736 | tf_op jit(solution)/shard_map/ppermute | solution.py:24
  123.4 2.8 %copy-start.9 = (bf16[2,256,512]{2,1,0:T(8,128)(2,1)S(1)}, bf16[2,256,512]{2,1,0:T(8,128)(2,1)}, u32[]{:S(2)}) copy-start(bf16[2,256,512]{2,1,0:T(8,128)(2,1)} %copy-done.8) | copy-start | bytes 1572868
  123.5 2.8 %copy-start.7 = (bf16[2,256,512]{2,1,0:T(8,128)(2,1)S(1)}, bf16[2,256,512]{2,1,0:T(8,128)(2,1)}, u32[]{:S(2)}) copy-start(bf16[2,256,512]{2,1,0:T(8,128)(2,1)} %copy-done.6) | copy-start | bytes 1572868
  123.5 4.8 %copy-start.5 = (bf16[2,256,512]{2,1,0:T(8,128)(2,1)S(1)}, bf16[2,256,512]{2,1,0:T(8,128)(2,1)}, u32[]{:S(2)}) copy-start(bf16[2,256,512]{2,1,0:T(8,128)(2,1)} %copy-done.4) | copy-start | bytes 1572868
  125.7 29.9 %collective-permute-start.6 = (bf16[256,1792]{1,0:T(8,128)(2,1)S(1)}, bf16[256,1792]{1,0:T(8,128)(2,1)S(1)}, u32[]{:S(2)}, u32[]{:S(2)}) collective-permute-start(bf16[256,1792]{1,0:T(8,128)(2,1)S(1)} %shard_map.68), channel_id=1, source_target_pairs={{0,64},{64,0},{1,65},{65,1},{2,66},{66,2},{3,67},{67,3},{4,68},{68... | collective-permute-start | bytes 2752520 | tf_op jit(solution)/shard_map/ppermute | solution.py:24
  126.3 14.7 %collective-permute-start.7 = (bf16[2,256,512]{2,1,0:T(8,128)(2,1)S(1)}, bf16[2,256,512]{2,1,0:T(8,128)(2,1)S(1)}, u32[]{:S(2)}, u32[]{:S(2)}) collective-permute-start(bf16[2,256,512]{2,1,0:T(8,128)(2,1)S(1)} %copy-done.9), channel_id=1, source_target_pairs={{0,16},{16,32},{32,48},{48,0},{1,17},{17,33},{33,49},{49,1},{2,18}... | collective-permute-start | bytes 1572872 | tf_op jit(solution)/shard_map/ppermute | solution.py:24
  126.3 24.6 %collective-permute-start.8 = (bf16[2,256,512]{2,1,0:T(8,128)(2,1)S(1)}, bf16[2,256,512]{2,1,0:T(8,128)(2,1)S(1)}, u32[]{:S(2)}, u32[]{:S(2)}) collective-permute-start(bf16[2,256,512]{2,1,0:T(8,128)(2,1)S(1)} %copy-done.7), channel_id=1, source_target_pairs={{0,32},{16,48},{32,0},{48,16},{1,33},{17,49},{33,1},{49,17},{2,34}... | collective-permute-start | bytes 1572872 | tf_op jit(solution)/shard_map/ppermute | solution.py:24
  128.3 23.6 %collective-permute-start.9 = (bf16[2,256,512]{2,1,0:T(8,128)(2,1)S(1)}, bf16[2,256,512]{2,1,0:T(8,128)(2,1)S(1)}, u32[]{:S(2)}, u32[]{:S(2)}) collective-permute-start(bf16[2,256,512]{2,1,0:T(8,128)(2,1)S(1)} %copy-done.5), channel_id=1, source_target_pairs={{0,48},{16,0},{32,16},{48,32},{1,49},{17,1},{33,17},{49,33},{2,50}... | collective-permute-start | bytes 1572872 | tf_op jit(solution)/shard_map/ppermute | solution.py:24
  152.2 6.1 %collective-permute-start.10 = (bf16[512,256]{1,0:T(8,128)(2,1)S(1)}, bf16[512,256]{1,0:T(8,128)(2,1)S(1)}, u32[]{:S(2)}, u32[]{:S(2)}) collective-permute-start(bf16[512,256]{1,0:T(8,128)(2,1)S(1)} %get-tuple-element.32), channel_id=1, source_target_pairs={{0,64},{64,0},{1,65},{65,1},{2,66},{66,2},{3,67},{67,3},{4,68},{68... | collective-permute-start | bytes 786440 | tf_op jit(solution)/shard_map/ppermute | solution.py:24
  (5 other events, 4.1 us)
Sparse Core Ops, SparseCore 0:
  9.7 77.5 all-gather.2

commit v23 on v22

--- a/solution.py
+++ b/solution.py
@@ -171,12 +171,15 @@
                 out[side, :, c : c + 256] = acc.astype(out.dtype)
 
 
-def term_sum_kernel(keep, r1, r2, r3, own, away):
+def term_add_kernel(keep, r2, out):
+    for side in range(2):
+        out[side] = keep[side] + r2[side].astype(F32)
+
+
+def term_sum_kernel(keep, r1, r3, own, away):
     y_lo = lax.axis_index("y_lo")
     for out, side in ((own, y_lo), (away, 1 - y_lo)):
-        value = keep[side]
-        for r in (r1, r2, r3):
-            value = value + r[side].astype(F32)
+        value = keep[side] + r1[side].astype(F32) + r3[side].astype(F32)
         out[...] = value.T.astype(out.dtype)
 
 
@@ -220,18 +223,22 @@
         codes, own, codes_o, swap(message, "core"),
         flops=2 * tokens * rank * outs,
     )
-    terms = [terms[0]] + [shift(terms[k], "x", 4, k) for k in (1, 2, 3)]
+    terms = list(terms)
+    far = shift(terms[2], "x", 4, 2)
 
     barrier = lax.optimization_barrier
     blocks, row, terms[0] = barrier((blocks, row, terms[0]))
     split = call(spread_kernel, [like((4, 8, sub, 2 * width))], blocks, scratch=[pltpu.VMEM((sub, rank), BF)], flops=15 * 10**9)
     grad = lax.all_to_all(split.reshape(32, sub, 2 * width), ("x", "z", "y_hi"), 0, 0)
     grad = grad.reshape(4, half, 2 * width)
+    kept = call(term_add_kernel, [like((2, width, outs), F32)], terms[0], far, flops=30 * 10**9)
+    grad, kept, plus, minus = barrier((grad, kept, terms[1], terms[3]))
+    near = [shift(plus, "x", 4, 1), shift(minus, "x", 4, 3)]
     grad_o = swap(grad, "core")
     away = last_call(grad, grad_o, row, 0, BF)
     away = swap(away, "y_lo").astype(F32)
     here = last_call(grad, grad_o, row, 1, F32)
-    term_o, term_a = call(term_sum_kernel, [like((outs, width), F32), like((outs, width))], *terms)
+    term_o, term_a = call(term_sum_kernel, [like((outs, width), F32), like((outs, width))], kept, *near)
     term_a = swap(term_a, "y_lo").astype(F32)
     grad_b = (here + away) * scale
     grad_b, term_o = barrier((grad_b, term_o))

time: 168 us -> 168 us (level)
  blocking collectives: 47.2 us -> 23.9 us
  local copies, waits for them, and re-layouts: 10.6 us -> 22 us
  starting transfers between devices: 20.5 us -> 28.7 us
  waiting for transfers between devices: 51.7 us -> 54.9 us
    all_to_all x1 -> x0, blocking collectives: 23.3 us -> none  [local(): lax.all_to_all(split.reshape(32, sub, 2 * width), ('x', 'z', 'y_hi'), 0, 0)]
    all_to_all x0 -> x1, waiting for transfers between devices: none -> 16.3 us  [local(): lax.all_to_all(split.reshape(32, sub, 2 * width), ('x', 'z', 'y_hi'), 0, 0)]
    ppermute x11, waiting for transfers between devices: 30.6 us -> 18.6 us  [shift(): lax.ppermute(array, axis, [(i, (i + step) % size) for i in range(size)])]
    unnamed x32, local copies, waits for them, and re-layouts: 10.5 us -> 22 us
    all_to_all x0 -> x1, starting transfers between devices: none -> 5.57 us  [local(): lax.all_to_all(split.reshape(32, sub, 2 * width), ('x', 'z', 'y_hi'), 0, 0)]
    ppermute x11, starting transfers between devices: 13.4 us -> 16 us  [shift(): lax.ppermute(array, axis, [(i, (i + step) % size) for i in range(size)])]
    pallas_call x9 -> x10, Pallas kernels: 13.3 us -> 14.8 us  [call(): pl.pallas_call(body, out_shape=outs if len(outs) > 1 else outs[0], in_spe...]
  transfers between devices with their start and end apart: 14 -> 15, of which waited for: 10 -> 9; matrix products, arithmetic and copies ran while one was open for 1% -> 1% of each run, Pallas kernels for 11% -> 12%
where the time goes in v23:
time: 168 us; the launch traced here: 167 us
  waiting for transfers between devices  54.9 us (33%)
  starting transfers between devices  28.7 us (17%)
  blocking collectives  23.9 us (14%)
  local copies, waits for them, and re-layouts  22 us (13%)
  Pallas kernels  20.7 us (12%)
  between operations  14.2 us (8%)
  other arithmetic  2.59 us (2%)
    all_to_all x1, blocking collectives, local(): blocks = lax.all_to_all(mine, ZY, 0, 0)  23.9 us
    unnamed x32, local copies, waits for them, and re-layouts  22 us
    ppermute x11, waiting for transfers between devices, shift(): lax.ppermute(array, axis, [(i, (i + step) % size) for i in range(size)])  18.6 us
    all_to_all x1, waiting for transfers between devices, local(): lax.all_to_all(split.reshape(32, sub, 2 * width), ('x', 'z', 'y_hi'), 0, 0)  16.3 us
    ppermute x11, starting transfers between devices, shift(): lax.ppermute(array, axis, [(i, (i + step) % size) for i in range(size)])  16 us
    pallas_call x10, Pallas kernels, call(): pl.pallas_call(body, out_shape=outs if len(outs) > 1 else outs[0], in_spe...  14.8 us
    all_to_all x1, waiting for transfers between devices, local(): codes = lax.all_to_all(codes, ZY, 0, 0).reshape(rank, half)  11.8 us
    all_to_all x1, waiting for transfers between devices, local(): blocks = lax.all_to_all(partial, ZY, 0, 0)  7.57 us
  transfers between devices with their start and end apart: 15, of which 9 were waited for; matrix products, arithmetic and copies ran while one was open for 1% of the time, Pallas kernels for 12%

profile of v23, /device:TPU:1, one launch (start us, length us, event | category | flops | bytes accessed | tf_op | source)
XLA Modules:
  0.0 167.1 jit_solution(10598429604910396375)
XLA Ops:
  8.7 3.1 %copy-done.4 = bf16[2048,1792]{1,0:T(8,128)(2,1)S(1)} copy-done((bf16[2048,1792]{1,0:T(8,128)(2,1)S(1)}, bf16[2048,1792]{1,0:T(8,128)(2,1)}, u32[]{:S(2)}) %copy-start.4) | copy-done | bytes 7340056
  11.7 2.9 %shard_map.60 = f32[2048,256]{1,0:T(8,128)S(1)} custom-call(bf16[512,1792]{1,0:T(8,128)(2,1)S(1)} %copy-done.5, bf16[2048,1792]{1,0:T(8,128)(2,1)S(1)} %copy-done.4), custom_call_target="tpu_custom_call" | custom-call | flops 1879048192 | bytes 7340032 | tf_op jit(solution)/shard_map/pallas_call | solution.py:69
  16.3 2.9 %shard_map.59 = f32[2048,256]{1,0:T(8,128)S(1)} custom-call(bf16[512,1792]{1,0:T(8,128)(2,1)S(1)} %copy-done.5, bf16[2048,1792]{1,0:T(8,128)(2,1)S(1)} %copy-done.4), custom_call_target="tpu_custom_call" | custom-call | flops 1879048192 | bytes 7340032 | tf_op jit(solution)/shard_map/pallas_call | solution.py:69
  19.2 2.8 %collective-permute-done = f32[2048,256]{1,0:T(8,128)S(1)} collective-permute-done((f32[2048,256]{1,0:T(8,128)S(1)}, f32[2048,256]{1,0:T(8,128)S(1)}, u32[]{:S(2)}, u32[]{:S(2)}) %collective-permute-start) | collective-permute-done | bytes 2097184 | tf_op jit(solution)/shard_map/ppermute | solution.py:24
  22.4 23.9 %all_to_all.20.blocks = bf16[8,256,256]{2,1,0:T(8,128)(2,1)S(1)} all-to-all(bf16[8,256,256]{2,1,0:T(8,128)(2,1)S(1)} %bitcast.18), channel_id=1, replica_groups=mesh['y_lo'=2,'x'=4,'z'=4,'y_hi'=2,'core'=2] {'z','y_hi'}, dimensions={0} | all-to-all | bytes 2097152 | tf_op jit(solution)/shard_map/all_to_all | solution.py:204
  47.3 3.6 %all-to-all-start.1 = ((bf16[8,256,256]{2,1,0:T(8,128)(2,1)}), bf16[8,256,256]{2,1,0:T(8,128)(2,1)S(1)}, u32[]{:S(2)}, u32[]{:S(2)}) async-start(bf16[8,256,256]{2,1,0:T(8,128)(2,1)} %shard_map.61), calls=%async_computation.1 | async-start | bytes 2097152 | tf_op jit(solution)/shard_map/all_to_all | solution.py:206
  51.1 1.9 %collective-permute-start.1 = (bf16[512,256]{1,0:T(8,128)(2,1)S(1)}, bf16[512,256]{1,0:T(8,128)(2,1)S(1)}, u32[]{:S(2)}, u32[]{:S(2)}) collective-permute-start(bf16[512,256]{1,0:T(8,128)(2,1)S(1)} %bitcast.19), channel_id=1, source_target_pairs={{0,1},{1,0},{2,3},{3,2},{4,5},{5,4},{6,7},{7,6},{8,9},{9,8},{10,11... | collective-permute-start | bytes 786440 | tf_op jit(solution)/shard_map/ppermute | solution.py:24
  54.2 11.8 %all-to-all-done.1 = bf16[8,256,256]{2,1,0:T(8,128)(2,1)S(1)} async-done(((bf16[8,256,256]{2,1,0:T(8,128)(2,1)}), bf16[8,256,256]{2,1,0:T(8,128)(2,1)S(1)}, u32[]{:S(2)}, u32[]{:S(2)}) %all-to-all-start.1) | async-done | bytes 1048608 | tf_op jit(solution)/shard_map/all_to_all | solution.py:206
  66.0 5.7 %shard_map.62 = (bf16[256,512]{1,0:T(8,128)(2,1)S(1)}, bf16[256,512]{1,0:T(8,128)(2,1)S(1)}, bf16[8,32,2048]{2,1,0:T(8,128)(2,1)}) custom-call(bf16[2048,256]{1,0:T(8,128)(2,1)S(1)} %bitcast.14, bf16[512,256]{1,0:T(8,128)(2,1)S(1)} %bitcast.17, bf16[512,256]{1,0:T(8,128)(2,1)S(1)} %collective-permute-done.1.far, bf16[512,2048]{1,0:T(8,128)(2,1)} %a0.1, ...), custom_call_target="tpu_custom_call" | custom-call | flops 2147483648 | bytes 7340032 | tf_op jit(solution)/shard_map/pallas_call | solution.py:33
  72.4 3.1 %collective-permute-start.3 = (bf16[2048,256]{1,0:T(8,128)(2,1)S(1)}, bf16[2048,256]{1,0:T(8,128)(2,1)S(1)}, u32[]{:S(2)}, u32[]{:S(2)}) collective-permute-start(bf16[2048,256]{1,0:T(8,128)(2,1)S(1)} %bitcast.15), channel_id=1, source_target_pairs={{0,1},{1,0},{2,3},{3,2},{4,5},{5,4},{6,7},{7,6},{8,9},{9,8},{10,11... | collective-permute-start | bytes 3145736 | tf_op jit(solution)/shard_map/ppermute | solution.py:24
  75.5 3.6 %all-to-all-start.2 = ((bf16[8,32,2048]{2,1,0:T(8,128)(2,1)}), bf16[8,32,2048]{2,1,0:T(8,128)(2,1)S(1)}, u32[]{:S(2)}, u32[]{:S(2)}) async-start(bf16[8,32,2048]{2,1,0:T(8,128)(2,1)} %get-tuple-element.23), calls=%async_computation.2 | async-start | bytes 2097152 | tf_op jit(solution)/shard_map/all_to_all | solution.py:217
  81.7 1.8 %shard_map.63 = (f32[2,256,512]{2,1,0:T(8,128)S(1)}, bf16[2,256,512]{2,1,0:T(8,128)(2,1)S(1)}, bf16[2,256,512]{2,1,0:T(8,128)(2,1)}, bf16[2,256,512]{2,1,0:T(8,128)(2,1)S(1)}) custom-call(bf16[2048,256]{1,0:T(8,128)(2,1)S(1)} %bitcast.16, bf16[256,512]{1,0:T(8,128)(2,1)S(1)} %copy-done.13, bf16[2048,256]{1,0:T(8,128)(2,1)S(1)} %collective-permute-done.3.codes_o, ...), custom_call_target="tpu_custom_call" | custom-call | flops 1073741824 | bytes 5242880 | tf_op jit(solution)/shard_map/pallas_call | solution.py:33
  86.1 2.7 %collective-permute-start.5 = (bf16[2,256,512]{2,1,0:T(8,128)(2,1)}, bf16[2,256,512]{2,1,0:T(8,128)(2,1)S(1)}, u32[]{:S(2)}, u32[]{:S(2)}) collective-permute-start(bf16[2,256,512]{2,1,0:T(8,128)(2,1)} %get-tuple-element.30), channel_id=1, source_target_pairs={{0,32},{16,48},{32,0},{48,16},{1,33},{17,49},{33,1},{49,17},{2,34}... | collective-permute-start | bytes 1572872 | tf_op jit(solution)/shard_map/ppermute | solution.py:24
  88.8 7.6 %all-to-all-done.2.blocks = bf16[8,32,2048]{2,1,0:T(8,128)(2,1)S(1)} async-done(((bf16[8,32,2048]{2,1,0:T(8,128)(2,1)}), bf16[8,32,2048]{2,1,0:T(8,128)(2,1)S(1)}, u32[]{:S(2)}, u32[]{:S(2)}) %all-to-all-start.2) | async-done | bytes 1048608 | tf_op jit(solution)/shard_map/all_to_all | solution.py:217
  97.7 5.6 %all-to-all-start.3 = ((bf16[32,32,512]{2,1,0:T(8,128)(2,1)}), bf16[32,32,512]{2,1,0:T(8,128)(2,1)S(1)}, u32[]{:S(2)}, u32[]{:S(2)}) async-start(bf16[32,32,512]{2,1,0:T(8,128)(2,1)} %bitcast.5), calls=%async_computation.3 | async-start | bytes 2097152 | tf_op jit(solution)/shard_map/all_to_all | solution.py:232
  104.6 16.3 %all-to-all-done.3 = bf16[32,32,512]{2,1,0:T(8,128)(2,1)S(1)} async-done(((bf16[32,32,512]{2,1,0:T(8,128)(2,1)}), bf16[32,32,512]{2,1,0:T(8,128)(2,1)S(1)}, u32[]{:S(2)}, u32[]{:S(2)}) %all-to-all-start.3) | async-done | bytes 1048608 | tf_op jit(solution)/shard_map/all_to_all | solution.py:232
  120.9 2.3 %collective-permute-start.6 = (bf16[4,256,512]{2,1,0:T(8,128)(2,1)S(1)}, bf16[4,256,512]{2,1,0:T(8,128)(2,1)S(1)}, u32[]{:S(2)}, u32[]{:S(2)}) collective-permute-start(bf16[4,256,512]{2,1,0:T(8,128)(2,1)S(1)} %bitcast.11), channel_id=1, source_target_pairs={{0,1},{1,0},{2,3},{3,2},{4,5},{5,4},{6,7},{7,6},{8,9},{9,8},{10,11... | collective-permute-start | bytes 3145736 | tf_op jit(solution)/shard_map/ppermute | solution.py:24
  123.2 3.1 %copy-done = bf16[2048,1792]{1,0:T(8,128)(2,1)S(1)} copy-done((bf16[2048,1792]{1,0:T(8,128)(2,1)S(1)}, bf16[2048,1792]{1,0:T(8,128)(2,1)}, u32[]{:S(2)}) %copy-start) | copy-done | bytes 7340056
  127.4 3.1 %copy-done.1 = bf16[2048,1792]{1,0:T(8,128)(2,1)S(1)} copy-done((bf16[2048,1792]{1,0:T(8,128)(2,1)S(1)}, bf16[2048,1792]{1,0:T(8,128)(2,1)}, u32[]{:S(2)}) %copy-start.1) | copy-done | bytes 7340056
  132.2 2.7 %collective-permute-start.9 = (bf16[2,256,512]{2,1,0:T(8,128)(2,1)S(1)}, bf16[2,256,512]{2,1,0:T(8,128)(2,1)S(1)}, u32[]{:S(2)}, u32[]{:S(2)}) collective-permute-start(bf16[2,256,512]{2,1,0:T(8,128)(2,1)S(1)} %copy-done.7), channel_id=1, source_target_pairs={{0,48},{16,0},{32,16},{48,32},{1,49},{17,1},{33,17},{49,33},{2,50}... | collective-permute-start | bytes 1572872 | tf_op jit(solution)/shard_map/ppermute | solution.py:24
  134.9 3.1 %copy-done.2 = bf16[2048,1792]{1,0:T(8,128)(2,1)S(1)} copy-done((bf16[2048,1792]{1,0:T(8,128)(2,1)S(1)}, bf16[2048,1792]{1,0:T(8,128)(2,1)}, u32[]{:S(2)}) %copy-start.2) | copy-done | bytes 7340056
  139.1 7.5 %collective-permute-done.8.r1 = bf16[2,256,512]{2,1,0:T(8,128)(2,1)S(1)} collective-permute-done((bf16[2,256,512]{2,1,0:T(8,128)(2,1)S(1)}, bf16[2,256,512]{2,1,0:T(8,128)(2,1)S(1)}, u32[]{:S(2)}, u32[]{:S(2)}) %collective-permute-start.8) | collective-permute-done | bytes 524320 | tf_op jit(solution)/shard_map/ppermute | solution.py:24
  148.1 3.1 %copy-done.3 = bf16[2048,1792]{1,0:T(8,128)(2,1)S(1)} copy-done((bf16[2048,1792]{1,0:T(8,128)(2,1)S(1)}, bf16[2048,1792]{1,0:T(8,128)(2,1)}, u32[]{:S(2)}) %copy-start.3) | copy-done | bytes 7340056
  155.2 4.2 %collective-permute-done.10 = bf16[512,256]{1,0:T(8,128)(2,1)S(1)} collective-permute-done((bf16[512,256]{1,0:T(8,128)(2,1)S(1)}, bf16[512,256]{1,0:T(8,128)(2,1)S(1)}, u32[]{:S(2)}, u32[]{:S(2)}) %collective-permute-start.10) | collective-permute-done | bytes 262176 | tf_op jit(solution)/shard_map/ppermute | solution.py:24
  (56 shorter events, 24.6 us)
Async XLA Ops:
  7.2 1.5 copy-start.5
  7.2 89.2 %all-gather.3.cloned.1.call-start = ((), (), s32[]{:S(2)}) async-start(), calls=%async_computation.4 | async-start | bytes 9175040 | tf_op jit(solution)/shard_map/all_gather | solution.py:196
  8.7 3.1 %copy-start.4 = (bf16[2048,1792]{1,0:T(8,128)(2,1)S(1)}, bf16[2048,1792]{1,0:T(8,128)(2,1)}, u32[]{:S(2)}) copy-start(bf16[2048,1792]{1,0:T(8,128)(2,1)} %b.3) | copy-start | bytes 22020100
  14.7 7.4 %collective-permute-start = (f32[2048,256]{1,0:T(8,128)S(1)}, f32[2048,256]{1,0:T(8,128)S(1)}, u32[]{:S(2)}, u32[]{:S(2)}) collective-permute-start(f32[2048,256]{1,0:T(8,128)S(1)} %shard_map.60), channel_id=1, source_target_pairs={{0,1},{1,0},{2,3},{3,2},{4,5},{5,4},{6,7},{7,6},{8,9},{9,8},{10,11... | collective-permute-start | bytes 6291464 | tf_op jit(solution)/shard_map/ppermute | solution.py:24
  16.2 38.0 %collective-permute-start.2 = (bf16[512,2048]{1,0:T(8,128)(2,1)}, bf16[512,2048]{1,0:T(8,128)(2,1)}, u32[]{:S(2)}, u32[]{:S(2)}) collective-permute-start(bf16[512,2048]{1,0:T(8,128)(2,1)} %a0.1), channel_id=1, source_target_pairs={{0,1},{1,0},{2,3},{3,2},{4,5},{5,4},{6,7},{7,6},{8,9},{9,8},{10,11... | collective-permute-start | bytes 6291464 | tf_op jit(solution)/shard_map/ppermute | solution.py:24
  46.2 4.7 %copy-start.14 = (bf16[512,512]{1,0:T(8,128)(2,1)S(1)}, bf16[512,512]{1,0:T(8,128)(2,1)}, u32[]{:S(2)}) copy-start(bf16[512,512]{1,0:T(8,128)(2,1)} %param.5) | copy-start | bytes 1572868
  47.3 18.6 %all-to-all-start.1 = ((bf16[8,256,256]{2,1,0:T(8,128)(2,1)}), bf16[8,256,256]{2,1,0:T(8,128)(2,1)S(1)}, u32[]{:S(2)}, u32[]{:S(2)}) async-start(bf16[8,256,256]{2,1,0:T(8,128)(2,1)} %shard_map.61), calls=%async_computation.1 | async-start | bytes 2097152 | tf_op jit(solution)/shard_map/all_to_all | solution.py:206
  51.1 3.1 %collective-permute-start.1 = (bf16[512,256]{1,0:T(8,128)(2,1)S(1)}, bf16[512,256]{1,0:T(8,128)(2,1)S(1)}, u32[]{:S(2)}, u32[]{:S(2)}) collective-permute-start(bf16[512,256]{1,0:T(8,128)(2,1)S(1)} %bitcast.19), channel_id=1, source_target_pairs={{0,1},{1,0},{2,3},{3,2},{4,5},{5,4},{6,7},{7,6},{8,9},{9,8},{10,11... | collective-permute-start | bytes 786440 | tf_op jit(solution)/shard_map/ppermute | solution.py:24
  72.4 8.3 %collective-permute-start.3 = (bf16[2048,256]{1,0:T(8,128)(2,1)S(1)}, bf16[2048,256]{1,0:T(8,128)(2,1)S(1)}, u32[]{:S(2)}, u32[]{:S(2)}) collective-permute-start(bf16[2048,256]{1,0:T(8,128)(2,1)S(1)} %bitcast.15), channel_id=1, source_target_pairs={{0,1},{1,0},{2,3},{3,2},{4,5},{5,4},{6,7},{7,6},{8,9},{9,8},{10,11... | collective-permute-start | bytes 3145736 | tf_op jit(solution)/shard_map/ppermute | solution.py:24
  75.5 20.9 %all-to-all-start.2 = ((bf16[8,32,2048]{2,1,0:T(8,128)(2,1)}), bf16[8,32,2048]{2,1,0:T(8,128)(2,1)S(1)}, u32[]{:S(2)}, u32[]{:S(2)}) async-start(bf16[8,32,2048]{2,1,0:T(8,128)(2,1)} %get-tuple-element.23), calls=%async_computation.2 | async-start | bytes 2097152 | tf_op jit(solution)/shard_map/all_to_all | solution.py:217
  79.1 1.6 collective-permute-start.4
  86.1 17.1 %collective-permute-start.5 = (bf16[2,256,512]{2,1,0:T(8,128)(2,1)}, bf16[2,256,512]{2,1,0:T(8,128)(2,1)S(1)}, u32[]{:S(2)}, u32[]{:S(2)}) collective-permute-start(bf16[2,256,512]{2,1,0:T(8,128)(2,1)} %get-tuple-element.30), channel_id=1, source_target_pairs={{0,32},{16,48},{32,0},{48,16},{1,33},{17,49},{33,1},{49,17},{2,34}... | collective-permute-start | bytes 1572872 | tf_op jit(solution)/shard_map/ppermute | solution.py:24
  97.7 23.2 %all-to-all-start.3 = ((bf16[32,32,512]{2,1,0:T(8,128)(2,1)}), bf16[32,32,512]{2,1,0:T(8,128)(2,1)S(1)}, u32[]{:S(2)}, u32[]{:S(2)}) async-start(bf16[32,32,512]{2,1,0:T(8,128)(2,1)} %bitcast.5), calls=%async_computation.3 | async-start | bytes 2097152 | tf_op jit(solution)/shard_map/all_to_all | solution.py:232
  120.9 6.6 %collective-permute-start.6 = (bf16[4,256,512]{2,1,0:T(8,128)(2,1)S(1)}, bf16[4,256,512]{2,1,0:T(8,128)(2,1)S(1)}, u32[]{:S(2)}, u32[]{:S(2)}) collective-permute-start(bf16[4,256,512]{2,1,0:T(8,128)(2,1)S(1)} %bitcast.11), channel_id=1, source_target_pairs={{0,1},{1,0},{2,3},{3,2},{4,5},{5,4},{6,7},{7,6},{8,9},{9,8},{10,11... | collective-permute-start | bytes 3145736 | tf_op jit(solution)/shard_map/ppermute | solution.py:24
  123.2 3.1 %copy-start = (bf16[2048,1792]{1,0:T(8,128)(2,1)S(1)}, bf16[2048,1792]{1,0:T(8,128)(2,1)}, u32[]{:S(2)}) copy-start(bf16[2048,1792]{1,0:T(8,128)(2,1)} %all-gather.3.cloned.1.call-done) | copy-start | bytes 22020100
  127.4 3.1 %copy-start.1 = (bf16[2048,1792]{1,0:T(8,128)(2,1)S(1)}, bf16[2048,1792]{1,0:T(8,128)(2,1)}, u32[]{:S(2)}) copy-start(bf16[2048,1792]{1,0:T(8,128)(2,1)} %all-gather.3.cloned.1.call-done) | copy-start | bytes 22020100
  130.5 1.7 %copy-start.9 = (bf16[2,256,512]{2,1,0:T(8,128)(2,1)S(1)}, bf16[2,256,512]{2,1,0:T(8,128)(2,1)}, u32[]{:S(2)}) copy-start(bf16[2,256,512]{2,1,0:T(8,128)(2,1)} %copy-done.8) | copy-start | bytes 1572868
  130.5 1.7 %copy-start.7 = (bf16[2,256,512]{2,1,0:T(8,128)(2,1)S(1)}, bf16[2,256,512]{2,1,0:T(8,128)(2,1)}, u32[]{:S(2)}) copy-start(bf16[2,256,512]{2,1,0:T(8,128)(2,1)} %copy-done.6) | copy-start | bytes 1572868
  131.7 22.1 %collective-permute-start.7 = (bf16[256,1792]{1,0:T(8,128)(2,1)S(1)}, bf16[256,1792]{1,0:T(8,128)(2,1)S(1)}, u32[]{:S(2)}, u32[]{:S(2)}) collective-permute-start(bf16[256,1792]{1,0:T(8,128)(2,1)S(1)} %shard_map.69), channel_id=1, source_target_pairs={{0,64},{64,0},{1,65},{65,1},{2,66},{66,2},{3,67},{67,3},{4,68},{68... | collective-permute-start | bytes 2752520 | tf_op jit(solution)/shard_map/ppermute | solution.py:24
  132.2 14.4 %collective-permute-start.8 = (bf16[2,256,512]{2,1,0:T(8,128)(2,1)S(1)}, bf16[2,256,512]{2,1,0:T(8,128)(2,1)S(1)}, u32[]{:S(2)}, u32[]{:S(2)}) collective-permute-start(bf16[2,256,512]{2,1,0:T(8,128)(2,1)S(1)} %copy-done.9), channel_id=1, source_target_pairs={{0,16},{16,32},{32,48},{48,0},{1,17},{17,33},{33,49},{49,1},{2,18}... | collective-permute-start | bytes 1572872 | tf_op jit(solution)/shard_map/ppermute | solution.py:24
  132.2 14.4 %collective-permute-start.9 = (bf16[2,256,512]{2,1,0:T(8,128)(2,1)S(1)}, bf16[2,256,512]{2,1,0:T(8,128)(2,1)S(1)}, u32[]{:S(2)}, u32[]{:S(2)}) collective-permute-start(bf16[2,256,512]{2,1,0:T(8,128)(2,1)S(1)} %copy-done.7), channel_id=1, source_target_pairs={{0,48},{16,0},{32,16},{48,32},{1,49},{17,1},{33,17},{49,33},{2,50}... | collective-permute-start | bytes 1572872 | tf_op jit(solution)/shard_map/ppermute | solution.py:24
  134.9 3.1 %copy-start.2 = (bf16[2048,1792]{1,0:T(8,128)(2,1)S(1)}, bf16[2048,1792]{1,0:T(8,128)(2,1)}, u32[]{:S(2)}) copy-start(bf16[2048,1792]{1,0:T(8,128)(2,1)} %all-gather.3.cloned.1.call-done) | copy-start | bytes 22020100
  146.9 12.4 %collective-permute-start.10 = (bf16[512,256]{1,0:T(8,128)(2,1)S(1)}, bf16[512,256]{1,0:T(8,128)(2,1)S(1)}, u32[]{:S(2)}, u32[]{:S(2)}) collective-permute-start(bf16[512,256]{1,0:T(8,128)(2,1)S(1)} %get-tuple-element.40), channel_id=1, source_target_pairs={{0,64},{64,0},{1,65},{65,1},{2,66},{66,2},{3,67},{67,3},{4,68},{68... | collective-permute-start | bytes 786440 | tf_op jit(solution)/shard_map/ppermute | solution.py:24
  148.1 3.1 %copy-start.3 = (bf16[2048,1792]{1,0:T(8,128)(2,1)S(1)}, bf16[2048,1792]{1,0:T(8,128)(2,1)}, u32[]{:S(2)}) copy-start(bf16[2048,1792]{1,0:T(8,128)(2,1)} %all-gather.3.cloned.1.call-done) | copy-start | bytes 22020100
  (6 other events, 5.6 us)
Sparse Core Ops, SparseCore 0:
  9.7 77.5 all-gather.2

commit v24 on v23

--- a/solution.py
+++ b/solution.py
@@ -231,7 +231,7 @@
     split = call(spread_kernel, [like((4, 8, sub, 2 * width))], blocks, scratch=[pltpu.VMEM((sub, rank), BF)], flops=15 * 10**9)
     grad = lax.all_to_all(split.reshape(32, sub, 2 * width), ("x", "z", "y_hi"), 0, 0)
     grad = grad.reshape(4, half, 2 * width)
-    kept = call(term_add_kernel, [like((2, width, outs), F32)], terms[0], far, flops=30 * 10**9)
+    kept = call(term_add_kernel, [like((2, width, outs), F32)], terms[0], far, flops=7 * 10**9)
     grad, kept, plus, minus = barrier((grad, kept, terms[1], terms[3]))
     near = [shift(plus, "x", 4, 1), shift(minus, "x", 4, 3)]
     grad_o = swap(grad, "core")

time: 168 us -> 168 us (level)
  waiting for transfers between devices: 54.9 us -> 58 us
  local copies, waits for them, and re-layouts: 22 us -> 19 us
    unnamed x32, local copies, waits for them, and re-layouts: 22 us -> 18.9 us
    ppermute x11, waiting for transfers between devices: 18.6 us -> 21.7 us  [shift(): lax.ppermute(array, axis, [(i, (i + step) % size) for i in range(size)])]
where the time goes in v24:
time: 168 us; the launch traced here: 167 us
  waiting for transfers between devices  58 us (35%)
  starting transfers between devices  28.7 us (17%)
  blocking collectives  23.9 us (14%)
  Pallas kernels  20.7 us (12%)
  local copies, waits for them, and re-layouts  19 us (11%)
  between operations  14.2 us (8%)
  other arithmetic  2.6 us (2%)
    all_to_all x1, blocking collectives, local(): blocks = lax.all_to_all(mine, ZY, 0, 0)  23.9 us
    ppermute x11, waiting for transfers between devices, shift(): lax.ppermute(array, axis, [(i, (i + step) % size) for i in range(size)])  21.7 us
    unnamed x32, local copies, waits for them, and re-layouts  18.9 us
    all_to_all x1, waiting for transfers between devices, local(): lax.all_to_all(split.reshape(32, sub, 2 * width), ('x', 'z', 'y_hi'), 0, 0)  16.3 us
    ppermute x11, starting transfers between devices, shift(): lax.ppermute(array, axis, [(i, (i + step) % size) for i in range(size)])  16 us
    pallas_call x10, Pallas kernels, call(): pl.pallas_call(body, out_shape=outs if len(outs) > 1 else outs[0], in_spe...  14.8 us
    all_to_all x1, waiting for transfers between devices, local(): codes = lax.all_to_all(codes, ZY, 0, 0).reshape(rank, half)  11.8 us
    all_to_all x1, waiting for transfers between devices, local(): blocks = lax.all_to_all(partial, ZY, 0, 0)  7.57 us
  transfers between devices with their start and end apart: 15, of which 9 were waited for; matrix products, arithmetic and copies ran while one was open for 1% of the time, Pallas kernels for 12%

profile of v24, /device:TPU:1, one launch (start us, length us, event | category | flops | bytes accessed | tf_op | source)
XLA Modules:
  0.0 167.1 jit_solution(12149466563452385358)
XLA Ops:
  8.7 3.1 %copy-done.4 = bf16[2048,1792]{1,0:T(8,128)(2,1)S(1)} copy-done((bf16[2048,1792]{1,0:T(8,128)(2,1)S(1)}, bf16[2048,1792]{1,0:T(8,128)(2,1)}, u32[]{:S(2)}) %copy-start.4) | copy-done | bytes 7340056
  11.7 2.9 %shard_map.60 = f32[2048,256]{1,0:T(8,128)S(1)} custom-call(bf16[512,1792]{1,0:T(8,128)(2,1)S(1)} %copy-done.5, bf16[2048,1792]{1,0:T(8,128)(2,1)S(1)} %copy-done.4), custom_call_target="tpu_custom_call" | custom-call | flops 1879048192 | bytes 7340032 | tf_op jit(solution)/shard_map/pallas_call | solution.py:69
  16.3 2.9 %shard_map.59 = f32[2048,256]{1,0:T(8,128)S(1)} custom-call(bf16[512,1792]{1,0:T(8,128)(2,1)S(1)} %copy-done.5, bf16[2048,1792]{1,0:T(8,128)(2,1)S(1)} %copy-done.4), custom_call_target="tpu_custom_call" | custom-call | flops 1879048192 | bytes 7340032 | tf_op jit(solution)/shard_map/pallas_call | solution.py:69
  19.2 2.8 %collective-permute-done = f32[2048,256]{1,0:T(8,128)S(1)} collective-permute-done((f32[2048,256]{1,0:T(8,128)S(1)}, f32[2048,256]{1,0:T(8,128)S(1)}, u32[]{:S(2)}, u32[]{:S(2)}) %collective-permute-start) | collective-permute-done | bytes 2097184 | tf_op jit(solution)/shard_map/ppermute | solution.py:24
  22.4 23.9 %all_to_all.20.blocks = bf16[8,256,256]{2,1,0:T(8,128)(2,1)S(1)} all-to-all(bf16[8,256,256]{2,1,0:T(8,128)(2,1)S(1)} %bitcast.18), channel_id=1, replica_groups=mesh['y_lo'=2,'x'=4,'z'=4,'y_hi'=2,'core'=2] {'z','y_hi'}, dimensions={0} | all-to-all | bytes 2097152 | tf_op jit(solution)/shard_map/all_to_all | solution.py:204
  47.3 3.6 %all-to-all-start.1 = ((bf16[8,256,256]{2,1,0:T(8,128)(2,1)}), bf16[8,256,256]{2,1,0:T(8,128)(2,1)S(1)}, u32[]{:S(2)}, u32[]{:S(2)}) async-start(bf16[8,256,256]{2,1,0:T(8,128)(2,1)} %shard_map.61), calls=%async_computation.1 | async-start | bytes 2097152 | tf_op jit(solution)/shard_map/all_to_all | solution.py:206
  51.1 1.9 %collective-permute-start.1 = (bf16[512,256]{1,0:T(8,128)(2,1)S(1)}, bf16[512,256]{1,0:T(8,128)(2,1)S(1)}, u32[]{:S(2)}, u32[]{:S(2)}) collective-permute-start(bf16[512,256]{1,0:T(8,128)(2,1)S(1)} %bitcast.19), channel_id=1, source_target_pairs={{0,1},{1,0},{2,3},{3,2},{4,5},{5,4},{6,7},{7,6},{8,9},{9,8},{10,11... | collective-permute-start | bytes 786440 | tf_op jit(solution)/shard_map/ppermute | solution.py:24
  54.2 11.8 %all-to-all-done.1 = bf16[8,256,256]{2,1,0:T(8,128)(2,1)S(1)} async-done(((bf16[8,256,256]{2,1,0:T(8,128)(2,1)}), bf16[8,256,256]{2,1,0:T(8,128)(2,1)S(1)}, u32[]{:S(2)}, u32[]{:S(2)}) %all-to-all-start.1) | async-done | bytes 1048608 | tf_op jit(solution)/shard_map/all_to_all | solution.py:206
  66.0 5.7 %shard_map.62 = (bf16[256,512]{1,0:T(8,128)(2,1)S(1)}, bf16[256,512]{1,0:T(8,128)(2,1)S(1)}, bf16[8,32,2048]{2,1,0:T(8,128)(2,1)}) custom-call(bf16[2048,256]{1,0:T(8,128)(2,1)S(1)} %bitcast.14, bf16[512,256]{1,0:T(8,128)(2,1)S(1)} %bitcast.17, bf16[512,256]{1,0:T(8,128)(2,1)S(1)} %collective-permute-done.1.far, bf16[512,2048]{1,0:T(8,128)(2,1)} %a0.1, ...), custom_call_target="tpu_custom_call" | custom-call | flops 2147483648 | bytes 7340032 | tf_op jit(solution)/shard_map/pallas_call | solution.py:33
  72.4 3.1 %collective-permute-start.3 = (bf16[2048,256]{1,0:T(8,128)(2,1)S(1)}, bf16[2048,256]{1,0:T(8,128)(2,1)S(1)}, u32[]{:S(2)}, u32[]{:S(2)}) collective-permute-start(bf16[2048,256]{1,0:T(8,128)(2,1)S(1)} %bitcast.15), channel_id=1, source_target_pairs={{0,1},{1,0},{2,3},{3,2},{4,5},{5,4},{6,7},{7,6},{8,9},{9,8},{10,11... | collective-permute-start | bytes 3145736 | tf_op jit(solution)/shard_map/ppermute | solution.py:24
  75.5 3.6 %all-to-all-start.2 = ((bf16[8,32,2048]{2,1,0:T(8,128)(2,1)}), bf16[8,32,2048]{2,1,0:T(8,128)(2,1)S(1)}, u32[]{:S(2)}, u32[]{:S(2)}) async-start(bf16[8,32,2048]{2,1,0:T(8,128)(2,1)} %get-tuple-element.23), calls=%async_computation.2 | async-start | bytes 2097152 | tf_op jit(solution)/shard_map/all_to_all | solution.py:217
  81.7 1.8 %shard_map.63 = (f32[2,256,512]{2,1,0:T(8,128)S(1)}, bf16[2,256,512]{2,1,0:T(8,128)(2,1)S(1)}, bf16[2,256,512]{2,1,0:T(8,128)(2,1)}, bf16[2,256,512]{2,1,0:T(8,128)(2,1)S(1)}) custom-call(bf16[2048,256]{1,0:T(8,128)(2,1)S(1)} %bitcast.16, bf16[256,512]{1,0:T(8,128)(2,1)S(1)} %copy-done.13, bf16[2048,256]{1,0:T(8,128)(2,1)S(1)} %collective-permute-done.3.codes_o, ...), custom_call_target="tpu_custom_call" | custom-call | flops 1073741824 | bytes 5242880 | tf_op jit(solution)/shard_map/pallas_call | solution.py:33
  86.1 2.7 %collective-permute-start.5 = (bf16[2,256,512]{2,1,0:T(8,128)(2,1)}, bf16[2,256,512]{2,1,0:T(8,128)(2,1)S(1)}, u32[]{:S(2)}, u32[]{:S(2)}) collective-permute-start(bf16[2,256,512]{2,1,0:T(8,128)(2,1)} %get-tuple-element.30), channel_id=1, source_target_pairs={{0,32},{16,48},{32,0},{48,16},{1,33},{17,49},{33,1},{49,17},{2,34}... | collective-permute-start | bytes 1572872 | tf_op jit(solution)/shard_map/ppermute | solution.py:24
  88.8 7.6 %all-to-all-done.2.blocks = bf16[8,32,2048]{2,1,0:T(8,128)(2,1)S(1)} async-done(((bf16[8,32,2048]{2,1,0:T(8,128)(2,1)}), bf16[8,32,2048]{2,1,0:T(8,128)(2,1)S(1)}, u32[]{:S(2)}, u32[]{:S(2)}) %all-to-all-start.2) | async-done | bytes 1048608 | tf_op jit(solution)/shard_map/all_to_all | solution.py:217
  97.7 5.6 %all-to-all-start.3 = ((bf16[32,32,512]{2,1,0:T(8,128)(2,1)}), bf16[32,32,512]{2,1,0:T(8,128)(2,1)S(1)}, u32[]{:S(2)}, u32[]{:S(2)}) async-start(bf16[32,32,512]{2,1,0:T(8,128)(2,1)} %bitcast.5), calls=%async_computation.3 | async-start | bytes 2097152 | tf_op jit(solution)/shard_map/all_to_all | solution.py:232
  104.6 16.3 %all-to-all-done.3 = bf16[32,32,512]{2,1,0:T(8,128)(2,1)S(1)} async-done(((bf16[32,32,512]{2,1,0:T(8,128)(2,1)}), bf16[32,32,512]{2,1,0:T(8,128)(2,1)S(1)}, u32[]{:S(2)}, u32[]{:S(2)}) %all-to-all-start.3) | async-done | bytes 1048608 | tf_op jit(solution)/shard_map/all_to_all | solution.py:232
  120.9 2.3 %collective-permute-start.6 = (bf16[4,256,512]{2,1,0:T(8,128)(2,1)S(1)}, bf16[4,256,512]{2,1,0:T(8,128)(2,1)S(1)}, u32[]{:S(2)}, u32[]{:S(2)}) collective-permute-start(bf16[4,256,512]{2,1,0:T(8,128)(2,1)S(1)} %bitcast.11), channel_id=1, source_target_pairs={{0,1},{1,0},{2,3},{3,2},{4,5},{5,4},{6,7},{7,6},{8,9},{9,8},{10,11... | collective-permute-start | bytes 3145736 | tf_op jit(solution)/shard_map/ppermute | solution.py:24
  123.2 3.1 %copy-done = bf16[2048,1792]{1,0:T(8,128)(2,1)S(1)} copy-done((bf16[2048,1792]{1,0:T(8,128)(2,1)S(1)}, bf16[2048,1792]{1,0:T(8,128)(2,1)}, u32[]{:S(2)}) %copy-start) | copy-done | bytes 7340056
  127.4 3.1 %copy-done.1 = bf16[2048,1792]{1,0:T(8,128)(2,1)S(1)} copy-done((bf16[2048,1792]{1,0:T(8,128)(2,1)S(1)}, bf16[2048,1792]{1,0:T(8,128)(2,1)}, u32[]{:S(2)}) %copy-start.1) | copy-done | bytes 7340056
  132.2 2.7 %collective-permute-start.9 = (bf16[2,256,512]{2,1,0:T(8,128)(2,1)S(1)}, bf16[2,256,512]{2,1,0:T(8,128)(2,1)S(1)}, u32[]{:S(2)}, u32[]{:S(2)}) collective-permute-start(bf16[2,256,512]{2,1,0:T(8,128)(2,1)S(1)} %copy-done.7), channel_id=1, source_target_pairs={{0,48},{16,0},{32,16},{48,32},{1,49},{17,1},{33,17},{49,33},{2,50}... | collective-permute-start | bytes 1572872 | tf_op jit(solution)/shard_map/ppermute | solution.py:24
  134.9 3.1 %copy-done.2 = bf16[2048,1792]{1,0:T(8,128)(2,1)S(1)} copy-done((bf16[2048,1792]{1,0:T(8,128)(2,1)S(1)}, bf16[2048,1792]{1,0:T(8,128)(2,1)}, u32[]{:S(2)}) %copy-start.2) | copy-done | bytes 7340056
  139.1 7.5 %collective-permute-done.8.r1 = bf16[2,256,512]{2,1,0:T(8,128)(2,1)S(1)} collective-permute-done((bf16[2,256,512]{2,1,0:T(8,128)(2,1)S(1)}, bf16[2,256,512]{2,1,0:T(8,128)(2,1)S(1)}, u32[]{:S(2)}, u32[]{:S(2)}) %collective-permute-start.8) | collective-permute-done | bytes 524320 | tf_op jit(solution)/shard_map/ppermute | solution.py:24
  149.2 4.5 %collective-permute-done.7 = bf16[256,1792]{1,0:T(8,128)(2,1)S(1)} collective-permute-done((bf16[256,1792]{1,0:T(8,128)(2,1)S(1)}, bf16[256,1792]{1,0:T(8,128)(2,1)S(1)}, u32[]{:S(2)}, u32[]{:S(2)}) %collective-permute-start.7) | collective-permute-done | bytes 917536 | tf_op jit(solution)/shard_map/ppermute | solution.py:24
  155.2 4.2 %collective-permute-done.10 = bf16[512,256]{1,0:T(8,128)(2,1)S(1)} collective-permute-done((bf16[512,256]{1,0:T(8,128)(2,1)S(1)}, bf16[512,256]{1,0:T(8,128)(2,1)S(1)}, u32[]{:S(2)}, u32[]{:S(2)}) %collective-permute-start.10) | collective-permute-done | bytes 262176 | tf_op jit(solution)/shard_map/ppermute | solution.py:24
  (56 shorter events, 23.2 us)
Async XLA Ops:
  7.2 1.5 copy-start.5
  7.2 89.2 %all-gather.3.cloned.1.call-start = ((), (), s32[]{:S(2)}) async-start(), calls=%async_computation.4 | async-start | bytes 9175040 | tf_op jit(solution)/shard_map/all_gather | solution.py:196
  8.7 3.1 %copy-start.4 = (bf16[2048,1792]{1,0:T(8,128)(2,1)S(1)}, bf16[2048,1792]{1,0:T(8,128)(2,1)}, u32[]{:S(2)}) copy-start(bf16[2048,1792]{1,0:T(8,128)(2,1)} %b.3) | copy-start | bytes 22020100
  14.7 7.4 %collective-permute-start = (f32[2048,256]{1,0:T(8,128)S(1)}, f32[2048,256]{1,0:T(8,128)S(1)}, u32[]{:S(2)}, u32[]{:S(2)}) collective-permute-start(f32[2048,256]{1,0:T(8,128)S(1)} %shard_map.60), channel_id=1, source_target_pairs={{0,1},{1,0},{2,3},{3,2},{4,5},{5,4},{6,7},{7,6},{8,9},{9,8},{10,11... | collective-permute-start | bytes 6291464 | tf_op jit(solution)/shard_map/ppermute | solution.py:24
  16.2 38.0 %collective-permute-start.2 = (bf16[512,2048]{1,0:T(8,128)(2,1)}, bf16[512,2048]{1,0:T(8,128)(2,1)}, u32[]{:S(2)}, u32[]{:S(2)}) collective-permute-start(bf16[512,2048]{1,0:T(8,128)(2,1)} %a0.1), channel_id=1, source_target_pairs={{0,1},{1,0},{2,3},{3,2},{4,5},{5,4},{6,7},{7,6},{8,9},{9,8},{10,11... | collective-permute-start | bytes 6291464 | tf_op jit(solution)/shard_map/ppermute | solution.py:24
  46.2 4.7 %copy-start.14 = (bf16[512,512]{1,0:T(8,128)(2,1)S(1)}, bf16[512,512]{1,0:T(8,128)(2,1)}, u32[]{:S(2)}) copy-start(bf16[512,512]{1,0:T(8,128)(2,1)} %param.5) | copy-start | bytes 1572868
  47.3 18.6 %all-to-all-start.1 = ((bf16[8,256,256]{2,1,0:T(8,128)(2,1)}), bf16[8,256,256]{2,1,0:T(8,128)(2,1)S(1)}, u32[]{:S(2)}, u32[]{:S(2)}) async-start(bf16[8,256,256]{2,1,0:T(8,128)(2,1)} %shard_map.61), calls=%async_computation.1 | async-start | bytes 2097152 | tf_op jit(solution)/shard_map/all_to_all | solution.py:206
  51.1 3.1 %collective-permute-start.1 = (bf16[512,256]{1,0:T(8,128)(2,1)S(1)}, bf16[512,256]{1,0:T(8,128)(2,1)S(1)}, u32[]{:S(2)}, u32[]{:S(2)}) collective-permute-start(bf16[512,256]{1,0:T(8,128)(2,1)S(1)} %bitcast.19), channel_id=1, source_target_pairs={{0,1},{1,0},{2,3},{3,2},{4,5},{5,4},{6,7},{7,6},{8,9},{9,8},{10,11... | collective-permute-start | bytes 786440 | tf_op jit(solution)/shard_map/ppermute | solution.py:24
  72.4 8.3 %collective-permute-start.3 = (bf16[2048,256]{1,0:T(8,128)(2,1)S(1)}, bf16[2048,256]{1,0:T(8,128)(2,1)S(1)}, u32[]{:S(2)}, u32[]{:S(2)}) collective-permute-start(bf16[2048,256]{1,0:T(8,128)(2,1)S(1)} %bitcast.15), channel_id=1, source_target_pairs={{0,1},{1,0},{2,3},{3,2},{4,5},{5,4},{6,7},{7,6},{8,9},{9,8},{10,11... | collective-permute-start | bytes 3145736 | tf_op jit(solution)/shard_map/ppermute | solution.py:24
  75.5 20.9 %all-to-all-start.2 = ((bf16[8,32,2048]{2,1,0:T(8,128)(2,1)}), bf16[8,32,2048]{2,1,0:T(8,128)(2,1)S(1)}, u32[]{:S(2)}, u32[]{:S(2)}) async-start(bf16[8,32,2048]{2,1,0:T(8,128)(2,1)} %get-tuple-element.23), calls=%async_computation.2 | async-start | bytes 2097152 | tf_op jit(solution)/shard_map/all_to_all | solution.py:217
  79.1 1.6 collective-permute-start.4
  86.1 17.1 %collective-permute-start.5 = (bf16[2,256,512]{2,1,0:T(8,128)(2,1)}, bf16[2,256,512]{2,1,0:T(8,128)(2,1)S(1)}, u32[]{:S(2)}, u32[]{:S(2)}) collective-permute-start(bf16[2,256,512]{2,1,0:T(8,128)(2,1)} %get-tuple-element.30), channel_id=1, source_target_pairs={{0,32},{16,48},{32,0},{48,16},{1,33},{17,49},{33,1},{49,17},{2,34}... | collective-permute-start | bytes 1572872 | tf_op jit(solution)/shard_map/ppermute | solution.py:24
  97.7 23.2 %all-to-all-start.3 = ((bf16[32,32,512]{2,1,0:T(8,128)(2,1)}), bf16[32,32,512]{2,1,0:T(8,128)(2,1)S(1)}, u32[]{:S(2)}, u32[]{:S(2)}) async-start(bf16[32,32,512]{2,1,0:T(8,128)(2,1)} %bitcast.5), calls=%async_computation.3 | async-start | bytes 2097152 | tf_op jit(solution)/shard_map/all_to_all | solution.py:232
  120.9 6.6 %collective-permute-start.6 = (bf16[4,256,512]{2,1,0:T(8,128)(2,1)S(1)}, bf16[4,256,512]{2,1,0:T(8,128)(2,1)S(1)}, u32[]{:S(2)}, u32[]{:S(2)}) collective-permute-start(bf16[4,256,512]{2,1,0:T(8,128)(2,1)S(1)} %bitcast.11), channel_id=1, source_target_pairs={{0,1},{1,0},{2,3},{3,2},{4,5},{5,4},{6,7},{7,6},{8,9},{9,8},{10,11... | collective-permute-start | bytes 3145736 | tf_op jit(solution)/shard_map/ppermute | solution.py:24
  123.2 3.1 %copy-start = (bf16[2048,1792]{1,0:T(8,128)(2,1)S(1)}, bf16[2048,1792]{1,0:T(8,128)(2,1)}, u32[]{:S(2)}) copy-start(bf16[2048,1792]{1,0:T(8,128)(2,1)} %all-gather.3.cloned.1.call-done) | copy-start | bytes 22020100
  127.4 3.1 %copy-start.1 = (bf16[2048,1792]{1,0:T(8,128)(2,1)S(1)}, bf16[2048,1792]{1,0:T(8,128)(2,1)}, u32[]{:S(2)}) copy-start(bf16[2048,1792]{1,0:T(8,128)(2,1)} %all-gather.3.cloned.1.call-done) | copy-start | bytes 22020100
  130.5 1.7 %copy-start.9 = (bf16[2,256,512]{2,1,0:T(8,128)(2,1)S(1)}, bf16[2,256,512]{2,1,0:T(8,128)(2,1)}, u32[]{:S(2)}) copy-start(bf16[2,256,512]{2,1,0:T(8,128)(2,1)} %copy-done.8) | copy-start | bytes 1572868
  130.5 1.7 %copy-start.7 = (bf16[2,256,512]{2,1,0:T(8,128)(2,1)S(1)}, bf16[2,256,512]{2,1,0:T(8,128)(2,1)}, u32[]{:S(2)}) copy-start(bf16[2,256,512]{2,1,0:T(8,128)(2,1)} %copy-done.6) | copy-start | bytes 1572868
  131.7 22.1 %collective-permute-start.7 = (bf16[256,1792]{1,0:T(8,128)(2,1)S(1)}, bf16[256,1792]{1,0:T(8,128)(2,1)S(1)}, u32[]{:S(2)}, u32[]{:S(2)}) collective-permute-start(bf16[256,1792]{1,0:T(8,128)(2,1)S(1)} %shard_map.69), channel_id=1, source_target_pairs={{0,64},{64,0},{1,65},{65,1},{2,66},{66,2},{3,67},{67,3},{4,68},{68... | collective-permute-start | bytes 2752520 | tf_op jit(solution)/shard_map/ppermute | solution.py:24
  132.2 14.4 %collective-permute-start.8 = (bf16[2,256,512]{2,1,0:T(8,128)(2,1)S(1)}, bf16[2,256,512]{2,1,0:T(8,128)(2,1)S(1)}, u32[]{:S(2)}, u32[]{:S(2)}) collective-permute-start(bf16[2,256,512]{2,1,0:T(8,128)(2,1)S(1)} %copy-done.9), channel_id=1, source_target_pairs={{0,16},{16,32},{32,48},{48,0},{1,17},{17,33},{33,49},{49,1},{2,18}... | collective-permute-start | bytes 1572872 | tf_op jit(solution)/shard_map/ppermute | solution.py:24
  132.2 14.4 %collective-permute-start.9 = (bf16[2,256,512]{2,1,0:T(8,128)(2,1)S(1)}, bf16[2,256,512]{2,1,0:T(8,128)(2,1)S(1)}, u32[]{:S(2)}, u32[]{:S(2)}) collective-permute-start(bf16[2,256,512]{2,1,0:T(8,128)(2,1)S(1)} %copy-done.7), channel_id=1, source_target_pairs={{0,48},{16,0},{32,16},{48,32},{1,49},{17,1},{33,17},{49,33},{2,50}... | collective-permute-start | bytes 1572872 | tf_op jit(solution)/shard_map/ppermute | solution.py:24
  134.9 3.1 %copy-start.2 = (bf16[2048,1792]{1,0:T(8,128)(2,1)S(1)}, bf16[2048,1792]{1,0:T(8,128)(2,1)}, u32[]{:S(2)}) copy-start(bf16[2048,1792]{1,0:T(8,128)(2,1)} %all-gather.3.cloned.1.call-done) | copy-start | bytes 22020100
  138.0 10.1 %copy-start.3 = (bf16[2048,1792]{1,0:T(8,128)(2,1)S(1)}, bf16[2048,1792]{1,0:T(8,128)(2,1)}, u32[]{:S(2)}) copy-start(bf16[2048,1792]{1,0:T(8,128)(2,1)} %all-gather.3.cloned.1.call-done) | copy-start | bytes 22020100
  146.9 12.4 %collective-permute-start.10 = (bf16[512,256]{1,0:T(8,128)(2,1)S(1)}, bf16[512,256]{1,0:T(8,128)(2,1)S(1)}, u32[]{:S(2)}, u32[]{:S(2)}) collective-permute-start(bf16[512,256]{1,0:T(8,128)(2,1)S(1)} %get-tuple-element.40), channel_id=1, source_target_pairs={{0,64},{64,0},{1,65},{65,1},{2,66},{66,2},{3,67},{67,3},{4,68},{68... | collective-permute-start | bytes 786440 | tf_op jit(solution)/shard_map/ppermute | solution.py:24
  (6 other events, 5.6 us)
Sparse Core Ops, SparseCore 0:
  9.7 77.5 all-gather.2

commit v25 on v22

--- a/solution.py
+++ b/solution.py
@@ -220,13 +220,16 @@
         codes, own, codes_o, swap(message, "core"),
         flops=2 * tokens * rank * outs,
     )
-    terms = [terms[0]] + [shift(terms[k], "x", 4, k) for k in (1, 2, 3)]
+    terms = list(terms)
+    far = shift(terms[2], "x", 4, 2)
 
     barrier = lax.optimization_barrier
     blocks, row, terms[0] = barrier((blocks, row, terms[0]))
     split = call(spread_kernel, [like((4, 8, sub, 2 * width))], blocks, scratch=[pltpu.VMEM((sub, rank), BF)], flops=15 * 10**9)
     grad = lax.all_to_all(split.reshape(32, sub, 2 * width), ("x", "z", "y_hi"), 0, 0)
     grad = grad.reshape(4, half, 2 * width)
+    grad, far, plus, minus = barrier((grad, far, terms[1], terms[3]))
+    terms = [terms[0], shift(plus, "x", 4, 1), far, shift(minus, "x", 4, 3)]
     grad_o = swap(grad, "core")
     away = last_call(grad, grad_o, row, 0, BF)
     away = swap(away, "y_lo").astype(F32)

time: 168 us -> 174 us (1.036)
  blocking collectives: 47.2 us -> 23.9 us
  waiting for transfers between devices: 51.7 us -> 68.4 us
  starting transfers between devices: 20.5 us -> 28.3 us
  local copies, waits for them, and re-layouts: 10.6 us -> 16.5 us
    all_to_all x1 -> x0, blocking collectives: 23.3 us -> none  [local(): lax.all_to_all(split.reshape(32, sub, 2 * width), ('x', 'z', 'y_hi'), 0, 0)]
    ppermute x11, waiting for transfers between devices: 30.6 us -> 47.3 us  [shift(): lax.ppermute(array, axis, [(i, (i + step) % size) for i in range(size)])]
    unnamed x32 -> x34, local copies, waits for them, and re-layouts: 10.5 us -> 16.5 us
    all_to_all x0 -> x1, starting transfers between devices: none -> 5.71 us  [local(): lax.all_to_all(split.reshape(32, sub, 2 * width), ('x', 'z', 'y_hi'), 0, 0)]
    ppermute x11, starting transfers between devices: 13.4 us -> 15.4 us  [shift(): lax.ppermute(array, axis, [(i, (i + step) % size) for i in range(size)])]
  transfers between devices with their start and end apart: 14 -> 15, of which waited for: 10 -> 9; matrix products, arithmetic and copies ran while one was open for 1% -> 1% of each run, Pallas kernels for 11% -> 10%
where the time goes in v25:
time: 174 us; the launch traced here: 173 us
  waiting for transfers between devices  68.4 us (39%)
  starting transfers between devices  28.3 us (16%)
  blocking collectives  23.9 us (14%)
  Pallas kernels  19.1 us (11%)
  local copies, waits for them, and re-layouts  16.5 us (9%)
  between operations  14.2 us (8%)
  other arithmetic  2.59 us (1%)
    ppermute x11, waiting for transfers between devices, shift(): lax.ppermute(array, axis, [(i, (i + step) % size) for i in range(size)])  47.3 us
    all_to_all x1, blocking collectives, local(): blocks = lax.all_to_all(mine, ZY, 0, 0)  23.9 us
    unnamed x34, local copies, waits for them, and re-layouts  16.5 us
    ppermute x11, starting transfers between devices, shift(): lax.ppermute(array, axis, [(i, (i + step) % size) for i in range(size)])  15.4 us
    pallas_call x9, Pallas kernels, call(): pl.pallas_call(body, out_shape=outs if len(outs) > 1 else outs[0], in_spe...  13.3 us
    all_to_all x1, waiting for transfers between devices, local(): codes = lax.all_to_all(codes, ZY, 0, 0).reshape(rank, half)  11.8 us
    all_to_all x1, waiting for transfers between devices, local(): blocks = lax.all_to_all(partial, ZY, 0, 0)  8.71 us
    pallas_call x2, Pallas kernels, codes_call(): pl.pallas_call(functools.partial(codes_kernel, other), grid=(rank // step...  5.82 us
  transfers between devices with their start and end apart: 15, of which 9 were waited for; matrix products, arithmetic and copies ran while one was open for 1% of the time, Pallas kernels for 10%

profile of v25, /device:TPU:1, one launch (start us, length us, event | category | flops | bytes accessed | tf_op | source)
XLA Modules:
  0.0 173.0 jit_solution(3840235292029784959)
XLA Ops:
  8.7 3.1 %copy-done.2 = bf16[2048,1792]{1,0:T(8,128)(2,1)S(1)} copy-done((bf16[2048,1792]{1,0:T(8,128)(2,1)S(1)}, bf16[2048,1792]{1,0:T(8,128)(2,1)}, u32[]{:S(2)}) %copy-start.2) | copy-done | bytes 7340056
  11.7 2.9 %shard_map.60 = f32[2048,256]{1,0:T(8,128)S(1)} custom-call(bf16[512,1792]{1,0:T(8,128)(2,1)S(1)} %copy-done.3, bf16[2048,1792]{1,0:T(8,128)(2,1)S(1)} %copy-done.2), custom_call_target="tpu_custom_call" | custom-call | flops 1879048192 | bytes 7340032 | tf_op jit(solution)/shard_map/pallas_call | solution.py:69
  14.7 1.5 collective-permute-start
  16.3 2.9 %shard_map.59 = f32[2048,256]{1,0:T(8,128)S(1)} custom-call(bf16[512,1792]{1,0:T(8,128)(2,1)S(1)} %copy-done.3, bf16[2048,1792]{1,0:T(8,128)(2,1)S(1)} %copy-done.2), custom_call_target="tpu_custom_call" | custom-call | flops 1879048192 | bytes 7340032 | tf_op jit(solution)/shard_map/pallas_call | solution.py:69
  19.2 2.8 %collective-permute-done = f32[2048,256]{1,0:T(8,128)S(1)} collective-permute-done((f32[2048,256]{1,0:T(8,128)S(1)}, f32[2048,256]{1,0:T(8,128)S(1)}, u32[]{:S(2)}, u32[]{:S(2)}) %collective-permute-start) | collective-permute-done | bytes 2097184 | tf_op jit(solution)/shard_map/ppermute | solution.py:24
  22.4 23.9 %all_to_all.20.blocks = bf16[8,256,256]{2,1,0:T(8,128)(2,1)S(1)} all-to-all(bf16[8,256,256]{2,1,0:T(8,128)(2,1)S(1)} %bitcast.19), channel_id=1, replica_groups=mesh['y_lo'=2,'x'=4,'z'=4,'y_hi'=2,'core'=2] {'z','y_hi'}, dimensions={0} | all-to-all | bytes 2097152 | tf_op jit(solution)/shard_map/all_to_all | solution.py:201
  47.3 3.6 %all-to-all-start.1 = ((bf16[8,256,256]{2,1,0:T(8,128)(2,1)}), bf16[8,256,256]{2,1,0:T(8,128)(2,1)S(1)}, u32[]{:S(2)}, u32[]{:S(2)}) async-start(bf16[8,256,256]{2,1,0:T(8,128)(2,1)} %shard_map.61), calls=%async_computation.1 | async-start | bytes 2097152 | tf_op jit(solution)/shard_map/all_to_all | solution.py:203
  51.1 1.9 %collective-permute-start.1 = (bf16[512,256]{1,0:T(8,128)(2,1)S(1)}, bf16[512,256]{1,0:T(8,128)(2,1)S(1)}, u32[]{:S(2)}, u32[]{:S(2)}) collective-permute-start(bf16[512,256]{1,0:T(8,128)(2,1)S(1)} %bitcast.20), channel_id=1, source_target_pairs={{0,1},{1,0},{2,3},{3,2},{4,5},{5,4},{6,7},{7,6},{8,9},{9,8},{10,11... | collective-permute-start | bytes 786440 | tf_op jit(solution)/shard_map/ppermute | solution.py:24
  54.2 11.8 %all-to-all-done.1 = bf16[8,256,256]{2,1,0:T(8,128)(2,1)S(1)} async-done(((bf16[8,256,256]{2,1,0:T(8,128)(2,1)}), bf16[8,256,256]{2,1,0:T(8,128)(2,1)S(1)}, u32[]{:S(2)}, u32[]{:S(2)}) %all-to-all-start.1) | async-done | bytes 1048608 | tf_op jit(solution)/shard_map/all_to_all | solution.py:203
  66.0 5.7 %shard_map.62 = (bf16[256,512]{1,0:T(8,128)(2,1)S(1)}, bf16[256,512]{1,0:T(8,128)(2,1)S(1)}, bf16[8,32,2048]{2,1,0:T(8,128)(2,1)}) custom-call(bf16[2048,256]{1,0:T(8,128)(2,1)S(1)} %bitcast.14, bf16[512,256]{1,0:T(8,128)(2,1)S(1)} %bitcast.18, bf16[512,256]{1,0:T(8,128)(2,1)S(1)} %collective-permute-done.1.far, bf16[512,2048]{1,0:T(8,128)(2,1)} %a0.1, ...), custom_call_target="tpu_custom_call" | custom-call | flops 2147483648 | bytes 7340032 | tf_op jit(solution)/shard_map/pallas_call | solution.py:33
  72.4 3.1 %collective-permute-start.3 = (bf16[2048,256]{1,0:T(8,128)(2,1)S(1)}, bf16[2048,256]{1,0:T(8,128)(2,1)S(1)}, u32[]{:S(2)}, u32[]{:S(2)}) collective-permute-start(bf16[2048,256]{1,0:T(8,128)(2,1)S(1)} %bitcast.15), channel_id=1, source_target_pairs={{0,1},{1,0},{2,3},{3,2},{4,5},{5,4},{6,7},{7,6},{8,9},{9,8},{10,11... | collective-permute-start | bytes 3145736 | tf_op jit(solution)/shard_map/ppermute | solution.py:24
  75.5 3.6 %all-to-all-start.2 = ((bf16[8,32,2048]{2,1,0:T(8,128)(2,1)}), bf16[8,32,2048]{2,1,0:T(8,128)(2,1)S(1)}, u32[]{:S(2)}, u32[]{:S(2)}) async-start(bf16[8,32,2048]{2,1,0:T(8,128)(2,1)} %get-tuple-element.23), calls=%async_computation.2 | async-start | bytes 2097152 | tf_op jit(solution)/shard_map/all_to_all | solution.py:214
  79.2 1.5 collective-permute-done.4.message
  87.7 8.7 %all-to-all-done.2.blocks = bf16[8,32,2048]{2,1,0:T(8,128)(2,1)S(1)} async-done(((bf16[8,32,2048]{2,1,0:T(8,128)(2,1)}), bf16[8,32,2048]{2,1,0:T(8,128)(2,1)S(1)}, u32[]{:S(2)}, u32[]{:S(2)}) %all-to-all-start.2) | async-done | bytes 1048608 | tf_op jit(solution)/shard_map/all_to_all | solution.py:214
  97.7 5.7 %all-to-all-start.3 = ((bf16[32,32,512]{2,1,0:T(8,128)(2,1)}), bf16[32,32,512]{2,1,0:T(8,128)(2,1)S(1)}, u32[]{:S(2)}, u32[]{:S(2)}) async-start(bf16[32,32,512]{2,1,0:T(8,128)(2,1)} %bitcast.17), calls=%async_computation.3 | async-start | bytes 2097152 | tf_op jit(solution)/shard_map/all_to_all | solution.py:229
  103.4 2.8 %collective-permute-start.5 = (bf16[2,256,512]{2,1,0:T(8,128)(2,1)S(1)}, bf16[2,256,512]{2,1,0:T(8,128)(2,1)S(1)}, u32[]{:S(2)}, u32[]{:S(2)}) collective-permute-start(bf16[2,256,512]{2,1,0:T(8,128)(2,1)S(1)} %copy-done.12), channel_id=1, source_target_pairs={{0,32},{16,48},{32,0},{48,16},{1,33},{17,49},{33,1},{49,17},{2,34}... | collective-permute-start | bytes 1572872 | tf_op jit(solution)/shard_map/ppermute | solution.py:24
  106.2 22.5 %collective-permute-done.5.r2 = bf16[2,256,512]{2,1,0:T(8,128)(2,1)S(1)} collective-permute-done((bf16[2,256,512]{2,1,0:T(8,128)(2,1)S(1)}, bf16[2,256,512]{2,1,0:T(8,128)(2,1)S(1)}, u32[]{:S(2)}, u32[]{:S(2)}) %collective-permute-start.5) | collective-permute-done | bytes 524320 | tf_op jit(solution)/shard_map/ppermute | solution.py:24
  128.7 1.6 collective-permute-start.6
  130.3 3.1 %copy-done = bf16[2048,1792]{1,0:T(8,128)(2,1)S(1)} copy-done((bf16[2048,1792]{1,0:T(8,128)(2,1)S(1)}, bf16[2048,1792]{1,0:T(8,128)(2,1)}, u32[]{:S(2)}) %copy-start) | copy-done | bytes 7340056
  134.6 1.9 %copy-done.1 = bf16[2048,1792]{1,0:T(8,128)(2,1)S(1)} copy-done((bf16[2048,1792]{1,0:T(8,128)(2,1)S(1)}, bf16[2048,1792]{1,0:T(8,128)(2,1)}, u32[]{:S(2)}) %copy-start.1) | copy-done | bytes 7340056
  138.5 2.4 %collective-permute-start.9 = (bf16[2,256,512]{2,1,0:T(8,128)(2,1)S(1)}, bf16[2,256,512]{2,1,0:T(8,128)(2,1)S(1)}, u32[]{:S(2)}, u32[]{:S(2)}) collective-permute-start(bf16[2,256,512]{2,1,0:T(8,128)(2,1)S(1)} %copy-done.8), channel_id=1, source_target_pairs={{0,48},{16,0},{32,16},{48,32},{1,49},{17,1},{33,17},{49,33},{2,50}... | collective-permute-start | bytes 1572872 | tf_op jit(solution)/shard_map/ppermute | solution.py:24
  142.1 10.6 %collective-permute-done.8.r1 = bf16[2,256,512]{2,1,0:T(8,128)(2,1)S(1)} collective-permute-done((bf16[2,256,512]{2,1,0:T(8,128)(2,1)S(1)}, bf16[2,256,512]{2,1,0:T(8,128)(2,1)S(1)}, u32[]{:S(2)}, u32[]{:S(2)}) %collective-permute-start.8) | collective-permute-done | bytes 524320 | tf_op jit(solution)/shard_map/ppermute | solution.py:24
  155.2 4.5 %collective-permute-done.7 = bf16[256,1792]{1,0:T(8,128)(2,1)S(1)} collective-permute-done((bf16[256,1792]{1,0:T(8,128)(2,1)S(1)}, bf16[256,1792]{1,0:T(8,128)(2,1)S(1)}, u32[]{:S(2)}, u32[]{:S(2)}) %collective-permute-start.7) | collective-permute-done | bytes 917536 | tf_op jit(solution)/shard_map/ppermute | solution.py:24
  161.1 4.2 %collective-permute-done.10 = bf16[512,256]{1,0:T(8,128)(2,1)S(1)} collective-permute-done((bf16[512,256]{1,0:T(8,128)(2,1)S(1)}, bf16[512,256]{1,0:T(8,128)(2,1)S(1)}, u32[]{:S(2)}, u32[]{:S(2)}) %collective-permute-start.10) | collective-permute-done | bytes 262176 | tf_op jit(solution)/shard_map/ppermute | solution.py:24
  (57 shorter events, 22.4 us)
Async XLA Ops:
  7.2 1.5 copy-start.3
  7.2 89.2 %all-gather.3.cloned.1.call-start = ((), (), s32[]{:S(2)}) async-start(), calls=%async_computation.4 | async-start | bytes 9175040 | tf_op jit(solution)/shard_map/all_gather | solution.py:193
  8.7 3.1 %copy-start.2 = (bf16[2048,1792]{1,0:T(8,128)(2,1)S(1)}, bf16[2048,1792]{1,0:T(8,128)(2,1)}, u32[]{:S(2)}) copy-start(bf16[2048,1792]{1,0:T(8,128)(2,1)} %b.3) | copy-start | bytes 22020100
  14.7 7.4 %collective-permute-start = (f32[2048,256]{1,0:T(8,128)S(1)}, f32[2048,256]{1,0:T(8,128)S(1)}, u32[]{:S(2)}, u32[]{:S(2)}) collective-permute-start(f32[2048,256]{1,0:T(8,128)S(1)} %shard_map.60), channel_id=1, source_target_pairs={{0,1},{1,0},{2,3},{3,2},{4,5},{5,4},{6,7},{7,6},{8,9},{9,8},{10,11... | collective-permute-start | bytes 6291464 | tf_op jit(solution)/shard_map/ppermute | solution.py:24
  16.2 38.0 %collective-permute-start.2 = (bf16[512,2048]{1,0:T(8,128)(2,1)}, bf16[512,2048]{1,0:T(8,128)(2,1)}, u32[]{:S(2)}, u32[]{:S(2)}) collective-permute-start(bf16[512,2048]{1,0:T(8,128)(2,1)} %a0.1), channel_id=1, source_target_pairs={{0,1},{1,0},{2,3},{3,2},{4,5},{5,4},{6,7},{7,6},{8,9},{9,8},{10,11... | collective-permute-start | bytes 6291464 | tf_op jit(solution)/shard_map/ppermute | solution.py:24
  46.2 4.7 %copy-start.15 = (bf16[512,512]{1,0:T(8,128)(2,1)S(1)}, bf16[512,512]{1,0:T(8,128)(2,1)}, u32[]{:S(2)}) copy-start(bf16[512,512]{1,0:T(8,128)(2,1)} %param.5) | copy-start | bytes 1572868
  47.3 18.6 %all-to-all-start.1 = ((bf16[8,256,256]{2,1,0:T(8,128)(2,1)}), bf16[8,256,256]{2,1,0:T(8,128)(2,1)S(1)}, u32[]{:S(2)}, u32[]{:S(2)}) async-start(bf16[8,256,256]{2,1,0:T(8,128)(2,1)} %shard_map.61), calls=%async_computation.1 | async-start | bytes 2097152 | tf_op jit(solution)/shard_map/all_to_all | solution.py:203
  51.1 3.1 %collective-permute-start.1 = (bf16[512,256]{1,0:T(8,128)(2,1)S(1)}, bf16[512,256]{1,0:T(8,128)(2,1)S(1)}, u32[]{:S(2)}, u32[]{:S(2)}) collective-permute-start(bf16[512,256]{1,0:T(8,128)(2,1)S(1)} %bitcast.20), channel_id=1, source_target_pairs={{0,1},{1,0},{2,3},{3,2},{4,5},{5,4},{6,7},{7,6},{8,9},{9,8},{10,11... | collective-permute-start | bytes 786440 | tf_op jit(solution)/shard_map/ppermute | solution.py:24
  72.4 8.3 %collective-permute-start.3 = (bf16[2048,256]{1,0:T(8,128)(2,1)S(1)}, bf16[2048,256]{1,0:T(8,128)(2,1)S(1)}, u32[]{:S(2)}, u32[]{:S(2)}) collective-permute-start(bf16[2048,256]{1,0:T(8,128)(2,1)S(1)} %bitcast.15), channel_id=1, source_target_pairs={{0,1},{1,0},{2,3},{3,2},{4,5},{5,4},{6,7},{7,6},{8,9},{9,8},{10,11... | collective-permute-start | bytes 3145736 | tf_op jit(solution)/shard_map/ppermute | solution.py:24
  75.5 20.9 %all-to-all-start.2 = ((bf16[8,32,2048]{2,1,0:T(8,128)(2,1)}), bf16[8,32,2048]{2,1,0:T(8,128)(2,1)S(1)}, u32[]{:S(2)}, u32[]{:S(2)}) async-start(bf16[8,32,2048]{2,1,0:T(8,128)(2,1)} %get-tuple-element.23), calls=%async_computation.2 | async-start | bytes 2097152 | tf_op jit(solution)/shard_map/all_to_all | solution.py:214
  79.1 1.6 collective-permute-start.4
  81.8 1.2 copy-start.6
  97.7 5.7 %copy-start.12 = (bf16[2,256,512]{2,1,0:T(8,128)(2,1)S(1)}, bf16[2,256,512]{2,1,0:T(8,128)(2,1)}, u32[]{:S(2)}) copy-start(bf16[2,256,512]{2,1,0:T(8,128)(2,1)} %copy-done.11) | copy-start | bytes 1572868
  97.7 31.1 %all-to-all-start.3 = ((bf16[32,32,512]{2,1,0:T(8,128)(2,1)}), bf16[32,32,512]{2,1,0:T(8,128)(2,1)S(1)}, u32[]{:S(2)}, u32[]{:S(2)}) async-start(bf16[32,32,512]{2,1,0:T(8,128)(2,1)} %bitcast.17), calls=%async_computation.3 | async-start | bytes 2097152 | tf_op jit(solution)/shard_map/all_to_all | solution.py:229
  103.4 25.3 %collective-permute-start.5 = (bf16[2,256,512]{2,1,0:T(8,128)(2,1)S(1)}, bf16[2,256,512]{2,1,0:T(8,128)(2,1)S(1)}, u32[]{:S(2)}, u32[]{:S(2)}) collective-permute-start(bf16[2,256,512]{2,1,0:T(8,128)(2,1)S(1)} %copy-done.12), channel_id=1, source_target_pairs={{0,32},{16,48},{32,0},{48,16},{1,33},{17,49},{33,1},{49,17},{2,34}... | collective-permute-start | bytes 1572872 | tf_op jit(solution)/shard_map/ppermute | solution.py:24
  128.7 5.9 %collective-permute-start.6 = (bf16[4,256,512]{2,1,0:T(8,128)(2,1)S(1)}, bf16[4,256,512]{2,1,0:T(8,128)(2,1)S(1)}, u32[]{:S(2)}, u32[]{:S(2)}) collective-permute-start(bf16[4,256,512]{2,1,0:T(8,128)(2,1)S(1)} %bitcast.11), channel_id=1, source_target_pairs={{0,1},{1,0},{2,3},{3,2},{4,5},{5,4},{6,7},{7,6},{8,9},{9,8},{10,11... | collective-permute-start | bytes 3145736 | tf_op jit(solution)/shard_map/ppermute | solution.py:24
  130.3 3.1 %copy-start = (bf16[2048,1792]{1,0:T(8,128)(2,1)S(1)}, bf16[2048,1792]{1,0:T(8,128)(2,1)}, u32[]{:S(2)}) copy-start(bf16[2048,1792]{1,0:T(8,128)(2,1)} %all-gather.3.cloned.1.call-done) | copy-start | bytes 22020100
  133.4 3.1 %copy-start.1 = (bf16[2048,1792]{1,0:T(8,128)(2,1)S(1)}, bf16[2048,1792]{1,0:T(8,128)(2,1)}, u32[]{:S(2)}) copy-start(bf16[2048,1792]{1,0:T(8,128)(2,1)} %all-gather.3.cloned.1.call-done) | copy-start | bytes 22020100
  134.6 3.7 %copy-start.10 = (bf16[2,256,512]{2,1,0:T(8,128)(2,1)S(1)}, bf16[2,256,512]{2,1,0:T(8,128)(2,1)}, u32[]{:S(2)}) copy-start(bf16[2,256,512]{2,1,0:T(8,128)(2,1)} %copy-done.9) | copy-start | bytes 1572868
  134.6 3.9 %copy-start.8 = (bf16[2,256,512]{2,1,0:T(8,128)(2,1)S(1)}, bf16[2,256,512]{2,1,0:T(8,128)(2,1)}, u32[]{:S(2)}) copy-start(bf16[2,256,512]{2,1,0:T(8,128)(2,1)} %copy-done.7) | copy-start | bytes 1572868
  137.7 22.1 %collective-permute-start.7 = (bf16[256,1792]{1,0:T(8,128)(2,1)S(1)}, bf16[256,1792]{1,0:T(8,128)(2,1)S(1)}, u32[]{:S(2)}, u32[]{:S(2)}) collective-permute-start(bf16[256,1792]{1,0:T(8,128)(2,1)S(1)} %shard_map.68), channel_id=1, source_target_pairs={{0,64},{64,0},{1,65},{65,1},{2,66},{66,2},{3,67},{67,3},{4,68},{68... | collective-permute-start | bytes 2752520 | tf_op jit(solution)/shard_map/ppermute | solution.py:24
  138.2 14.4 %collective-permute-start.8 = (bf16[2,256,512]{2,1,0:T(8,128)(2,1)S(1)}, bf16[2,256,512]{2,1,0:T(8,128)(2,1)S(1)}, u32[]{:S(2)}, u32[]{:S(2)}) collective-permute-start(bf16[2,256,512]{2,1,0:T(8,128)(2,1)S(1)} %copy-done.10), channel_id=1, source_target_pairs={{0,16},{16,32},{32,48},{48,0},{1,17},{17,33},{33,49},{49,1},{2,18}... | collective-permute-start | bytes 1572872 | tf_op jit(solution)/shard_map/ppermute | solution.py:24
  138.5 14.2 %collective-permute-start.9 = (bf16[2,256,512]{2,1,0:T(8,128)(2,1)S(1)}, bf16[2,256,512]{2,1,0:T(8,128)(2,1)S(1)}, u32[]{:S(2)}, u32[]{:S(2)}) collective-permute-start(bf16[2,256,512]{2,1,0:T(8,128)(2,1)S(1)} %copy-done.8), channel_id=1, source_target_pairs={{0,48},{16,0},{32,16},{48,32},{1,49},{17,1},{33,17},{49,33},{2,50}... | collective-permute-start | bytes 1572872 | tf_op jit(solution)/shard_map/ppermute | solution.py:24
  153.0 12.4 %collective-permute-start.10 = (bf16[512,256]{1,0:T(8,128)(2,1)S(1)}, bf16[512,256]{1,0:T(8,128)(2,1)S(1)}, u32[]{:S(2)}, u32[]{:S(2)}) collective-permute-start(bf16[512,256]{1,0:T(8,128)(2,1)S(1)} %get-tuple-element.40), channel_id=1, source_target_pairs={{0,64},{64,0},{1,65},{65,1},{2,66},{66,2},{3,67},{67,3},{4,68},{68... | collective-permute-start | bytes 786440 | tf_op jit(solution)/shard_map/ppermute | solution.py:24
  (7 other events, 6.2 us)
Sparse Core Ops, SparseCore 0:
  9.7 77.5 all-gather.2

commit v26 on v20

--- a/solution.py
+++ b/solution.py
@@ -233,8 +233,8 @@
     here = last_call(grad, grad_o, row, 1, F32)
     term_o, term_a = call(term_sum_kernel, [like((width, outs), F32), like((width, outs))], *terms)
     term_a = swap(term_a, "y_lo").astype(F32)
-    here, term_o = barrier((here, term_o))
-    return (((term_o + term_a) * scale).T, (here + away) * scale)
+    grad_b, term_o = barrier(((here + away) * scale, term_o))
+    return (((term_o + term_a) * scale).T, grad_b)
 
 
 def solution(mesh):

time: 167 us -> 168 us (level)
  transfers between devices with their start and end apart: 14 -> 14, of which waited for: 8 -> 10; matrix products, arithmetic and copies ran while one was open for 1% -> 1% of each run, Pallas kernels for 11% -> 11%
where the time goes in v26:
time: 168 us; the launch traced here: 166 us
  waiting for transfers between devices  51.7 us (31%)
  blocking collectives  47.2 us (28%)
  starting transfers between devices  20.5 us (12%)
  Pallas kernels  19 us (11%)
  between operations  14.2 us (8%)
  local copies, waits for them, and re-layouts  11.6 us (7%)
  other arithmetic  1.81 us (1%)
    ppermute x11, waiting for transfers between devices, shift(): lax.ppermute(array, axis, [(i, (i + step) % size) for i in range(size)])  30.6 us
    all_to_all x1, blocking collectives, local(): blocks = lax.all_to_all(mine, ZY, 0, 0)  23.9 us
    all_to_all x1, blocking collectives, local(): lax.all_to_all(split.reshape(32, sub, 2 * width), ('x', 'z', 'y_hi'), 0, 0)  23.3 us
    ppermute x11, starting transfers between devices, shift(): lax.ppermute(array, axis, [(i, (i + step) % size) for i in range(size)])  13.4 us
    pallas_call x9, Pallas kernels, call(): pl.pallas_call(body, out_shape=outs if len(outs) > 1 else outs[0], in_spe...  13.2 us
    all_to_all x1, waiting for transfers between devices, local(): codes = lax.all_to_all(codes, ZY, 0, 0).reshape(rank, half)  11.8 us
    unnamed x33, local copies, waits for them, and re-layouts  11.5 us
    all_to_all x1, waiting for transfers between devices, local(): blocks = lax.all_to_all(partial, ZY, 0, 0)  8.72 us
  transfers between devices with their start and end apart: 14, of which 10 were waited for; matrix products, arithmetic and copies ran while one was open for 1% of the time, Pallas kernels for 11%

profile of v26, /device:TPU:1, one launch (start us, length us, event | category | flops | bytes accessed | tf_op | source)
XLA Modules:
  0.0 166.1 jit_solution(1501160356173653515)
XLA Ops:
  8.7 3.1 %copy-done = bf16[2048,1792]{1,0:T(8,128)(2,1)S(1)} copy-done((bf16[2048,1792]{1,0:T(8,128)(2,1)S(1)}, bf16[2048,1792]{1,0:T(8,128)(2,1)}, u32[]{:S(2)}) %copy-start) | copy-done | bytes 7340056
  11.7 2.9 %shard_map.60 = f32[2048,256]{1,0:T(8,128)S(1)} custom-call(bf16[512,1792]{1,0:T(8,128)(2,1)S(1)} %copy-done.1, bf16[2048,1792]{1,0:T(8,128)(2,1)S(1)} %copy-done), custom_call_target="tpu_custom_call" | custom-call | flops 1879048192 | bytes 7340032 | tf_op jit(solution)/shard_map/pallas_call | solution.py:69
  14.7 1.5 collective-permute-start
  16.3 2.9 %shard_map.59 = f32[2048,256]{1,0:T(8,128)S(1)} custom-call(bf16[512,1792]{1,0:T(8,128)(2,1)S(1)} %copy-done.1, bf16[2048,1792]{1,0:T(8,128)(2,1)S(1)} %copy-done), custom_call_target="tpu_custom_call" | custom-call | flops 1879048192 | bytes 7340032 | tf_op jit(solution)/shard_map/pallas_call | solution.py:69
  19.2 2.8 %collective-permute-done = f32[2048,256]{1,0:T(8,128)S(1)} collective-permute-done((f32[2048,256]{1,0:T(8,128)S(1)}, f32[2048,256]{1,0:T(8,128)S(1)}, u32[]{:S(2)}, u32[]{:S(2)}) %collective-permute-start) | collective-permute-done | bytes 2097184 | tf_op jit(solution)/shard_map/ppermute | solution.py:24
  22.4 23.9 %all_to_all.20.blocks = bf16[8,256,256]{2,1,0:T(8,128)(2,1)S(1)} all-to-all(bf16[8,256,256]{2,1,0:T(8,128)(2,1)S(1)} %bitcast.23), channel_id=1, replica_groups=mesh['y_lo'=2,'x'=4,'z'=4,'y_hi'=2,'core'=2] {'z','y_hi'}, dimensions={0} | all-to-all | bytes 2097152 | tf_op jit(solution)/shard_map/all_to_all | solution.py:201
  47.3 3.6 %all-to-all-start.1 = ((bf16[8,256,256]{2,1,0:T(8,128)(2,1)}), bf16[8,256,256]{2,1,0:T(8,128)(2,1)S(1)}, u32[]{:S(2)}, u32[]{:S(2)}) async-start(bf16[8,256,256]{2,1,0:T(8,128)(2,1)} %shard_map.61), calls=%async_computation.1 | async-start | bytes 2097152 | tf_op jit(solution)/shard_map/all_to_all | solution.py:203
  51.1 1.9 %collective-permute-start.1 = (bf16[512,256]{1,0:T(8,128)(2,1)S(1)}, bf16[512,256]{1,0:T(8,128)(2,1)S(1)}, u32[]{:S(2)}, u32[]{:S(2)}) collective-permute-start(bf16[512,256]{1,0:T(8,128)(2,1)S(1)} %bitcast.24), channel_id=1, source_target_pairs={{0,1},{1,0},{2,3},{3,2},{4,5},{5,4},{6,7},{7,6},{8,9},{9,8},{10,11... | collective-permute-start | bytes 786440 | tf_op jit(solution)/shard_map/ppermute | solution.py:24
  54.2 11.8 %all-to-all-done.1 = bf16[8,256,256]{2,1,0:T(8,128)(2,1)S(1)} async-done(((bf16[8,256,256]{2,1,0:T(8,128)(2,1)}), bf16[8,256,256]{2,1,0:T(8,128)(2,1)S(1)}, u32[]{:S(2)}, u32[]{:S(2)}) %all-to-all-start.1) | async-done | bytes 1048608 | tf_op jit(solution)/shard_map/all_to_all | solution.py:203
  66.0 5.7 %shard_map.62 = (bf16[256,512]{1,0:T(8,128)(2,1)S(1)}, bf16[256,512]{1,0:T(8,128)(2,1)S(1)}, bf16[8,32,2048]{2,1,0:T(8,128)(2,1)}) custom-call(bf16[2048,256]{1,0:T(8,128)(2,1)S(1)} %bitcast.18, bf16[512,256]{1,0:T(8,128)(2,1)S(1)} %bitcast.22, bf16[512,256]{1,0:T(8,128)(2,1)S(1)} %collective-permute-done.1.far, bf16[512,2048]{1,0:T(8,128)(2,1)} %a0.1, ...), custom_call_target="tpu_custom_call" | custom-call | flops 2147483648 | bytes 7340032 | tf_op jit(solution)/shard_map/pallas_call | solution.py:33
  72.4 3.1 %collective-permute-start.3 = (bf16[2048,256]{1,0:T(8,128)(2,1)S(1)}, bf16[2048,256]{1,0:T(8,128)(2,1)S(1)}, u32[]{:S(2)}, u32[]{:S(2)}) collective-permute-start(bf16[2048,256]{1,0:T(8,128)(2,1)S(1)} %bitcast.19), channel_id=1, source_target_pairs={{0,1},{1,0},{2,3},{3,2},{4,5},{5,4},{6,7},{7,6},{8,9},{9,8},{10,11... | collective-permute-start | bytes 3145736 | tf_op jit(solution)/shard_map/ppermute | solution.py:24
  75.5 3.6 %all-to-all-start.2 = ((bf16[8,32,2048]{2,1,0:T(8,128)(2,1)}), bf16[8,32,2048]{2,1,0:T(8,128)(2,1)S(1)}, u32[]{:S(2)}, u32[]{:S(2)}) async-start(bf16[8,32,2048]{2,1,0:T(8,128)(2,1)} %get-tuple-element.19), calls=%async_computation.2 | async-start | bytes 2097152 | tf_op jit(solution)/shard_map/all_to_all | solution.py:214
  79.2 1.5 collective-permute-done.4.message
  81.8 1.2 copy-done.3
  84.0 1.2 shard_map.63
  87.7 8.7 %all-to-all-done.2.blocks = bf16[8,32,2048]{2,1,0:T(8,128)(2,1)S(1)} async-done(((bf16[8,32,2048]{2,1,0:T(8,128)(2,1)}), bf16[8,32,2048]{2,1,0:T(8,128)(2,1)S(1)}, u32[]{:S(2)}, u32[]{:S(2)}) %all-to-all-start.2) | async-done | bytes 1048608 | tf_op jit(solution)/shard_map/all_to_all | solution.py:214
  96.7 23.3 %all_to_all.21 = bf16[32,32,512]{2,1,0:T(8,128)(2,1)S(1)} all-to-all(bf16[32,32,512]{2,1,0:T(8,128)(2,1)S(1)} %bitcast.21), channel_id=1, replica_groups=mesh['y_lo'=2,'x'=4,'z'=4,'y_hi'=2,'core'=2] {'x','z','y_hi'}, dimensions={0} | all-to-all | bytes 2097152 | tf_op jit(solution)/shard_map/all_to_all | solution.py:228
  120.0 2.3 %collective-permute-start.5 = (bf16[4,256,512]{2,1,0:T(8,128)(2,1)S(1)}, bf16[4,256,512]{2,1,0:T(8,128)(2,1)S(1)}, u32[]{:S(2)}, u32[]{:S(2)}) collective-permute-start(bf16[4,256,512]{2,1,0:T(8,128)(2,1)S(1)} %bitcast.15), channel_id=1, source_target_pairs={{0,1},{1,0},{2,3},{3,2},{4,5},{5,4},{6,7},{7,6},{8,9},{9,8},{10,11... | collective-permute-start | bytes 3145736 | tf_op jit(solution)/shard_map/ppermute | solution.py:24
  126.3 2.0 %collective-permute-start.8 = (bf16[2,256,512]{2,1,0:T(8,128)(2,1)S(1)}, bf16[2,256,512]{2,1,0:T(8,128)(2,1)S(1)}, u32[]{:S(2)}, u32[]{:S(2)}) collective-permute-start(bf16[2,256,512]{2,1,0:T(8,128)(2,1)S(1)} %copy-done.7), channel_id=1, source_target_pairs={{0,32},{16,48},{32,0},{48,16},{1,33},{17,49},{33,1},{49,17},{2,34}... | collective-permute-start | bytes 1572872 | tf_op jit(solution)/shard_map/ppermute | solution.py:24
  129.0 12.0 %collective-permute-done.7.r1 = bf16[2,256,512]{2,1,0:T(8,128)(2,1)S(1)} collective-permute-done((bf16[2,256,512]{2,1,0:T(8,128)(2,1)S(1)}, bf16[2,256,512]{2,1,0:T(8,128)(2,1)S(1)}, u32[]{:S(2)}, u32[]{:S(2)}) %collective-permute-start.7) | collective-permute-done | bytes 524320 | tf_op jit(solution)/shard_map/ppermute | solution.py:24
  141.0 9.9 %collective-permute-done.8.r2 = bf16[2,256,512]{2,1,0:T(8,128)(2,1)S(1)} collective-permute-done((bf16[2,256,512]{2,1,0:T(8,128)(2,1)S(1)}, bf16[2,256,512]{2,1,0:T(8,128)(2,1)S(1)}, u32[]{:S(2)}, u32[]{:S(2)}) %collective-permute-start.8) | collective-permute-done | bytes 524320 | tf_op jit(solution)/shard_map/ppermute | solution.py:24
  154.4 1.2 shard_map.66
  155.5 1.4 add_multiply_fusion
  156.9 1.2 collective-permute-done.10
  (56 shorter events, 19.1 us)
Async XLA Ops:
  7.2 1.5 copy-start.1
  7.2 89.2 %all-gather.3.cloned.1.call-start = ((), (), s32[]{:S(2)}) async-start(), calls=%async_computation.4 | async-start | bytes 9175040 | tf_op jit(solution)/shard_map/all_gather | solution.py:193
  8.7 3.1 %copy-start = (bf16[2048,1792]{1,0:T(8,128)(2,1)S(1)}, bf16[2048,1792]{1,0:T(8,128)(2,1)}, u32[]{:S(2)}) copy-start(bf16[2048,1792]{1,0:T(8,128)(2,1)} %b.3) | copy-start | bytes 22020100
  14.7 7.4 %collective-permute-start = (f32[2048,256]{1,0:T(8,128)S(1)}, f32[2048,256]{1,0:T(8,128)S(1)}, u32[]{:S(2)}, u32[]{:S(2)}) collective-permute-start(f32[2048,256]{1,0:T(8,128)S(1)} %shard_map.60), channel_id=1, source_target_pairs={{0,1},{1,0},{2,3},{3,2},{4,5},{5,4},{6,7},{7,6},{8,9},{9,8},{10,11... | collective-permute-start | bytes 6291464 | tf_op jit(solution)/shard_map/ppermute | solution.py:24
  16.2 38.0 %collective-permute-start.2 = (bf16[512,2048]{1,0:T(8,128)(2,1)}, bf16[512,2048]{1,0:T(8,128)(2,1)}, u32[]{:S(2)}, u32[]{:S(2)}) collective-permute-start(bf16[512,2048]{1,0:T(8,128)(2,1)} %a0.1), channel_id=1, source_target_pairs={{0,1},{1,0},{2,3},{3,2},{4,5},{5,4},{6,7},{7,6},{8,9},{9,8},{10,11... | collective-permute-start | bytes 6291464 | tf_op jit(solution)/shard_map/ppermute | solution.py:24
  46.2 4.7 %copy-start.12 = (bf16[512,512]{1,0:T(8,128)(2,1)S(1)}, bf16[512,512]{1,0:T(8,128)(2,1)}, u32[]{:S(2)}) copy-start(bf16[512,512]{1,0:T(8,128)(2,1)} %param.5) | copy-start | bytes 1572868
  47.3 18.6 %all-to-all-start.1 = ((bf16[8,256,256]{2,1,0:T(8,128)(2,1)}), bf16[8,256,256]{2,1,0:T(8,128)(2,1)S(1)}, u32[]{:S(2)}, u32[]{:S(2)}) async-start(bf16[8,256,256]{2,1,0:T(8,128)(2,1)} %shard_map.61), calls=%async_computation.1 | async-start | bytes 2097152 | tf_op jit(solution)/shard_map/all_to_all | solution.py:203
  51.1 3.1 %collective-permute-start.1 = (bf16[512,256]{1,0:T(8,128)(2,1)S(1)}, bf16[512,256]{1,0:T(8,128)(2,1)S(1)}, u32[]{:S(2)}, u32[]{:S(2)}) collective-permute-start(bf16[512,256]{1,0:T(8,128)(2,1)S(1)} %bitcast.24), channel_id=1, source_target_pairs={{0,1},{1,0},{2,3},{3,2},{4,5},{5,4},{6,7},{7,6},{8,9},{9,8},{10,11... | collective-permute-start | bytes 786440 | tf_op jit(solution)/shard_map/ppermute | solution.py:24
  72.4 8.3 %collective-permute-start.3 = (bf16[2048,256]{1,0:T(8,128)(2,1)S(1)}, bf16[2048,256]{1,0:T(8,128)(2,1)S(1)}, u32[]{:S(2)}, u32[]{:S(2)}) collective-permute-start(bf16[2048,256]{1,0:T(8,128)(2,1)S(1)} %bitcast.19), channel_id=1, source_target_pairs={{0,1},{1,0},{2,3},{3,2},{4,5},{5,4},{6,7},{7,6},{8,9},{9,8},{10,11... | collective-permute-start | bytes 3145736 | tf_op jit(solution)/shard_map/ppermute | solution.py:24
  75.5 20.9 %all-to-all-start.2 = ((bf16[8,32,2048]{2,1,0:T(8,128)(2,1)}), bf16[8,32,2048]{2,1,0:T(8,128)(2,1)S(1)}, u32[]{:S(2)}, u32[]{:S(2)}) async-start(bf16[8,32,2048]{2,1,0:T(8,128)(2,1)} %get-tuple-element.19), calls=%async_computation.2 | async-start | bytes 2097152 | tf_op jit(solution)/shard_map/all_to_all | solution.py:214
  79.1 1.6 collective-permute-start.4
  80.7 1.1 copy-start.2
  81.8 1.2 copy-start.3
  96.4 25.9 %slice-start = ((s8[7340032]{0:T(1024)(128)(4,1)}), s8[4194304]{0:T(1024)(128)(4,1)S(1)}, s32[]{:S(2)}) async-start(s8[7340032]{0:T(1024)(128)(4,1)} %bitcast.9), calls=%async_computation.5 | async-start | bytes 8388608
  96.4 25.9 %slice-start.1 = ((s8[7340032]{0:T(1024)(128)(4,1)}), s8[3145728]{0:T(1024)(128)(4,1)S(1)}, s32[]{:S(2)}) async-start(s8[7340032]{0:T(1024)(128)(4,1)} %bitcast.9), calls=%async_computation.6 | async-start | bytes 6291456
  120.0 4.6 %collective-permute-start.5 = (bf16[4,256,512]{2,1,0:T(8,128)(2,1)S(1)}, bf16[4,256,512]{2,1,0:T(8,128)(2,1)S(1)}, u32[]{:S(2)}, u32[]{:S(2)}) collective-permute-start(bf16[4,256,512]{2,1,0:T(8,128)(2,1)S(1)} %bitcast.15), channel_id=1, source_target_pairs={{0,1},{1,0},{2,3},{3,2},{4,5},{5,4},{6,7},{7,6},{8,9},{9,8},{10,11... | collective-permute-start | bytes 3145736 | tf_op jit(solution)/shard_map/ppermute | solution.py:24
  123.4 2.8 %copy-start.9 = (bf16[2,256,512]{2,1,0:T(8,128)(2,1)S(1)}, bf16[2,256,512]{2,1,0:T(8,128)(2,1)}, u32[]{:S(2)}) copy-start(bf16[2,256,512]{2,1,0:T(8,128)(2,1)} %copy-done.8) | copy-start | bytes 1572868
  123.5 2.8 %copy-start.7 = (bf16[2,256,512]{2,1,0:T(8,128)(2,1)S(1)}, bf16[2,256,512]{2,1,0:T(8,128)(2,1)}, u32[]{:S(2)}) copy-start(bf16[2,256,512]{2,1,0:T(8,128)(2,1)} %copy-done.6) | copy-start | bytes 1572868
  123.5 4.8 %copy-start.5 = (bf16[2,256,512]{2,1,0:T(8,128)(2,1)S(1)}, bf16[2,256,512]{2,1,0:T(8,128)(2,1)}, u32[]{:S(2)}) copy-start(bf16[2,256,512]{2,1,0:T(8,128)(2,1)} %copy-done.4) | copy-start | bytes 1572868
  125.7 29.8 %collective-permute-start.6 = (bf16[256,1792]{1,0:T(8,128)(2,1)S(1)}, bf16[256,1792]{1,0:T(8,128)(2,1)S(1)}, u32[]{:S(2)}, u32[]{:S(2)}) collective-permute-start(bf16[256,1792]{1,0:T(8,128)(2,1)S(1)} %shard_map.68), channel_id=1, source_target_pairs={{0,64},{64,0},{1,65},{65,1},{2,66},{66,2},{3,67},{67,3},{4,68},{68... | collective-permute-start | bytes 2752520 | tf_op jit(solution)/shard_map/ppermute | solution.py:24
  126.3 14.7 %collective-permute-start.7 = (bf16[2,256,512]{2,1,0:T(8,128)(2,1)S(1)}, bf16[2,256,512]{2,1,0:T(8,128)(2,1)S(1)}, u32[]{:S(2)}, u32[]{:S(2)}) collective-permute-start(bf16[2,256,512]{2,1,0:T(8,128)(2,1)S(1)} %copy-done.9), channel_id=1, source_target_pairs={{0,16},{16,32},{32,48},{48,0},{1,17},{17,33},{33,49},{49,1},{2,18}... | collective-permute-start | bytes 1572872 | tf_op jit(solution)/shard_map/ppermute | solution.py:24
  126.3 24.6 %collective-permute-start.8 = (bf16[2,256,512]{2,1,0:T(8,128)(2,1)S(1)}, bf16[2,256,512]{2,1,0:T(8,128)(2,1)S(1)}, u32[]{:S(2)}, u32[]{:S(2)}) collective-permute-start(bf16[2,256,512]{2,1,0:T(8,128)(2,1)S(1)} %copy-done.7), channel_id=1, source_target_pairs={{0,32},{16,48},{32,0},{48,16},{1,33},{17,49},{33,1},{49,17},{2,34}... | collective-permute-start | bytes 1572872 | tf_op jit(solution)/shard_map/ppermute | solution.py:24
  128.3 23.6 %collective-permute-start.9 = (bf16[2,256,512]{2,1,0:T(8,128)(2,1)S(1)}, bf16[2,256,512]{2,1,0:T(8,128)(2,1)S(1)}, u32[]{:S(2)}, u32[]{:S(2)}) collective-permute-start(bf16[2,256,512]{2,1,0:T(8,128)(2,1)S(1)} %copy-done.5), channel_id=1, source_target_pairs={{0,48},{16,0},{32,16},{48,32},{1,49},{17,1},{33,17},{49,33},{2,50}... | collective-permute-start | bytes 1572872 | tf_op jit(solution)/shard_map/ppermute | solution.py:24
  152.1 6.1 %collective-permute-start.10 = (bf16[256,512]{1,0:T(8,128)(2,1)S(1)}, bf16[256,512]{1,0:T(8,128)(2,1)S(1)}, u32[]{:S(2)}, u32[]{:S(2)}) collective-permute-start(bf16[256,512]{1,0:T(8,128)(2,1)S(1)} %get-tuple-element.32), channel_id=1, source_target_pairs={{0,64},{64,0},{1,65},{65,1},{2,66},{66,2},{3,67},{67,3},{4,68},{68... | collective-permute-start | bytes 786440 | tf_op jit(solution)/shard_map/ppermute | solution.py:24
  (5 other events, 4.1 us)
Sparse Core Ops, SparseCore 0:
  9.7 77.5 all-gather.2
